TPU v7x, 512 devices: a whole 4x8x8 slice. The times are simulated.
512 devices in a mesh: row: 16 (over y_hi, z), col: 8 (over y_lo, core), depth: 4 (over x).
Axes of the slice: x: 4, y: 8 (y_hi: 2, y_lo: 4; y = y_hi * 4 + y_lo), z: 8, core: 2. Of those that a mesh axis runs over, the one named last changes fastest.
Arguments:
- integrals: bfloat16 [4096, 16384], P('row', ('col', 'depth')), may hold values from -0.046875 to 0.046875
- amplitudes: bfloat16 [16384, 4096], P(('row', 'depth'), 'col'), may hold values from -6 to 6
Outputs:
- ladder: float32 [4096, 4096], P('row', ('col', 'depth'))
All inputs are finite; a program needn't handle non-finite values.
Results may differ from a plain program's by a relative error of at most 0.0003.
Values may be sent and summed in bfloat16 or wider, within the bound.
No kernel may reach another device: no remote copies, remote signals or barrier semaphores. Data moves between devices by JAX's collectives and lax.ppermute only.
A program may use at most 64 MiB of HBM per device.

v0:
```python
import jax
import jax.numpy as jnp
from jax import lax
from jax.sharding import PartitionSpec as P


def shifted(x, axis, by):
    size = lax.axis_size(axis)
    return lax.ppermute(x, axis, [(i, (i + by) % size) for i in range(size)])


def bit_count(value):
    return value.bit_length() - 1


def column_step(tile_data, offset):
    return shifted(tile_data, "col", offset)


def row_step(tile_data, offset):
    return shifted(tile_data, "row", offset)


def turn_columns(tile_data, amount, column_count):
    for bit_level in range(bit_count(column_count)):
        arrived = column_step(tile_data, -(1 << bit_level))
        tile_data = jnp.where(amount >> bit_level & 1 == 1, arrived, tile_data)
    return tile_data


def turn_rows(tile_data, amount, block_count):
    for bit_level in range(bit_count(block_count)):
        arrived = row_step(tile_data, -(1 << bit_level))
        tile_data = jnp.where(amount >> bit_level & 1 == 1, arrived, tile_data)
    return tile_data


def per_device(integrals, amplitudes):
    row_count = lax.axis_size("row")
    column_count = lax.axis_size("col")
    layer_count = lax.axis_size("depth")
    step_count = row_count // layer_count
    spread = row_count // column_count
    row_index = lax.axis_index("row")
    column_index = lax.axis_index("col")
    layer_index = lax.axis_index("depth")
    slab_shift = (row_index + layer_index * step_count) // spread % column_count
    doubles_shift = (spread * column_index + layer_index * step_count) % row_count
    slab_tile, doubles_tile = (
        lax.all_gather(integrals[None], "depth", axis=0, tiled=True),
        lax.all_gather(amplitudes, "depth", axis=0, tiled=True),
    )
    slab_tile = turn_columns(slab_tile, slab_shift, column_count)
    doubles_tile = turn_rows(doubles_tile, doubles_shift, row_count)
    piece_width = integrals.shape[1]
    piece_group = layer_count // spread
    partial_value = jnp.zeros((integrals.shape[0], amplitudes.shape[1]), jnp.float32)
    for step_number in range(step_count):
        current = (row_index + doubles_shift + step_number) % row_count
        element = current % spread
        slab_part = lax.dynamic_slice_in_dim(slab_tile, element * piece_group, piece_group, 0)
        doubles_part = doubles_tile.reshape(piece_group, piece_width, amplitudes.shape[1])
        partial_value = partial_value + jnp.einsum(
            "dmk,dkn->mn", slab_part, doubles_part, preferred_element_type=jnp.float32
        )
        if step_number + 1 < step_count:
            arrived = column_step(slab_tile, -1)
            slab_tile = jnp.where((current + 1) % spread == 0, arrived, slab_tile)
            doubles_tile = row_step(doubles_tile, -1)
    return lax.psum_scatter(partial_value, "depth", scatter_dimension=1, tiled=True)


def solution(mesh):
    return jax.shard_map(
        per_device,
        mesh=mesh,
        in_specs=(P("row", ("col", "depth")), P(("row", "depth"), "col")),
        out_specs=P("row", ("col", "depth")),
        check_vma=False,
    )
```

profile of v0, /device:TPU:56, one launch (start us, length us, event | category | flops | bytes accessed | tf_op | source)
XLA Modules:
  0.0 544.2 jit_solution(7205707420804933608)
XLA Ops:
  6.5 0.0 all-gather.4.cloned.1.call-start
  6.5 0.7 all-gather.4.cloned.1.call-update
  7.3 0.0 all-gather.6.cloned.1.call-start
  7.3 0.7 all-gather.6.cloned.1.call-update
  8.0 0.0 reduce-scatter.2.cloned.1.call-start
  8.1 34.8 %all-gather.4.cloned.1.call-done = bf16[1024,512]{1,0:T(8,128)(2,1)} async-done(((bf16[256,512]{1,0:T(8,128)(2,1)}), bf16[1024,512]{1,0:T(8,128)(2,1)}) %all-gather.4.cloned.1.call-update) | async-done | bytes 1048592 | tf_op jit(solution)/shard_map/all_gather | solution.py:51
  42.8 8.5 %collective-permute-start.3 = (bf16[1024,512]{1,0:T(8,128)(2,1)}, bf16[1024,512]{1,0:T(8,128)(2,1)S(1)}, u32[]{:S(2)}, u32[]{:S(2)}) collective-permute-start(bf16[1024,512]{1,0:T(8,128)(2,1)} %all-gather.4.cloned.1.call-done), channel_id=1, source_target_pairs={{0,480},{32,0},{64,32},{96,64},{128,96},{160,128},{192,160},{224,1... | collective-permute-start | bytes 3145736 | tf_op jit(solution)/shard_map/ppermute | solution.py:9
  51.3 23.3 %all-gather.6.cloned.1.call-done = bf16[1024,512]{1,0:T(8,128)(2,1)} async-done(((bf16[256,512]{1,0:T(8,128)(2,1)}), bf16[1024,512]{1,0:T(8,128)(2,1)}) %all-gather.6.cloned.1.call-update) | async-done | bytes 1048592 | tf_op jit(solution)/shard_map/all_gather | solution.py:50
  74.6 1.9 collective-permute-start
  76.6 12.6 %collective-permute-done.3 = bf16[1024,512]{1,0:T(8,128)(2,1)S(1)} collective-permute-done((bf16[1024,512]{1,0:T(8,128)(2,1)}, bf16[1024,512]{1,0:T(8,128)(2,1)S(1)}, u32[]{:S(2)}, u32[]{:S(2)}) %collective-permute-start.3) | collective-permute-done | bytes 1048608 | tf_op jit(solution)/shard_map/ppermute | solution.py:9
  89.2 1.3 broadcast_select_fusion.2
  90.5 1.9 collective-permute-start.4
  92.5 34.5 %collective-permute-done = bf16[4,256,512]{2,1,0:T(8,128)(2,1)} collective-permute-done((bf16[4,256,512]{2,1,0:T(8,128)(2,1)}, bf16[4,256,512]{2,1,0:T(8,128)(2,1)}, u32[]{:S(2)}, u32[]{:S(2)}) %collective-permute-start) | collective-permute-done | bytes 1048608 | tf_op jit(solution)/shard_map/ppermute | solution.py:9
  127.0 0.1 broadcast_select_fusion.6
  127.1 3.2 collective-permute-start.1
  130.4 28.5 %collective-permute-done.4 = bf16[1024,512]{1,0:T(8,128)(2,1)} collective-permute-done((bf16[1024,512]{1,0:T(8,128)(2,1)S(1)}, bf16[1024,512]{1,0:T(8,128)(2,1)}, u32[]{:S(2)}, u32[]{:S(2)}) %collective-permute-start.4) | collective-permute-done | bytes 1048608 | tf_op jit(solution)/shard_map/ppermute | solution.py:9
  158.9 1.1 broadcast_select_fusion.3
  160.0 1.9 collective-permute-start.5
  161.9 56.2 %collective-permute-done.1 = bf16[4,256,512]{2,1,0:T(8,128)(2,1)} collective-permute-done((bf16[4,256,512]{2,1,0:T(8,128)(2,1)S(1)}, bf16[4,256,512]{2,1,0:T(8,128)(2,1)}, u32[]{:S(2)}, u32[]{:S(2)}) %collective-permute-start.1) | collective-permute-done | bytes 1048608 | tf_op jit(solution)/shard_map/ppermute | solution.py:9
  218.1 0.1 broadcast_select_fusion.7
  218.2 1.9 collective-permute-start.2
  220.1 39.8 %collective-permute-done.5 = bf16[1024,512]{1,0:T(8,128)(2,1)S(1)} collective-permute-done((bf16[1024,512]{1,0:T(8,128)(2,1)}, bf16[1024,512]{1,0:T(8,128)(2,1)S(1)}, u32[]{:S(2)}, u32[]{:S(2)}) %collective-permute-start.5) | collective-permute-done | bytes 1048608 | tf_op jit(solution)/shard_map/ppermute | solution.py:9
  259.9 0.1 broadcast_select_fusion.4
  260.0 1.9 collective-permute-start.6
  262.0 54.4 %collective-permute-done.2 = bf16[4,256,512]{2,1,0:T(8,128)(2,1)} collective-permute-done((bf16[4,256,512]{2,1,0:T(8,128)(2,1)S(1)}, bf16[4,256,512]{2,1,0:T(8,128)(2,1)}, u32[]{:S(2)}, u32[]{:S(2)}) %collective-permute-start.2) | collective-permute-done | bytes 1048608 | tf_op jit(solution)/shard_map/ppermute | solution.py:9
  316.4 1.3 broadcast_select_fusion.8
  317.7 1.9 collective-permute-start.7
  319.7 0.0 collective-permute-done.6
  319.7 1.3 broadcast_select_fusion.5
  321.0 1.9 collective-permute-start.8
  323.0 29.7 %collective-permute-done.7 = bf16[4,256,512]{2,1,0:T(8,128)(2,1)} collective-permute-done((bf16[4,256,512]{2,1,0:T(8,128)(2,1)S(1)}, bf16[4,256,512]{2,1,0:T(8,128)(2,1)}, u32[]{:S(2)}, u32[]{:S(2)}) %collective-permute-start.7) | collective-permute-done | bytes 1048608 | tf_op jit(solution)/shard_map/ppermute | solution.py:9
  352.7 0.1 broadcast_select_fusion.1
  352.8 5.8 %collective-permute-start.9 = (bf16[4,256,512]{2,1,0:T(8,128)(2,1)S(1)}, bf16[4,256,512]{2,1,0:T(8,128)(2,1)}, u32[]{:S(2)}, u32[]{:S(2)}) collective-permute-start(bf16[4,256,512]{2,1,0:T(8,128)(2,1)S(1)} %broadcast_select_fusion.1), channel_id=1, source_target_pairs={{0,28},{4,0},{8,4},{12,8},{16,12},{20,16},{24,20},{28,24},{1,29},{... | collective-permute-start | bytes 3145736 | tf_op jit(solution)/shard_map/ppermute | solution.py:9
  358.7 20.4 %collective-permute-done.8 = bf16[1024,512]{1,0:T(8,128)(2,1)} collective-permute-done((bf16[1024,512]{1,0:T(8,128)(2,1)S(1)}, bf16[1024,512]{1,0:T(8,128)(2,1)}, u32[]{:S(2)}, u32[]{:S(2)}) %collective-permute-start.8) | collective-permute-done | bytes 1048608 | tf_op jit(solution)/shard_map/ppermute | solution.py:9
  379.1 10.5 %collective-permute-start.10 = (bf16[1024,512]{1,0:T(8,128)(2,1)}, bf16[1024,512]{1,0:T(8,128)(2,1)}, u32[]{:S(2)}, u32[]{:S(2)}) collective-permute-start(bf16[1024,512]{1,0:T(8,128)(2,1)} %collective-permute-done.8), channel_id=1, source_target_pairs={{0,480},{32,0},{64,32},{96,64},{128,96},{160,128},{192,160},{224,1... | collective-permute-start | bytes 3145736 | tf_op jit(solution)/shard_map/ppermute | solution.py:9
  389.6 20.7 %collective-permute-done.9 = bf16[4,256,512]{2,1,0:T(8,128)(2,1)} collective-permute-done((bf16[4,256,512]{2,1,0:T(8,128)(2,1)S(1)}, bf16[4,256,512]{2,1,0:T(8,128)(2,1)}, u32[]{:S(2)}, u32[]{:S(2)}) %collective-permute-start.9) | collective-permute-done | bytes 1048608 | tf_op jit(solution)/shard_map/ppermute | solution.py:9
  410.3 2.3 broadcast_select_fusion
  412.6 5.8 %collective-permute-start.11 = (bf16[4,256,512]{2,1,0:T(8,128)(2,1)}, bf16[4,256,512]{2,1,0:T(8,128)(2,1)}, u32[]{:S(2)}, u32[]{:S(2)}) collective-permute-start(bf16[4,256,512]{2,1,0:T(8,128)(2,1)} %broadcast_select_fusion), channel_id=1, source_target_pairs={{0,28},{4,0},{8,4},{12,8},{16,12},{20,16},{24,20},{28,24},{1,29},{... | collective-permute-start | bytes 3145736 | tf_op jit(solution)/shard_map/ppermute | solution.py:9
  418.4 18.1 %collective-permute-done.10 = bf16[1024,512]{1,0:T(8,128)(2,1)} collective-permute-done((bf16[1024,512]{1,0:T(8,128)(2,1)}, bf16[1024,512]{1,0:T(8,128)(2,1)}, u32[]{:S(2)}, u32[]{:S(2)}) %collective-permute-start.10) | collective-permute-done | bytes 1048608 | tf_op jit(solution)/shard_map/ppermute | solution.py:9
  436.6 10.4 %collective-permute-start.12 = (bf16[1024,512]{1,0:T(8,128)(2,1)}, bf16[1024,512]{1,0:T(8,128)(2,1)}, u32[]{:S(2)}, u32[]{:S(2)}) collective-permute-start(bf16[1024,512]{1,0:T(8,128)(2,1)} %collective-permute-done.10), channel_id=1, source_target_pairs={{0,480},{32,0},{64,32},{96,64},{128,96},{160,128},{192,160},{224,1... | collective-permute-start | bytes 3145736 | tf_op jit(solution)/shard_map/ppermute | solution.py:9
  447.2 1.7 convolution_bitcast_fusion.2
  448.8 0.4 fusion
  449.3 1.8 fusion.1
  451.1 17.5 %collective-permute-done.11 = bf16[4,256,512]{2,1,0:T(8,128)(2,1)} collective-permute-done((bf16[4,256,512]{2,1,0:T(8,128)(2,1)}, bf16[4,256,512]{2,1,0:T(8,128)(2,1)}, u32[]{:S(2)}, u32[]{:S(2)}) %collective-permute-start.11) | collective-permute-done | bytes 1048608 | tf_op jit(solution)/shard_map/ppermute | solution.py:9
  468.6 20.7 %collective-permute-done.12 = bf16[1024,512]{1,0:T(8,128)(2,1)} collective-permute-done((bf16[1024,512]{1,0:T(8,128)(2,1)}, bf16[1024,512]{1,0:T(8,128)(2,1)}, u32[]{:S(2)}, u32[]{:S(2)}) %collective-permute-start.12) | collective-permute-done | bytes 1048608 | tf_op jit(solution)/shard_map/ppermute | solution.py:9
  489.4 2.8 fusion.2
  492.1 0.0 reduce-scatter.2.cloned.1.call-update
  492.2 45.5 %reduce-scatter.2.cloned.1.call-done = f32[256,128]{1,0:T(8,128)} async-done(((f32[256,512]{1,0:T(8,128)}), f32[256,128]{1,0:T(8,128)}) %reduce-scatter.2.cloned.1.call-update) | async-done | bytes 131088 | tf_op jit(solution)/shard_map/reduce_scatter | solution.py:70
  (2 shorter events, 0.0 us)
Async XLA Ops:
  6.5 36.3 %all-gather.4.cloned.1.call-start = ((), (), s32[]{:S(2)}) async-start(), calls=%async_computation.1 | async-start | bytes 1310720 | tf_op jit(solution)/shard_map/all_gather | solution.py:51
  7.3 67.3 %all-gather.6.cloned.1.call-start = ((), (), s32[]{:S(2)}) async-start(), calls=%async_computation.3 | async-start | bytes 1310720 | tf_op jit(solution)/shard_map/all_gather | solution.py:50
  8.0 529.7 %reduce-scatter.2.cloned.1.call-start = ((), (), s32[]{:S(2)}) async-start(), calls=%async_computation.2 | async-start | bytes 655360 | tf_op jit(solution)/shard_map/reduce_scatter | solution.py:70
  42.8 46.4 %collective-permute-start.3 = (bf16[1024,512]{1,0:T(8,128)(2,1)}, bf16[1024,512]{1,0:T(8,128)(2,1)S(1)}, u32[]{:S(2)}, u32[]{:S(2)}) collective-permute-start(bf16[1024,512]{1,0:T(8,128)(2,1)} %all-gather.4.cloned.1.call-done), channel_id=1, source_target_pairs={{0,480},{32,0},{64,32},{96,64},{128,96},{160,128},{192,160},{224,1... | collective-permute-start | bytes 3145736 | tf_op jit(solution)/shard_map/ppermute | solution.py:9
  74.6 52.4 %collective-permute-start = (bf16[4,256,512]{2,1,0:T(8,128)(2,1)}, bf16[4,256,512]{2,1,0:T(8,128)(2,1)}, u32[]{:S(2)}, u32[]{:S(2)}) collective-permute-start(bf16[4,256,512]{2,1,0:T(8,128)(2,1)} %bitcast.24), channel_id=1, source_target_pairs={{0,28},{4,0},{8,4},{12,8},{16,12},{20,16},{24,20},{28,24},{1,29},{... | collective-permute-start | bytes 3145736 | tf_op jit(solution)/shard_map/ppermute | solution.py:9
  76.5 50.4 %copy-start = (bf16[1024,512]{1,0:T(8,128)(2,1)S(1)}, bf16[1024,512]{1,0:T(8,128)(2,1)}, u32[]{:S(2)}) copy-start(bf16[1024,512]{1,0:T(8,128)(2,1)} %all-gather.6.cloned.1.call-done) | copy-start | bytes 3145732
  90.5 68.3 %collective-permute-start.4 = (bf16[1024,512]{1,0:T(8,128)(2,1)S(1)}, bf16[1024,512]{1,0:T(8,128)(2,1)}, u32[]{:S(2)}, u32[]{:S(2)}) collective-permute-start(bf16[1024,512]{1,0:T(8,128)(2,1)S(1)} %broadcast_select_fusion.2), channel_id=1, source_target_pairs={{0,448},{32,480},{64,0},{96,32},{128,64},{160,96},{192,128},{224,1... | collective-permute-start | bytes 3145736 | tf_op jit(solution)/shard_map/ppermute | solution.py:9
  127.1 91.0 %collective-permute-start.1 = (bf16[4,256,512]{2,1,0:T(8,128)(2,1)S(1)}, bf16[4,256,512]{2,1,0:T(8,128)(2,1)}, u32[]{:S(2)}, u32[]{:S(2)}) collective-permute-start(bf16[4,256,512]{2,1,0:T(8,128)(2,1)S(1)} %broadcast_select_fusion.6), channel_id=1, source_target_pairs={{0,24},{4,28},{8,0},{12,4},{16,8},{20,12},{24,16},{28,20},{1,25},{... | collective-permute-start | bytes 3145736 | tf_op jit(solution)/shard_map/ppermute | solution.py:9
  160.0 100.0 %collective-permute-start.5 = (bf16[1024,512]{1,0:T(8,128)(2,1)}, bf16[1024,512]{1,0:T(8,128)(2,1)S(1)}, u32[]{:S(2)}, u32[]{:S(2)}) collective-permute-start(bf16[1024,512]{1,0:T(8,128)(2,1)} %broadcast_select_fusion.3), channel_id=1, source_target_pairs={{0,384},{32,416},{64,448},{96,480},{128,0},{160,32},{192,64},{224,... | collective-permute-start | bytes 3145736 | tf_op jit(solution)/shard_map/ppermute | solution.py:9
  218.2 98.2 %collective-permute-start.2 = (bf16[4,256,512]{2,1,0:T(8,128)(2,1)S(1)}, bf16[4,256,512]{2,1,0:T(8,128)(2,1)}, u32[]{:S(2)}, u32[]{:S(2)}) collective-permute-start(bf16[4,256,512]{2,1,0:T(8,128)(2,1)S(1)} %broadcast_select_fusion.7), channel_id=1, source_target_pairs={{0,16},{4,20},{8,24},{12,28},{16,0},{20,4},{24,8},{28,12},{1,17},{... | collective-permute-start | bytes 3145736 | tf_op jit(solution)/shard_map/ppermute | solution.py:9
  260.0 59.6 %collective-permute-start.6 = (bf16[1024,512]{1,0:T(8,128)(2,1)S(1)}, bf16[1024,512]{1,0:T(8,128)(2,1)}, u32[]{:S(2)}, u32[]{:S(2)}) collective-permute-start(bf16[1024,512]{1,0:T(8,128)(2,1)S(1)} %broadcast_select_fusion.4), channel_id=1, source_target_pairs={{0,256},{32,288},{64,320},{96,352},{128,384},{160,416},{192,448},{... | collective-permute-start | bytes 3145736 | tf_op jit(solution)/shard_map/ppermute | solution.py:9
  317.7 35.0 %collective-permute-start.7 = (bf16[4,256,512]{2,1,0:T(8,128)(2,1)S(1)}, bf16[4,256,512]{2,1,0:T(8,128)(2,1)}, u32[]{:S(2)}, u32[]{:S(2)}) collective-permute-start(bf16[4,256,512]{2,1,0:T(8,128)(2,1)S(1)} %broadcast_select_fusion.8), channel_id=1, source_target_pairs={{0,28},{4,0},{8,4},{12,8},{16,12},{20,16},{24,20},{28,24},{1,29},{... | collective-permute-start | bytes 3145736 | tf_op jit(solution)/shard_map/ppermute | solution.py:9
  321.0 58.0 %collective-permute-start.8 = (bf16[1024,512]{1,0:T(8,128)(2,1)S(1)}, bf16[1024,512]{1,0:T(8,128)(2,1)}, u32[]{:S(2)}, u32[]{:S(2)}) collective-permute-start(bf16[1024,512]{1,0:T(8,128)(2,1)S(1)} %broadcast_select_fusion.5), channel_id=1, source_target_pairs={{0,480},{32,0},{64,32},{96,64},{128,96},{160,128},{192,160},{224,1... | collective-permute-start | bytes 3145736 | tf_op jit(solution)/shard_map/ppermute | solution.py:9
  352.8 57.5 %collective-permute-start.9 = (bf16[4,256,512]{2,1,0:T(8,128)(2,1)S(1)}, bf16[4,256,512]{2,1,0:T(8,128)(2,1)}, u32[]{:S(2)}, u32[]{:S(2)}) collective-permute-start(bf16[4,256,512]{2,1,0:T(8,128)(2,1)S(1)} %broadcast_select_fusion.1), channel_id=1, source_target_pairs={{0,28},{4,0},{8,4},{12,8},{16,12},{20,16},{24,20},{28,24},{1,29},{... | collective-permute-start | bytes 3145736 | tf_op jit(solution)/shard_map/ppermute | solution.py:9
  379.1 57.5 %collective-permute-start.10 = (bf16[1024,512]{1,0:T(8,128)(2,1)}, bf16[1024,512]{1,0:T(8,128)(2,1)}, u32[]{:S(2)}, u32[]{:S(2)}) collective-permute-start(bf16[1024,512]{1,0:T(8,128)(2,1)} %collective-permute-done.8), channel_id=1, source_target_pairs={{0,480},{32,0},{64,32},{96,64},{128,96},{160,128},{192,160},{224,1... | collective-permute-start | bytes 3145736 | tf_op jit(solution)/shard_map/ppermute | solution.py:9
  412.6 56.0 %collective-permute-start.11 = (bf16[4,256,512]{2,1,0:T(8,128)(2,1)}, bf16[4,256,512]{2,1,0:T(8,128)(2,1)}, u32[]{:S(2)}, u32[]{:S(2)}) collective-permute-start(bf16[4,256,512]{2,1,0:T(8,128)(2,1)} %broadcast_select_fusion), channel_id=1, source_target_pairs={{0,28},{4,0},{8,4},{12,8},{16,12},{20,16},{24,20},{28,24},{1,29},{... | collective-permute-start | bytes 3145736 | tf_op jit(solution)/shard_map/ppermute | solution.py:9
  436.6 52.8 %collective-permute-start.12 = (bf16[1024,512]{1,0:T(8,128)(2,1)}, bf16[1024,512]{1,0:T(8,128)(2,1)}, u32[]{:S(2)}, u32[]{:S(2)}) collective-permute-start(bf16[1024,512]{1,0:T(8,128)(2,1)} %collective-permute-done.10), channel_id=1, source_target_pairs={{0,480},{32,0},{64,32},{96,64},{128,96},{160,128},{192,160},{224,1... | collective-permute-start | bytes 3145736 | tf_op jit(solution)/shard_map/ppermute | solution.py:9
Sparse Core Ops, SparseCore 0:
  9.5 33.2 all-gather.3
  44.9 29.6 all-gather.5
  492.3 45.3 reduce-scatter.1
where the time goes:
time: 546 us; the launch traced here: 544 us
  waiting for transfers between devices  458 us (84%)
  starting transfers between devices  57.8 us (11%)
  between operations  13.6 us (2%)
  other arithmetic  7.87 us (1%)
  matrix products  6.69 us (1%)
    ppermute x13, waiting for transfers between devices, shifted(): return lax.ppermute(x, axis, [(i, (i + by) % size) for i in range(size)])  353 us
    ppermute x13, starting transfers between devices, shifted(): return lax.ppermute(x, axis, [(i, (i + by) % size) for i in range(size)])  57.7 us
    reduce_scatter x1, waiting for transfers between devices, per_device(): lax.psum_scatter(partial_value, 'depth', scatter_dimension=1, tiled=True)  45.5 us
    all_gather x1, waiting for transfers between devices, per_device(): lax.all_gather(amplitudes, 'depth', axis=0, tiled=True)  34.8 us
    all_gather x1, waiting for transfers between devices, per_device(): lax.all_gather(integrals[None], 'depth', axis=0, tiled=True)  23.3 us
  transfers between devices with their start and end apart: 16, of which 15 were waited for; matrix products, arithmetic and copies ran while one was open for 2% of the time, Pallas kernels for 0%

commit v1 on v0

v1 whole, which is shorter than its diff:
```python
import functools

import jax
import jax.numpy as jnp
import numpy as np
from jax import lax
from jax.experimental import pallas as pl
from jax.experimental.pallas import tpu as pltpu
from jax.sharding import Mesh, PartitionSpec as P

AXES = ("yh", "z", "yl", "core", "x")
UNIT = 256


def moved(value, sizes, axes, where):
    shape = [sizes[a] for a in axes]
    perm = []
    for i in range(int(np.prod(shape))):
        place = dict(zip(axes, (int(v) for v in np.unravel_index(i, shape))))
        there = where(**place)
        perm.append((i, int(np.ravel_multi_index([there[a] for a in axes], shape))))
    return lax.ppermute(value, axes, perm)


def around_z(value, sizes, by):
    return moved(value, sizes, ("z",), lambda z: {"z": (z + by) % sizes["z"]})


def across_yl(value, sizes, mask):
    return moved(value, sizes, ("yl",), lambda yl: {"yl": yl ^ mask})


def regroup(value, sizes, second):
    def where(yh, yl, x):
        half = (x >> 1) ^ second
        return {"yh": yl >> 1, "yl": 2 * yh + (yl & 1), "x": 2 * (x & 1) + half}

    return moved(value, sizes, ("yh", "yl", "x"), where)


def product_kernel(place, w_ref, *refs):
    t_refs, out_ref = refs[:-1], refs[-1]
    for step, t_ref in enumerate(t_refs):
        t = t_ref[...]
        for rel in range(2):
            w = w_ref[place[2 * step + rel]]
            part = jnp.dot(w, t, preferred_element_type=jnp.float32)
            for block in range(4):
                cols = part[:, block * 128 : (block + 1) * 128]
                if step == 0:
                    out_ref[block, rel] = cols
                else:
                    out_ref[block, rel] += cols


def per_device(sizes, integrals, amplitudes):
    yh, z, yl, x = (lax.axis_index(a) for a in ("yh", "z", "yl", "x"))
    rows = integrals.shape[0]
    halves = jnp.stack([integrals[:, :UNIT], integrals[:, UNIT:]])
    high = x >> 1
    first = regroup(lax.dynamic_index_in_dim(halves, high, 0, False), sizes, 0)
    second = regroup(lax.dynamic_index_in_dim(halves, 1 - high, 0, False), sizes, 1)
    own = jnp.stack([first, second])
    by1 = across_yl(own, sizes, 1)
    by2 = across_yl(own, sizes, 2)
    by3 = across_yl(by1, sizes, 2)
    slab = lax.all_gather(jnp.stack([own, by1, by2, by3]), "core", axis=0)
    slab = slab.reshape(-1, rows, UNIT)
    up, down = [amplitudes], [amplitudes]
    for _ in range(3):
        up.append(around_z(up[-1], sizes, 1))
        down.append(around_z(down[-1], sizes, -1))
    up.append(around_z(up[-1], sizes, 1))
    tiles = up + down[1:]
    offsets = [-i for i in range(5)] + [1, 2, 3]
    place = []
    for offset in offsets:
        unit = (z + offset) % sizes["z"]
        u4, u3, u2 = unit >> 2, (unit >> 1) & 1, unit & 1
        for rel in range(2):
            m = yh ^ rel
            slot = ((m ^ (yl >> 1)) << 1) | (u4 ^ (yl & 1))
            place.append((u3 * 4 + slot) * 2 + (u2 ^ (x & 1)))
    place = jnp.stack(place).astype(jnp.int32)
    vmem = pl.BlockSpec(memory_space=pltpu.VMEM)
    part = pl.pallas_call(
        product_kernel,
        out_shape=jax.ShapeDtypeStruct((4, 2, rows, 128), jnp.float32),
        in_specs=[pl.BlockSpec(memory_space=pltpu.SMEM)] + [vmem] * 9,
        out_specs=vmem,
        compiler_params=pltpu.CompilerParams(vmem_limit_bytes=48 * 1024 * 1024),
    )(place, slab, *tiles)
    part = lax.all_to_all(part, "x", split_axis=0, concat_axis=0, tiled=True)
    total = part.sum(axis=0)
    other = moved(total[1], sizes, ("yh",), lambda yh: {"yh": 1 - yh})
    return total[0] + other


def solution(mesh):
    fine = Mesh(mesh.devices.reshape(2, 8, 4, 2, 4), AXES)
    sizes = dict(fine.shape)
    return jax.shard_map(
        functools.partial(per_device, sizes),
        mesh=fine,
        in_specs=(P(("yh", "z"), ("yl", "core", "x")), P(("yh", "z", "x"), ("yl", "core"))),
        out_specs=P(("yh", "z"), ("yl", "core", "x")),
        check_vma=False,
    )
```

time: 546 us -> 144 us (0.26)
  the two profiles are of different devices: /device:TPU:56 before, /device:TPU:24 now
where the time goes in v1:
time: 144 us; the launch traced here: 143 us
  waiting for transfers between devices  57.1 us (40%)
  starting transfers between devices  50.7 us (35%)
  blocking collectives  15.3 us (11%)
  between operations  13.7 us (10%)
  local copies, waits for them, and re-layouts  2.69 us (2%)
  other arithmetic  2 us (1%)
  Pallas kernels  1.78 us (1%)
    ppermute x13, waiting for transfers between devices, moved(): return lax.ppermute(value, axes, perm)  57.1 us
    ppermute x13, starting transfers between devices, moved(): return lax.ppermute(value, axes, perm)  50.7 us
    all_to_all x1, blocking collectives, per_device(): part = lax.all_to_all(part, 'x', split_axis=0, concat_axis=0, tiled=True)  15.3 us
  transfers between devices with their start and end apart: 14, of which 10 were waited for; matrix products, arithmetic and copies ran while one was open for 0% of the time, Pallas kernels for 0%

profile of v1, /device:TPU:24, one launch (start us, length us, event | category | flops | bytes accessed | tf_op | source)
XLA Modules:
  0.0 143.3 jit_solution(6187854970976607150)
XLA Ops:
  6.5 0.0 all-gather.3.cloned.1.call-start
  6.5 1.0 slice_bitcast_fusion.2
  7.5 0.1 fusion.3
  7.7 0.0 copy-start.1
  7.7 4.9 %collective-permute-start = (bf16[256,256]{1,0:T(8,128)(2,1)S(1)}, bf16[256,256]{1,0:T(8,128)(2,1)S(1)}, u32[]{:S(2)}, u32[]{:S(2)}) collective-permute-start(bf16[256,256]{1,0:T(8,128)(2,1)S(1)} %get-tuple-element.7), channel_id=1, source_target_pairs={{0,0},{1,2},{2,1},{3,3},{8,8},{9,10},{10,9},{11,11},{16,256},{17,2... | collective-permute-start | bytes 393224 | tf_op jit(solution)/shard_map/ppermute | solution.py:22
  12.6 5.0 %collective-permute-start.1 = (bf16[256,256]{1,0:T(8,128)(2,1)S(1)}, bf16[256,256]{1,0:T(8,128)(2,1)S(1)}, u32[]{:S(2)}, u32[]{:S(2)}) collective-permute-start(bf16[256,256]{1,0:T(8,128)(2,1)S(1)} %get-tuple-element.8), channel_id=1, source_target_pairs={{0,1},{1,3},{2,0},{3,2},{8,9},{9,11},{10,8},{11,10},{16,257},{17,2... | collective-permute-start | bytes 393224 | tf_op jit(solution)/shard_map/ppermute | solution.py:22
  17.6 4.2 %collective-permute-done = bf16[256,256]{1,0:T(8,128)(2,1)S(1)} collective-permute-done((bf16[256,256]{1,0:T(8,128)(2,1)S(1)}, bf16[256,256]{1,0:T(8,128)(2,1)S(1)}, u32[]{:S(2)}, u32[]{:S(2)}) %collective-permute-start) | collective-permute-done | bytes 131104 | tf_op jit(solution)/shard_map/ppermute | solution.py:22
  21.9 2.2 %collective-permute-done.1 = bf16[256,256]{1,0:T(8,128)(2,1)S(1)} collective-permute-done((bf16[256,256]{1,0:T(8,128)(2,1)S(1)}, bf16[256,256]{1,0:T(8,128)(2,1)S(1)}, u32[]{:S(2)}, u32[]{:S(2)}) %collective-permute-start.1) | collective-permute-done | bytes 131104 | tf_op jit(solution)/shard_map/ppermute | solution.py:22
  24.1 6.2 %collective-permute-start.2 = (bf16[2,256,256]{2,1,0:T(8,128)(2,1)S(1)}, bf16[2,256,256]{2,1,0:T(8,128)(2,1)S(1)}, u32[]{:S(2)}, u32[]{:S(2)}) collective-permute-start(bf16[2,256,256]{2,1,0:T(8,128)(2,1)S(1)} %get-tuple-element.6), channel_id=1, source_target_pairs={{0,8},{8,0},{16,24},{24,16},{1,9},{9,1},{17,25},{25,17},{2,10},{10... | collective-permute-start | bytes 786440 | tf_op jit(solution)/shard_map/ppermute | solution.py:22
  30.3 1.9 %collective-permute-start.3 = (bf16[2,256,256]{2,1,0:T(8,128)(2,1)S(1)}, bf16[2,256,256]{2,1,0:T(8,128)(2,1)S(1)}, u32[]{:S(2)}, u32[]{:S(2)}) collective-permute-start(bf16[2,256,256]{2,1,0:T(8,128)(2,1)S(1)} %get-tuple-element.6), channel_id=1, source_target_pairs={{0,16},{8,24},{16,0},{24,8},{1,17},{9,25},{17,1},{25,9},{2,18},{10... | collective-permute-start | bytes 786440 | tf_op jit(solution)/shard_map/ppermute | solution.py:22
  32.2 4.7 %collective-permute-done.2 = bf16[2,256,256]{2,1,0:T(8,128)(2,1)S(1)} collective-permute-done((bf16[2,256,256]{2,1,0:T(8,128)(2,1)S(1)}, bf16[2,256,256]{2,1,0:T(8,128)(2,1)S(1)}, u32[]{:S(2)}, u32[]{:S(2)}) %collective-permute-start.2) | collective-permute-done | bytes 262176 | tf_op jit(solution)/shard_map/ppermute | solution.py:22
  37.0 1.9 %collective-permute-start.4 = (bf16[2,256,256]{2,1,0:T(8,128)(2,1)S(1)}, bf16[2,256,256]{2,1,0:T(8,128)(2,1)S(1)}, u32[]{:S(2)}, u32[]{:S(2)}) collective-permute-start(bf16[2,256,256]{2,1,0:T(8,128)(2,1)S(1)} %collective-permute-done.2), channel_id=1, source_target_pairs={{0,16},{8,24},{16,0},{24,8},{1,17},{9,25},{17,1},{25,9},{2,18},{10... | collective-permute-start | bytes 786440 | tf_op jit(solution)/shard_map/ppermute | solution.py:22
  38.9 13.2 %collective-permute-done.3 = bf16[2,256,256]{2,1,0:T(8,128)(2,1)S(1)} collective-permute-done((bf16[2,256,256]{2,1,0:T(8,128)(2,1)S(1)}, bf16[2,256,256]{2,1,0:T(8,128)(2,1)S(1)}, u32[]{:S(2)}, u32[]{:S(2)}) %collective-permute-start.3) | collective-permute-done | bytes 262176 | tf_op jit(solution)/shard_map/ppermute | solution.py:22
  52.0 5.5 %collective-permute-done.4 = bf16[2,256,256]{2,1,0:T(8,128)(2,1)S(1)} collective-permute-done((bf16[2,256,256]{2,1,0:T(8,128)(2,1)S(1)}, bf16[2,256,256]{2,1,0:T(8,128)(2,1)S(1)}, u32[]{:S(2)}, u32[]{:S(2)}) %collective-permute-start.4) | collective-permute-done | bytes 262176 | tf_op jit(solution)/shard_map/ppermute | solution.py:22
  57.6 1.1 pad_maximum_fusion
  58.7 0.0 all-gather.3.cloned.1.call-update
  58.7 0.0 copy-done.1
  58.7 4.3 %collective-permute-start.5 = (bf16[256,512]{1,0:T(8,128)(2,1)S(1)}, bf16[256,512]{1,0:T(8,128)(2,1)S(1)}, u32[]{:S(2)}, u32[]{:S(2)}) collective-permute-start(bf16[256,512]{1,0:T(8,128)(2,1)S(1)} %copy-done.1), channel_id=1, source_target_pairs={{0,32},{32,64},{64,96},{96,128},{128,160},{160,192},{192,224},{224... | collective-permute-start | bytes 786440 | tf_op jit(solution)/shard_map/ppermute | solution.py:22
  63.0 8.6 %collective-permute-start.9 = (bf16[256,512]{1,0:T(8,128)(2,1)S(1)}, bf16[256,512]{1,0:T(8,128)(2,1)S(1)}, u32[]{:S(2)}, u32[]{:S(2)}) collective-permute-start(bf16[256,512]{1,0:T(8,128)(2,1)S(1)} %copy-done.1), channel_id=1, source_target_pairs={{0,224},{32,0},{64,32},{96,64},{128,96},{160,128},{192,160},{224,1... | collective-permute-start | bytes 786440 | tf_op jit(solution)/shard_map/ppermute | solution.py:22
  71.6 4.5 %collective-permute-done.5.refs_1_ = bf16[256,512]{1,0:T(8,128)(2,1)S(1)} collective-permute-done((bf16[256,512]{1,0:T(8,128)(2,1)S(1)}, bf16[256,512]{1,0:T(8,128)(2,1)S(1)}, u32[]{:S(2)}, u32[]{:S(2)}) %collective-permute-start.5) | collective-permute-done | bytes 262176 | tf_op jit(solution)/shard_map/ppermute | solution.py:22
  76.1 1.9 %collective-permute-start.6 = (bf16[256,512]{1,0:T(8,128)(2,1)S(1)}, bf16[256,512]{1,0:T(8,128)(2,1)S(1)}, u32[]{:S(2)}, u32[]{:S(2)}) collective-permute-start(bf16[256,512]{1,0:T(8,128)(2,1)S(1)} %collective-permute-done.5.refs_1_), channel_id=1, source_target_pairs={{0,32},{32,64},{64,96},{96,128},{128,160},{160,192},{192,224},{224... | collective-permute-start | bytes 786440 | tf_op jit(solution)/shard_map/ppermute | solution.py:22
  78.1 0.0 collective-permute-done.9.refs_5_
  78.1 5.1 %collective-permute-start.10 = (bf16[256,512]{1,0:T(8,128)(2,1)S(1)}, bf16[256,512]{1,0:T(8,128)(2,1)S(1)}, u32[]{:S(2)}, u32[]{:S(2)}) collective-permute-start(bf16[256,512]{1,0:T(8,128)(2,1)S(1)} %collective-permute-done.9.refs_5_), channel_id=1, source_target_pairs={{0,224},{32,0},{64,32},{96,64},{128,96},{160,128},{192,160},{224,1... | collective-permute-start | bytes 786440 | tf_op jit(solution)/shard_map/ppermute | solution.py:22
  83.2 3.7 %collective-permute-done.6.refs_2_ = bf16[256,512]{1,0:T(8,128)(2,1)S(1)} collective-permute-done((bf16[256,512]{1,0:T(8,128)(2,1)S(1)}, bf16[256,512]{1,0:T(8,128)(2,1)S(1)}, u32[]{:S(2)}, u32[]{:S(2)}) %collective-permute-start.6) | collective-permute-done | bytes 262176 | tf_op jit(solution)/shard_map/ppermute | solution.py:22
  86.9 1.9 %collective-permute-start.7 = (bf16[256,512]{1,0:T(8,128)(2,1)S(1)}, bf16[256,512]{1,0:T(8,128)(2,1)S(1)}, u32[]{:S(2)}, u32[]{:S(2)}) collective-permute-start(bf16[256,512]{1,0:T(8,128)(2,1)S(1)} %collective-permute-done.6.refs_2_), channel_id=1, source_target_pairs={{0,32},{32,64},{64,96},{96,128},{128,160},{160,192},{192,224},{224... | collective-permute-start | bytes 786440 | tf_op jit(solution)/shard_map/ppermute | solution.py:22
  88.8 0.0 collective-permute-done.10.refs_6_
  88.9 5.1 %collective-permute-start.11 = (bf16[256,512]{1,0:T(8,128)(2,1)S(1)}, bf16[256,512]{1,0:T(8,128)(2,1)S(1)}, u32[]{:S(2)}, u32[]{:S(2)}) collective-permute-start(bf16[256,512]{1,0:T(8,128)(2,1)S(1)} %collective-permute-done.10.refs_6_), channel_id=1, source_target_pairs={{0,224},{32,0},{64,32},{96,64},{128,96},{160,128},{192,160},{224,1... | collective-permute-start | bytes 786440 | tf_op jit(solution)/shard_map/ppermute | solution.py:22
  94.0 2.8 %collective-permute-done.7.refs_3_ = bf16[256,512]{1,0:T(8,128)(2,1)S(1)} collective-permute-done((bf16[256,512]{1,0:T(8,128)(2,1)S(1)}, bf16[256,512]{1,0:T(8,128)(2,1)S(1)}, u32[]{:S(2)}, u32[]{:S(2)}) %collective-permute-start.7) | collective-permute-done | bytes 262176 | tf_op jit(solution)/shard_map/ppermute | solution.py:22
  96.8 1.9 %collective-permute-start.8 = (bf16[256,512]{1,0:T(8,128)(2,1)S(1)}, bf16[256,512]{1,0:T(8,128)(2,1)S(1)}, u32[]{:S(2)}, u32[]{:S(2)}) collective-permute-start(bf16[256,512]{1,0:T(8,128)(2,1)S(1)} %collective-permute-done.7.refs_3_), channel_id=1, source_target_pairs={{0,32},{32,64},{64,96},{96,128},{128,160},{160,192},{192,224},{224... | collective-permute-start | bytes 786440 | tf_op jit(solution)/shard_map/ppermute | solution.py:22
  98.9 0.1 stack.100.place
  99.0 0.0 collective-permute-done.11.refs_7_
  99.0 7.3 %collective-permute-done.8.refs_4_ = bf16[256,512]{1,0:T(8,128)(2,1)S(1)} collective-permute-done((bf16[256,512]{1,0:T(8,128)(2,1)S(1)}, bf16[256,512]{1,0:T(8,128)(2,1)S(1)}, u32[]{:S(2)}, u32[]{:S(2)}) %collective-permute-start.8) | collective-permute-done | bytes 262176 | tf_op jit(solution)/shard_map/ppermute | solution.py:22
  106.3 0.0 all-gather.3.cloned.1.call-done
  106.3 0.0 copy-start
  106.3 1.6 %copy-done = bf16[8,2,256,256]{3,2,1,0:T(8,128)(2,1)S(1)} copy-done((bf16[8,2,256,256]{3,2,1,0:T(8,128)(2,1)S(1)}, bf16[8,2,256,256]{3,2,1,0:T(8,128)(2,1)}, u32[]{:S(2)}) %copy-start) | copy-done | bytes 2097176
  107.9 1.8 %shard_map.28 = f32[4,2,256,128]{3,2,1,0:T(8,128)S(1)} custom-call(s32[16]{0:T(128)S(1)} %stack.100.place, bf16[16,256,256]{2,1,0:T(8,128)(2,1)S(1)} %bitcast.38, bf16[256,512]{1,0:T(8,128)(2,1)S(1)} %copy-done.1, bf16[256,512]{1,0:T(8,128)(2,1)S(1)} %collective-permute-done.5.refs_1_, bf16[256,512]{1,0:T(8,128)(2,1)S(1)} %collective-permute-done.6.refs_2_, ...), custom_call_target="tpu_custom_call" | custom-call | tf_op jit(solution)/shard_map/pallas_call | solution.py:86
  109.6 15.3 %all_to_all.5 = f32[4,2,256,128]{3,2,1,0:T(8,128)S(1)} all-to-all(f32[4,2,256,128]{3,2,1,0:T(8,128)S(1)} %shard_map.28), channel_id=1, replica_groups=mesh['yh'=2,'z'=8,'yl'=4,'core'=2,'x'=4] {'x'}, dimensions={0} | all-to-all | bytes 2097152 | tf_op jit(solution)/shard_map/all_to_all | solution.py:93
  125.0 0.1 reduce_sum.9
  125.1 1.9 %collective-permute-start.12 = (f32[256,128]{1,0:T(8,128)S(1)}, f32[256,128]{1,0:T(8,128)S(1)}, u32[]{:S(2)}, u32[]{:S(2)}) collective-permute-start(f32[256,128]{1,0:T(8,128)S(1)} %slice_bitcast_fusion), channel_id=1, source_target_pairs={{0,256},{256,0},{1,257},{257,1},{2,258},{258,2},{3,259},{259,3},{4... | collective-permute-start | bytes 393224 | tf_op jit(solution)/shard_map/ppermute | solution.py:22
  127.0 8.8 %collective-permute-done.12 = f32[256,128]{1,0:T(8,128)S(1)} collective-permute-done((f32[256,128]{1,0:T(8,128)S(1)}, f32[256,128]{1,0:T(8,128)S(1)}, u32[]{:S(2)}, u32[]{:S(2)}) %collective-permute-start.12) | collective-permute-done | bytes 131104 | tf_op jit(solution)/shard_map/ppermute | solution.py:22
  135.8 0.7 fusion.4
  (2 shorter events, 0.0 us)
Async XLA Ops:
  6.5 99.7 %all-gather.3.cloned.1.call-start = ((), (), s32[]{:S(2)}) async-start(), calls=%async_computation.1 | async-start | bytes 3145728 | tf_op jit(solution)/shard_map/all_gather | solution.py:67
  7.7 51.1 %copy-start.1 = (bf16[256,512]{1,0:T(8,128)(2,1)S(1)}, bf16[256,512]{1,0:T(8,128)(2,1)}, u32[]{:S(2)}) copy-start(bf16[256,512]{1,0:T(8,128)(2,1)} %refs_0_.1) | copy-start | bytes 786436
  7.7 14.2 %collective-permute-start = (bf16[256,256]{1,0:T(8,128)(2,1)S(1)}, bf16[256,256]{1,0:T(8,128)(2,1)S(1)}, u32[]{:S(2)}, u32[]{:S(2)}) collective-permute-start(bf16[256,256]{1,0:T(8,128)(2,1)S(1)} %get-tuple-element.7), channel_id=1, source_target_pairs={{0,0},{1,2},{2,1},{3,3},{8,8},{9,10},{10,9},{11,11},{16,256},{17,2... | collective-permute-start | bytes 393224 | tf_op jit(solution)/shard_map/ppermute | solution.py:22
  12.6 11.5 %collective-permute-start.1 = (bf16[256,256]{1,0:T(8,128)(2,1)S(1)}, bf16[256,256]{1,0:T(8,128)(2,1)S(1)}, u32[]{:S(2)}, u32[]{:S(2)}) collective-permute-start(bf16[256,256]{1,0:T(8,128)(2,1)S(1)} %get-tuple-element.8), channel_id=1, source_target_pairs={{0,1},{1,3},{2,0},{3,2},{8,9},{9,11},{10,8},{11,10},{16,257},{17,2... | collective-permute-start | bytes 393224 | tf_op jit(solution)/shard_map/ppermute | solution.py:22
  24.1 12.9 %collective-permute-start.2 = (bf16[2,256,256]{2,1,0:T(8,128)(2,1)S(1)}, bf16[2,256,256]{2,1,0:T(8,128)(2,1)S(1)}, u32[]{:S(2)}, u32[]{:S(2)}) collective-permute-start(bf16[2,256,256]{2,1,0:T(8,128)(2,1)S(1)} %get-tuple-element.6), channel_id=1, source_target_pairs={{0,8},{8,0},{16,24},{24,16},{1,9},{9,1},{17,25},{25,17},{2,10},{10... | collective-permute-start | bytes 786440 | tf_op jit(solution)/shard_map/ppermute | solution.py:22
  30.3 21.7 %collective-permute-start.3 = (bf16[2,256,256]{2,1,0:T(8,128)(2,1)S(1)}, bf16[2,256,256]{2,1,0:T(8,128)(2,1)S(1)}, u32[]{:S(2)}, u32[]{:S(2)}) collective-permute-start(bf16[2,256,256]{2,1,0:T(8,128)(2,1)S(1)} %get-tuple-element.6), channel_id=1, source_target_pairs={{0,16},{8,24},{16,0},{24,8},{1,17},{9,25},{17,1},{25,9},{2,18},{10... | collective-permute-start | bytes 786440 | tf_op jit(solution)/shard_map/ppermute | solution.py:22
  37.0 20.6 %collective-permute-start.4 = (bf16[2,256,256]{2,1,0:T(8,128)(2,1)S(1)}, bf16[2,256,256]{2,1,0:T(8,128)(2,1)S(1)}, u32[]{:S(2)}, u32[]{:S(2)}) collective-permute-start(bf16[2,256,256]{2,1,0:T(8,128)(2,1)S(1)} %collective-permute-done.2), channel_id=1, source_target_pairs={{0,16},{8,24},{16,0},{24,8},{1,17},{9,25},{17,1},{25,9},{2,18},{10... | collective-permute-start | bytes 786440 | tf_op jit(solution)/shard_map/ppermute | solution.py:22
  58.7 17.4 %collective-permute-start.5 = (bf16[256,512]{1,0:T(8,128)(2,1)S(1)}, bf16[256,512]{1,0:T(8,128)(2,1)S(1)}, u32[]{:S(2)}, u32[]{:S(2)}) collective-permute-start(bf16[256,512]{1,0:T(8,128)(2,1)S(1)} %copy-done.1), channel_id=1, source_target_pairs={{0,32},{32,64},{64,96},{96,128},{128,160},{160,192},{192,224},{224... | collective-permute-start | bytes 786440 | tf_op jit(solution)/shard_map/ppermute | solution.py:22
  63.0 15.1 %collective-permute-start.9 = (bf16[256,512]{1,0:T(8,128)(2,1)S(1)}, bf16[256,512]{1,0:T(8,128)(2,1)S(1)}, u32[]{:S(2)}, u32[]{:S(2)}) collective-permute-start(bf16[256,512]{1,0:T(8,128)(2,1)S(1)} %copy-done.1), channel_id=1, source_target_pairs={{0,224},{32,0},{64,32},{96,64},{128,96},{160,128},{192,160},{224,1... | collective-permute-start | bytes 786440 | tf_op jit(solution)/shard_map/ppermute | solution.py:22
  76.1 10.8 %collective-permute-start.6 = (bf16[256,512]{1,0:T(8,128)(2,1)S(1)}, bf16[256,512]{1,0:T(8,128)(2,1)S(1)}, u32[]{:S(2)}, u32[]{:S(2)}) collective-permute-start(bf16[256,512]{1,0:T(8,128)(2,1)S(1)} %collective-permute-done.5.refs_1_), channel_id=1, source_target_pairs={{0,32},{32,64},{64,96},{96,128},{128,160},{160,192},{192,224},{224... | collective-permute-start | bytes 786440 | tf_op jit(solution)/shard_map/ppermute | solution.py:22
  78.1 10.8 %collective-permute-start.10 = (bf16[256,512]{1,0:T(8,128)(2,1)S(1)}, bf16[256,512]{1,0:T(8,128)(2,1)S(1)}, u32[]{:S(2)}, u32[]{:S(2)}) collective-permute-start(bf16[256,512]{1,0:T(8,128)(2,1)S(1)} %collective-permute-done.9.refs_5_), channel_id=1, source_target_pairs={{0,224},{32,0},{64,32},{96,64},{128,96},{160,128},{192,160},{224,1... | collective-permute-start | bytes 786440 | tf_op jit(solution)/shard_map/ppermute | solution.py:22
  86.9 9.9 %collective-permute-start.7 = (bf16[256,512]{1,0:T(8,128)(2,1)S(1)}, bf16[256,512]{1,0:T(8,128)(2,1)S(1)}, u32[]{:S(2)}, u32[]{:S(2)}) collective-permute-start(bf16[256,512]{1,0:T(8,128)(2,1)S(1)} %collective-permute-done.6.refs_2_), channel_id=1, source_target_pairs={{0,32},{32,64},{64,96},{96,128},{128,160},{160,192},{192,224},{224... | collective-permute-start | bytes 786440 | tf_op jit(solution)/shard_map/ppermute | solution.py:22
  88.9 10.1 %collective-permute-start.11 = (bf16[256,512]{1,0:T(8,128)(2,1)S(1)}, bf16[256,512]{1,0:T(8,128)(2,1)S(1)}, u32[]{:S(2)}, u32[]{:S(2)}) collective-permute-start(bf16[256,512]{1,0:T(8,128)(2,1)S(1)} %collective-permute-done.10.refs_6_), channel_id=1, source_target_pairs={{0,224},{32,0},{64,32},{96,64},{128,96},{160,128},{192,160},{224,1... | collective-permute-start | bytes 786440 | tf_op jit(solution)/shard_map/ppermute | solution.py:22
  96.8 9.5 %collective-permute-start.8 = (bf16[256,512]{1,0:T(8,128)(2,1)S(1)}, bf16[256,512]{1,0:T(8,128)(2,1)S(1)}, u32[]{:S(2)}, u32[]{:S(2)}) collective-permute-start(bf16[256,512]{1,0:T(8,128)(2,1)S(1)} %collective-permute-done.7.refs_3_), channel_id=1, source_target_pairs={{0,32},{32,64},{64,96},{96,128},{128,160},{160,192},{192,224},{224... | collective-permute-start | bytes 786440 | tf_op jit(solution)/shard_map/ppermute | solution.py:22
  106.3 1.6 %copy-start = (bf16[8,2,256,256]{3,2,1,0:T(8,128)(2,1)S(1)}, bf16[8,2,256,256]{3,2,1,0:T(8,128)(2,1)}, u32[]{:S(2)}) copy-start(bf16[8,2,256,256]{3,2,1,0:T(8,128)(2,1)} %all-gather.3.cloned.1.call-done) | copy-start | bytes 6291460
  125.1 10.8 %collective-permute-start.12 = (f32[256,128]{1,0:T(8,128)S(1)}, f32[256,128]{1,0:T(8,128)S(1)}, u32[]{:S(2)}, u32[]{:S(2)}) collective-permute-start(f32[256,128]{1,0:T(8,128)S(1)} %slice_bitcast_fusion), channel_id=1, source_target_pairs={{0,256},{256,0},{1,257},{257,1},{2,258},{258,2},{3,259},{259,3},{4... | collective-permute-start | bytes 393224 | tf_op jit(solution)/shard_map/ppermute | solution.py:22
Sparse Core Ops, SparseCore 0:
  58.8 21.6 all-gather.2

commit v2 on v1

v2 whole, which is shorter than its diff:
```python
import functools

import jax
import jax.numpy as jnp
import numpy as np
from jax import lax
from jax.experimental import pallas as pl
from jax.experimental.pallas import tpu as pltpu
from jax.sharding import Mesh, PartitionSpec as P

AXES = ("yh", "z", "yl", "core", "x")
UNIT = 256


def moved(value, sizes, axes, where):
    shape = [sizes[a] for a in axes]
    perm = []
    for i in range(int(np.prod(shape))):
        place = dict(zip(axes, (int(v) for v in np.unravel_index(i, shape))))
        there = where(**place)
        perm.append((i, int(np.ravel_multi_index([there[a] for a in axes], shape))))
    return lax.ppermute(value, axes, perm)


def around_z(value, sizes):
    return moved(
        value, sizes, ("z", "core"), lambda z, core: {"z": (z + 1 - 2 * core) % sizes["z"], "core": core}
    )


def along_yl(value, sizes):
    return moved(value, sizes, ("yl",), lambda yl: {"yl": (yl + 1) % sizes["yl"]})


def core_swap(value, sizes):
    return moved(value, sizes, ("core",), lambda core: {"core": 1 - core})


def regroup(value, sizes, second):
    def where(yh, yl, x):
        half = (x >> 1) ^ second
        return {"yh": yl >> 1, "yl": 2 * yh + (yl & 1), "x": 2 * (x & 1) + half}

    return moved(value, sizes, ("yh", "yl", "x"), where)


def product_kernel(place, own_ref, other_ref, *refs):
    t_refs, out_ref = refs[:-1], refs[-1]
    for step, t_ref in enumerate(t_refs):
        t = t_ref[...]
        same = place[3 * step] == 1
        for rel in range(2):
            slot = place[3 * step + 1 + rel]
            w = jnp.where(same, own_ref[slot], other_ref[slot])
            part = jnp.dot(w, t, preferred_element_type=jnp.float32)
            for block in range(4):
                cols = part[:, block * 128 : (block + 1) * 128]
                if step == 0:
                    out_ref[block, rel] = cols
                else:
                    out_ref[block, rel] += cols


def per_device(sizes, integrals, amplitudes):
    yh, z, yl, core, x = (lax.axis_index(a) for a in AXES)
    rows = integrals.shape[0]
    tiles = [amplitudes]
    for _ in range(sizes["z"] - 1):
        tiles.append(around_z(tiles[-1], sizes))
    halves = jnp.stack([integrals[:, :UNIT], integrals[:, UNIT:]])
    high = x >> 1
    first = regroup(lax.dynamic_index_in_dim(halves, high, 0, False), sizes, 0)
    second = regroup(lax.dynamic_index_in_dim(halves, 1 - high, 0, False), sizes, 1)
    slabs = [jnp.stack([first, second])]
    for _ in range(sizes["yl"] - 1):
        slabs.append(along_yl(slabs[-1], sizes))
    own = jnp.concatenate(slabs)
    other = core_swap(own, sizes)
    place = []
    for step in range(sizes["z"]):
        unit = (z + step * (2 * core - 1)) % sizes["z"]
        u4, u3, u2 = unit >> 2, (unit >> 1) & 1, unit & 1
        place.append(jnp.where(u3 == core, 1, 0))
        for rel in range(2):
            source = 2 * (yh ^ rel) + u4
            place.append(((yl - source) % sizes["yl"]) * 2 + (u2 ^ (x & 1)))
    place = jnp.stack(place).astype(jnp.int32)
    vmem = pl.BlockSpec(memory_space=pltpu.VMEM)
    part = pl.pallas_call(
        product_kernel,
        out_shape=jax.ShapeDtypeStruct((4, 2, rows, 128), jnp.float32),
        in_specs=[pl.BlockSpec(memory_space=pltpu.SMEM)] + [vmem] * 10,
        out_specs=vmem,
        compiler_params=pltpu.CompilerParams(vmem_limit_bytes=48 * 1024 * 1024),
    )(place, own, other, *tiles)
    part = lax.all_to_all(part, "x", split_axis=0, concat_axis=0, tiled=True)
    total = part.sum(axis=0)
    other = moved(total[1], sizes, ("yh",), lambda yh: {"yh": 1 - yh})
    return total[0] + other


def solution(mesh):
    fine = Mesh(mesh.devices.reshape(2, 8, 4, 2, 4), AXES)
    sizes = dict(fine.shape)
    return jax.shard_map(
        functools.partial(per_device, sizes),
        mesh=fine,
        in_specs=(P(("yh", "z"), ("yl", "core", "x")), P(("yh", "z", "x"), ("yl", "core"))),
        out_specs=P(("yh", "z"), ("yl", "core", "x")),
        check_vma=False,
    )
```

time: 144 us -> 119 us (0.83)
  the two profiles are of different devices: /device:TPU:24 before, /device:TPU:56 now
where the time goes in v2:
time: 119 us; the launch traced here: 118 us
  starting transfers between devices  52.1 us (44%)
  waiting for transfers between devices  44 us (37%)
  blocking collectives  15.2 us (13%)
  local copies, waits for them, and re-layouts  2.84 us (2%)
  Pallas kernels  2.28 us (2%)
    ppermute x14, starting transfers between devices, moved(): return lax.ppermute(value, axes, perm)  52.1 us
    ppermute x14, waiting for transfers between devices, moved(): return lax.ppermute(value, axes, perm)  44 us
    all_to_all x1, blocking collectives, per_device(): part = lax.all_to_all(part, 'x', split_axis=0, concat_axis=0, tiled=True)  15.2 us
  transfers between devices with their start and end apart: 14, of which 11 were waited for; matrix products, arithmetic and copies ran while one was open for 0% of the time, Pallas kernels for 0%

profile of v2, /device:TPU:56, one launch (start us, length us, event | category | flops | bytes accessed | tf_op | source)
XLA Modules:
  0.0 118.0 jit_solution(3559275865333450370)
XLA Ops:
  0.0 1.0 slice_bitcast_fusion.2
  1.0 0.0 copy-start
  1.0 0.1 fusion.1
  1.1 3.4 %collective-permute-start.1 = (bf16[256,256]{1,0:T(8,128)(2,1)S(1)}, bf16[256,256]{1,0:T(8,128)(2,1)S(1)}, u32[]{:S(2)}, u32[]{:S(2)}) collective-permute-start(bf16[256,256]{1,0:T(8,128)(2,1)S(1)} %get-tuple-element.5), channel_id=1, source_target_pairs={{0,1},{1,3},{2,0},{3,2},{8,9},{9,11},{10,8},{11,10},{16,257},{17,2... | collective-permute-start | bytes 393224 | tf_op jit(solution)/shard_map/ppermute | solution.py:22
  4.5 0.7 collective-permute-start
  5.2 0.0 copy-done
  5.2 4.3 %collective-permute-start.6 = (bf16[256,512]{1,0:T(8,128)(2,1)S(1)}, bf16[256,512]{1,0:T(8,128)(2,1)S(1)}, u32[]{:S(2)}, u32[]{:S(2)}) collective-permute-start(bf16[256,512]{1,0:T(8,128)(2,1)S(1)} %copy-done), channel_id=1, source_target_pairs={{0,32},{4,228},{32,64},{36,4},{64,96},{68,36},{96,128},{100,68},{1... | collective-permute-start | bytes 786440 | tf_op jit(solution)/shard_map/ppermute | solution.py:22
  9.5 0.3 collective-permute-done.1
  9.8 0.0 collective-permute-done
  9.8 10.5 %collective-permute-start.2 = (bf16[2,256,256]{2,1,0:T(8,128)(2,1)S(1)}, bf16[2,256,256]{2,1,0:T(8,128)(2,1)S(1)}, u32[]{:S(2)}, u32[]{:S(2)}) collective-permute-start(bf16[2,256,256]{2,1,0:T(8,128)(2,1)S(1)} %pad_maximum_fusion), channel_id=1, source_target_pairs={{0,8},{8,16},{16,24},{24,0},{1,9},{9,17},{17,25},{25,1},{2,10},{10... | collective-permute-start | bytes 786440 | tf_op jit(solution)/shard_map/ppermute | solution.py:22
  20.3 0.2 collective-permute-done.6.refs_1_
  20.5 4.1 %collective-permute-start.7 = (bf16[256,512]{1,0:T(8,128)(2,1)S(1)}, bf16[256,512]{1,0:T(8,128)(2,1)S(1)}, u32[]{:S(2)}, u32[]{:S(2)}) collective-permute-start(bf16[256,512]{1,0:T(8,128)(2,1)S(1)} %collective-permute-done.6.refs_1_), channel_id=1, source_target_pairs={{0,32},{4,228},{32,64},{36,4},{64,96},{68,36},{96,128},{100,68},{1... | collective-permute-start | bytes 786440 | tf_op jit(solution)/shard_map/ppermute | solution.py:22
  24.6 0.0 collective-permute-done.2
  24.6 8.5 %collective-permute-start.3 = (bf16[2,256,256]{2,1,0:T(8,128)(2,1)S(1)}, bf16[2,256,256]{2,1,0:T(8,128)(2,1)S(1)}, u32[]{:S(2)}, u32[]{:S(2)}) collective-permute-start(bf16[2,256,256]{2,1,0:T(8,128)(2,1)S(1)} %collective-permute-done.2), channel_id=1, source_target_pairs={{0,8},{8,16},{16,24},{24,0},{1,9},{9,17},{17,25},{25,1},{2,10},{10... | collective-permute-start | bytes 786440 | tf_op jit(solution)/shard_map/ppermute | solution.py:22
  33.2 2.5 %collective-permute-done.7.refs_2_ = bf16[256,512]{1,0:T(8,128)(2,1)S(1)} collective-permute-done((bf16[256,512]{1,0:T(8,128)(2,1)S(1)}, bf16[256,512]{1,0:T(8,128)(2,1)S(1)}, u32[]{:S(2)}, u32[]{:S(2)}) %collective-permute-start.7) | collective-permute-done | bytes 262176 | tf_op jit(solution)/shard_map/ppermute | solution.py:22
  35.6 1.9 %collective-permute-start.8 = (bf16[256,512]{1,0:T(8,128)(2,1)S(1)}, bf16[256,512]{1,0:T(8,128)(2,1)S(1)}, u32[]{:S(2)}, u32[]{:S(2)}) collective-permute-start(bf16[256,512]{1,0:T(8,128)(2,1)S(1)} %collective-permute-done.7.refs_2_), channel_id=1, source_target_pairs={{0,32},{4,228},{32,64},{36,4},{64,96},{68,36},{96,128},{100,68},{1... | collective-permute-start | bytes 786440 | tf_op jit(solution)/shard_map/ppermute | solution.py:22
  37.5 2.0 %collective-permute-done.3 = bf16[2,256,256]{2,1,0:T(8,128)(2,1)S(1)} collective-permute-done((bf16[2,256,256]{2,1,0:T(8,128)(2,1)S(1)}, bf16[2,256,256]{2,1,0:T(8,128)(2,1)S(1)}, u32[]{:S(2)}, u32[]{:S(2)}) %collective-permute-start.3) | collective-permute-done | bytes 262176 | tf_op jit(solution)/shard_map/ppermute | solution.py:22
  39.5 4.9 %collective-permute-start.4 = (bf16[2,256,256]{2,1,0:T(8,128)(2,1)S(1)}, bf16[2,256,256]{2,1,0:T(8,128)(2,1)S(1)}, u32[]{:S(2)}, u32[]{:S(2)}) collective-permute-start(bf16[2,256,256]{2,1,0:T(8,128)(2,1)S(1)} %collective-permute-done.3), channel_id=1, source_target_pairs={{0,8},{8,16},{16,24},{24,0},{1,9},{9,17},{17,25},{25,1},{2,10},{10... | collective-permute-start | bytes 786440 | tf_op jit(solution)/shard_map/ppermute | solution.py:22
  44.5 3.1 %collective-permute-done.8.refs_3_ = bf16[256,512]{1,0:T(8,128)(2,1)S(1)} collective-permute-done((bf16[256,512]{1,0:T(8,128)(2,1)S(1)}, bf16[256,512]{1,0:T(8,128)(2,1)S(1)}, u32[]{:S(2)}, u32[]{:S(2)}) %collective-permute-start.8) | collective-permute-done | bytes 262176 | tf_op jit(solution)/shard_map/ppermute | solution.py:22
  47.5 1.9 %collective-permute-start.9 = (bf16[256,512]{1,0:T(8,128)(2,1)S(1)}, bf16[256,512]{1,0:T(8,128)(2,1)S(1)}, u32[]{:S(2)}, u32[]{:S(2)}) collective-permute-start(bf16[256,512]{1,0:T(8,128)(2,1)S(1)} %collective-permute-done.8.refs_3_), channel_id=1, source_target_pairs={{0,32},{4,228},{32,64},{36,4},{64,96},{68,36},{96,128},{100,68},{1... | collective-permute-start | bytes 786440 | tf_op jit(solution)/shard_map/ppermute | solution.py:22
  49.5 1.2 %collective-permute-done.4 = bf16[2,256,256]{2,1,0:T(8,128)(2,1)S(1)} collective-permute-done((bf16[2,256,256]{2,1,0:T(8,128)(2,1)S(1)}, bf16[2,256,256]{2,1,0:T(8,128)(2,1)S(1)}, u32[]{:S(2)}, u32[]{:S(2)}) %collective-permute-start.4) | collective-permute-done | bytes 262176 | tf_op jit(solution)/shard_map/ppermute | solution.py:22
  50.7 3.2 %collective-permute-start.5 = (bf16[8,256,256]{2,1,0:T(8,128)(2,1)S(1)}, bf16[8,256,256]{2,1,0:T(8,128)(2,1)S(1)}, u32[]{:S(2)}, u32[]{:S(2)}) collective-permute-start(bf16[8,256,256]{2,1,0:T(8,128)(2,1)S(1)} %constant_dynamic-update-slice_fusion.own_ref), channel_id=1, source_target_pairs={{0,4},{4,0},{1,5},{5,1},{2,6},{6,2},{3,7},{7,3},{8,12},{12,8},{9,1... | collective-permute-start | bytes 3145736 | tf_op jit(solution)/shard_map/ppermute | solution.py:22
  53.9 4.7 %collective-permute-done.9.refs_4_ = bf16[256,512]{1,0:T(8,128)(2,1)S(1)} collective-permute-done((bf16[256,512]{1,0:T(8,128)(2,1)S(1)}, bf16[256,512]{1,0:T(8,128)(2,1)S(1)}, u32[]{:S(2)}, u32[]{:S(2)}) %collective-permute-start.9) | collective-permute-done | bytes 262176 | tf_op jit(solution)/shard_map/ppermute | solution.py:22
  58.6 1.9 %collective-permute-start.10 = (bf16[256,512]{1,0:T(8,128)(2,1)S(1)}, bf16[256,512]{1,0:T(8,128)(2,1)S(1)}, u32[]{:S(2)}, u32[]{:S(2)}) collective-permute-start(bf16[256,512]{1,0:T(8,128)(2,1)S(1)} %collective-permute-done.9.refs_4_), channel_id=1, source_target_pairs={{0,32},{4,228},{32,64},{36,4},{64,96},{68,36},{96,128},{100,68},{1... | collective-permute-start | bytes 786440 | tf_op jit(solution)/shard_map/ppermute | solution.py:22
  60.5 7.5 %collective-permute-done.10.refs_5_ = bf16[256,512]{1,0:T(8,128)(2,1)S(1)} collective-permute-done((bf16[256,512]{1,0:T(8,128)(2,1)S(1)}, bf16[256,512]{1,0:T(8,128)(2,1)S(1)}, u32[]{:S(2)}, u32[]{:S(2)}) %collective-permute-start.10) | collective-permute-done | bytes 262176 | tf_op jit(solution)/shard_map/ppermute | solution.py:22
  68.1 1.9 %collective-permute-start.11 = (bf16[256,512]{1,0:T(8,128)(2,1)S(1)}, bf16[256,512]{1,0:T(8,128)(2,1)}, u32[]{:S(2)}, u32[]{:S(2)}) collective-permute-start(bf16[256,512]{1,0:T(8,128)(2,1)S(1)} %collective-permute-done.10.refs_5_), channel_id=1, source_target_pairs={{0,32},{4,228},{32,64},{36,4},{64,96},{68,36},{96,128},{100,68},{1... | collective-permute-start | bytes 786440 | tf_op jit(solution)/shard_map/ppermute | solution.py:22
  70.0 0.0 copy-start.1
  70.0 0.7 copy-done.1
  70.7 6.9 %collective-permute-done.11.refs_6_ = bf16[256,512]{1,0:T(8,128)(2,1)} collective-permute-done((bf16[256,512]{1,0:T(8,128)(2,1)S(1)}, bf16[256,512]{1,0:T(8,128)(2,1)}, u32[]{:S(2)}, u32[]{:S(2)}) %collective-permute-start.11) | collective-permute-done | bytes 262176 | tf_op jit(solution)/shard_map/ppermute | solution.py:22
  77.7 1.9 %collective-permute-start.12 = (bf16[256,512]{1,0:T(8,128)(2,1)}, bf16[256,512]{1,0:T(8,128)(2,1)}, u32[]{:S(2)}, u32[]{:S(2)}) collective-permute-start(bf16[256,512]{1,0:T(8,128)(2,1)} %collective-permute-done.11.refs_6_), channel_id=1, source_target_pairs={{0,32},{4,228},{32,64},{36,4},{64,96},{68,36},{96,128},{100,68},{1... | collective-permute-start | bytes 786440 | tf_op jit(solution)/shard_map/ppermute | solution.py:22
  80.1 0.1 stack.117.place
  80.2 7.2 %collective-permute-done.12.refs_7_ = bf16[256,512]{1,0:T(8,128)(2,1)} collective-permute-done((bf16[256,512]{1,0:T(8,128)(2,1)}, bf16[256,512]{1,0:T(8,128)(2,1)}, u32[]{:S(2)}, u32[]{:S(2)}) %collective-permute-start.12) | collective-permute-done | bytes 262176 | tf_op jit(solution)/shard_map/ppermute | solution.py:22
  87.4 0.0 collective-permute-done.5.other_ref
  87.5 0.0 copy-start.2
  87.5 0.9 copy-done.2
  88.4 2.3 %shard_map.28 = f32[4,2,256,128]{3,2,1,0:T(8,128)S(1)} custom-call(s32[24]{0:T(128)S(1)} %stack.117.place, bf16[8,256,256]{2,1,0:T(8,128)(2,1)S(1)} %constant_dynamic-update-slice_fusion.own_ref, bf16[8,256,256]{2,1,0:T(8,128)(2,1)S(1)} %collective-permute-done.5.other_ref, bf16[256,512]{1,0:T(8,128)(2,1)S(1)} %copy-done, ...), custom_call_target="tpu_custom_call" | custom-call | tf_op jit(solution)/shard_map/pallas_call | solution.py:89
  90.7 15.2 %all_to_all.5 = f32[4,2,256,128]{3,2,1,0:T(8,128)S(1)} all-to-all(f32[4,2,256,128]{3,2,1,0:T(8,128)S(1)} %shard_map.28), channel_id=1, replica_groups=mesh['yh'=2,'z'=8,'yl'=4,'core'=2,'x'=4] {'x'}, dimensions={0} | all-to-all | bytes 2097152 | tf_op jit(solution)/shard_map/all_to_all | solution.py:96
  105.9 0.1 reduce_sum.9
  106.0 3.0 %collective-permute-start.13 = (f32[256,128]{1,0:T(8,128)S(1)}, f32[256,128]{1,0:T(8,128)S(1)}, u32[]{:S(2)}, u32[]{:S(2)}) collective-permute-start(f32[256,128]{1,0:T(8,128)S(1)} %slice_bitcast_fusion), channel_id=1, source_target_pairs={{0,256},{256,0},{1,257},{257,1},{2,258},{258,2},{3,259},{259,3},{4... | collective-permute-start | bytes 393224 | tf_op jit(solution)/shard_map/ppermute | solution.py:22
  109.0 8.4 %collective-permute-done.13 = f32[256,128]{1,0:T(8,128)S(1)} collective-permute-done((f32[256,128]{1,0:T(8,128)S(1)}, f32[256,128]{1,0:T(8,128)S(1)}, u32[]{:S(2)}, u32[]{:S(2)}) %collective-permute-start.13) | collective-permute-done | bytes 131104 | tf_op jit(solution)/shard_map/ppermute | solution.py:22
  117.4 0.7 fusion.4
  (7 shorter events, 0.1 us)
Async XLA Ops:
  1.0 4.2 %copy-start = (bf16[256,512]{1,0:T(8,128)(2,1)S(1)}, bf16[256,512]{1,0:T(8,128)(2,1)}, u32[]{:S(2)}) copy-start(bf16[256,512]{1,0:T(8,128)(2,1)} %refs_0_.1) | copy-start | bytes 786436
  1.1 8.6 %collective-permute-start.1 = (bf16[256,256]{1,0:T(8,128)(2,1)S(1)}, bf16[256,256]{1,0:T(8,128)(2,1)S(1)}, u32[]{:S(2)}, u32[]{:S(2)}) collective-permute-start(bf16[256,256]{1,0:T(8,128)(2,1)S(1)} %get-tuple-element.5), channel_id=1, source_target_pairs={{0,1},{1,3},{2,0},{3,2},{8,9},{9,11},{10,8},{11,10},{16,257},{17,2... | collective-permute-start | bytes 393224 | tf_op jit(solution)/shard_map/ppermute | solution.py:22
  4.5 5.2 %collective-permute-start = (bf16[256,256]{1,0:T(8,128)(2,1)S(1)}, bf16[256,256]{1,0:T(8,128)(2,1)S(1)}, u32[]{:S(2)}, u32[]{:S(2)}) collective-permute-start(bf16[256,256]{1,0:T(8,128)(2,1)S(1)} %get-tuple-element.6), channel_id=1, source_target_pairs={{0,0},{1,2},{2,1},{3,3},{8,8},{9,10},{10,9},{11,11},{16,256},{17,2... | collective-permute-start | bytes 393224 | tf_op jit(solution)/shard_map/ppermute | solution.py:22
  5.2 15.3 %collective-permute-start.6 = (bf16[256,512]{1,0:T(8,128)(2,1)S(1)}, bf16[256,512]{1,0:T(8,128)(2,1)S(1)}, u32[]{:S(2)}, u32[]{:S(2)}) collective-permute-start(bf16[256,512]{1,0:T(8,128)(2,1)S(1)} %copy-done), channel_id=1, source_target_pairs={{0,32},{4,228},{32,64},{36,4},{64,96},{68,36},{96,128},{100,68},{1... | collective-permute-start | bytes 786440 | tf_op jit(solution)/shard_map/ppermute | solution.py:22
  9.8 14.8 %collective-permute-start.2 = (bf16[2,256,256]{2,1,0:T(8,128)(2,1)S(1)}, bf16[2,256,256]{2,1,0:T(8,128)(2,1)S(1)}, u32[]{:S(2)}, u32[]{:S(2)}) collective-permute-start(bf16[2,256,256]{2,1,0:T(8,128)(2,1)S(1)} %pad_maximum_fusion), channel_id=1, source_target_pairs={{0,8},{8,16},{16,24},{24,0},{1,9},{9,17},{17,25},{25,1},{2,10},{10... | collective-permute-start | bytes 786440 | tf_op jit(solution)/shard_map/ppermute | solution.py:22
  20.5 15.1 %collective-permute-start.7 = (bf16[256,512]{1,0:T(8,128)(2,1)S(1)}, bf16[256,512]{1,0:T(8,128)(2,1)S(1)}, u32[]{:S(2)}, u32[]{:S(2)}) collective-permute-start(bf16[256,512]{1,0:T(8,128)(2,1)S(1)} %collective-permute-done.6.refs_1_), channel_id=1, source_target_pairs={{0,32},{4,228},{32,64},{36,4},{64,96},{68,36},{96,128},{100,68},{1... | collective-permute-start | bytes 786440 | tf_op jit(solution)/shard_map/ppermute | solution.py:22
  24.6 14.9 %collective-permute-start.3 = (bf16[2,256,256]{2,1,0:T(8,128)(2,1)S(1)}, bf16[2,256,256]{2,1,0:T(8,128)(2,1)S(1)}, u32[]{:S(2)}, u32[]{:S(2)}) collective-permute-start(bf16[2,256,256]{2,1,0:T(8,128)(2,1)S(1)} %collective-permute-done.2), channel_id=1, source_target_pairs={{0,8},{8,16},{16,24},{24,0},{1,9},{9,17},{17,25},{25,1},{2,10},{10... | collective-permute-start | bytes 786440 | tf_op jit(solution)/shard_map/ppermute | solution.py:22
  35.6 11.9 %collective-permute-start.8 = (bf16[256,512]{1,0:T(8,128)(2,1)S(1)}, bf16[256,512]{1,0:T(8,128)(2,1)S(1)}, u32[]{:S(2)}, u32[]{:S(2)}) collective-permute-start(bf16[256,512]{1,0:T(8,128)(2,1)S(1)} %collective-permute-done.7.refs_2_), channel_id=1, source_target_pairs={{0,32},{4,228},{32,64},{36,4},{64,96},{68,36},{96,128},{100,68},{1... | collective-permute-start | bytes 786440 | tf_op jit(solution)/shard_map/ppermute | solution.py:22
  39.5 11.2 %collective-permute-start.4 = (bf16[2,256,256]{2,1,0:T(8,128)(2,1)S(1)}, bf16[2,256,256]{2,1,0:T(8,128)(2,1)S(1)}, u32[]{:S(2)}, u32[]{:S(2)}) collective-permute-start(bf16[2,256,256]{2,1,0:T(8,128)(2,1)S(1)} %collective-permute-done.3), channel_id=1, source_target_pairs={{0,8},{8,16},{16,24},{24,0},{1,9},{9,17},{17,25},{25,1},{2,10},{10... | collective-permute-start | bytes 786440 | tf_op jit(solution)/shard_map/ppermute | solution.py:22
  47.5 11.1 %collective-permute-start.9 = (bf16[256,512]{1,0:T(8,128)(2,1)S(1)}, bf16[256,512]{1,0:T(8,128)(2,1)S(1)}, u32[]{:S(2)}, u32[]{:S(2)}) collective-permute-start(bf16[256,512]{1,0:T(8,128)(2,1)S(1)} %collective-permute-done.8.refs_3_), channel_id=1, source_target_pairs={{0,32},{4,228},{32,64},{36,4},{64,96},{68,36},{96,128},{100,68},{1... | collective-permute-start | bytes 786440 | tf_op jit(solution)/shard_map/ppermute | solution.py:22
  50.7 36.7 %collective-permute-start.5 = (bf16[8,256,256]{2,1,0:T(8,128)(2,1)S(1)}, bf16[8,256,256]{2,1,0:T(8,128)(2,1)S(1)}, u32[]{:S(2)}, u32[]{:S(2)}) collective-permute-start(bf16[8,256,256]{2,1,0:T(8,128)(2,1)S(1)} %constant_dynamic-update-slice_fusion.own_ref), channel_id=1, source_target_pairs={{0,4},{4,0},{1,5},{5,1},{2,6},{6,2},{3,7},{7,3},{8,12},{12,8},{9,1... | collective-permute-start | bytes 3145736 | tf_op jit(solution)/shard_map/ppermute | solution.py:22
  58.6 9.5 %collective-permute-start.10 = (bf16[256,512]{1,0:T(8,128)(2,1)S(1)}, bf16[256,512]{1,0:T(8,128)(2,1)S(1)}, u32[]{:S(2)}, u32[]{:S(2)}) collective-permute-start(bf16[256,512]{1,0:T(8,128)(2,1)S(1)} %collective-permute-done.9.refs_4_), channel_id=1, source_target_pairs={{0,32},{4,228},{32,64},{36,4},{64,96},{68,36},{96,128},{100,68},{1... | collective-permute-start | bytes 786440 | tf_op jit(solution)/shard_map/ppermute | solution.py:22
  68.1 9.6 %collective-permute-start.11 = (bf16[256,512]{1,0:T(8,128)(2,1)S(1)}, bf16[256,512]{1,0:T(8,128)(2,1)}, u32[]{:S(2)}, u32[]{:S(2)}) collective-permute-start(bf16[256,512]{1,0:T(8,128)(2,1)S(1)} %collective-permute-done.10.refs_5_), channel_id=1, source_target_pairs={{0,32},{4,228},{32,64},{36,4},{64,96},{68,36},{96,128},{100,68},{1... | collective-permute-start | bytes 786440 | tf_op jit(solution)/shard_map/ppermute | solution.py:22
  70.0 0.7 copy-start.1
  77.7 9.8 %collective-permute-start.12 = (bf16[256,512]{1,0:T(8,128)(2,1)}, bf16[256,512]{1,0:T(8,128)(2,1)}, u32[]{:S(2)}, u32[]{:S(2)}) collective-permute-start(bf16[256,512]{1,0:T(8,128)(2,1)} %collective-permute-done.11.refs_6_), channel_id=1, source_target_pairs={{0,32},{4,228},{32,64},{36,4},{64,96},{68,36},{96,128},{100,68},{1... | collective-permute-start | bytes 786440 | tf_op jit(solution)/shard_map/ppermute | solution.py:22
  87.5 1.0 copy-start.2
  106.0 11.4 %collective-permute-start.13 = (f32[256,128]{1,0:T(8,128)S(1)}, f32[256,128]{1,0:T(8,128)S(1)}, u32[]{:S(2)}, u32[]{:S(2)}) collective-permute-start(f32[256,128]{1,0:T(8,128)S(1)} %slice_bitcast_fusion), channel_id=1, source_target_pairs={{0,256},{256,0},{1,257},{257,1},{2,258},{258,2},{3,259},{259,3},{4... | collective-permute-start | bytes 393224 | tf_op jit(solution)/shard_map/ppermute | solution.py:22

commit v3 on v2

--- a/solution.py
+++ b/solution.py
@@ -22,14 +22,19 @@
     return lax.ppermute(value, axes, perm)
 
 
-def around_z(value, sizes):
+def around_z(value, sizes, by):
+    return moved(value, sizes, ("z",), lambda z: {"z": (z + by) % sizes["z"]})
+
+
+def opposite_z(up, down, core, sizes):
+    value = jnp.where(core == 0, up, down)
     return moved(
-        value, sizes, ("z", "core"), lambda z, core: {"z": (z + 1 - 2 * core) % sizes["z"], "core": core}
+        value, sizes, ("z", "core"), lambda z, core: {"z": (z + 2 - 4 * core) % sizes["z"], "core": core}
     )
 
 
-def along_yl(value, sizes):
-    return moved(value, sizes, ("yl",), lambda yl: {"yl": (yl + 1) % sizes["yl"]})
+def along_yl(value, sizes, by):
+    return moved(value, sizes, ("yl",), lambda yl: {"yl": (yl + by) % sizes["yl"]})
 
 
 def core_swap(value, sizes):
@@ -64,21 +69,22 @@
 def per_device(sizes, integrals, amplitudes):
     yh, z, yl, core, x = (lax.axis_index(a) for a in AXES)
     rows = integrals.shape[0]
-    tiles = [amplitudes]
-    for _ in range(sizes["z"] - 1):
-        tiles.append(around_z(tiles[-1], sizes))
+    tiles = {0: amplitudes}
+    for by in (1, -1, 2, -2):
+        tiles[-by] = around_z(amplitudes, sizes, by)
+    tiles[-3] = around_z(tiles[-2], sizes, 1)
+    tiles[3] = around_z(tiles[2], sizes, -1)
+    tiles[4] = opposite_z(tiles[-2], tiles[2], core, sizes)
     halves = jnp.stack([integrals[:, :UNIT], integrals[:, UNIT:]])
     high = x >> 1
     first = regroup(lax.dynamic_index_in_dim(halves, high, 0, False), sizes, 0)
     second = regroup(lax.dynamic_index_in_dim(halves, 1 - high, 0, False), sizes, 1)
-    slabs = [jnp.stack([first, second])]
-    for _ in range(sizes["yl"] - 1):
-        slabs.append(along_yl(slabs[-1], sizes))
-    own = jnp.concatenate(slabs)
+    slab = jnp.stack([first, second])
+    own = jnp.concatenate([slab] + [along_yl(slab, sizes, by) for by in range(1, sizes["yl"])])
     other = core_swap(own, sizes)
     place = []
-    for step in range(sizes["z"]):
-        unit = (z + step * (2 * core - 1)) % sizes["z"]
+    for offset in tiles:
+        unit = (z + offset) % sizes["z"]
         u4, u3, u2 = unit >> 2, (unit >> 1) & 1, unit & 1
         place.append(jnp.where(u3 == core, 1, 0))
         for rel in range(2):
@@ -92,7 +98,7 @@
         in_specs=[pl.BlockSpec(memory_space=pltpu.SMEM)] + [vmem] * 10,
         out_specs=vmem,
         compiler_params=pltpu.CompilerParams(vmem_limit_bytes=48 * 1024 * 1024),
-    )(place, own, other, *tiles)
+    )(place, own, other, *tiles.values())
     part = lax.all_to_all(part, "x", split_axis=0, concat_axis=0, tiled=True)
     total = part.sum(axis=0)
     other = moved(total[1], sizes, ("yh",), lambda yh: {"yh": 1 - yh})

time: 119 us -> 126 us (1.059)
  the two profiles are of different devices: /device:TPU:56 before, /device:TPU:32 now
where the time goes in v3:
time: 126 us
  starting transfers between devices  59 us (47%)
  waiting for transfers between devices  42.7 us (34%)
  blocking collectives  18.1 us (14%)
  Pallas kernels  2.37 us (2%)
  other arithmetic  1.63 us (1%)
    ppermute x14, starting transfers between devices, moved(): return lax.ppermute(value, axes, perm)  59 us
    ppermute x14, waiting for transfers between devices, moved(): return lax.ppermute(value, axes, perm)  42.7 us
    all_to_all x1, blocking collectives, per_device(): part = lax.all_to_all(part, 'x', split_axis=0, concat_axis=0, tiled=True)  18.1 us
  transfers between devices with their start and end apart: 14, of which 7 were waited for; matrix products, arithmetic and copies ran while one was open for 1% of the time, Pallas kernels for 0%

profile of v3, /device:TPU:32, one launch (start us, length us, event | category | flops | bytes accessed | tf_op | source)
XLA Modules:
  0.0 125.8 jit_solution(10403550746299552048)
XLA Ops:
  0.0 1.0 slice_bitcast_fusion.2
  1.0 0.1 fusion.1
  1.1 3.2 %collective-permute-start.1 = (bf16[256,256]{1,0:T(8,128)(2,1)S(1)}, bf16[256,256]{1,0:T(8,128)(2,1)S(1)}, u32[]{:S(2)}, u32[]{:S(2)}) collective-permute-start(bf16[256,256]{1,0:T(8,128)(2,1)S(1)} %get-tuple-element.5), channel_id=1, source_target_pairs={{0,1},{1,3},{2,0},{3,2},{8,9},{9,11},{10,8},{11,10},{16,257},{17,2... | collective-permute-start | bytes 393224 | tf_op jit(solution)/shard_map/ppermute | solution.py:22
  4.3 5.7 %collective-permute-start = (bf16[256,256]{1,0:T(8,128)(2,1)S(1)}, bf16[256,256]{1,0:T(8,128)(2,1)S(1)}, u32[]{:S(2)}, u32[]{:S(2)}) collective-permute-start(bf16[256,256]{1,0:T(8,128)(2,1)S(1)} %get-tuple-element.6), channel_id=1, source_target_pairs={{0,0},{1,2},{2,1},{3,3},{8,8},{9,10},{10,9},{11,11},{16,256},{17,2... | collective-permute-start | bytes 393224 | tf_op jit(solution)/shard_map/ppermute | solution.py:22
  10.0 2.9 %collective-permute-done.1 = bf16[256,256]{1,0:T(8,128)(2,1)S(1)} collective-permute-done((bf16[256,256]{1,0:T(8,128)(2,1)S(1)}, bf16[256,256]{1,0:T(8,128)(2,1)S(1)}, u32[]{:S(2)}, u32[]{:S(2)}) %collective-permute-start.1) | collective-permute-done | bytes 131104 | tf_op jit(solution)/shard_map/ppermute | solution.py:22
  12.9 2.6 %collective-permute-done = bf16[256,256]{1,0:T(8,128)(2,1)S(1)} collective-permute-done((bf16[256,256]{1,0:T(8,128)(2,1)S(1)}, bf16[256,256]{1,0:T(8,128)(2,1)S(1)}, u32[]{:S(2)}, u32[]{:S(2)}) %collective-permute-start) | collective-permute-done | bytes 131104 | tf_op jit(solution)/shard_map/ppermute | solution.py:22
  15.5 1.9 %collective-permute-start.4 = (bf16[2,256,256]{2,1,0:T(8,128)(2,1)S(1)}, bf16[2,256,256]{2,1,0:T(8,128)(2,1)S(1)}, u32[]{:S(2)}, u32[]{:S(2)}) collective-permute-start(bf16[2,256,256]{2,1,0:T(8,128)(2,1)S(1)} %pad_maximum_fusion), channel_id=1, source_target_pairs={{0,24},{8,0},{16,8},{24,16},{1,25},{9,1},{17,9},{25,17},{2,26},{10... | collective-permute-start | bytes 786440 | tf_op jit(solution)/shard_map/ppermute | solution.py:22
  17.4 8.3 %collective-permute-start.3 = (bf16[2,256,256]{2,1,0:T(8,128)(2,1)S(1)}, bf16[2,256,256]{2,1,0:T(8,128)(2,1)S(1)}, u32[]{:S(2)}, u32[]{:S(2)}) collective-permute-start(bf16[2,256,256]{2,1,0:T(8,128)(2,1)S(1)} %pad_maximum_fusion), channel_id=1, source_target_pairs={{0,16},{8,24},{16,0},{24,8},{1,17},{9,25},{17,1},{25,9},{2,18},{10... | collective-permute-start | bytes 786440 | tf_op jit(solution)/shard_map/ppermute | solution.py:22
  25.7 1.9 %collective-permute-start.2 = (bf16[2,256,256]{2,1,0:T(8,128)(2,1)S(1)}, bf16[2,256,256]{2,1,0:T(8,128)(2,1)S(1)}, u32[]{:S(2)}, u32[]{:S(2)}) collective-permute-start(bf16[2,256,256]{2,1,0:T(8,128)(2,1)S(1)} %pad_maximum_fusion), channel_id=1, source_target_pairs={{0,8},{8,16},{16,24},{24,0},{1,9},{9,17},{17,25},{25,1},{2,10},{10... | collective-permute-start | bytes 786440 | tf_op jit(solution)/shard_map/ppermute | solution.py:22
  27.7 10.0 %collective-permute-done.2 = bf16[2,256,256]{2,1,0:T(8,128)(2,1)S(1)} collective-permute-done((bf16[2,256,256]{2,1,0:T(8,128)(2,1)S(1)}, bf16[2,256,256]{2,1,0:T(8,128)(2,1)S(1)}, u32[]{:S(2)}, u32[]{:S(2)}) %collective-permute-start.2) | collective-permute-done | bytes 262176 | tf_op jit(solution)/shard_map/ppermute | solution.py:22
  37.7 8.3 %collective-permute-done.3 = bf16[2,256,256]{2,1,0:T(8,128)(2,1)S(1)} collective-permute-done((bf16[2,256,256]{2,1,0:T(8,128)(2,1)S(1)}, bf16[2,256,256]{2,1,0:T(8,128)(2,1)S(1)}, u32[]{:S(2)}, u32[]{:S(2)}) %collective-permute-start.3) | collective-permute-done | bytes 262176 | tf_op jit(solution)/shard_map/ppermute | solution.py:22
  46.0 0.0 copy-start
  46.1 0.0 collective-permute-done.4
  46.1 2.1 %collective-permute-start.5 = (bf16[8,256,256]{2,1,0:T(8,128)(2,1)S(1)}, bf16[8,256,256]{2,1,0:T(8,128)(2,1)S(1)}, u32[]{:S(2)}, u32[]{:S(2)}) collective-permute-start(bf16[8,256,256]{2,1,0:T(8,128)(2,1)S(1)} %constant_dynamic-update-slice_fusion.own_ref), channel_id=1, source_target_pairs={{0,4},{4,0},{1,5},{5,1},{2,6},{6,2},{3,7},{7,3},{8,12},{12,8},{9,1... | collective-permute-start | bytes 3145736 | tf_op jit(solution)/shard_map/ppermute | solution.py:22
  48.2 0.0 copy-done
  48.2 6.1 %collective-permute-start.8 = (bf16[256,512]{1,0:T(8,128)(2,1)S(1)}, bf16[256,512]{1,0:T(8,128)(2,1)S(1)}, u32[]{:S(2)}, u32[]{:S(2)}) collective-permute-start(bf16[256,512]{1,0:T(8,128)(2,1)S(1)} %copy-done), channel_id=1, source_target_pairs={{0,64},{32,96},{64,128},{96,160},{128,192},{160,224},{192,0},{224,... | collective-permute-start | bytes 786440 | tf_op jit(solution)/shard_map/ppermute | solution.py:22
  54.3 6.8 %collective-permute-start.9 = (bf16[256,512]{1,0:T(8,128)(2,1)S(1)}, bf16[256,512]{1,0:T(8,128)(2,1)S(1)}, u32[]{:S(2)}, u32[]{:S(2)}) collective-permute-start(bf16[256,512]{1,0:T(8,128)(2,1)S(1)} %copy-done), channel_id=1, source_target_pairs={{0,192},{32,224},{64,0},{96,32},{128,64},{160,96},{192,128},{224,1... | collective-permute-start | bytes 786440 | tf_op jit(solution)/shard_map/ppermute | solution.py:22
  61.0 4.8 %collective-permute-start.7 = (bf16[256,512]{1,0:T(8,128)(2,1)S(1)}, bf16[256,512]{1,0:T(8,128)(2,1)S(1)}, u32[]{:S(2)}, u32[]{:S(2)}) collective-permute-start(bf16[256,512]{1,0:T(8,128)(2,1)S(1)} %copy-done), channel_id=1, source_target_pairs={{0,224},{32,0},{64,32},{96,64},{128,96},{160,128},{192,160},{224,1... | collective-permute-start | bytes 786440 | tf_op jit(solution)/shard_map/ppermute | solution.py:22
  65.9 1.9 %collective-permute-start.6 = (bf16[256,512]{1,0:T(8,128)(2,1)S(1)}, bf16[256,512]{1,0:T(8,128)(2,1)S(1)}, u32[]{:S(2)}, u32[]{:S(2)}) collective-permute-start(bf16[256,512]{1,0:T(8,128)(2,1)S(1)} %copy-done), channel_id=1, source_target_pairs={{0,32},{32,64},{64,96},{96,128},{128,160},{160,192},{192,224},{224... | collective-permute-start | bytes 786440 | tf_op jit(solution)/shard_map/ppermute | solution.py:22
  67.8 0.0 collective-permute-done.8.refs_3_
  67.8 6.0 %collective-permute-done.9.refs_4_ = bf16[256,512]{1,0:T(8,128)(2,1)S(1)} collective-permute-done((bf16[256,512]{1,0:T(8,128)(2,1)S(1)}, bf16[256,512]{1,0:T(8,128)(2,1)S(1)}, u32[]{:S(2)}, u32[]{:S(2)}) %collective-permute-start.9) | collective-permute-done | bytes 262176 | tf_op jit(solution)/shard_map/ppermute | solution.py:22
  73.9 0.7 broadcast_select_fusion
  74.6 6.5 %collective-permute-start.12 = (bf16[256,512]{1,0:T(8,128)(2,1)}, bf16[256,512]{1,0:T(8,128)(2,1)}, u32[]{:S(2)}, u32[]{:S(2)}) collective-permute-start(bf16[256,512]{1,0:T(8,128)(2,1)} %broadcast_select_fusion), channel_id=1, source_target_pairs={{0,64},{4,196},{32,96},{36,228},{64,128},{68,4},{96,160},{100,36},... | collective-permute-start | bytes 786440 | tf_op jit(solution)/shard_map/ppermute | solution.py:22
  81.1 2.4 %collective-permute-start.10 = (bf16[256,512]{1,0:T(8,128)(2,1)S(1)}, bf16[256,512]{1,0:T(8,128)(2,1)}, u32[]{:S(2)}, u32[]{:S(2)}) collective-permute-start(bf16[256,512]{1,0:T(8,128)(2,1)S(1)} %collective-permute-done.8.refs_3_), channel_id=1, source_target_pairs={{0,32},{32,64},{64,96},{96,128},{128,160},{160,192},{192,224},{224... | collective-permute-start | bytes 786440 | tf_op jit(solution)/shard_map/ppermute | solution.py:22
  83.5 0.0 collective-permute-done.7.refs_2_
  83.5 4.6 %collective-permute-start.11 = (bf16[256,512]{1,0:T(8,128)(2,1)S(1)}, bf16[256,512]{1,0:T(8,128)(2,1)}, u32[]{:S(2)}, u32[]{:S(2)}) collective-permute-start(bf16[256,512]{1,0:T(8,128)(2,1)S(1)} %collective-permute-done.9.refs_4_), channel_id=1, source_target_pairs={{0,224},{32,0},{64,32},{96,64},{128,96},{160,128},{192,160},{224,1... | collective-permute-start | bytes 786440 | tf_op jit(solution)/shard_map/ppermute | solution.py:22
  88.6 0.1 stack.117.place
  88.8 0.0 collective-permute-done.6.refs_1_
  88.8 5.0 %collective-permute-done.10.refs_5_ = bf16[256,512]{1,0:T(8,128)(2,1)} collective-permute-done((bf16[256,512]{1,0:T(8,128)(2,1)S(1)}, bf16[256,512]{1,0:T(8,128)(2,1)}, u32[]{:S(2)}, u32[]{:S(2)}) %collective-permute-start.10) | collective-permute-done | bytes 262176 | tf_op jit(solution)/shard_map/ppermute | solution.py:22
  93.7 0.0 collective-permute-done.12.refs_7_
  93.7 0.0 collective-permute-done.11.refs_6_
  93.7 0.0 collective-permute-done.5.other_ref
  93.7 2.4 %shard_map.28 = f32[4,2,256,128]{3,2,1,0:T(8,128)S(1)} custom-call(s32[24]{0:T(128)S(1)} %stack.117.place, bf16[8,256,256]{2,1,0:T(8,128)(2,1)S(1)} %constant_dynamic-update-slice_fusion.own_ref, bf16[8,256,256]{2,1,0:T(8,128)(2,1)S(1)} %collective-permute-done.5.other_ref, bf16[256,512]{1,0:T(8,128)(2,1)S(1)} %copy-done, ...), custom_call_target="tpu_custom_call" | custom-call | tf_op jit(solution)/shard_map/pallas_call | solution.py:95
  96.1 18.1 %all_to_all.5 = f32[4,2,256,128]{3,2,1,0:T(8,128)S(1)} all-to-all(f32[4,2,256,128]{3,2,1,0:T(8,128)S(1)} %shard_map.28), channel_id=1, replica_groups=mesh['yh'=2,'z'=8,'yl'=4,'core'=2,'x'=4] {'x'}, dimensions={0} | all-to-all | bytes 2097152 | tf_op jit(solution)/shard_map/all_to_all | solution.py:102
  114.2 0.1 reduce_sum.9
  114.3 2.9 %collective-permute-start.13 = (f32[256,128]{1,0:T(8,128)S(1)}, f32[256,128]{1,0:T(8,128)S(1)}, u32[]{:S(2)}, u32[]{:S(2)}) collective-permute-start(f32[256,128]{1,0:T(8,128)S(1)} %slice_bitcast_fusion), channel_id=1, source_target_pairs={{0,256},{256,0},{1,257},{257,1},{2,258},{258,2},{3,259},{259,3},{4... | collective-permute-start | bytes 393224 | tf_op jit(solution)/shard_map/ppermute | solution.py:22
  117.2 7.9 %collective-permute-done.13 = f32[256,128]{1,0:T(8,128)S(1)} collective-permute-done((f32[256,128]{1,0:T(8,128)S(1)}, f32[256,128]{1,0:T(8,128)S(1)}, u32[]{:S(2)}, u32[]{:S(2)}) %collective-permute-start.13) | collective-permute-done | bytes 131104 | tf_op jit(solution)/shard_map/ppermute | solution.py:22
  125.1 0.7 fusion.4
  (7 shorter events, 0.1 us)
Async XLA Ops:
  1.1 11.7 %collective-permute-start.1 = (bf16[256,256]{1,0:T(8,128)(2,1)S(1)}, bf16[256,256]{1,0:T(8,128)(2,1)S(1)}, u32[]{:S(2)}, u32[]{:S(2)}) collective-permute-start(bf16[256,256]{1,0:T(8,128)(2,1)S(1)} %get-tuple-element.5), channel_id=1, source_target_pairs={{0,1},{1,3},{2,0},{3,2},{8,9},{9,11},{10,8},{11,10},{16,257},{17,2... | collective-permute-start | bytes 393224 | tf_op jit(solution)/shard_map/ppermute | solution.py:22
  4.3 11.2 %collective-permute-start = (bf16[256,256]{1,0:T(8,128)(2,1)S(1)}, bf16[256,256]{1,0:T(8,128)(2,1)S(1)}, u32[]{:S(2)}, u32[]{:S(2)}) collective-permute-start(bf16[256,256]{1,0:T(8,128)(2,1)S(1)} %get-tuple-element.6), channel_id=1, source_target_pairs={{0,0},{1,2},{2,1},{3,3},{8,8},{9,10},{10,9},{11,11},{16,256},{17,2... | collective-permute-start | bytes 393224 | tf_op jit(solution)/shard_map/ppermute | solution.py:22
  15.5 30.6 %collective-permute-start.4 = (bf16[2,256,256]{2,1,0:T(8,128)(2,1)S(1)}, bf16[2,256,256]{2,1,0:T(8,128)(2,1)S(1)}, u32[]{:S(2)}, u32[]{:S(2)}) collective-permute-start(bf16[2,256,256]{2,1,0:T(8,128)(2,1)S(1)} %pad_maximum_fusion), channel_id=1, source_target_pairs={{0,24},{8,0},{16,8},{24,16},{1,25},{9,1},{17,9},{25,17},{2,26},{10... | collective-permute-start | bytes 786440 | tf_op jit(solution)/shard_map/ppermute | solution.py:22
  17.4 28.6 %collective-permute-start.3 = (bf16[2,256,256]{2,1,0:T(8,128)(2,1)S(1)}, bf16[2,256,256]{2,1,0:T(8,128)(2,1)S(1)}, u32[]{:S(2)}, u32[]{:S(2)}) collective-permute-start(bf16[2,256,256]{2,1,0:T(8,128)(2,1)S(1)} %pad_maximum_fusion), channel_id=1, source_target_pairs={{0,16},{8,24},{16,0},{24,8},{1,17},{9,25},{17,1},{25,9},{2,18},{10... | collective-permute-start | bytes 786440 | tf_op jit(solution)/shard_map/ppermute | solution.py:22
  25.7 12.0 %collective-permute-start.2 = (bf16[2,256,256]{2,1,0:T(8,128)(2,1)S(1)}, bf16[2,256,256]{2,1,0:T(8,128)(2,1)S(1)}, u32[]{:S(2)}, u32[]{:S(2)}) collective-permute-start(bf16[2,256,256]{2,1,0:T(8,128)(2,1)S(1)} %pad_maximum_fusion), channel_id=1, source_target_pairs={{0,8},{8,16},{16,24},{24,0},{1,9},{9,17},{17,25},{25,1},{2,10},{10... | collective-permute-start | bytes 786440 | tf_op jit(solution)/shard_map/ppermute | solution.py:22
  46.0 2.1 %copy-start = (bf16[256,512]{1,0:T(8,128)(2,1)S(1)}, bf16[256,512]{1,0:T(8,128)(2,1)}, u32[]{:S(2)}) copy-start(bf16[256,512]{1,0:T(8,128)(2,1)} %refs_0_.1) | copy-start | bytes 786436
  46.1 47.6 %collective-permute-start.5 = (bf16[8,256,256]{2,1,0:T(8,128)(2,1)S(1)}, bf16[8,256,256]{2,1,0:T(8,128)(2,1)S(1)}, u32[]{:S(2)}, u32[]{:S(2)}) collective-permute-start(bf16[8,256,256]{2,1,0:T(8,128)(2,1)S(1)} %constant_dynamic-update-slice_fusion.own_ref), channel_id=1, source_target_pairs={{0,4},{4,0},{1,5},{5,1},{2,6},{6,2},{3,7},{7,3},{8,12},{12,8},{9,1... | collective-permute-start | bytes 3145736 | tf_op jit(solution)/shard_map/ppermute | solution.py:22
  48.2 19.7 %collective-permute-start.8 = (bf16[256,512]{1,0:T(8,128)(2,1)S(1)}, bf16[256,512]{1,0:T(8,128)(2,1)S(1)}, u32[]{:S(2)}, u32[]{:S(2)}) collective-permute-start(bf16[256,512]{1,0:T(8,128)(2,1)S(1)} %copy-done), channel_id=1, source_target_pairs={{0,64},{32,96},{64,128},{96,160},{128,192},{160,224},{192,0},{224,... | collective-permute-start | bytes 786440 | tf_op jit(solution)/shard_map/ppermute | solution.py:22
  54.3 19.6 %collective-permute-start.9 = (bf16[256,512]{1,0:T(8,128)(2,1)S(1)}, bf16[256,512]{1,0:T(8,128)(2,1)S(1)}, u32[]{:S(2)}, u32[]{:S(2)}) collective-permute-start(bf16[256,512]{1,0:T(8,128)(2,1)S(1)} %copy-done), channel_id=1, source_target_pairs={{0,192},{32,224},{64,0},{96,32},{128,64},{160,96},{192,128},{224,1... | collective-permute-start | bytes 786440 | tf_op jit(solution)/shard_map/ppermute | solution.py:22
  61.0 22.5 %collective-permute-start.7 = (bf16[256,512]{1,0:T(8,128)(2,1)S(1)}, bf16[256,512]{1,0:T(8,128)(2,1)S(1)}, u32[]{:S(2)}, u32[]{:S(2)}) collective-permute-start(bf16[256,512]{1,0:T(8,128)(2,1)S(1)} %copy-done), channel_id=1, source_target_pairs={{0,224},{32,0},{64,32},{96,64},{128,96},{160,128},{192,160},{224,1... | collective-permute-start | bytes 786440 | tf_op jit(solution)/shard_map/ppermute | solution.py:22
  65.9 22.9 %collective-permute-start.6 = (bf16[256,512]{1,0:T(8,128)(2,1)S(1)}, bf16[256,512]{1,0:T(8,128)(2,1)S(1)}, u32[]{:S(2)}, u32[]{:S(2)}) collective-permute-start(bf16[256,512]{1,0:T(8,128)(2,1)S(1)} %copy-done), channel_id=1, source_target_pairs={{0,32},{32,64},{64,96},{96,128},{128,160},{160,192},{192,224},{224... | collective-permute-start | bytes 786440 | tf_op jit(solution)/shard_map/ppermute | solution.py:22
  74.6 19.1 %collective-permute-start.12 = (bf16[256,512]{1,0:T(8,128)(2,1)}, bf16[256,512]{1,0:T(8,128)(2,1)}, u32[]{:S(2)}, u32[]{:S(2)}) collective-permute-start(bf16[256,512]{1,0:T(8,128)(2,1)} %broadcast_select_fusion), channel_id=1, source_target_pairs={{0,64},{4,196},{32,96},{36,228},{64,128},{68,4},{96,160},{100,36},... | collective-permute-start | bytes 786440 | tf_op jit(solution)/shard_map/ppermute | solution.py:22
  81.1 12.6 %collective-permute-start.10 = (bf16[256,512]{1,0:T(8,128)(2,1)S(1)}, bf16[256,512]{1,0:T(8,128)(2,1)}, u32[]{:S(2)}, u32[]{:S(2)}) collective-permute-start(bf16[256,512]{1,0:T(8,128)(2,1)S(1)} %collective-permute-done.8.refs_3_), channel_id=1, source_target_pairs={{0,32},{32,64},{64,96},{96,128},{128,160},{160,192},{192,224},{224... | collective-permute-start | bytes 786440 | tf_op jit(solution)/shard_map/ppermute | solution.py:22
  83.5 10.2 %collective-permute-start.11 = (bf16[256,512]{1,0:T(8,128)(2,1)S(1)}, bf16[256,512]{1,0:T(8,128)(2,1)}, u32[]{:S(2)}, u32[]{:S(2)}) collective-permute-start(bf16[256,512]{1,0:T(8,128)(2,1)S(1)} %collective-permute-done.9.refs_4_), channel_id=1, source_target_pairs={{0,224},{32,0},{64,32},{96,64},{128,96},{160,128},{192,160},{224,1... | collective-permute-start | bytes 786440 | tf_op jit(solution)/shard_map/ppermute | solution.py:22
  114.3 10.8 %collective-permute-start.13 = (f32[256,128]{1,0:T(8,128)S(1)}, f32[256,128]{1,0:T(8,128)S(1)}, u32[]{:S(2)}, u32[]{:S(2)}) collective-permute-start(f32[256,128]{1,0:T(8,128)S(1)} %slice_bitcast_fusion), channel_id=1, source_target_pairs={{0,256},{256,0},{1,257},{257,1},{2,258},{258,2},{3,259},{259,3},{4... | collective-permute-start | bytes 393224 | tf_op jit(solution)/shard_map/ppermute | solution.py:22

commit v4 on v1

v4 whole, which is shorter than its diff:
```python
import functools

import jax
import jax.numpy as jnp
import numpy as np
from jax import lax
from jax.experimental import pallas as pl
from jax.experimental.pallas import tpu as pltpu
from jax.sharding import Mesh, PartitionSpec as P

AXES = ("yh", "zh", "zl", "yl", "core", "x")
SHAPE = (2, 4, 2, 4, 2, 4)
SIZES = dict(zip(AXES, SHAPE))
UNIT = 256


def moved(value, axes, where):
    shape = [SIZES[a] for a in axes]
    perm = []
    for i in range(int(np.prod(shape))):
        place = dict(zip(axes, (int(v) for v in np.unravel_index(i, shape))))
        there = where(**place)
        perm.append((i, int(np.ravel_multi_index([there[a] for a in axes], shape))))
    return lax.ppermute(value, axes, perm)


def along_z(value, by):
    def where(zh, zl):
        z = (2 * zh + zl + by) % 8
        return {"zh": z >> 1, "zl": z & 1}

    return moved(value, ("zh", "zl"), where)


def regrouped(value, turned, second):
    def where(yh, yl, x):
        half = (x >> 1) ^ second
        return {"yh": yl >> 1, "yl": 2 * (yh ^ turned) + (yl & 1), "x": 2 * (x & 1) + half}

    return moved(value, ("yh", "yl", "x"), where)


def core_swap(value):
    return moved(value, ("core",), lambda core: {"core": 1 - core})


def product_kernel(rel, place, near_ref, far_ref, near2_ref, far2_ref, even_ref, up_ref, down_ref, out_ref):
    tiles = [even_ref.at[i] for i in range(4)] + [up_ref.at[i] for i in range(2)] + [down_ref.at[i] for i in range(2)]
    for step, t_ref in enumerate(tiles):
        same, near, slot = place[4 * step] == 1, place[4 * step + 1] == 1, place[4 * step + 2 + rel]
        w = jnp.where(
            same,
            jnp.where(near, near_ref[slot], far_ref[slot]),
            jnp.where(near, near2_ref[slot], far2_ref[slot]),
        )
        part = jnp.dot(w, t_ref[...], preferred_element_type=jnp.float32)
        for block in range(4):
            cols = part[:, block * 128 : (block + 1) * 128]
            if step == 0:
                out_ref[block] = cols
            else:
                out_ref[block] += cols


def product(rel, place, *operands):
    vmem = pl.BlockSpec(memory_space=pltpu.VMEM)
    return pl.pallas_call(
        functools.partial(product_kernel, rel),
        out_shape=jax.ShapeDtypeStruct((4, UNIT, 128), jnp.float32),
        in_specs=[pl.BlockSpec(memory_space=pltpu.SMEM)] + [vmem] * len(operands),
        out_specs=vmem,
        compiler_params=pltpu.CompilerParams(vmem_limit_bytes=40 * 1024 * 1024),
    )(place, *operands)


def over_depth(part):
    return lax.all_to_all(part, "x", split_axis=0, concat_axis=0, tiled=True).sum(axis=0)


def per_device(integrals, amplitudes):
    yh, zh, zl, yl, core, x = (lax.axis_index(a) for a in AXES)
    copies = jnp.broadcast_to(amplitudes[None], (4,) + amplitudes.shape)
    even = lax.all_to_all(copies, "zh", split_axis=0, concat_axis=0, tiled=True)
    from_up = along_z(even[:2], -1)
    from_down = along_z(even[2:], 1)
    halves = jnp.stack([integrals[:, :UNIT], integrals[:, UNIT:]])
    high = x >> 1
    picked = [lax.dynamic_index_in_dim(halves, high ^ second, 0, False) for second in (0, 1)]
    near = jnp.stack([regrouped(picked[second], turned, second) for turned in (0, 1) for second in (0, 1)])
    far = moved(near, ("yl",), lambda yl: {"yl": yl ^ 1})
    near2, far2 = core_swap(near), core_swap(far)
    place = []
    for their_zh, their_zl in [(i, zl) for i in range(4)] + [(i, 1 - zl) for i in range(4)]:
        u4, u3, u2 = their_zh >> 1, their_zh & 1, their_zl
        place += [jnp.where(core == u3, 1, 0), jnp.where((yl & 1) == u4, 1, 0)]
        place += [((yh ^ rel) ^ (yl >> 1)) * 2 + (u2 ^ (x & 1)) for rel in (0, 1)]
    place = jnp.stack(place).astype(jnp.int32)
    operands = (near, far, near2, far2, even, from_up, from_down)
    other = over_depth(product(1, place, *operands))
    other = moved(other, ("yh",), lambda yh: {"yh": 1 - yh})
    return over_depth(product(0, place, *operands)) + other


def solution(mesh):
    return jax.shard_map(
        per_device,
        mesh=Mesh(mesh.devices.reshape(SHAPE), AXES),
        in_specs=(P(("yh", "zh", "zl"), ("yl", "core", "x")), P(("yh", "zh", "zl", "x"), ("yl", "core"))),
        out_specs=P(("yh", "zh", "zl"), ("yl", "core", "x")),
        check_vma=False,
    )
```

time: 144 us -> 113 us (0.78)
  the two profiles are of different devices: /device:TPU:24 before, /device:TPU:18 now
where the time goes in v4:
time: 113 us
  starting transfers between devices  55.5 us (49%)
  waiting for transfers between devices  46.4 us (41%)
  local copies, waits for them, and re-layouts  4.8 us (4%)
  Pallas kernels  3.81 us (3%)
  other arithmetic  1.96 us (2%)
    ppermute x10, waiting for transfers between devices, moved(): return lax.ppermute(value, axes, perm)  36.6 us
    ppermute x10, starting transfers between devices, moved(): return lax.ppermute(value, axes, perm)  32.9 us
    all_to_all x2, starting transfers between devices, over_depth(): lax.all_to_all(part, 'x', split_axis=0, concat_axis=0, tiled=True)  12.2 us
    all_to_all x1, starting transfers between devices, per_device(): even = lax.all_to_all(copies, 'zh', split_axis=0, concat_axis=0, tiled=True)  10.4 us
    all_to_all x2, waiting for transfers between devices, over_depth(): lax.all_to_all(part, 'x', split_axis=0, concat_axis=0, tiled=True)  9.86 us
    pallas_call x2, Pallas kernels, product(): pl.pallas_call(functools.partial(product_kernel, rel), out_shape=jax.Shap...  3.81 us
  transfers between devices with their start and end apart: 13, of which 8 were waited for; matrix products, arithmetic and copies ran while one was open for 2% of the time, Pallas kernels for 2%

profile of v4, /device:TPU:18, one launch (start us, length us, event | category | flops | bytes accessed | tf_op | source)
XLA Modules:
  0.0 112.7 jit_solution(2308758389863413273)
XLA Ops:
  0.0 2.0 %broadcast_in_dim.2 = bf16[4,256,512]{2,1,0:T(8,128)(2,1)} broadcast(bf16[256,512]{1,0:T(8,128)(2,1)} %param.3), dimensions={1,2} | broadcast | bytes 1310720 | tf_op jit(solution)/shard_map/broadcast_in_dim | solution.py:82
  2.0 0.0 copy-start.2
  2.0 10.4 %all-to-all-start = ((bf16[4,256,512]{2,1,0:T(8,128)(2,1)}), bf16[4,256,512]{2,1,0:T(8,128)(2,1)S(1)}, u32[]{:S(2)}, u32[]{:S(2)}) async-start(bf16[4,256,512]{2,1,0:T(8,128)(2,1)} %broadcast_in_dim.2), calls=%async_computation | async-start | bytes 2097152 | tf_op jit(solution)/shard_map/all_to_all | solution.py:83
  12.4 0.0 copy-done.2
  12.5 0.1 fusion.3
  12.6 6.9 %collective-permute-start.2 = (bf16[256,256]{1,0:T(8,128)(2,1)S(1)}, bf16[256,256]{1,0:T(8,128)(2,1)S(1)}, u32[]{:S(2)}, u32[]{:S(2)}) collective-permute-start(bf16[256,256]{1,0:T(8,128)(2,1)S(1)} %get-tuple-element.7), channel_id=1, source_target_pairs={{0,16},{1,18},{2,17},{3,19},{8,24},{9,26},{10,25},{11,27},{16,272}... | collective-permute-start | bytes 393224 | tf_op jit(solution)/shard_map/ppermute | solution.py:24
  19.5 1.9 %collective-permute-start = (bf16[256,256]{1,0:T(8,128)(2,1)S(1)}, bf16[256,256]{1,0:T(8,128)(2,1)S(1)}, u32[]{:S(2)}, u32[]{:S(2)}) collective-permute-start(bf16[256,256]{1,0:T(8,128)(2,1)S(1)} %get-tuple-element.7), channel_id=1, source_target_pairs={{0,0},{1,2},{2,1},{3,3},{8,8},{9,10},{10,9},{11,11},{16,256},{17,2... | collective-permute-start | bytes 393224 | tf_op jit(solution)/shard_map/ppermute | solution.py:24
  21.4 3.4 %collective-permute-start.3 = (bf16[256,256]{1,0:T(8,128)(2,1)S(1)}, bf16[256,256]{1,0:T(8,128)(2,1)S(1)}, u32[]{:S(2)}, u32[]{:S(2)}) collective-permute-start(bf16[256,256]{1,0:T(8,128)(2,1)S(1)} %get-tuple-element.8), channel_id=1, source_target_pairs={{0,17},{1,19},{2,16},{3,18},{8,25},{9,27},{10,24},{11,26},{16,273}... | collective-permute-start | bytes 393224 | tf_op jit(solution)/shard_map/ppermute | solution.py:24
  24.8 5.2 %collective-permute-start.1 = (bf16[256,256]{1,0:T(8,128)(2,1)S(1)}, bf16[256,256]{1,0:T(8,128)(2,1)S(1)}, u32[]{:S(2)}, u32[]{:S(2)}) collective-permute-start(bf16[256,256]{1,0:T(8,128)(2,1)S(1)} %get-tuple-element.8), channel_id=1, source_target_pairs={{0,1},{1,3},{2,0},{3,2},{8,9},{9,11},{10,8},{11,10},{16,257},{17,2... | collective-permute-start | bytes 393224 | tf_op jit(solution)/shard_map/ppermute | solution.py:24
  30.0 0.0 collective-permute-done.2
  30.0 4.6 %collective-permute-done = bf16[256,256]{1,0:T(8,128)(2,1)S(1)} collective-permute-done((bf16[256,256]{1,0:T(8,128)(2,1)S(1)}, bf16[256,256]{1,0:T(8,128)(2,1)S(1)}, u32[]{:S(2)}, u32[]{:S(2)}) %collective-permute-start) | collective-permute-done | bytes 131104 | tf_op jit(solution)/shard_map/ppermute | solution.py:24
  34.6 0.0 collective-permute-done.3
  34.7 4.0 %collective-permute-done.1 = bf16[256,256]{1,0:T(8,128)(2,1)S(1)} collective-permute-done((bf16[256,256]{1,0:T(8,128)(2,1)S(1)}, bf16[256,256]{1,0:T(8,128)(2,1)S(1)}, u32[]{:S(2)}, u32[]{:S(2)}) %collective-permute-start.1) | collective-permute-done | bytes 131104 | tf_op jit(solution)/shard_map/ppermute | solution.py:24
  38.6 0.1 pad_maximum_fusion.near_ref
  38.7 2.1 %collective-permute-start.4 = (bf16[4,256,256]{2,1,0:T(8,128)(2,1)S(1)}, bf16[4,256,256]{2,1,0:T(8,128)(2,1)S(1)}, u32[]{:S(2)}, u32[]{:S(2)}) collective-permute-start(bf16[4,256,256]{2,1,0:T(8,128)(2,1)S(1)} %pad_maximum_fusion.near_ref), channel_id=1, source_target_pairs={{0,8},{8,0},{16,24},{24,16},{1,9},{9,1},{17,25},{25,17},{2,10},{10... | collective-permute-start | bytes 1572872 | tf_op jit(solution)/shard_map/ppermute | solution.py:24
  40.8 1.9 %collective-permute-start.5 = (bf16[4,256,256]{2,1,0:T(8,128)(2,1)S(1)}, bf16[4,256,256]{2,1,0:T(8,128)(2,1)S(1)}, u32[]{:S(2)}, u32[]{:S(2)}) collective-permute-start(bf16[4,256,256]{2,1,0:T(8,128)(2,1)S(1)} %pad_maximum_fusion.near_ref), channel_id=1, source_target_pairs={{0,4},{4,0},{1,5},{5,1},{2,6},{6,2},{3,7},{7,3},{8,12},{12,8},{9,1... | collective-permute-start | bytes 1572872 | tf_op jit(solution)/shard_map/ppermute | solution.py:24
  42.7 11.1 %collective-permute-done.4.far_ref = bf16[4,256,256]{2,1,0:T(8,128)(2,1)S(1)} collective-permute-done((bf16[4,256,256]{2,1,0:T(8,128)(2,1)S(1)}, bf16[4,256,256]{2,1,0:T(8,128)(2,1)S(1)}, u32[]{:S(2)}, u32[]{:S(2)}) %collective-permute-start.4) | collective-permute-done | bytes 524320 | tf_op jit(solution)/shard_map/ppermute | solution.py:24
  53.8 1.9 %collective-permute-start.6 = (bf16[4,256,256]{2,1,0:T(8,128)(2,1)S(1)}, bf16[4,256,256]{2,1,0:T(8,128)(2,1)S(1)}, u32[]{:S(2)}, u32[]{:S(2)}) collective-permute-start(bf16[4,256,256]{2,1,0:T(8,128)(2,1)S(1)} %collective-permute-done.4.far_ref), channel_id=1, source_target_pairs={{0,4},{4,0},{1,5},{5,1},{2,6},{6,2},{3,7},{7,3},{8,12},{12,8},{9,1... | collective-permute-start | bytes 1572872 | tf_op jit(solution)/shard_map/ppermute | solution.py:24
  55.7 0.0 all-to-all-done.even_ref
  55.7 1.1 fusion.4
  56.8 3.4 %collective-permute-start.8 = (bf16[2,256,512]{2,1,0:T(8,128)(2,1)}, bf16[2,256,512]{2,1,0:T(8,128)(2,1)}, u32[]{:S(2)}, u32[]{:S(2)}) collective-permute-start(bf16[2,256,512]{2,1,0:T(8,128)(2,1)} %get-tuple-element.5), channel_id=1, source_target_pairs={{0,32},{32,64},{64,96},{96,128},{128,160},{160,192},{192,224},{224... | collective-permute-start | bytes 1572872 | tf_op jit(solution)/shard_map/ppermute | solution.py:24
  60.2 4.3 %collective-permute-start.7 = (bf16[2,256,512]{2,1,0:T(8,128)(2,1)}, bf16[2,256,512]{2,1,0:T(8,128)(2,1)}, u32[]{:S(2)}, u32[]{:S(2)}) collective-permute-start(bf16[2,256,512]{2,1,0:T(8,128)(2,1)} %get-tuple-element.6), channel_id=1, source_target_pairs={{0,224},{32,0},{64,32},{96,64},{128,96},{160,128},{192,160},{224,1... | collective-permute-start | bytes 1572872 | tf_op jit(solution)/shard_map/ppermute | solution.py:24
  64.5 0.1 stack.83.place
  64.6 0.0 collective-permute-done.5.near2_ref
  64.7 0.0 collective-permute-done.6.far2_ref
  64.7 10.8 %collective-permute-done.8.down_ref = bf16[2,256,512]{2,1,0:T(8,128)(2,1)} collective-permute-done((bf16[2,256,512]{2,1,0:T(8,128)(2,1)}, bf16[2,256,512]{2,1,0:T(8,128)(2,1)}, u32[]{:S(2)}, u32[]{:S(2)}) %collective-permute-start.8) | collective-permute-done | bytes 524320 | tf_op jit(solution)/shard_map/ppermute | solution.py:24
  75.5 1.2 %collective-permute-done.7.up_ref = bf16[2,256,512]{2,1,0:T(8,128)(2,1)} collective-permute-done((bf16[2,256,512]{2,1,0:T(8,128)(2,1)}, bf16[2,256,512]{2,1,0:T(8,128)(2,1)}, u32[]{:S(2)}, u32[]{:S(2)}) %collective-permute-start.7) | collective-permute-done | bytes 524320 | tf_op jit(solution)/shard_map/ppermute | solution.py:24
  76.6 1.9 %shard_map.29 = f32[4,256,128]{2,1,0:T(8,128)S(1)} custom-call(s32[32]{0:T(128)S(1)} %stack.83.place, bf16[4,256,256]{2,1,0:T(8,128)(2,1)S(1)} %pad_maximum_fusion.near_ref, bf16[4,256,256]{2,1,0:T(8,128)(2,1)S(1)} %collective-permute-done.4.far_ref, bf16[4,256,256]{2,1,0:T(8,128)(2,1)S(1)} %collective-permute-done.5.near2_ref, ...), custom_call_target="tpu_custom_call" | custom-call | tf_op jit(solution)/shard_map/pallas_call | solution.py:67
  78.6 0.0 copy-start.1
  78.6 0.8 copy-done.1
  79.4 7.3 %all-to-all-start.2 = ((f32[4,256,128]{2,1,0:T(8,128)}), f32[4,256,128]{2,1,0:T(8,128)}, u32[]{:S(2)}, u32[]{:S(2)}) async-start(f32[4,256,128]{2,1,0:T(8,128)} %copy-done.1), calls=%async_computation.2 | async-start | bytes 1048576 | tf_op jit(solution)/shard_map/all_to_all | solution.py:77
  86.7 1.9 %shard_map.28 = f32[4,256,128]{2,1,0:T(8,128)S(1)} custom-call(s32[32]{0:T(128)S(1)} %stack.83.place, bf16[4,256,256]{2,1,0:T(8,128)(2,1)S(1)} %pad_maximum_fusion.near_ref, bf16[4,256,256]{2,1,0:T(8,128)(2,1)S(1)} %collective-permute-done.4.far_ref, bf16[4,256,256]{2,1,0:T(8,128)(2,1)S(1)} %collective-permute-done.5.near2_ref, ...), custom_call_target="tpu_custom_call" | custom-call | tf_op jit(solution)/shard_map/pallas_call | solution.py:67
  88.6 0.0 copy-start
  88.6 0.8 copy-done
  89.4 5.6 %all-to-all-done.2 = f32[4,256,128]{2,1,0:T(8,128)} async-done(((f32[4,256,128]{2,1,0:T(8,128)}), f32[4,256,128]{2,1,0:T(8,128)}, u32[]{:S(2)}, u32[]{:S(2)}) %all-to-all-start.2) | async-done | bytes 524320 | tf_op jit(solution)/shard_map/all_to_all | solution.py:77
  94.9 4.9 %all-to-all-start.1 = ((f32[4,256,128]{2,1,0:T(8,128)}), f32[4,256,128]{2,1,0:T(8,128)S(1)}, u32[]{:S(2)}, u32[]{:S(2)}) async-start(f32[4,256,128]{2,1,0:T(8,128)} %copy-done), calls=%async_computation.1 | async-start | bytes 1048576 | tf_op jit(solution)/shard_map/all_to_all | solution.py:77
  99.8 1.1 reduce_sum.19
  100.9 1.9 %collective-permute-start.9 = (f32[256,128]{1,0:T(8,128)S(1)}, f32[256,128]{1,0:T(8,128)S(1)}, u32[]{:S(2)}, u32[]{:S(2)}) collective-permute-start(f32[256,128]{1,0:T(8,128)S(1)} %reduce_sum.19), channel_id=1, source_target_pairs={{0,256},{256,0},{1,257},{257,1},{2,258},{258,2},{3,259},{259,3},{4... | collective-permute-start | bytes 393224 | tf_op jit(solution)/shard_map/ppermute | solution.py:24
  102.9 4.3 %all-to-all-done.1 = f32[4,256,128]{2,1,0:T(8,128)S(1)} async-done(((f32[4,256,128]{2,1,0:T(8,128)}), f32[4,256,128]{2,1,0:T(8,128)S(1)}, u32[]{:S(2)}, u32[]{:S(2)}) %all-to-all-start.1) | async-done | bytes 524320 | tf_op jit(solution)/shard_map/all_to_all | solution.py:77
  107.2 4.9 %collective-permute-done.9 = f32[256,128]{1,0:T(8,128)S(1)} collective-permute-done((f32[256,128]{1,0:T(8,128)S(1)}, f32[256,128]{1,0:T(8,128)S(1)}, u32[]{:S(2)}, u32[]{:S(2)}) %collective-permute-start.9) | collective-permute-done | bytes 131104 | tf_op jit(solution)/shard_map/ppermute | solution.py:24
  112.1 0.7 add.40
  (2 shorter events, 0.0 us)
Async XLA Ops:
  2.0 10.4 %copy-start.2 = (bf16[256,512]{1,0:T(8,128)(2,1)S(1)}, bf16[256,512]{1,0:T(8,128)(2,1)}, u32[]{:S(2)}) copy-start(bf16[256,512]{1,0:T(8,128)(2,1)} %param.2) | copy-start | bytes 786436
  2.0 53.7 %all-to-all-start = ((bf16[4,256,512]{2,1,0:T(8,128)(2,1)}), bf16[4,256,512]{2,1,0:T(8,128)(2,1)S(1)}, u32[]{:S(2)}, u32[]{:S(2)}) async-start(bf16[4,256,512]{2,1,0:T(8,128)(2,1)} %broadcast_in_dim.2), calls=%async_computation | async-start | bytes 2097152 | tf_op jit(solution)/shard_map/all_to_all | solution.py:83
  12.6 17.5 %collective-permute-start.2 = (bf16[256,256]{1,0:T(8,128)(2,1)S(1)}, bf16[256,256]{1,0:T(8,128)(2,1)S(1)}, u32[]{:S(2)}, u32[]{:S(2)}) collective-permute-start(bf16[256,256]{1,0:T(8,128)(2,1)S(1)} %get-tuple-element.7), channel_id=1, source_target_pairs={{0,16},{1,18},{2,17},{3,19},{8,24},{9,26},{10,25},{11,27},{16,272}... | collective-permute-start | bytes 393224 | tf_op jit(solution)/shard_map/ppermute | solution.py:24
  19.5 15.2 %collective-permute-start = (bf16[256,256]{1,0:T(8,128)(2,1)S(1)}, bf16[256,256]{1,0:T(8,128)(2,1)S(1)}, u32[]{:S(2)}, u32[]{:S(2)}) collective-permute-start(bf16[256,256]{1,0:T(8,128)(2,1)S(1)} %get-tuple-element.7), channel_id=1, source_target_pairs={{0,0},{1,2},{2,1},{3,3},{8,8},{9,10},{10,9},{11,11},{16,256},{17,2... | collective-permute-start | bytes 393224 | tf_op jit(solution)/shard_map/ppermute | solution.py:24
  21.4 13.3 %collective-permute-start.3 = (bf16[256,256]{1,0:T(8,128)(2,1)S(1)}, bf16[256,256]{1,0:T(8,128)(2,1)S(1)}, u32[]{:S(2)}, u32[]{:S(2)}) collective-permute-start(bf16[256,256]{1,0:T(8,128)(2,1)S(1)} %get-tuple-element.8), channel_id=1, source_target_pairs={{0,17},{1,19},{2,16},{3,18},{8,25},{9,27},{10,24},{11,26},{16,273}... | collective-permute-start | bytes 393224 | tf_op jit(solution)/shard_map/ppermute | solution.py:24
  24.8 13.8 %collective-permute-start.1 = (bf16[256,256]{1,0:T(8,128)(2,1)S(1)}, bf16[256,256]{1,0:T(8,128)(2,1)S(1)}, u32[]{:S(2)}, u32[]{:S(2)}) collective-permute-start(bf16[256,256]{1,0:T(8,128)(2,1)S(1)} %get-tuple-element.8), channel_id=1, source_target_pairs={{0,1},{1,3},{2,0},{3,2},{8,9},{9,11},{10,8},{11,10},{16,257},{17,2... | collective-permute-start | bytes 393224 | tf_op jit(solution)/shard_map/ppermute | solution.py:24
  38.7 15.1 %collective-permute-start.4 = (bf16[4,256,256]{2,1,0:T(8,128)(2,1)S(1)}, bf16[4,256,256]{2,1,0:T(8,128)(2,1)S(1)}, u32[]{:S(2)}, u32[]{:S(2)}) collective-permute-start(bf16[4,256,256]{2,1,0:T(8,128)(2,1)S(1)} %pad_maximum_fusion.near_ref), channel_id=1, source_target_pairs={{0,8},{8,0},{16,24},{24,16},{1,9},{9,1},{17,25},{25,17},{2,10},{10... | collective-permute-start | bytes 1572872 | tf_op jit(solution)/shard_map/ppermute | solution.py:24
  40.8 23.9 %collective-permute-start.5 = (bf16[4,256,256]{2,1,0:T(8,128)(2,1)S(1)}, bf16[4,256,256]{2,1,0:T(8,128)(2,1)S(1)}, u32[]{:S(2)}, u32[]{:S(2)}) collective-permute-start(bf16[4,256,256]{2,1,0:T(8,128)(2,1)S(1)} %pad_maximum_fusion.near_ref), channel_id=1, source_target_pairs={{0,4},{4,0},{1,5},{5,1},{2,6},{6,2},{3,7},{7,3},{8,12},{12,8},{9,1... | collective-permute-start | bytes 1572872 | tf_op jit(solution)/shard_map/ppermute | solution.py:24
  53.8 10.8 %collective-permute-start.6 = (bf16[4,256,256]{2,1,0:T(8,128)(2,1)S(1)}, bf16[4,256,256]{2,1,0:T(8,128)(2,1)S(1)}, u32[]{:S(2)}, u32[]{:S(2)}) collective-permute-start(bf16[4,256,256]{2,1,0:T(8,128)(2,1)S(1)} %collective-permute-done.4.far_ref), channel_id=1, source_target_pairs={{0,4},{4,0},{1,5},{5,1},{2,6},{6,2},{3,7},{7,3},{8,12},{12,8},{9,1... | collective-permute-start | bytes 1572872 | tf_op jit(solution)/shard_map/ppermute | solution.py:24
  56.8 18.7 %collective-permute-start.8 = (bf16[2,256,512]{2,1,0:T(8,128)(2,1)}, bf16[2,256,512]{2,1,0:T(8,128)(2,1)}, u32[]{:S(2)}, u32[]{:S(2)}) collective-permute-start(bf16[2,256,512]{2,1,0:T(8,128)(2,1)} %get-tuple-element.5), channel_id=1, source_target_pairs={{0,32},{32,64},{64,96},{96,128},{128,160},{160,192},{192,224},{224... | collective-permute-start | bytes 1572872 | tf_op jit(solution)/shard_map/ppermute | solution.py:24
  60.2 16.5 %collective-permute-start.7 = (bf16[2,256,512]{2,1,0:T(8,128)(2,1)}, bf16[2,256,512]{2,1,0:T(8,128)(2,1)}, u32[]{:S(2)}, u32[]{:S(2)}) collective-permute-start(bf16[2,256,512]{2,1,0:T(8,128)(2,1)} %get-tuple-element.6), channel_id=1, source_target_pairs={{0,224},{32,0},{64,32},{96,64},{128,96},{160,128},{192,160},{224,1... | collective-permute-start | bytes 1572872 | tf_op jit(solution)/shard_map/ppermute | solution.py:24
  78.6 0.8 copy-start.1
  79.4 15.6 %all-to-all-start.2 = ((f32[4,256,128]{2,1,0:T(8,128)}), f32[4,256,128]{2,1,0:T(8,128)}, u32[]{:S(2)}, u32[]{:S(2)}) async-start(f32[4,256,128]{2,1,0:T(8,128)} %copy-done.1), calls=%async_computation.2 | async-start | bytes 1048576 | tf_op jit(solution)/shard_map/all_to_all | solution.py:77
  88.6 0.8 copy-start
  94.9 12.2 %all-to-all-start.1 = ((f32[4,256,128]{2,1,0:T(8,128)}), f32[4,256,128]{2,1,0:T(8,128)S(1)}, u32[]{:S(2)}, u32[]{:S(2)}) async-start(f32[4,256,128]{2,1,0:T(8,128)} %copy-done), calls=%async_computation.1 | async-start | bytes 1048576 | tf_op jit(solution)/shard_map/all_to_all | solution.py:77
  100.9 11.1 %collective-permute-start.9 = (f32[256,128]{1,0:T(8,128)S(1)}, f32[256,128]{1,0:T(8,128)S(1)}, u32[]{:S(2)}, u32[]{:S(2)}) collective-permute-start(f32[256,128]{1,0:T(8,128)S(1)} %reduce_sum.19), channel_id=1, source_target_pairs={{0,256},{256,0},{1,257},{257,1},{2,258},{258,2},{3,259},{259,3},{4... | collective-permute-start | bytes 393224 | tf_op jit(solution)/shard_map/ppermute | solution.py:24

commit v5 on v4

v5 whole, which is shorter than its diff:
```python
import functools

import jax
import jax.numpy as jnp
import numpy as np
from jax import lax
from jax.experimental import pallas as pl
from jax.experimental.pallas import tpu as pltpu
from jax.sharding import Mesh, PartitionSpec as P

AXES = ("yh", "z", "yl", "core", "x")
SHAPE = (2, 8, 4, 2, 4)
SIZES = dict(zip(AXES, SHAPE))
UNIT = 256


def moved(value, axes, where):
    shape = [SIZES[a] for a in axes]
    perm = []
    for i in range(int(np.prod(shape))):
        place = dict(zip(axes, (int(v) for v in np.unravel_index(i, shape))))
        there = where(**place)
        perm.append((i, int(np.ravel_multi_index([there[a] for a in axes], shape))))
    return lax.ppermute(value, axes, perm)


def regrouped(value, second):
    def where(yh, yl, x):
        half = (x >> 1) ^ second
        return {"yh": yl >> 1, "yl": 2 * yh + (yl & 1), "x": 2 * (x & 1) + half}

    return moved(value, ("yh", "yl", "x"), where)


def across_yl(value, mask):
    return moved(value, ("yl",), lambda yl: {"yl": yl ^ mask})


def core_swap(value):
    return moved(value, ("core",), lambda core: {"core": 1 - core})


def product_kernel(place, near_ref, far_ref, near2_ref, far2_ref, t_ref, out_ref):
    for unit in range(8):
        t = t_ref[unit]
        same, near = place[4 * unit] == 1, place[4 * unit + 1] == 1
        for rel in range(2):
            slot = place[4 * unit + 2 + rel]
            w = jnp.where(
                same,
                jnp.where(near, near_ref[slot], far_ref[slot]),
                jnp.where(near, near2_ref[slot], far2_ref[slot]),
            )
            part = jnp.dot(w, t, preferred_element_type=jnp.float32)
            for block in range(4):
                cols = part[:, block * 128 : (block + 1) * 128]
                if unit == 0:
                    out_ref[block, rel] = cols
                else:
                    out_ref[block, rel] += cols


def product(place, *operands):
    vmem = pl.BlockSpec(memory_space=pltpu.VMEM)
    return pl.pallas_call(
        product_kernel,
        out_shape=jax.ShapeDtypeStruct((4, 2, UNIT, 128), jnp.float32),
        in_specs=[pl.BlockSpec(memory_space=pltpu.SMEM)] + [vmem] * len(operands),
        out_specs=vmem,
        compiler_params=pltpu.CompilerParams(vmem_limit_bytes=40 * 1024 * 1024),
    )(place, *operands)


def per_device(integrals, amplitudes):
    yh, z, yl, core, x = (lax.axis_index(a) for a in AXES)
    copies = jnp.broadcast_to(amplitudes[None], (8,) + amplitudes.shape)
    tiles = lax.all_to_all(copies, "z", split_axis=0, concat_axis=0, tiled=True)
    halves = jnp.stack([integrals[:, :UNIT], integrals[:, UNIT:]])
    high = x >> 1
    own = jnp.stack([regrouped(lax.dynamic_index_in_dim(halves, high ^ i, 0, False), i) for i in (0, 1)])
    near = jnp.concatenate([own, across_yl(own, 2)])
    far = across_yl(near, 1)
    near2, far2 = core_swap(near), core_swap(far)
    place = []
    for unit in range(8):
        u4, u3, u2 = unit >> 2, (unit >> 1) & 1, unit & 1
        place += [jnp.where(core == u3, 1, 0), jnp.where((yl & 1) == u4, 1, 0)]
        place += [((yh ^ rel) ^ (yl >> 1)) * 2 + (u2 ^ (x & 1)) for rel in (0, 1)]
    place = jnp.stack(place).astype(jnp.int32)
    part = product(place, near, far, near2, far2, tiles)
    part = lax.all_to_all(part, "x", split_axis=0, concat_axis=0, tiled=True).sum(axis=0)
    return part[0] + moved(part[1], ("yh",), lambda yh: {"yh": 1 - yh})


def solution(mesh):
    return jax.shard_map(
        per_device,
        mesh=Mesh(mesh.devices.reshape(SHAPE), AXES),
        in_specs=(P(("yh", "z"), ("yl", "core", "x")), P(("yh", "z", "x"), ("yl", "core"))),
        out_specs=P(("yh", "z"), ("yl", "core", "x")),
        check_vma=False,
    )
```

time: 113 us -> 100 us (0.88)
  the two profiles are of different devices: /device:TPU:18 before, /device:TPU:64 now
where the time goes in v5:
time: 100 us; the launch traced here: 99.6 us
  starting transfers between devices  40.3 us (40%)
  waiting for transfers between devices  33.7 us (34%)
  blocking collectives  19.5 us (20%)
  local copies, waits for them, and re-layouts  2.61 us (3%)
  Pallas kernels  2.46 us (2%)
    ppermute x7, waiting for transfers between devices, moved(): return lax.ppermute(value, axes, perm)  33.7 us
    ppermute x7, starting transfers between devices, moved(): return lax.ppermute(value, axes, perm)  30.2 us
    all_to_all x1, blocking collectives, per_device(): lax.all_to_all(part, 'x', split_axis=0, concat_axis=0, tiled=True)  19.5 us
    all_to_all x1, starting transfers between devices, per_device(): tiles = lax.all_to_all(copies, 'z', split_axis=0, concat_axis=0, tiled=True)  10.1 us
    broadcast_in_dim x1, local copies, waits for them, and re-layouts, per_device(): copies = jnp.broadcast_to(amplitudes[None], (8,) + amplitudes.shape)  2.47 us
    pallas_call x1, Pallas kernels, product(): pl.pallas_call(product_kernel, out_shape=jax.ShapeDtypeStruct((4, 2, UNIT...  2.46 us
  transfers between devices with their start and end apart: 8, of which 5 were waited for; matrix products, arithmetic and copies ran while one was open for 0% of the time, Pallas kernels for 0%

profile of v5, /device:TPU:64, one launch (start us, length us, event | category | flops | bytes accessed | tf_op | source)
XLA Modules:
  0.0 99.6 jit_solution(5182363108755644402)
XLA Ops:
  0.0 2.5 %broadcast_in_dim.2 = bf16[8,256,512]{2,1,0:T(8,128)(2,1)} broadcast(bf16[256,512]{1,0:T(8,128)(2,1)} %param.3), dimensions={1,2} | broadcast | bytes 2359296 | tf_op jit(solution)/shard_map/broadcast_in_dim | solution.py:76
  2.5 0.0 copy-start
  2.5 10.1 %all-to-all-start = ((bf16[8,256,512]{2,1,0:T(8,128)(2,1)}), bf16[8,256,512]{2,1,0:T(8,128)(2,1)S(1)}, u32[]{:S(2)}, u32[]{:S(2)}) async-start(bf16[8,256,512]{2,1,0:T(8,128)(2,1)} %broadcast_in_dim.2), calls=%async_computation | async-start | bytes 4194304 | tf_op jit(solution)/shard_map/all_to_all | solution.py:77
  12.6 0.0 copy-done
  12.6 0.1 fusion.3
  12.7 0.7 collective-permute-start
  13.4 6.1 %collective-permute-start.1 = (bf16[256,256]{1,0:T(8,128)(2,1)S(1)}, bf16[256,256]{1,0:T(8,128)(2,1)S(1)}, u32[]{:S(2)}, u32[]{:S(2)}) collective-permute-start(bf16[256,256]{1,0:T(8,128)(2,1)S(1)} %get-tuple-element.6), channel_id=1, source_target_pairs={{0,1},{1,3},{2,0},{3,2},{8,9},{9,11},{10,8},{11,10},{16,257},{17,2... | collective-permute-start | bytes 393224 | tf_op jit(solution)/shard_map/ppermute | solution.py:24
  19.5 0.0 collective-permute-done
  19.5 3.5 %collective-permute-done.1 = bf16[256,256]{1,0:T(8,128)(2,1)S(1)} collective-permute-done((bf16[256,256]{1,0:T(8,128)(2,1)S(1)}, bf16[256,256]{1,0:T(8,128)(2,1)S(1)}, u32[]{:S(2)}, u32[]{:S(2)}) %collective-permute-start.1) | collective-permute-done | bytes 131104 | tf_op jit(solution)/shard_map/ppermute | solution.py:24
  23.1 13.7 %collective-permute-start.2 = (bf16[2,256,256]{2,1,0:T(8,128)(2,1)S(1)}, bf16[2,256,256]{2,1,0:T(8,128)(2,1)S(1)}, u32[]{:S(2)}, u32[]{:S(2)}) collective-permute-start(bf16[2,256,256]{2,1,0:T(8,128)(2,1)S(1)} %pad_maximum_fusion.1), channel_id=1, source_target_pairs={{0,16},{8,24},{16,0},{24,8},{1,17},{9,25},{17,1},{25,9},{2,18},{10... | collective-permute-start | bytes 786440 | tf_op jit(solution)/shard_map/ppermute | solution.py:24
  36.8 8.1 %collective-permute-done.2 = bf16[2,256,256]{2,1,0:T(8,128)(2,1)S(1)} collective-permute-done((bf16[2,256,256]{2,1,0:T(8,128)(2,1)S(1)}, bf16[2,256,256]{2,1,0:T(8,128)(2,1)S(1)}, u32[]{:S(2)}, u32[]{:S(2)}) %collective-permute-start.2) | collective-permute-done | bytes 262176 | tf_op jit(solution)/shard_map/ppermute | solution.py:24
  44.9 0.1 pad_maximum_fusion.near_ref
  45.0 1.9 %collective-permute-start.3 = (bf16[4,256,256]{2,1,0:T(8,128)(2,1)S(1)}, bf16[4,256,256]{2,1,0:T(8,128)(2,1)S(1)}, u32[]{:S(2)}, u32[]{:S(2)}) collective-permute-start(bf16[4,256,256]{2,1,0:T(8,128)(2,1)S(1)} %pad_maximum_fusion.near_ref), channel_id=1, source_target_pairs={{0,8},{8,0},{16,24},{24,16},{1,9},{9,1},{17,25},{25,17},{2,10},{10... | collective-permute-start | bytes 1572872 | tf_op jit(solution)/shard_map/ppermute | solution.py:24
  46.9 1.9 %collective-permute-start.4 = (bf16[4,256,256]{2,1,0:T(8,128)(2,1)S(1)}, bf16[4,256,256]{2,1,0:T(8,128)(2,1)}, u32[]{:S(2)}, u32[]{:S(2)}) collective-permute-start(bf16[4,256,256]{2,1,0:T(8,128)(2,1)S(1)} %pad_maximum_fusion.near_ref), channel_id=1, source_target_pairs={{0,4},{4,0},{1,5},{5,1},{2,6},{6,2},{3,7},{7,3},{8,12},{12,8},{9,1... | collective-permute-start | bytes 1572872 | tf_op jit(solution)/shard_map/ppermute | solution.py:24
  48.8 11.9 %collective-permute-done.3.far_ref = bf16[4,256,256]{2,1,0:T(8,128)(2,1)S(1)} collective-permute-done((bf16[4,256,256]{2,1,0:T(8,128)(2,1)S(1)}, bf16[4,256,256]{2,1,0:T(8,128)(2,1)S(1)}, u32[]{:S(2)}, u32[]{:S(2)}) %collective-permute-start.3) | collective-permute-done | bytes 524320 | tf_op jit(solution)/shard_map/ppermute | solution.py:24
  60.7 1.9 %collective-permute-start.5 = (bf16[4,256,256]{2,1,0:T(8,128)(2,1)S(1)}, bf16[4,256,256]{2,1,0:T(8,128)(2,1)}, u32[]{:S(2)}, u32[]{:S(2)}) collective-permute-start(bf16[4,256,256]{2,1,0:T(8,128)(2,1)S(1)} %collective-permute-done.3.far_ref), channel_id=1, source_target_pairs={{0,4},{4,0},{1,5},{5,1},{2,6},{6,2},{3,7},{7,3},{8,12},{12,8},{9,1... | collective-permute-start | bytes 1572872 | tf_op jit(solution)/shard_map/ppermute | solution.py:24
  62.7 0.1 stack.38.place
  62.8 0.0 collective-permute-done.4.near2_ref
  62.8 1.9 %collective-permute-done.5.far2_ref = bf16[4,256,256]{2,1,0:T(8,128)(2,1)} collective-permute-done((bf16[4,256,256]{2,1,0:T(8,128)(2,1)S(1)}, bf16[4,256,256]{2,1,0:T(8,128)(2,1)}, u32[]{:S(2)}, u32[]{:S(2)}) %collective-permute-start.5) | collective-permute-done | bytes 524320 | tf_op jit(solution)/shard_map/ppermute | solution.py:24
  64.6 0.0 all-to-all-done.t_ref
  64.6 2.5 %shard_map.28 = f32[4,2,256,128]{3,2,1,0:T(8,128)S(1)} custom-call(s32[32]{0:T(128)S(1)} %stack.38.place, bf16[4,256,256]{2,1,0:T(8,128)(2,1)S(1)} %pad_maximum_fusion.near_ref, bf16[4,256,256]{2,1,0:T(8,128)(2,1)S(1)} %collective-permute-done.3.far_ref, bf16[4,256,256]{2,1,0:T(8,128)(2,1)} %collective-permute-done.4.near2_ref, ...), custom_call_target="tpu_custom_call" | custom-call | tf_op jit(solution)/shard_map/pallas_call | solution.py:65
  67.1 19.5 %all_to_all.10 = f32[4,2,256,128]{3,2,1,0:T(8,128)S(1)} all-to-all(f32[4,2,256,128]{3,2,1,0:T(8,128)S(1)} %shard_map.28), channel_id=1, replica_groups=mesh['yh'=2,'z'=8,'yl'=4,'core'=2,'x'=4] {'x'}, dimensions={0} | all-to-all | bytes 2097152 | tf_op jit(solution)/shard_map/all_to_all | solution.py:91
  86.6 0.1 reduce_sum.9
  86.7 3.9 %collective-permute-start.6 = (f32[256,128]{1,0:T(8,128)S(1)}, f32[256,128]{1,0:T(8,128)S(1)}, u32[]{:S(2)}, u32[]{:S(2)}) collective-permute-start(f32[256,128]{1,0:T(8,128)S(1)} %slice_bitcast_fusion), channel_id=1, source_target_pairs={{0,256},{256,0},{1,257},{257,1},{2,258},{258,2},{3,259},{259,3},{4... | collective-permute-start | bytes 393224 | tf_op jit(solution)/shard_map/ppermute | solution.py:24
  90.6 8.4 %collective-permute-done.6 = f32[256,128]{1,0:T(8,128)S(1)} collective-permute-done((f32[256,128]{1,0:T(8,128)S(1)}, f32[256,128]{1,0:T(8,128)S(1)}, u32[]{:S(2)}, u32[]{:S(2)}) %collective-permute-start.6) | collective-permute-done | bytes 131104 | tf_op jit(solution)/shard_map/ppermute | solution.py:24
  99.0 0.7 fusion.4
  (3 shorter events, 0.1 us)
Async XLA Ops:
  2.5 10.1 %copy-start = (bf16[256,512]{1,0:T(8,128)(2,1)S(1)}, bf16[256,512]{1,0:T(8,128)(2,1)}, u32[]{:S(2)}) copy-start(bf16[256,512]{1,0:T(8,128)(2,1)} %param.2) | copy-start | bytes 786436
  2.5 62.2 %all-to-all-start = ((bf16[8,256,512]{2,1,0:T(8,128)(2,1)}), bf16[8,256,512]{2,1,0:T(8,128)(2,1)S(1)}, u32[]{:S(2)}, u32[]{:S(2)}) async-start(bf16[8,256,512]{2,1,0:T(8,128)(2,1)} %broadcast_in_dim.2), calls=%async_computation | async-start | bytes 4194304 | tf_op jit(solution)/shard_map/all_to_all | solution.py:77
  12.7 6.8 %collective-permute-start = (bf16[256,256]{1,0:T(8,128)(2,1)S(1)}, bf16[256,256]{1,0:T(8,128)(2,1)S(1)}, u32[]{:S(2)}, u32[]{:S(2)}) collective-permute-start(bf16[256,256]{1,0:T(8,128)(2,1)S(1)} %get-tuple-element.5), channel_id=1, source_target_pairs={{0,0},{1,2},{2,1},{3,3},{8,8},{9,10},{10,9},{11,11},{16,256},{17,2... | collective-permute-start | bytes 393224 | tf_op jit(solution)/shard_map/ppermute | solution.py:24
  13.4 9.6 %collective-permute-start.1 = (bf16[256,256]{1,0:T(8,128)(2,1)S(1)}, bf16[256,256]{1,0:T(8,128)(2,1)S(1)}, u32[]{:S(2)}, u32[]{:S(2)}) collective-permute-start(bf16[256,256]{1,0:T(8,128)(2,1)S(1)} %get-tuple-element.6), channel_id=1, source_target_pairs={{0,1},{1,3},{2,0},{3,2},{8,9},{9,11},{10,8},{11,10},{16,257},{17,2... | collective-permute-start | bytes 393224 | tf_op jit(solution)/shard_map/ppermute | solution.py:24
  23.1 21.8 %collective-permute-start.2 = (bf16[2,256,256]{2,1,0:T(8,128)(2,1)S(1)}, bf16[2,256,256]{2,1,0:T(8,128)(2,1)S(1)}, u32[]{:S(2)}, u32[]{:S(2)}) collective-permute-start(bf16[2,256,256]{2,1,0:T(8,128)(2,1)S(1)} %pad_maximum_fusion.1), channel_id=1, source_target_pairs={{0,16},{8,24},{16,0},{24,8},{1,17},{9,25},{17,1},{25,9},{2,18},{10... | collective-permute-start | bytes 786440 | tf_op jit(solution)/shard_map/ppermute | solution.py:24
  45.0 15.7 %collective-permute-start.3 = (bf16[4,256,256]{2,1,0:T(8,128)(2,1)S(1)}, bf16[4,256,256]{2,1,0:T(8,128)(2,1)S(1)}, u32[]{:S(2)}, u32[]{:S(2)}) collective-permute-start(bf16[4,256,256]{2,1,0:T(8,128)(2,1)S(1)} %pad_maximum_fusion.near_ref), channel_id=1, source_target_pairs={{0,8},{8,0},{16,24},{24,16},{1,9},{9,1},{17,25},{25,17},{2,10},{10... | collective-permute-start | bytes 1572872 | tf_op jit(solution)/shard_map/ppermute | solution.py:24
  46.9 15.9 %collective-permute-start.4 = (bf16[4,256,256]{2,1,0:T(8,128)(2,1)S(1)}, bf16[4,256,256]{2,1,0:T(8,128)(2,1)}, u32[]{:S(2)}, u32[]{:S(2)}) collective-permute-start(bf16[4,256,256]{2,1,0:T(8,128)(2,1)S(1)} %pad_maximum_fusion.near_ref), channel_id=1, source_target_pairs={{0,4},{4,0},{1,5},{5,1},{2,6},{6,2},{3,7},{7,3},{8,12},{12,8},{9,1... | collective-permute-start | bytes 1572872 | tf_op jit(solution)/shard_map/ppermute | solution.py:24
  60.7 3.9 %collective-permute-start.5 = (bf16[4,256,256]{2,1,0:T(8,128)(2,1)S(1)}, bf16[4,256,256]{2,1,0:T(8,128)(2,1)}, u32[]{:S(2)}, u32[]{:S(2)}) collective-permute-start(bf16[4,256,256]{2,1,0:T(8,128)(2,1)S(1)} %collective-permute-done.3.far_ref), channel_id=1, source_target_pairs={{0,4},{4,0},{1,5},{5,1},{2,6},{6,2},{3,7},{7,3},{8,12},{12,8},{9,1... | collective-permute-start | bytes 1572872 | tf_op jit(solution)/shard_map/ppermute | solution.py:24
  86.7 12.3 %collective-permute-start.6 = (f32[256,128]{1,0:T(8,128)S(1)}, f32[256,128]{1,0:T(8,128)S(1)}, u32[]{:S(2)}, u32[]{:S(2)}) collective-permute-start(f32[256,128]{1,0:T(8,128)S(1)} %slice_bitcast_fusion), channel_id=1, source_target_pairs={{0,256},{256,0},{1,257},{257,1},{2,258},{258,2},{3,259},{259,3},{4... | collective-permute-start | bytes 393224 | tf_op jit(solution)/shard_map/ppermute | solution.py:24

commit v6 on v4

v6 whole, which is shorter than its diff:
```python
import jax
import jax.numpy as jnp
import numpy as np
from jax import lax
from jax.experimental import pallas as pl
from jax.experimental.pallas import tpu as pltpu
from jax.sharding import Mesh, PartitionSpec as P

AXES = ("yh", "zh", "zl", "yl", "core", "x")
SHAPE = (2, 4, 2, 4, 2, 4)
SIZES = dict(zip(AXES, SHAPE))
UNIT = 256


def moved(value, axes, where):
    shape = [SIZES[a] for a in axes]
    perm = []
    for i in range(int(np.prod(shape))):
        place = dict(zip(axes, (int(v) for v in np.unravel_index(i, shape))))
        there = where(**place)
        perm.append((i, int(np.ravel_multi_index([there[a] for a in axes], shape))))
    return lax.ppermute(value, axes, perm)


def aligned(value):
    def where(yh, zh, zl, core, x):
        return {"yh": core, "zh": 2 * (zh >> 1) + yh, "zl": x & 1, "core": zh & 1, "x": 2 * zl + (x >> 1)}

    return moved(value, ("yh", "zh", "zl", "core", "x"), where)


def along_z(value, by):
    def where(zh, zl):
        z = (2 * zh + zl + by) % 8
        return {"zh": z >> 1, "zl": z & 1}

    return moved(value, ("zh", "zl"), where)


def product_kernel(place, w_ref, even_ref, up_ref, down_ref, out_ref):
    core, parity = place[0], place[1]
    for i in range(4):
        u4, u5 = i >> 1, i & 1
        same, other = even_ref[i], (up_ref if i < 2 else down_ref)[i % 2]
        for rel in range(2):
            w = w_ref[4 * (core ^ rel) + 2 * u5 + u4]
            low, high = w[:, :UNIT], w[:, UNIT:]
            part = jnp.dot(jnp.where(parity == 0, low, high), same, preferred_element_type=jnp.float32)
            part += jnp.dot(jnp.where(parity == 0, high, low), other, preferred_element_type=jnp.float32)
            for block in range(4):
                cols = part[:, block * 128 : (block + 1) * 128]
                if i == 0:
                    out_ref[rel, block] = cols
                else:
                    out_ref[rel, block] += cols


def product(place, *operands):
    vmem = pl.BlockSpec(memory_space=pltpu.VMEM)
    return pl.pallas_call(
        product_kernel,
        out_shape=jax.ShapeDtypeStruct((2, 4, UNIT, 128), jnp.float32),
        in_specs=[pl.BlockSpec(memory_space=pltpu.SMEM)] + [vmem] * len(operands),
        out_specs=vmem,
        compiler_params=pltpu.CompilerParams(vmem_limit_bytes=40 * 1024 * 1024),
    )(place, *operands)


def to_all(value, axes):
    copies = jnp.broadcast_to(value[None], (int(np.prod([SIZES[a] for a in axes])),) + value.shape)
    return lax.all_to_all(copies, axes, split_axis=0, concat_axis=0, tiled=True)


def per_device(integrals, amplitudes):
    even = to_all(aligned(amplitudes), ("zh",))
    from_up = along_z(even[:2], -1)
    from_down = along_z(even[2:], 1)
    slab = to_all(integrals, ("yh", "yl"))
    place = jnp.stack([lax.axis_index("core"), lax.axis_index("zl")]).astype(jnp.int32)
    part = product(place, slab, even, from_up, from_down)
    part = part[0] + moved(part[1], ("core",), lambda core: {"core": 1 - core})
    part = lax.all_to_all(part, "x", split_axis=0, concat_axis=0, tiled=True).sum(axis=0)
    return moved(part, ("yh", "core"), lambda yh, core: {"yh": core, "core": yh})


def solution(mesh):
    return jax.shard_map(
        per_device,
        mesh=Mesh(mesh.devices.reshape(SHAPE), AXES),
        in_specs=(P(("yh", "zh", "zl"), ("yl", "core", "x")), P(("yh", "zh", "zl", "x"), ("yl", "core"))),
        out_specs=P(("yh", "zh", "zl"), ("yl", "core", "x")),
        check_vma=False,
    )
```

time: 113 us -> 146 us (1.29)
  the two profiles are of different devices: /device:TPU:18 before, /device:TPU:1 now
where the time goes in v6:
time: 146 us
  waiting for transfers between devices  54.3 us (37%)
  blocking collectives  47.6 us (33%)
  starting transfers between devices  38.1 us (26%)
  local copies, waits for them, and re-layouts  3.36 us (2%)
  Pallas kernels  2.45 us (2%)
    all_to_all x1, blocking collectives, to_all(): return lax.all_to_all(copies, axes, split_axis=0, concat_axis=0, tiled=True)  29.3 us
    all_to_all x1, waiting for transfers between devices, to_all(): return lax.all_to_all(copies, axes, split_axis=0, concat_axis=0, tiled=True)  28.5 us
    ppermute x5, waiting for transfers between devices, moved(): return lax.ppermute(value, axes, perm)  25.8 us
    ppermute x5, starting transfers between devices, moved(): return lax.ppermute(value, axes, perm)  20 us
    all_to_all x1, blocking collectives, per_device(): lax.all_to_all(part, 'x', split_axis=0, concat_axis=0, tiled=True)  18.3 us
    all_to_all x1, starting transfers between devices, to_all(): return lax.all_to_all(copies, axes, split_axis=0, concat_axis=0, tiled=True)  18.1 us
  transfers between devices with their start and end apart: 6, of which 6 were waited for; matrix products, arithmetic and copies ran while one was open for 1% of the time, Pallas kernels for 0%

profile of v6, /device:TPU:1, one launch (start us, length us, event | category | flops | bytes accessed | tf_op | source)
XLA Modules:
  0.0 146.1 jit_solution(15617265212422375958)
XLA Ops:
  0.0 0.0 copy-start
  0.0 9.0 %collective-permute-start = (bf16[256,512]{1,0:T(8,128)(2,1)}, bf16[256,512]{1,0:T(8,128)(2,1)S(1)}, u32[]{:S(2)}, u32[]{:S(2)}) collective-permute-start(bf16[256,512]{1,0:T(8,128)(2,1)} %param.3), channel_id=1, source_target_pairs={{0,0},{1,32},{2,1},{3,33},{4,256},{5,288},{6,257},{7,289},{32,2},{... | collective-permute-start | bytes 786440 | tf_op jit(solution)/shard_map/ppermute | solution.py:22
  9.0 5.5 %collective-permute-done = bf16[256,512]{1,0:T(8,128)(2,1)S(1)} collective-permute-done((bf16[256,512]{1,0:T(8,128)(2,1)}, bf16[256,512]{1,0:T(8,128)(2,1)S(1)}, u32[]{:S(2)}, u32[]{:S(2)}) %collective-permute-start) | collective-permute-done | bytes 262176 | tf_op jit(solution)/shard_map/ppermute | solution.py:22
  14.5 0.1 broadcast_in_dim.5
  14.6 29.3 %all_to_all.15.even_ref = bf16[4,256,512]{2,1,0:T(8,128)(2,1)S(1)} all-to-all(bf16[4,256,512]{2,1,0:T(8,128)(2,1)S(1)} %broadcast_in_dim.5), channel_id=1, replica_groups=mesh['yh'=2,'zh'=4,'zl'=2,'yl'=4,'core'=2,'x'=4] {'zh'}, dimensions={0} | all-to-all | bytes 2097152 | tf_op jit(solution)/shard_map/all_to_all | solution.py:71
  43.9 0.0 copy-done
  43.9 1.5 %broadcast_in_dim.4 = bf16[8,256,512]{2,1,0:T(8,128)(2,1)} broadcast(bf16[256,512]{1,0:T(8,128)(2,1)S(1)} %copy-done), dimensions={1,2} | broadcast | bytes 2359296 | tf_op jit(solution)/shard_map/broadcast_in_dim | solution.py:70
  45.4 18.1 %all-to-all-start = ((bf16[8,256,512]{2,1,0:T(8,128)(2,1)}), bf16[8,256,512]{2,1,0:T(8,128)(2,1)S(1)}, u32[]{:S(2)}, u32[]{:S(2)}) async-start(bf16[8,256,512]{2,1,0:T(8,128)(2,1)} %broadcast_in_dim.4), calls=%async_computation | async-start | bytes 4194304 | tf_op jit(solution)/shard_map/all_to_all | solution.py:71
  63.5 1.1 fusion.1
  64.6 1.9 %collective-permute-start.1 = (bf16[2,256,512]{2,1,0:T(8,128)(2,1)}, bf16[2,256,512]{2,1,0:T(8,128)(2,1)}, u32[]{:S(2)}, u32[]{:S(2)}) collective-permute-start(bf16[2,256,512]{2,1,0:T(8,128)(2,1)} %get-tuple-element.6), channel_id=1, source_target_pairs={{0,224},{32,0},{64,32},{96,64},{128,96},{160,128},{192,160},{224,1... | collective-permute-start | bytes 1572872 | tf_op jit(solution)/shard_map/ppermute | solution.py:22
  66.5 3.4 %collective-permute-start.2 = (bf16[2,256,512]{2,1,0:T(8,128)(2,1)}, bf16[2,256,512]{2,1,0:T(8,128)(2,1)}, u32[]{:S(2)}, u32[]{:S(2)}) collective-permute-start(bf16[2,256,512]{2,1,0:T(8,128)(2,1)} %get-tuple-element.5), channel_id=1, source_target_pairs={{0,32},{32,64},{64,96},{96,128},{128,160},{160,192},{192,224},{224... | collective-permute-start | bytes 1572872 | tf_op jit(solution)/shard_map/ppermute | solution.py:22
  69.9 0.1 pad_add_fusion.place
  70.0 10.7 %collective-permute-done.1.up_ref = bf16[2,256,512]{2,1,0:T(8,128)(2,1)} collective-permute-done((bf16[2,256,512]{2,1,0:T(8,128)(2,1)}, bf16[2,256,512]{2,1,0:T(8,128)(2,1)}, u32[]{:S(2)}, u32[]{:S(2)}) %collective-permute-start.1) | collective-permute-done | bytes 524320 | tf_op jit(solution)/shard_map/ppermute | solution.py:22
  80.7 1.1 collective-permute-done.2.down_ref
  81.8 28.5 %all-to-all-done.w_ref = bf16[8,256,512]{2,1,0:T(8,128)(2,1)S(1)} async-done(((bf16[8,256,512]{2,1,0:T(8,128)(2,1)}), bf16[8,256,512]{2,1,0:T(8,128)(2,1)S(1)}, u32[]{:S(2)}, u32[]{:S(2)}) %all-to-all-start) | async-done | bytes 2097184 | tf_op jit(solution)/shard_map/all_to_all | solution.py:71
  110.3 2.4 %shard_map.28 = f32[2,4,256,128]{3,2,1,0:T(8,128)S(1)} custom-call(s32[2]{0:T(128)S(1)} %pad_add_fusion.place, bf16[8,256,512]{2,1,0:T(8,128)(2,1)S(1)} %all-to-all-done.w_ref, bf16[4,256,512]{2,1,0:T(8,128)(2,1)S(1)} %all_to_all.15.even_ref, bf16[2,256,512]{2,1,0:T(8,128)(2,1)} %collective-permute-done.1.up_ref, ...), custom_call_target="tpu_custom_call" | custom-call | tf_op jit(solution)/shard_map/pallas_call | solution.py:60
  112.8 1.9 %collective-permute-start.3 = (f32[4,256,128]{2,1,0:T(8,128)S(1)}, f32[4,256,128]{2,1,0:T(8,128)S(1)}, u32[]{:S(2)}, u32[]{:S(2)}) collective-permute-start(f32[4,256,128]{2,1,0:T(8,128)S(1)} %slice_bitcast_fusion), channel_id=1, source_target_pairs={{0,4},{4,0},{1,5},{5,1},{2,6},{6,2},{3,7},{7,3},{8,12},{12,8},{9,1... | collective-permute-start | bytes 1572872 | tf_op jit(solution)/shard_map/ppermute | solution.py:22
  114.7 1.9 %collective-permute-done.3 = f32[4,256,128]{2,1,0:T(8,128)S(1)} collective-permute-done((f32[4,256,128]{2,1,0:T(8,128)S(1)}, f32[4,256,128]{2,1,0:T(8,128)S(1)}, u32[]{:S(2)}, u32[]{:S(2)}) %collective-permute-start.3) | collective-permute-done | bytes 524320 | tf_op jit(solution)/shard_map/ppermute | solution.py:22
  116.6 0.1 fusion
  116.7 18.3 %all_to_all.16 = f32[4,256,128]{2,1,0:T(8,128)S(1)} all-to-all(f32[4,256,128]{2,1,0:T(8,128)S(1)} %fusion), channel_id=1, replica_groups=mesh['yh'=2,'zh'=4,'zl'=2,'yl'=4,'core'=2,'x'=4] {'x'}, dimensions={0} | all-to-all | bytes 1048576 | tf_op jit(solution)/shard_map/all_to_all | solution.py:82
  135.0 3.8 %collective-permute-start.4 = (f32[256,128]{1,0:T(8,128)S(1)}, f32[256,128]{1,0:T(8,128)S(1)}, u32[]{:S(2)}, u32[]{:S(2)}) collective-permute-start(f32[256,128]{1,0:T(8,128)S(1)} %reduce_sum.9), channel_id=1, source_target_pairs={{0,0},{4,256},{256,4},{260,260},{1,1},{5,257},{257,5},{261,261},{2... | collective-permute-start | bytes 393224 | tf_op jit(solution)/shard_map/ppermute | solution.py:22
  138.8 6.6 %collective-permute-done.4 = f32[256,128]{1,0:T(8,128)S(1)} collective-permute-done((f32[256,128]{1,0:T(8,128)S(1)}, f32[256,128]{1,0:T(8,128)S(1)}, u32[]{:S(2)}, u32[]{:S(2)}) %collective-permute-start.4) | collective-permute-done | bytes 131104 | tf_op jit(solution)/shard_map/ppermute | solution.py:22
  145.4 0.7 copy.4
  (2 shorter events, 0.1 us)
Async XLA Ops:
  0.0 43.9 %copy-start = (bf16[256,512]{1,0:T(8,128)(2,1)S(1)}, bf16[256,512]{1,0:T(8,128)(2,1)}, u32[]{:S(2)}) copy-start(bf16[256,512]{1,0:T(8,128)(2,1)} %param.2) | copy-start | bytes 786436
  0.0 14.5 %collective-permute-start = (bf16[256,512]{1,0:T(8,128)(2,1)}, bf16[256,512]{1,0:T(8,128)(2,1)S(1)}, u32[]{:S(2)}, u32[]{:S(2)}) collective-permute-start(bf16[256,512]{1,0:T(8,128)(2,1)} %param.3), channel_id=1, source_target_pairs={{0,0},{1,32},{2,1},{3,33},{4,256},{5,288},{6,257},{7,289},{32,2},{... | collective-permute-start | bytes 786440 | tf_op jit(solution)/shard_map/ppermute | solution.py:22
  45.4 64.9 %all-to-all-start = ((bf16[8,256,512]{2,1,0:T(8,128)(2,1)}), bf16[8,256,512]{2,1,0:T(8,128)(2,1)S(1)}, u32[]{:S(2)}, u32[]{:S(2)}) async-start(bf16[8,256,512]{2,1,0:T(8,128)(2,1)} %broadcast_in_dim.4), calls=%async_computation | async-start | bytes 4194304 | tf_op jit(solution)/shard_map/all_to_all | solution.py:71
  64.6 16.1 %collective-permute-start.1 = (bf16[2,256,512]{2,1,0:T(8,128)(2,1)}, bf16[2,256,512]{2,1,0:T(8,128)(2,1)}, u32[]{:S(2)}, u32[]{:S(2)}) collective-permute-start(bf16[2,256,512]{2,1,0:T(8,128)(2,1)} %get-tuple-element.6), channel_id=1, source_target_pairs={{0,224},{32,0},{64,32},{96,64},{128,96},{160,128},{192,160},{224,1... | collective-permute-start | bytes 1572872 | tf_op jit(solution)/shard_map/ppermute | solution.py:22
  66.5 15.3 %collective-permute-start.2 = (bf16[2,256,512]{2,1,0:T(8,128)(2,1)}, bf16[2,256,512]{2,1,0:T(8,128)(2,1)}, u32[]{:S(2)}, u32[]{:S(2)}) collective-permute-start(bf16[2,256,512]{2,1,0:T(8,128)(2,1)} %get-tuple-element.5), channel_id=1, source_target_pairs={{0,32},{32,64},{64,96},{96,128},{128,160},{160,192},{192,224},{224... | collective-permute-start | bytes 1572872 | tf_op jit(solution)/shard_map/ppermute | solution.py:22
  112.8 3.8 %collective-permute-start.3 = (f32[4,256,128]{2,1,0:T(8,128)S(1)}, f32[4,256,128]{2,1,0:T(8,128)S(1)}, u32[]{:S(2)}, u32[]{:S(2)}) collective-permute-start(f32[4,256,128]{2,1,0:T(8,128)S(1)} %slice_bitcast_fusion), channel_id=1, source_target_pairs={{0,4},{4,0},{1,5},{5,1},{2,6},{6,2},{3,7},{7,3},{8,12},{12,8},{9,1... | collective-permute-start | bytes 1572872 | tf_op jit(solution)/shard_map/ppermute | solution.py:22
  135.0 10.4 %collective-permute-start.4 = (f32[256,128]{1,0:T(8,128)S(1)}, f32[256,128]{1,0:T(8,128)S(1)}, u32[]{:S(2)}, u32[]{:S(2)}) collective-permute-start(f32[256,128]{1,0:T(8,128)S(1)} %reduce_sum.9), channel_id=1, source_target_pairs={{0,0},{4,256},{256,4},{260,260},{1,1},{5,257},{257,5},{261,261},{2... | collective-permute-start | bytes 393224 | tf_op jit(solution)/shard_map/ppermute | solution.py:22

commit v7 on v5

--- a/solution.py
+++ b/solution.py
@@ -8,8 +8,8 @@
 from jax.experimental.pallas import tpu as pltpu
 from jax.sharding import Mesh, PartitionSpec as P
 
-AXES = ("yh", "z", "yl", "core", "x")
-SHAPE = (2, 8, 4, 2, 4)
+AXES = ("yh", "zh", "zl", "yl", "core", "x")
+SHAPE = (2, 4, 2, 4, 2, 4)
 SIZES = dict(zip(AXES, SHAPE))
 UNIT = 256
 
@@ -22,6 +22,14 @@
         there = where(**place)
         perm.append((i, int(np.ravel_multi_index([there[a] for a in axes], shape))))
     return lax.ppermute(value, axes, perm)
+
+
+def along_z(value, by):
+    def where(zh, zl):
+        z = (2 * zh + zl + by) % 8
+        return {"zh": z >> 1, "zl": z & 1}
+
+    return moved(value, ("zh", "zl"), where)
 
 
 def regrouped(value, second):
@@ -40,9 +48,26 @@
     return moved(value, ("core",), lambda core: {"core": 1 - core})
 
 
-def product_kernel(place, near_ref, far_ref, near2_ref, far2_ref, t_ref, out_ref):
-    for unit in range(8):
-        t = t_ref[unit]
+def join_kernel(first_ref, second_ref, arrived_ref, out_ref):
+    out_ref[:2] = first_ref[...]
+    out_ref[2:] = second_ref[...]
+
+
+def joined(first, second, arrived):
+    vmem = pl.BlockSpec(memory_space=pltpu.VMEM)
+    return pl.pallas_call(
+        join_kernel,
+        out_shape=jax.ShapeDtypeStruct((4,) + first.shape[1:], first.dtype),
+        in_specs=[vmem] * 3,
+        out_specs=vmem,
+        compiler_params=pltpu.CompilerParams(vmem_limit_bytes=24 * 1024 * 1024),
+    )(first, second, arrived)
+
+
+def product_kernel(place, near_ref, far_ref, near2_ref, far2_ref, even_ref, up_ref, down_ref, out_ref):
+    tiles = [even_ref.at[i] for i in range(4)] + [up_ref.at[i] for i in range(2)] + [down_ref.at[i] for i in range(2)]
+    for unit, t_ref in enumerate(tiles):
+        t = t_ref[...]
         same, near = place[4 * unit] == 1, place[4 * unit + 1] == 1
         for rel in range(2):
             slot = place[4 * unit + 2 + rel]
@@ -67,27 +92,28 @@
         out_shape=jax.ShapeDtypeStruct((4, 2, UNIT, 128), jnp.float32),
         in_specs=[pl.BlockSpec(memory_space=pltpu.SMEM)] + [vmem] * len(operands),
         out_specs=vmem,
-        compiler_params=pltpu.CompilerParams(vmem_limit_bytes=40 * 1024 * 1024),
+        compiler_params=pltpu.CompilerParams(vmem_limit_bytes=24 * 1024 * 1024),
     )(place, *operands)
 
 
 def per_device(integrals, amplitudes):
-    yh, z, yl, core, x = (lax.axis_index(a) for a in AXES)
-    copies = jnp.broadcast_to(amplitudes[None], (8,) + amplitudes.shape)
-    tiles = lax.all_to_all(copies, "z", split_axis=0, concat_axis=0, tiled=True)
+    yh, zh, zl, yl, core, x = (lax.axis_index(a) for a in AXES)
+    copies = jnp.broadcast_to(amplitudes[None], (4,) + amplitudes.shape)
+    even = lax.all_to_all(copies, "zh", split_axis=0, concat_axis=0, tiled=True)
+    from_up = along_z(even[:2], -1)
+    from_down = along_z(even[2:], 1)
     halves = jnp.stack([integrals[:, :UNIT], integrals[:, UNIT:]])
     high = x >> 1
     own = jnp.stack([regrouped(lax.dynamic_index_in_dim(halves, high ^ i, 0, False), i) for i in (0, 1)])
-    near = jnp.concatenate([own, across_yl(own, 2)])
+    near = joined(own, across_yl(own, 2), even)
     far = across_yl(near, 1)
     near2, far2 = core_swap(near), core_swap(far)
     place = []
-    for unit in range(8):
-        u4, u3, u2 = unit >> 2, (unit >> 1) & 1, unit & 1
+    for u4, u3, u2 in [(i >> 1, i & 1, zl) for i in range(4)] + [(i >> 1, i & 1, 1 - zl) for i in range(4)]:
         place += [jnp.where(core == u3, 1, 0), jnp.where((yl & 1) == u4, 1, 0)]
         place += [((yh ^ rel) ^ (yl >> 1)) * 2 + (u2 ^ (x & 1)) for rel in (0, 1)]
     place = jnp.stack(place).astype(jnp.int32)
-    part = product(place, near, far, near2, far2, tiles)
+    part = product(place, near, far, near2, far2, even, from_up, from_down)
     part = lax.all_to_all(part, "x", split_axis=0, concat_axis=0, tiled=True).sum(axis=0)
     return part[0] + moved(part[1], ("yh",), lambda yh: {"yh": 1 - yh})
 
@@ -96,7 +122,7 @@
     return jax.shard_map(
         per_device,
         mesh=Mesh(mesh.devices.reshape(SHAPE), AXES),
-        in_specs=(P(("yh", "z"), ("yl", "core", "x")), P(("yh", "z", "x"), ("yl", "core"))),
-        out_specs=P(("yh", "z"), ("yl", "core", "x")),
+        in_specs=(P(("yh", "zh", "zl"), ("yl", "core", "x")), P(("yh", "zh", "zl", "x"), ("yl", "core"))),
+        out_specs=P(("yh", "zh", "zl"), ("yl", "core", "x")),
         check_vma=False,
     )

time: 100 us -> 105 us (1.050)
  the two profiles are of different devices: /device:TPU:64 before, /device:TPU:16 now
where the time goes in v7:
time: 105 us; the launch traced here: 104 us
  starting transfers between devices  41.6 us (40%)
  waiting for transfers between devices  37 us (35%)
  blocking collectives  19 us (18%)
  local copies, waits for them, and re-layouts  3.2 us (3%)
  Pallas kernels  2.49 us (2%)
    ppermute x9, waiting for transfers between devices, moved(): return lax.ppermute(value, axes, perm)  37 us
    ppermute x9, starting transfers between devices, moved(): return lax.ppermute(value, axes, perm)  31.2 us
    all_to_all x1, blocking collectives, per_device(): lax.all_to_all(part, 'x', split_axis=0, concat_axis=0, tiled=True)  19 us
    all_to_all x1, starting transfers between devices, per_device(): even = lax.all_to_all(copies, 'zh', split_axis=0, concat_axis=0, tiled=True)  10.4 us
    pallas_call x1, Pallas kernels, product(): pl.pallas_call(product_kernel, out_shape=jax.ShapeDtypeStruct((4, 2, UNIT...  2.45 us
  transfers between devices with their start and end apart: 10, of which 7 were waited for; matrix products, arithmetic and copies ran while one was open for 1% of the time, Pallas kernels for 0%

profile of v7, /device:TPU:16, one launch (start us, length us, event | category | flops | bytes accessed | tf_op | source)
XLA Modules:
  0.0 104.4 jit_solution(7576570175049527588)
XLA Ops:
  0.0 2.0 %broadcast_in_dim.2 = bf16[4,256,512]{2,1,0:T(8,128)(2,1)} broadcast(bf16[256,512]{1,0:T(8,128)(2,1)} %param.3), dimensions={1,2} | broadcast | bytes 1310720 | tf_op jit(solution)/shard_map/broadcast_in_dim | solution.py:101
  2.0 0.0 copy-start
  2.0 10.4 %all-to-all-start = ((bf16[4,256,512]{2,1,0:T(8,128)(2,1)}), bf16[4,256,512]{2,1,0:T(8,128)(2,1)S(1)}, u32[]{:S(2)}, u32[]{:S(2)}) async-start(bf16[4,256,512]{2,1,0:T(8,128)(2,1)} %broadcast_in_dim.2), calls=%async_computation | async-start | bytes 2097152 | tf_op jit(solution)/shard_map/all_to_all | solution.py:102
  12.4 0.0 copy-done
  12.5 0.1 fusion.3
  12.6 5.7 %collective-permute-start = (bf16[256,256]{1,0:T(8,128)(2,1)S(1)}, bf16[256,256]{1,0:T(8,128)(2,1)S(1)}, u32[]{:S(2)}, u32[]{:S(2)}) collective-permute-start(bf16[256,256]{1,0:T(8,128)(2,1)S(1)} %get-tuple-element.7), channel_id=1, source_target_pairs={{0,0},{1,2},{2,1},{3,3},{8,8},{9,10},{10,9},{11,11},{16,256},{17,2... | collective-permute-start | bytes 393224 | tf_op jit(solution)/shard_map/ppermute | solution.py:24
  18.3 4.1 %collective-permute-start.1 = (bf16[256,256]{1,0:T(8,128)(2,1)S(1)}, bf16[256,256]{1,0:T(8,128)(2,1)S(1)}, u32[]{:S(2)}, u32[]{:S(2)}) collective-permute-start(bf16[256,256]{1,0:T(8,128)(2,1)S(1)} %get-tuple-element.8), channel_id=1, source_target_pairs={{0,1},{1,3},{2,0},{3,2},{8,9},{9,11},{10,8},{11,10},{16,257},{17,2... | collective-permute-start | bytes 393224 | tf_op jit(solution)/shard_map/ppermute | solution.py:24
  22.4 1.9 %collective-permute-done = bf16[256,256]{1,0:T(8,128)(2,1)S(1)} collective-permute-done((bf16[256,256]{1,0:T(8,128)(2,1)S(1)}, bf16[256,256]{1,0:T(8,128)(2,1)S(1)}, u32[]{:S(2)}, u32[]{:S(2)}) %collective-permute-start) | collective-permute-done | bytes 131104 | tf_op jit(solution)/shard_map/ppermute | solution.py:24
  24.4 8.0 %collective-permute-done.1 = bf16[256,256]{1,0:T(8,128)(2,1)S(1)} collective-permute-done((bf16[256,256]{1,0:T(8,128)(2,1)S(1)}, bf16[256,256]{1,0:T(8,128)(2,1)S(1)}, u32[]{:S(2)}, u32[]{:S(2)}) %collective-permute-start.1) | collective-permute-done | bytes 131104 | tf_op jit(solution)/shard_map/ppermute | solution.py:24
  32.4 1.9 %collective-permute-start.2 = (bf16[2,256,256]{2,1,0:T(8,128)(2,1)S(1)}, bf16[2,256,256]{2,1,0:T(8,128)(2,1)S(1)}, u32[]{:S(2)}, u32[]{:S(2)}) collective-permute-start(bf16[2,256,256]{2,1,0:T(8,128)(2,1)S(1)} %pad_maximum_fusion.first_ref), channel_id=1, source_target_pairs={{0,16},{8,24},{16,0},{24,8},{1,17},{9,25},{17,1},{25,9},{2,18},{10... | collective-permute-start | bytes 786440 | tf_op jit(solution)/shard_map/ppermute | solution.py:24
  34.4 9.1 %collective-permute-done.2.second_ref = bf16[2,256,256]{2,1,0:T(8,128)(2,1)S(1)} collective-permute-done((bf16[2,256,256]{2,1,0:T(8,128)(2,1)S(1)}, bf16[2,256,256]{2,1,0:T(8,128)(2,1)S(1)}, u32[]{:S(2)}, u32[]{:S(2)}) %collective-permute-start.2) | collective-permute-done | bytes 262176 | tf_op jit(solution)/shard_map/ppermute | solution.py:24
  43.5 0.0 all-to-all-done.arrived_ref.even_ref
  43.5 4.1 %collective-permute-start.3 = (bf16[4,256,256]{2,1,0:T(8,128)(2,1)S(1)}, bf16[4,256,256]{2,1,0:T(8,128)(2,1)S(1)}, u32[]{:S(2)}, u32[]{:S(2)}) collective-permute-start(bf16[4,256,256]{2,1,0:T(8,128)(2,1)S(1)} %shard_map.28.near_ref), channel_id=1, source_target_pairs={{0,8},{8,0},{16,24},{24,16},{1,9},{9,1},{17,25},{25,17},{2,10},{10... | collective-permute-start | bytes 1572872 | tf_op jit(solution)/shard_map/ppermute | solution.py:24
  47.6 1.9 %collective-permute-start.4 = (bf16[4,256,256]{2,1,0:T(8,128)(2,1)S(1)}, bf16[4,256,256]{2,1,0:T(8,128)(2,1)S(1)}, u32[]{:S(2)}, u32[]{:S(2)}) collective-permute-start(bf16[4,256,256]{2,1,0:T(8,128)(2,1)S(1)} %shard_map.28.near_ref), channel_id=1, source_target_pairs={{0,4},{4,0},{1,5},{5,1},{2,6},{6,2},{3,7},{7,3},{8,12},{12,8},{9,1... | collective-permute-start | bytes 1572872 | tf_op jit(solution)/shard_map/ppermute | solution.py:24
  49.6 1.1 %fusion.5 = (bf16[2,256,512]{2,1,0:T(8,128)(2,1)}, bf16[2,256,512]{2,1,0:T(8,128)(2,1)}) fusion(bf16[4,256,512]{2,1,0:T(8,128)(2,1)S(1)} %all-to-all-done.arrived_ref.even_ref), kind=kLoop, calls=%fused_computation.14 | loop fusion | bytes 2097152 | tf_op jit(solution)/shard_map/slice | solution.py:104
  50.6 3.4 %collective-permute-start.7 = (bf16[2,256,512]{2,1,0:T(8,128)(2,1)}, bf16[2,256,512]{2,1,0:T(8,128)(2,1)S(1)}, u32[]{:S(2)}, u32[]{:S(2)}) collective-permute-start(bf16[2,256,512]{2,1,0:T(8,128)(2,1)} %get-tuple-element.5), channel_id=1, source_target_pairs={{0,32},{32,64},{64,96},{96,128},{128,160},{160,192},{192,224},{224... | collective-permute-start | bytes 1572872 | tf_op jit(solution)/shard_map/ppermute | solution.py:24
  54.0 4.3 %collective-permute-start.6 = (bf16[2,256,512]{2,1,0:T(8,128)(2,1)}, bf16[2,256,512]{2,1,0:T(8,128)(2,1)}, u32[]{:S(2)}, u32[]{:S(2)}) collective-permute-start(bf16[2,256,512]{2,1,0:T(8,128)(2,1)} %get-tuple-element.6), channel_id=1, source_target_pairs={{0,224},{32,0},{64,32},{96,64},{128,96},{160,128},{192,160},{224,1... | collective-permute-start | bytes 1572872 | tf_op jit(solution)/shard_map/ppermute | solution.py:24
  58.3 0.1 collective-permute-done.3.far_ref
  58.4 2.1 %collective-permute-start.5 = (bf16[4,256,256]{2,1,0:T(8,128)(2,1)S(1)}, bf16[4,256,256]{2,1,0:T(8,128)(2,1)}, u32[]{:S(2)}, u32[]{:S(2)}) collective-permute-start(bf16[4,256,256]{2,1,0:T(8,128)(2,1)S(1)} %collective-permute-done.3.far_ref), channel_id=1, source_target_pairs={{0,4},{4,0},{1,5},{5,1},{2,6},{6,2},{3,7},{7,3},{8,12},{12,8},{9,1... | collective-permute-start | bytes 1572872 | tf_op jit(solution)/shard_map/ppermute | solution.py:24
  60.5 0.1 stack.38.place
  60.6 0.0 collective-permute-done.4.near2_ref
  60.6 8.6 %collective-permute-done.7.down_ref = bf16[2,256,512]{2,1,0:T(8,128)(2,1)S(1)} collective-permute-done((bf16[2,256,512]{2,1,0:T(8,128)(2,1)}, bf16[2,256,512]{2,1,0:T(8,128)(2,1)S(1)}, u32[]{:S(2)}, u32[]{:S(2)}) %collective-permute-start.7) | collective-permute-done | bytes 524320 | tf_op jit(solution)/shard_map/ppermute | solution.py:24
  69.2 1.3 %collective-permute-done.6.up_ref = bf16[2,256,512]{2,1,0:T(8,128)(2,1)} collective-permute-done((bf16[2,256,512]{2,1,0:T(8,128)(2,1)}, bf16[2,256,512]{2,1,0:T(8,128)(2,1)}, u32[]{:S(2)}, u32[]{:S(2)}) %collective-permute-start.6) | collective-permute-done | bytes 524320 | tf_op jit(solution)/shard_map/ppermute | solution.py:24
  70.5 0.0 collective-permute-done.5.far2_ref
  70.5 2.5 %shard_map.29 = f32[4,2,256,128]{3,2,1,0:T(8,128)S(1)} custom-call(s32[32]{0:T(128)S(1)} %stack.38.place, bf16[4,256,256]{2,1,0:T(8,128)(2,1)S(1)} %shard_map.28.near_ref, bf16[4,256,256]{2,1,0:T(8,128)(2,1)S(1)} %collective-permute-done.3.far_ref, bf16[4,256,256]{2,1,0:T(8,128)(2,1)S(1)} %collective-permute-done.4.near2_ref, ...), custom_call_target="tpu_custom_call" | custom-call | tf_op jit(solution)/shard_map/pallas_call | solution.py:90
  72.9 19.0 %all_to_all.10 = f32[4,2,256,128]{3,2,1,0:T(8,128)S(1)} all-to-all(f32[4,2,256,128]{3,2,1,0:T(8,128)S(1)} %shard_map.29), channel_id=1, replica_groups=mesh['yh'=2,'zh'=4,'zl'=2,'yl'=4,'core'=2,'x'=4] {'x'}, dimensions={0} | all-to-all | bytes 2097152 | tf_op jit(solution)/shard_map/all_to_all | solution.py:117
  92.0 0.1 reduce_sum.9
  92.0 3.7 %collective-permute-start.8 = (f32[256,128]{1,0:T(8,128)S(1)}, f32[256,128]{1,0:T(8,128)S(1)}, u32[]{:S(2)}, u32[]{:S(2)}) collective-permute-start(f32[256,128]{1,0:T(8,128)S(1)} %slice_bitcast_fusion), channel_id=1, source_target_pairs={{0,256},{256,0},{1,257},{257,1},{2,258},{258,2},{3,259},{259,3},{4... | collective-permute-start | bytes 393224 | tf_op jit(solution)/shard_map/ppermute | solution.py:24
  95.8 8.0 %collective-permute-done.8 = f32[256,128]{1,0:T(8,128)S(1)} collective-permute-done((f32[256,128]{1,0:T(8,128)S(1)}, f32[256,128]{1,0:T(8,128)S(1)}, u32[]{:S(2)}, u32[]{:S(2)}) %collective-permute-start.8) | collective-permute-done | bytes 131104 | tf_op jit(solution)/shard_map/ppermute | solution.py:24
  103.8 0.7 fusion.4
  (4 shorter events, 0.1 us)
Async XLA Ops:
  2.0 10.4 %copy-start = (bf16[256,512]{1,0:T(8,128)(2,1)S(1)}, bf16[256,512]{1,0:T(8,128)(2,1)}, u32[]{:S(2)}) copy-start(bf16[256,512]{1,0:T(8,128)(2,1)} %param.2) | copy-start | bytes 786436
  2.0 41.5 %all-to-all-start = ((bf16[4,256,512]{2,1,0:T(8,128)(2,1)}), bf16[4,256,512]{2,1,0:T(8,128)(2,1)S(1)}, u32[]{:S(2)}, u32[]{:S(2)}) async-start(bf16[4,256,512]{2,1,0:T(8,128)(2,1)} %broadcast_in_dim.2), calls=%async_computation | async-start | bytes 2097152 | tf_op jit(solution)/shard_map/all_to_all | solution.py:102
  12.6 11.8 %collective-permute-start = (bf16[256,256]{1,0:T(8,128)(2,1)S(1)}, bf16[256,256]{1,0:T(8,128)(2,1)S(1)}, u32[]{:S(2)}, u32[]{:S(2)}) collective-permute-start(bf16[256,256]{1,0:T(8,128)(2,1)S(1)} %get-tuple-element.7), channel_id=1, source_target_pairs={{0,0},{1,2},{2,1},{3,3},{8,8},{9,10},{10,9},{11,11},{16,256},{17,2... | collective-permute-start | bytes 393224 | tf_op jit(solution)/shard_map/ppermute | solution.py:24
  18.3 14.1 %collective-permute-start.1 = (bf16[256,256]{1,0:T(8,128)(2,1)S(1)}, bf16[256,256]{1,0:T(8,128)(2,1)S(1)}, u32[]{:S(2)}, u32[]{:S(2)}) collective-permute-start(bf16[256,256]{1,0:T(8,128)(2,1)S(1)} %get-tuple-element.8), channel_id=1, source_target_pairs={{0,1},{1,3},{2,0},{3,2},{8,9},{9,11},{10,8},{11,10},{16,257},{17,2... | collective-permute-start | bytes 393224 | tf_op jit(solution)/shard_map/ppermute | solution.py:24
  32.4 11.1 %collective-permute-start.2 = (bf16[2,256,256]{2,1,0:T(8,128)(2,1)S(1)}, bf16[2,256,256]{2,1,0:T(8,128)(2,1)S(1)}, u32[]{:S(2)}, u32[]{:S(2)}) collective-permute-start(bf16[2,256,256]{2,1,0:T(8,128)(2,1)S(1)} %pad_maximum_fusion.first_ref), channel_id=1, source_target_pairs={{0,16},{8,24},{16,0},{24,8},{1,17},{9,25},{17,1},{25,9},{2,18},{10... | collective-permute-start | bytes 786440 | tf_op jit(solution)/shard_map/ppermute | solution.py:24
  43.5 14.8 %collective-permute-start.3 = (bf16[4,256,256]{2,1,0:T(8,128)(2,1)S(1)}, bf16[4,256,256]{2,1,0:T(8,128)(2,1)S(1)}, u32[]{:S(2)}, u32[]{:S(2)}) collective-permute-start(bf16[4,256,256]{2,1,0:T(8,128)(2,1)S(1)} %shard_map.28.near_ref), channel_id=1, source_target_pairs={{0,8},{8,0},{16,24},{24,16},{1,9},{9,1},{17,25},{25,17},{2,10},{10... | collective-permute-start | bytes 1572872 | tf_op jit(solution)/shard_map/ppermute | solution.py:24
  47.6 13.0 %collective-permute-start.4 = (bf16[4,256,256]{2,1,0:T(8,128)(2,1)S(1)}, bf16[4,256,256]{2,1,0:T(8,128)(2,1)S(1)}, u32[]{:S(2)}, u32[]{:S(2)}) collective-permute-start(bf16[4,256,256]{2,1,0:T(8,128)(2,1)S(1)} %shard_map.28.near_ref), channel_id=1, source_target_pairs={{0,4},{4,0},{1,5},{5,1},{2,6},{6,2},{3,7},{7,3},{8,12},{12,8},{9,1... | collective-permute-start | bytes 1572872 | tf_op jit(solution)/shard_map/ppermute | solution.py:24
  50.6 18.5 %collective-permute-start.7 = (bf16[2,256,512]{2,1,0:T(8,128)(2,1)}, bf16[2,256,512]{2,1,0:T(8,128)(2,1)S(1)}, u32[]{:S(2)}, u32[]{:S(2)}) collective-permute-start(bf16[2,256,512]{2,1,0:T(8,128)(2,1)} %get-tuple-element.5), channel_id=1, source_target_pairs={{0,32},{32,64},{64,96},{96,128},{128,160},{160,192},{192,224},{224... | collective-permute-start | bytes 1572872 | tf_op jit(solution)/shard_map/ppermute | solution.py:24
  54.0 16.4 %collective-permute-start.6 = (bf16[2,256,512]{2,1,0:T(8,128)(2,1)}, bf16[2,256,512]{2,1,0:T(8,128)(2,1)}, u32[]{:S(2)}, u32[]{:S(2)}) collective-permute-start(bf16[2,256,512]{2,1,0:T(8,128)(2,1)} %get-tuple-element.6), channel_id=1, source_target_pairs={{0,224},{32,0},{64,32},{96,64},{128,96},{160,128},{192,160},{224,1... | collective-permute-start | bytes 1572872 | tf_op jit(solution)/shard_map/ppermute | solution.py:24
  58.4 12.1 %collective-permute-start.5 = (bf16[4,256,256]{2,1,0:T(8,128)(2,1)S(1)}, bf16[4,256,256]{2,1,0:T(8,128)(2,1)}, u32[]{:S(2)}, u32[]{:S(2)}) collective-permute-start(bf16[4,256,256]{2,1,0:T(8,128)(2,1)S(1)} %collective-permute-done.3.far_ref), channel_id=1, source_target_pairs={{0,4},{4,0},{1,5},{5,1},{2,6},{6,2},{3,7},{7,3},{8,12},{12,8},{9,1... | collective-permute-start | bytes 1572872 | tf_op jit(solution)/shard_map/ppermute | solution.py:24
  92.0 11.7 %collective-permute-start.8 = (f32[256,128]{1,0:T(8,128)S(1)}, f32[256,128]{1,0:T(8,128)S(1)}, u32[]{:S(2)}, u32[]{:S(2)}) collective-permute-start(f32[256,128]{1,0:T(8,128)S(1)} %slice_bitcast_fusion), channel_id=1, source_target_pairs={{0,256},{256,0},{1,257},{257,1},{2,258},{258,2},{3,259},{259,3},{4... | collective-permute-start | bytes 393224 | tf_op jit(solution)/shard_map/ppermute | solution.py:24

commit v8 on v5

--- a/solution.py
+++ b/solution.py
@@ -24,32 +24,28 @@
     return lax.ppermute(value, axes, perm)
 
 
-def regrouped(value, second):
-    def where(yh, yl, x):
-        half = (x >> 1) ^ second
-        return {"yh": yl >> 1, "yl": 2 * yh + (yl & 1), "x": 2 * (x & 1) + half}
+def spread(value, mask):
+    def where(yh, yl, core, x):
+        half = (x >> 1) ^ core
+        return {"yh": yl >> 1, "yl": (2 * yh + (yl & 1)) ^ mask, "core": core, "x": 2 * (x & 1) + half}
 
-    return moved(value, ("yh", "yl", "x"), where)
-
-
-def across_yl(value, mask):
-    return moved(value, ("yl",), lambda yl: {"yl": yl ^ mask})
+    return moved(value, ("yh", "yl", "core", "x"), where)
 
 
 def core_swap(value):
     return moved(value, ("core",), lambda core: {"core": 1 - core})
 
 
-def product_kernel(place, near_ref, far_ref, near2_ref, far2_ref, t_ref, out_ref):
+def product_kernel(place, own_a, own_b, other_a, other_b, t_ref, out_ref):
     for unit in range(8):
         t = t_ref[unit]
-        same, near = place[4 * unit] == 1, place[4 * unit + 1] == 1
+        same = place[5 * unit] == 1
         for rel in range(2):
-            slot = place[4 * unit + 2 + rel]
+            first, slot = place[5 * unit + 1 + 2 * rel] == 1, place[5 * unit + 2 + 2 * rel]
             w = jnp.where(
                 same,
-                jnp.where(near, near_ref[slot], far_ref[slot]),
-                jnp.where(near, near2_ref[slot], far2_ref[slot]),
+                jnp.where(first, own_a[slot], own_b[slot]),
+                jnp.where(first, other_a[slot], other_b[slot]),
             )
             part = jnp.dot(w, t, preferred_element_type=jnp.float32)
             for block in range(4):
@@ -75,19 +71,20 @@
     yh, z, yl, core, x = (lax.axis_index(a) for a in AXES)
     copies = jnp.broadcast_to(amplitudes[None], (8,) + amplitudes.shape)
     tiles = lax.all_to_all(copies, "z", split_axis=0, concat_axis=0, tiled=True)
-    halves = jnp.stack([integrals[:, :UNIT], integrals[:, UNIT:]])
-    high = x >> 1
-    own = jnp.stack([regrouped(lax.dynamic_index_in_dim(halves, high ^ i, 0, False), i) for i in (0, 1)])
-    near = jnp.concatenate([own, across_yl(own, 2)])
-    far = across_yl(near, 1)
-    near2, far2 = core_swap(near), core_swap(far)
+    both = lax.all_gather(integrals, "core", axis=0)
+    half = lax.dynamic_slice_in_dim(both, ((x >> 1) ^ core) * UNIT, UNIT, 2)
+    own_a = jnp.concatenate([spread(half, mask) for mask in (0, 1)])
+    own_b = jnp.concatenate([spread(half, mask) for mask in (2, 3)])
+    other_a, other_b = core_swap(own_a), core_swap(own_b)
     place = []
     for unit in range(8):
         u4, u3, u2 = unit >> 2, (unit >> 1) & 1, unit & 1
-        place += [jnp.where(core == u3, 1, 0), jnp.where((yl & 1) == u4, 1, 0)]
-        place += [((yh ^ rel) ^ (yl >> 1)) * 2 + (u2 ^ (x & 1)) for rel in (0, 1)]
+        place.append(jnp.where(u2 ^ (x & 1) == core, 1, 0))
+        for rel in (0, 1):
+            mask = yl ^ (2 * (yh ^ rel) + u4)
+            place += [jnp.where(mask < 2, 1, 0), (mask & 1) * 2 + u3]
     place = jnp.stack(place).astype(jnp.int32)
-    part = product(place, near, far, near2, far2, tiles)
+    part = product(place, own_a, own_b, other_a, other_b, tiles)
     part = lax.all_to_all(part, "x", split_axis=0, concat_axis=0, tiled=True).sum(axis=0)
     return part[0] + moved(part[1], ("yh",), lambda yh: {"yh": 1 - yh})
 

time: 100 us -> 98.5 us (0.985)
  the two profiles are of different devices: /device:TPU:64 before, /device:TPU:56 now
where the time goes in v8:
time: 98.5 us; the launch traced here: 98.1 us
  starting transfers between devices  47 us (48%)
  waiting for transfers between devices  24.5 us (25%)
  blocking collectives  20.5 us (21%)
  local copies, waits for them, and re-layouts  2.7 us (3%)
  Pallas kernels  2.46 us (2%)
    ppermute x7, starting transfers between devices, moved(): return lax.ppermute(value, axes, perm)  36.5 us
    ppermute x7, waiting for transfers between devices, moved(): return lax.ppermute(value, axes, perm)  24.5 us
    all_to_all x1, blocking collectives, per_device(): lax.all_to_all(part, 'x', split_axis=0, concat_axis=0, tiled=True)  18.3 us
    all_to_all x1, starting transfers between devices, per_device(): tiles = lax.all_to_all(copies, 'z', split_axis=0, concat_axis=0, tiled=True)  10.4 us
    broadcast_in_dim x1, local copies, waits for them, and re-layouts, per_device(): copies = jnp.broadcast_to(amplitudes[None], (8,) + amplitudes.shape)  2.48 us
    pallas_call x1, Pallas kernels, product(): pl.pallas_call(product_kernel, out_shape=jax.ShapeDtypeStruct((4, 2, UNIT...  2.46 us
    all_gather x1, blocking collectives, per_device(): both = lax.all_gather(integrals, 'core', axis=0)  2.18 us
  transfers between devices with their start and end apart: 8, of which 4 were waited for; matrix products, arithmetic and copies ran while one was open for 0% of the time, Pallas kernels for 0%

profile of v8, /device:TPU:56, one launch (start us, length us, event | category | flops | bytes accessed | tf_op | source)
XLA Modules:
  0.0 98.1 jit_solution(13274170990845150881)
XLA Ops:
  0.0 2.5 %broadcast_in_dim.2 = bf16[8,256,512]{2,1,0:T(8,128)(2,1)} broadcast(bf16[256,512]{1,0:T(8,128)(2,1)} %param.3), dimensions={1,2} | broadcast | bytes 2359296 | tf_op jit(solution)/shard_map/broadcast_in_dim | solution.py:72
  2.5 0.0 copy-start
  2.5 10.4 %all-to-all-start = ((bf16[8,256,512]{2,1,0:T(8,128)(2,1)}), bf16[8,256,512]{2,1,0:T(8,128)(2,1)S(1)}, u32[]{:S(2)}, u32[]{:S(2)}) async-start(bf16[8,256,512]{2,1,0:T(8,128)(2,1)} %broadcast_in_dim.2), calls=%async_computation | async-start | bytes 4194304 | tf_op jit(solution)/shard_map/all_to_all | solution.py:73
  12.9 0.0 copy-done
  12.9 2.2 %all-gather = bf16[512,512]{1,0:T(8,128)(2,1)S(1)} all-gather(bf16[256,512]{1,0:T(8,128)(2,1)S(1)} %copy-done), channel_id=2, replica_groups=mesh['yh'=2,'z'=8,'yl'=4,'core'=2,'x'=4] {'core'}, dimensions={0}, use_global_device_ids=true | all-gather | bytes 786432 | tf_op jit(solution)/shard_map/all_gather | solution.py:74
  15.1 0.7 collective-permute-start
  15.8 3.3 %collective-permute-start.1 = (bf16[2,256,256]{2,1,0:T(8,128)(2,1)S(1)}, bf16[2,256,256]{2,1,0:T(8,128)(2,1)S(1)}, u32[]{:S(2)}, u32[]{:S(2)}) collective-permute-start(bf16[2,256,256]{2,1,0:T(8,128)(2,1)S(1)} %constant_dynamic-slice_fusion), channel_id=1, source_target_pairs={{0,8},{1,10},{2,9},{3,11},{4,13},{5,15},{6,12},{7,14},{8,0},{9,2},... | collective-permute-start | bytes 786440 | tf_op jit(solution)/shard_map/ppermute | solution.py:24
  19.1 8.8 %collective-permute-start.2 = (bf16[2,256,256]{2,1,0:T(8,128)(2,1)S(1)}, bf16[2,256,256]{2,1,0:T(8,128)(2,1)S(1)}, u32[]{:S(2)}, u32[]{:S(2)}) collective-permute-start(bf16[2,256,256]{2,1,0:T(8,128)(2,1)S(1)} %constant_dynamic-slice_fusion), channel_id=1, source_target_pairs={{0,16},{1,18},{2,17},{3,19},{4,21},{5,23},{6,20},{7,22},{8,24},{9,... | collective-permute-start | bytes 786440 | tf_op jit(solution)/shard_map/ppermute | solution.py:24
  27.9 1.9 %collective-permute-start.3 = (bf16[2,256,256]{2,1,0:T(8,128)(2,1)S(1)}, bf16[2,256,256]{2,1,0:T(8,128)(2,1)S(1)}, u32[]{:S(2)}, u32[]{:S(2)}) collective-permute-start(bf16[2,256,256]{2,1,0:T(8,128)(2,1)S(1)} %constant_dynamic-slice_fusion), channel_id=1, source_target_pairs={{0,24},{1,26},{2,25},{3,27},{4,29},{5,31},{6,28},{7,30},{8,16},{9,... | collective-permute-start | bytes 786440 | tf_op jit(solution)/shard_map/ppermute | solution.py:24
  29.9 0.0 collective-permute-done
  29.9 0.0 collective-permute-done.1
  29.9 4.0 %collective-permute-start.4 = (bf16[4,256,256]{2,1,0:T(8,128)(2,1)S(1)}, bf16[4,256,256]{2,1,0:T(8,128)(2,1)}, u32[]{:S(2)}, u32[]{:S(2)}) collective-permute-start(bf16[4,256,256]{2,1,0:T(8,128)(2,1)S(1)} %constant_dynamic-update-slice_fusion.own_a), channel_id=1, source_target_pairs={{0,4},{4,0},{1,5},{5,1},{2,6},{6,2},{3,7},{7,3},{8,12},{12,8},{9,1... | collective-permute-start | bytes 1572872 | tf_op jit(solution)/shard_map/ppermute | solution.py:24
  33.9 10.6 %collective-permute-done.2 = bf16[2,256,256]{2,1,0:T(8,128)(2,1)S(1)} collective-permute-done((bf16[2,256,256]{2,1,0:T(8,128)(2,1)S(1)}, bf16[2,256,256]{2,1,0:T(8,128)(2,1)S(1)}, u32[]{:S(2)}, u32[]{:S(2)}) %collective-permute-start.2) | collective-permute-done | bytes 262176 | tf_op jit(solution)/shard_map/ppermute | solution.py:24
  44.5 2.8 %collective-permute-done.3 = bf16[2,256,256]{2,1,0:T(8,128)(2,1)S(1)} collective-permute-done((bf16[2,256,256]{2,1,0:T(8,128)(2,1)S(1)}, bf16[2,256,256]{2,1,0:T(8,128)(2,1)S(1)}, u32[]{:S(2)}, u32[]{:S(2)}) %collective-permute-start.3) | collective-permute-done | bytes 262176 | tf_op jit(solution)/shard_map/ppermute | solution.py:24
  47.3 16.0 %collective-permute-start.5 = (bf16[4,256,256]{2,1,0:T(8,128)(2,1)S(1)}, bf16[4,256,256]{2,1,0:T(8,128)(2,1)}, u32[]{:S(2)}, u32[]{:S(2)}) collective-permute-start(bf16[4,256,256]{2,1,0:T(8,128)(2,1)S(1)} %constant_dynamic-update-slice_fusion.2.own_b), channel_id=1, source_target_pairs={{0,4},{4,0},{1,5},{5,1},{2,6},{6,2},{3,7},{7,3},{8,12},{12,8},{9,1... | collective-permute-start | bytes 1572872 | tf_op jit(solution)/shard_map/ppermute | solution.py:24
  63.3 0.1 stack.85.place
  63.5 0.0 collective-permute-done.4.other_a
  63.5 1.5 %collective-permute-done.5.other_b = bf16[4,256,256]{2,1,0:T(8,128)(2,1)} collective-permute-done((bf16[4,256,256]{2,1,0:T(8,128)(2,1)S(1)}, bf16[4,256,256]{2,1,0:T(8,128)(2,1)}, u32[]{:S(2)}, u32[]{:S(2)}) %collective-permute-start.5) | collective-permute-done | bytes 524320 | tf_op jit(solution)/shard_map/ppermute | solution.py:24
  64.9 0.0 all-to-all-done.t_ref
  65.0 2.5 %shard_map.28 = f32[4,2,256,128]{3,2,1,0:T(8,128)S(1)} custom-call(s32[40]{0:T(128)S(1)} %stack.85.place, bf16[4,256,256]{2,1,0:T(8,128)(2,1)S(1)} %constant_dynamic-update-slice_fusion.own_a, bf16[4,256,256]{2,1,0:T(8,128)(2,1)S(1)} %constant_dynamic-update-slice_fusion.2.own_b, bf16[4,256,256]{2,1,0:T(8,128)(2,1)} %collective-permute-done.4.other_a, ...), custom_call_target="tpu_custom_call" | custom-call | tf_op jit(solution)/shard_map/pallas_call | solution.py:61
  67.4 18.3 %all_to_all.10 = f32[4,2,256,128]{3,2,1,0:T(8,128)S(1)} all-to-all(f32[4,2,256,128]{3,2,1,0:T(8,128)S(1)} %shard_map.28), channel_id=1, replica_groups=mesh['yh'=2,'z'=8,'yl'=4,'core'=2,'x'=4] {'x'}, dimensions={0} | all-to-all | bytes 2097152 | tf_op jit(solution)/shard_map/all_to_all | solution.py:88
  85.8 0.1 reduce_sum.9
  85.8 1.9 %collective-permute-start.6 = (f32[256,128]{1,0:T(8,128)S(1)}, f32[256,128]{1,0:T(8,128)S(1)}, u32[]{:S(2)}, u32[]{:S(2)}) collective-permute-start(f32[256,128]{1,0:T(8,128)S(1)} %slice_bitcast_fusion), channel_id=1, source_target_pairs={{0,256},{256,0},{1,257},{257,1},{2,258},{258,2},{3,259},{259,3},{4... | collective-permute-start | bytes 393224 | tf_op jit(solution)/shard_map/ppermute | solution.py:24
  87.8 9.7 %collective-permute-done.6 = f32[256,128]{1,0:T(8,128)S(1)} collective-permute-done((f32[256,128]{1,0:T(8,128)S(1)}, f32[256,128]{1,0:T(8,128)S(1)}, u32[]{:S(2)}, u32[]{:S(2)}) %collective-permute-start.6) | collective-permute-done | bytes 131104 | tf_op jit(solution)/shard_map/ppermute | solution.py:24
  97.4 0.7 fusion
  (6 shorter events, 0.1 us)
Async XLA Ops:
  2.5 10.5 %copy-start = (bf16[256,512]{1,0:T(8,128)(2,1)S(1)}, bf16[256,512]{1,0:T(8,128)(2,1)}, u32[]{:S(2)}) copy-start(bf16[256,512]{1,0:T(8,128)(2,1)} %param.2) | copy-start | bytes 786436
  2.5 62.5 %all-to-all-start = ((bf16[8,256,512]{2,1,0:T(8,128)(2,1)}), bf16[8,256,512]{2,1,0:T(8,128)(2,1)S(1)}, u32[]{:S(2)}, u32[]{:S(2)}) async-start(bf16[8,256,512]{2,1,0:T(8,128)(2,1)} %broadcast_in_dim.2), calls=%async_computation | async-start | bytes 4194304 | tf_op jit(solution)/shard_map/all_to_all | solution.py:73
  15.1 14.7 %collective-permute-start = (bf16[2,256,256]{2,1,0:T(8,128)(2,1)S(1)}, bf16[2,256,256]{2,1,0:T(8,128)(2,1)S(1)}, u32[]{:S(2)}, u32[]{:S(2)}) collective-permute-start(bf16[2,256,256]{2,1,0:T(8,128)(2,1)S(1)} %constant_dynamic-slice_fusion), channel_id=1, source_target_pairs={{0,0},{1,2},{2,1},{3,3},{4,5},{5,7},{6,4},{7,6},{8,8},{9,10},{10,9... | collective-permute-start | bytes 786440 | tf_op jit(solution)/shard_map/ppermute | solution.py:24
  15.8 14.1 %collective-permute-start.1 = (bf16[2,256,256]{2,1,0:T(8,128)(2,1)S(1)}, bf16[2,256,256]{2,1,0:T(8,128)(2,1)S(1)}, u32[]{:S(2)}, u32[]{:S(2)}) collective-permute-start(bf16[2,256,256]{2,1,0:T(8,128)(2,1)S(1)} %constant_dynamic-slice_fusion), channel_id=1, source_target_pairs={{0,8},{1,10},{2,9},{3,11},{4,13},{5,15},{6,12},{7,14},{8,0},{9,2},... | collective-permute-start | bytes 786440 | tf_op jit(solution)/shard_map/ppermute | solution.py:24
  19.1 25.4 %collective-permute-start.2 = (bf16[2,256,256]{2,1,0:T(8,128)(2,1)S(1)}, bf16[2,256,256]{2,1,0:T(8,128)(2,1)S(1)}, u32[]{:S(2)}, u32[]{:S(2)}) collective-permute-start(bf16[2,256,256]{2,1,0:T(8,128)(2,1)S(1)} %constant_dynamic-slice_fusion), channel_id=1, source_target_pairs={{0,16},{1,18},{2,17},{3,19},{4,21},{5,23},{6,20},{7,22},{8,24},{9,... | collective-permute-start | bytes 786440 | tf_op jit(solution)/shard_map/ppermute | solution.py:24
  27.9 19.4 %collective-permute-start.3 = (bf16[2,256,256]{2,1,0:T(8,128)(2,1)S(1)}, bf16[2,256,256]{2,1,0:T(8,128)(2,1)S(1)}, u32[]{:S(2)}, u32[]{:S(2)}) collective-permute-start(bf16[2,256,256]{2,1,0:T(8,128)(2,1)S(1)} %constant_dynamic-slice_fusion), channel_id=1, source_target_pairs={{0,24},{1,26},{2,25},{3,27},{4,29},{5,31},{6,28},{7,30},{8,16},{9,... | collective-permute-start | bytes 786440 | tf_op jit(solution)/shard_map/ppermute | solution.py:24
  29.9 33.5 %collective-permute-start.4 = (bf16[4,256,256]{2,1,0:T(8,128)(2,1)S(1)}, bf16[4,256,256]{2,1,0:T(8,128)(2,1)}, u32[]{:S(2)}, u32[]{:S(2)}) collective-permute-start(bf16[4,256,256]{2,1,0:T(8,128)(2,1)S(1)} %constant_dynamic-update-slice_fusion.own_a), channel_id=1, source_target_pairs={{0,4},{4,0},{1,5},{5,1},{2,6},{6,2},{3,7},{7,3},{8,12},{12,8},{9,1... | collective-permute-start | bytes 1572872 | tf_op jit(solution)/shard_map/ppermute | solution.py:24
  47.3 17.6 %collective-permute-start.5 = (bf16[4,256,256]{2,1,0:T(8,128)(2,1)S(1)}, bf16[4,256,256]{2,1,0:T(8,128)(2,1)}, u32[]{:S(2)}, u32[]{:S(2)}) collective-permute-start(bf16[4,256,256]{2,1,0:T(8,128)(2,1)S(1)} %constant_dynamic-update-slice_fusion.2.own_b), channel_id=1, source_target_pairs={{0,4},{4,0},{1,5},{5,1},{2,6},{6,2},{3,7},{7,3},{8,12},{12,8},{9,1... | collective-permute-start | bytes 1572872 | tf_op jit(solution)/shard_map/ppermute | solution.py:24
  85.8 11.6 %collective-permute-start.6 = (f32[256,128]{1,0:T(8,128)S(1)}, f32[256,128]{1,0:T(8,128)S(1)}, u32[]{:S(2)}, u32[]{:S(2)}) collective-permute-start(f32[256,128]{1,0:T(8,128)S(1)} %slice_bitcast_fusion), channel_id=1, source_target_pairs={{0,256},{256,0},{1,257},{257,1},{2,258},{258,2},{3,259},{259,3},{4... | collective-permute-start | bytes 393224 | tf_op jit(solution)/shard_map/ppermute | solution.py:24

commit v9 on v8

v9 whole, which is shorter than its diff:
```python
import functools

import jax
import jax.numpy as jnp
import numpy as np
from jax import lax
from jax.experimental import pallas as pl
from jax.experimental.pallas import tpu as pltpu
from jax.sharding import Mesh, PartitionSpec as P

AXES = ("yh", "z", "yl", "core", "x")
SHAPE = (2, 8, 4, 2, 4)
SIZES = dict(zip(AXES, SHAPE))
UNIT = 256


def moved(value, axes, where):
    shape = [SIZES[a] for a in axes]
    perm = []
    for i in range(int(np.prod(shape))):
        place = dict(zip(axes, (int(v) for v in np.unravel_index(i, shape))))
        there = where(**place)
        perm.append((i, int(np.ravel_multi_index([there[a] for a in axes], shape))))
    return lax.ppermute(value, axes, perm)


def spread(value, mask):
    def where(yh, yl, core, x):
        half = (x >> 1) ^ core ^ (mask & 1)
        return {"yh": yl >> 1, "yl": (2 * yh + (yl & 1)) ^ mask, "core": core, "x": 2 * (x & 1) + half}

    return moved(value, ("yh", "yl", "core", "x"), where)


def core_swap(value):
    return moved(value, ("core",), lambda core: {"core": 1 - core})


def product_kernel(place, own_a, own_b, other_a, other_b, t_ref, out_ref):
    for unit in range(8):
        t = t_ref[unit]
        for m in range(2):
            same, first, slot = (place[3 * (2 * unit + m) + i] for i in range(3))
            w = jnp.where(
                same == 1,
                jnp.where(first == 1, own_a[slot], own_b[slot]),
                jnp.where(first == 1, other_a[slot], other_b[slot]),
            )
            part = jnp.dot(w, t, preferred_element_type=jnp.float32)
            for block in range(4):
                cols = part[:, block * 128 : (block + 1) * 128]
                if unit == 0:
                    out_ref[4 * m + block] = cols
                else:
                    out_ref[4 * m + block] += cols


def product(place, *operands):
    vmem = pl.BlockSpec(memory_space=pltpu.VMEM)
    return pl.pallas_call(
        product_kernel,
        out_shape=jax.ShapeDtypeStruct((8, UNIT, 128), jnp.float32),
        in_specs=[pl.BlockSpec(memory_space=pltpu.SMEM)] + [vmem] * len(operands),
        out_specs=vmem,
        compiler_params=pltpu.CompilerParams(vmem_limit_bytes=40 * 1024 * 1024),
    )(place, *operands)


def per_device(integrals, amplitudes):
    yl, core, x = (lax.axis_index(a) for a in ("yl", "core", "x"))
    copies = jnp.broadcast_to(amplitudes[None], (8,) + amplitudes.shape)
    tiles = lax.all_to_all(copies, "z", split_axis=0, concat_axis=0, tiled=True)
    both = lax.all_gather(integrals, "core", axis=0)
    halves = [lax.dynamic_slice_in_dim(both, ((x >> 1) ^ core ^ i) * UNIT, UNIT, 2) for i in (0, 1)]
    own_a = jnp.concatenate([spread(halves[mask & 1], mask) for mask in (0, 1)])
    own_b = jnp.concatenate([spread(halves[mask & 1], mask) for mask in (2, 3)])
    other_a, other_b = core_swap(own_a), core_swap(own_b)
    place = []
    for unit in range(8):
        u4, u3, u2 = unit >> 2, (unit >> 1) & 1, unit & 1
        for m in (0, 1):
            mask = yl ^ (2 * m + u4)
            place.append(jnp.where(u2 ^ (x & 1) == core ^ (mask & 1), 1, 0))
            place += [jnp.where(mask < 2, 1, 0), (mask & 1) * 2 + u3]
    place = jnp.stack(place).astype(jnp.int32)
    part = product(place, own_a, own_b, other_a, other_b, tiles)
    return lax.all_to_all(part, ("yh", "x"), split_axis=0, concat_axis=0, tiled=True).sum(axis=0)


def solution(mesh):
    return jax.shard_map(
        per_device,
        mesh=Mesh(mesh.devices.reshape(SHAPE), AXES),
        in_specs=(P(("yh", "z"), ("yl", "core", "x")), P(("yh", "z", "x"), ("yl", "core"))),
        out_specs=P(("yh", "z"), ("yl", "core", "x")),
        check_vma=False,
    )
```

time: 98.5 us -> 104 us (1.056)
  the two profiles are of different devices: /device:TPU:56 before, /device:TPU:16 now
where the time goes in v9:
time: 104 us
  blocking collectives  38.7 us (37%)
  starting transfers between devices  34 us (33%)
  waiting for transfers between devices  25.1 us (24%)
  local copies, waits for them, and re-layouts  2.72 us (3%)
  Pallas kernels  2.45 us (2%)
    all_to_all x1, blocking collectives, per_device(): lax.all_to_all(part, ('yh', 'x'), split_axis=0, concat_axis=0, tiled=True)  36.5 us
    ppermute x6, starting transfers between devices, moved(): return lax.ppermute(value, axes, perm)  23.6 us
    ppermute x6, waiting for transfers between devices, moved(): return lax.ppermute(value, axes, perm)  21.4 us
    all_to_all x1, starting transfers between devices, per_device(): tiles = lax.all_to_all(copies, 'z', split_axis=0, concat_axis=0, tiled=True)  10.4 us
    all_to_all x1, waiting for transfers between devices, per_device(): tiles = lax.all_to_all(copies, 'z', split_axis=0, concat_axis=0, tiled=True)  3.62 us
    broadcast_in_dim x1, local copies, waits for them, and re-layouts, per_device(): copies = jnp.broadcast_to(amplitudes[None], (8,) + amplitudes.shape)  2.48 us
    pallas_call x1, Pallas kernels, product(): pl.pallas_call(product_kernel, out_shape=jax.ShapeDtypeStruct((8, UNIT, 1...  2.45 us
    all_gather x1, blocking collectives, per_device(): both = lax.all_gather(integrals, 'core', axis=0)  2.18 us
  transfers between devices with their start and end apart: 7, of which 5 were waited for; matrix products, arithmetic and copies ran while one was open for 0% of the time, Pallas kernels for 0%

profile of v9, /device:TPU:16, one launch (start us, length us, event | category | flops | bytes accessed | tf_op | source)
XLA Modules:
  0.0 103.8 jit_solution(13306778629257671411)
XLA Ops:
  0.0 2.5 %broadcast_in_dim.2 = bf16[8,256,512]{2,1,0:T(8,128)(2,1)} broadcast(bf16[256,512]{1,0:T(8,128)(2,1)} %param.3), dimensions={1,2} | broadcast | bytes 2359296 | tf_op jit(solution)/shard_map/broadcast_in_dim | solution.py:71
  2.5 0.0 copy-start
  2.5 10.4 %all-to-all-start = ((bf16[8,256,512]{2,1,0:T(8,128)(2,1)}), bf16[8,256,512]{2,1,0:T(8,128)(2,1)S(1)}, u32[]{:S(2)}, u32[]{:S(2)}) async-start(bf16[8,256,512]{2,1,0:T(8,128)(2,1)} %broadcast_in_dim.2), calls=%async_computation | async-start | bytes 4194304 | tf_op jit(solution)/shard_map/all_to_all | solution.py:72
  12.9 0.0 copy-done
  12.9 2.2 %all-gather = bf16[512,512]{1,0:T(8,128)(2,1)S(1)} all-gather(bf16[256,512]{1,0:T(8,128)(2,1)S(1)} %copy-done), channel_id=2, replica_groups=mesh['yh'=2,'z'=8,'yl'=4,'core'=2,'x'=4] {'core'}, dimensions={0}, use_global_device_ids=true | all-gather | bytes 786432 | tf_op jit(solution)/shard_map/all_gather | solution.py:73
  15.2 5.7 %collective-permute-start = (bf16[2,256,256]{2,1,0:T(8,128)(2,1)S(1)}, bf16[2,256,256]{2,1,0:T(8,128)(2,1)S(1)}, u32[]{:S(2)}, u32[]{:S(2)}) collective-permute-start(bf16[2,256,256]{2,1,0:T(8,128)(2,1)S(1)} %get-tuple-element.6), channel_id=1, source_target_pairs={{0,0},{1,2},{2,1},{3,3},{4,5},{5,7},{6,4},{7,6},{8,8},{9,10},{10,9... | collective-permute-start | bytes 786440 | tf_op jit(solution)/shard_map/ppermute | solution.py:24
  20.9 5.1 %collective-permute-start.1 = (bf16[2,256,256]{2,1,0:T(8,128)(2,1)S(1)}, bf16[2,256,256]{2,1,0:T(8,128)(2,1)S(1)}, u32[]{:S(2)}, u32[]{:S(2)}) collective-permute-start(bf16[2,256,256]{2,1,0:T(8,128)(2,1)S(1)} %get-tuple-element.5), channel_id=1, source_target_pairs={{0,9},{1,11},{2,8},{3,10},{4,12},{5,14},{6,13},{7,15},{8,1},{9,3},... | collective-permute-start | bytes 786440 | tf_op jit(solution)/shard_map/ppermute | solution.py:24
  26.0 2.0 %collective-permute-start.2 = (bf16[2,256,256]{2,1,0:T(8,128)(2,1)S(1)}, bf16[2,256,256]{2,1,0:T(8,128)(2,1)S(1)}, u32[]{:S(2)}, u32[]{:S(2)}) collective-permute-start(bf16[2,256,256]{2,1,0:T(8,128)(2,1)S(1)} %get-tuple-element.6), channel_id=1, source_target_pairs={{0,16},{1,18},{2,17},{3,19},{4,21},{5,23},{6,20},{7,22},{8,24},{9,... | collective-permute-start | bytes 786440 | tf_op jit(solution)/shard_map/ppermute | solution.py:24
  28.0 6.9 %collective-permute-start.3 = (bf16[2,256,256]{2,1,0:T(8,128)(2,1)S(1)}, bf16[2,256,256]{2,1,0:T(8,128)(2,1)S(1)}, u32[]{:S(2)}, u32[]{:S(2)}) collective-permute-start(bf16[2,256,256]{2,1,0:T(8,128)(2,1)S(1)} %get-tuple-element.5), channel_id=1, source_target_pairs={{0,25},{1,27},{2,24},{3,26},{4,28},{5,30},{6,29},{7,31},{8,17},{9,... | collective-permute-start | bytes 786440 | tf_op jit(solution)/shard_map/ppermute | solution.py:24
  34.9 7.7 %collective-permute-done = bf16[2,256,256]{2,1,0:T(8,128)(2,1)S(1)} collective-permute-done((bf16[2,256,256]{2,1,0:T(8,128)(2,1)S(1)}, bf16[2,256,256]{2,1,0:T(8,128)(2,1)S(1)}, u32[]{:S(2)}, u32[]{:S(2)}) %collective-permute-start) | collective-permute-done | bytes 262176 | tf_op jit(solution)/shard_map/ppermute | solution.py:24
  42.6 0.0 collective-permute-done.1
  42.7 1.9 %collective-permute-start.4 = (bf16[4,256,256]{2,1,0:T(8,128)(2,1)S(1)}, bf16[4,256,256]{2,1,0:T(8,128)(2,1)}, u32[]{:S(2)}, u32[]{:S(2)}) collective-permute-start(bf16[4,256,256]{2,1,0:T(8,128)(2,1)S(1)} %constant_dynamic-update-slice_fusion.own_a), channel_id=1, source_target_pairs={{0,4},{4,0},{1,5},{5,1},{2,6},{6,2},{3,7},{7,3},{8,12},{12,8},{9,1... | collective-permute-start | bytes 1572872 | tf_op jit(solution)/shard_map/ppermute | solution.py:24
  44.6 5.5 %collective-permute-done.2 = bf16[2,256,256]{2,1,0:T(8,128)(2,1)S(1)} collective-permute-done((bf16[2,256,256]{2,1,0:T(8,128)(2,1)S(1)}, bf16[2,256,256]{2,1,0:T(8,128)(2,1)S(1)}, u32[]{:S(2)}, u32[]{:S(2)}) %collective-permute-start.2) | collective-permute-done | bytes 262176 | tf_op jit(solution)/shard_map/ppermute | solution.py:24
  50.1 6.4 %collective-permute-done.3 = bf16[2,256,256]{2,1,0:T(8,128)(2,1)S(1)} collective-permute-done((bf16[2,256,256]{2,1,0:T(8,128)(2,1)S(1)}, bf16[2,256,256]{2,1,0:T(8,128)(2,1)S(1)}, u32[]{:S(2)}, u32[]{:S(2)}) %collective-permute-start.3) | collective-permute-done | bytes 262176 | tf_op jit(solution)/shard_map/ppermute | solution.py:24
  56.6 1.9 %collective-permute-start.5 = (bf16[4,256,256]{2,1,0:T(8,128)(2,1)S(1)}, bf16[4,256,256]{2,1,0:T(8,128)(2,1)}, u32[]{:S(2)}, u32[]{:S(2)}) collective-permute-start(bf16[4,256,256]{2,1,0:T(8,128)(2,1)S(1)} %constant_dynamic-update-slice_fusion.2.own_b), channel_id=1, source_target_pairs={{0,4},{4,0},{1,5},{5,1},{2,6},{6,2},{3,7},{7,3},{8,12},{12,8},{9,1... | collective-permute-start | bytes 1572872 | tf_op jit(solution)/shard_map/ppermute | solution.py:24
  58.6 0.1 stack.111.place
  58.7 0.0 collective-permute-done.4.other_a
  58.7 1.8 %collective-permute-done.5.other_b = bf16[4,256,256]{2,1,0:T(8,128)(2,1)} collective-permute-done((bf16[4,256,256]{2,1,0:T(8,128)(2,1)S(1)}, bf16[4,256,256]{2,1,0:T(8,128)(2,1)}, u32[]{:S(2)}, u32[]{:S(2)}) %collective-permute-start.5) | collective-permute-done | bytes 524320 | tf_op jit(solution)/shard_map/ppermute | solution.py:24
  60.5 3.6 %all-to-all-done.t_ref = bf16[8,256,512]{2,1,0:T(8,128)(2,1)S(1)} async-done(((bf16[8,256,512]{2,1,0:T(8,128)(2,1)}), bf16[8,256,512]{2,1,0:T(8,128)(2,1)S(1)}, u32[]{:S(2)}, u32[]{:S(2)}) %all-to-all-start) | async-done | bytes 2097184 | tf_op jit(solution)/shard_map/all_to_all | solution.py:72
  64.1 2.5 %shard_map.28 = f32[8,256,128]{2,1,0:T(8,128)S(1)} custom-call(s32[48]{0:T(128)S(1)} %stack.111.place, bf16[4,256,256]{2,1,0:T(8,128)(2,1)S(1)} %constant_dynamic-update-slice_fusion.own_a, bf16[4,256,256]{2,1,0:T(8,128)(2,1)S(1)} %constant_dynamic-update-slice_fusion.2.own_b, bf16[4,256,256]{2,1,0:T(8,128)(2,1)} %collective-permute-done.4.other_a, ...), custom_call_target="tpu_custom_call" | custom-call | tf_op jit(solution)/shard_map/pallas_call | solution.py:60
  66.6 36.5 %all_to_all.10 = f32[8,256,128]{2,1,0:T(8,128)S(1)} all-to-all(f32[8,256,128]{2,1,0:T(8,128)S(1)} %shard_map.28), channel_id=1, replica_groups=mesh['yh'=2,'z'=8,'yl'=4,'core'=2,'x'=4] {'yh','x'}, dimensions={0} | all-to-all | bytes 2097152 | tf_op jit(solution)/shard_map/all_to_all | solution.py:87
  103.1 0.7 reduce_sum.9
  (5 shorter events, 0.1 us)
Async XLA Ops:
  2.5 10.5 %copy-start = (bf16[256,512]{1,0:T(8,128)(2,1)S(1)}, bf16[256,512]{1,0:T(8,128)(2,1)}, u32[]{:S(2)}) copy-start(bf16[256,512]{1,0:T(8,128)(2,1)} %param.2) | copy-start | bytes 786436
  2.5 61.6 %all-to-all-start = ((bf16[8,256,512]{2,1,0:T(8,128)(2,1)}), bf16[8,256,512]{2,1,0:T(8,128)(2,1)S(1)}, u32[]{:S(2)}, u32[]{:S(2)}) async-start(bf16[8,256,512]{2,1,0:T(8,128)(2,1)} %broadcast_in_dim.2), calls=%async_computation | async-start | bytes 4194304 | tf_op jit(solution)/shard_map/all_to_all | solution.py:72
  15.2 27.5 %collective-permute-start = (bf16[2,256,256]{2,1,0:T(8,128)(2,1)S(1)}, bf16[2,256,256]{2,1,0:T(8,128)(2,1)S(1)}, u32[]{:S(2)}, u32[]{:S(2)}) collective-permute-start(bf16[2,256,256]{2,1,0:T(8,128)(2,1)S(1)} %get-tuple-element.6), channel_id=1, source_target_pairs={{0,0},{1,2},{2,1},{3,3},{4,5},{5,7},{6,4},{7,6},{8,8},{9,10},{10,9... | collective-permute-start | bytes 786440 | tf_op jit(solution)/shard_map/ppermute | solution.py:24
  20.9 21.8 %collective-permute-start.1 = (bf16[2,256,256]{2,1,0:T(8,128)(2,1)S(1)}, bf16[2,256,256]{2,1,0:T(8,128)(2,1)S(1)}, u32[]{:S(2)}, u32[]{:S(2)}) collective-permute-start(bf16[2,256,256]{2,1,0:T(8,128)(2,1)S(1)} %get-tuple-element.5), channel_id=1, source_target_pairs={{0,9},{1,11},{2,8},{3,10},{4,12},{5,14},{6,13},{7,15},{8,1},{9,3},... | collective-permute-start | bytes 786440 | tf_op jit(solution)/shard_map/ppermute | solution.py:24
  26.0 24.1 %collective-permute-start.2 = (bf16[2,256,256]{2,1,0:T(8,128)(2,1)S(1)}, bf16[2,256,256]{2,1,0:T(8,128)(2,1)S(1)}, u32[]{:S(2)}, u32[]{:S(2)}) collective-permute-start(bf16[2,256,256]{2,1,0:T(8,128)(2,1)S(1)} %get-tuple-element.6), channel_id=1, source_target_pairs={{0,16},{1,18},{2,17},{3,19},{4,21},{5,23},{6,20},{7,22},{8,24},{9,... | collective-permute-start | bytes 786440 | tf_op jit(solution)/shard_map/ppermute | solution.py:24
  28.0 28.5 %collective-permute-start.3 = (bf16[2,256,256]{2,1,0:T(8,128)(2,1)S(1)}, bf16[2,256,256]{2,1,0:T(8,128)(2,1)S(1)}, u32[]{:S(2)}, u32[]{:S(2)}) collective-permute-start(bf16[2,256,256]{2,1,0:T(8,128)(2,1)S(1)} %get-tuple-element.5), channel_id=1, source_target_pairs={{0,25},{1,27},{2,24},{3,26},{4,28},{5,30},{6,29},{7,31},{8,17},{9,... | collective-permute-start | bytes 786440 | tf_op jit(solution)/shard_map/ppermute | solution.py:24
  42.7 16.0 %collective-permute-start.4 = (bf16[4,256,256]{2,1,0:T(8,128)(2,1)S(1)}, bf16[4,256,256]{2,1,0:T(8,128)(2,1)}, u32[]{:S(2)}, u32[]{:S(2)}) collective-permute-start(bf16[4,256,256]{2,1,0:T(8,128)(2,1)S(1)} %constant_dynamic-update-slice_fusion.own_a), channel_id=1, source_target_pairs={{0,4},{4,0},{1,5},{5,1},{2,6},{6,2},{3,7},{7,3},{8,12},{12,8},{9,1... | collective-permute-start | bytes 1572872 | tf_op jit(solution)/shard_map/ppermute | solution.py:24
  56.6 3.9 %collective-permute-start.5 = (bf16[4,256,256]{2,1,0:T(8,128)(2,1)S(1)}, bf16[4,256,256]{2,1,0:T(8,128)(2,1)}, u32[]{:S(2)}, u32[]{:S(2)}) collective-permute-start(bf16[4,256,256]{2,1,0:T(8,128)(2,1)S(1)} %constant_dynamic-update-slice_fusion.2.own_b), channel_id=1, source_target_pairs={{0,4},{4,0},{1,5},{5,1},{2,6},{6,2},{3,7},{7,3},{8,12},{12,8},{9,1... | collective-permute-start | bytes 1572872 | tf_op jit(solution)/shard_map/ppermute | solution.py:24

commit v10 on v8

--- a/solution.py
+++ b/solution.py
@@ -73,8 +73,10 @@
     tiles = lax.all_to_all(copies, "z", split_axis=0, concat_axis=0, tiled=True)
     both = lax.all_gather(integrals, "core", axis=0)
     half = lax.dynamic_slice_in_dim(both, ((x >> 1) ^ core) * UNIT, UNIT, 2)
-    own_a = jnp.concatenate([spread(half, mask) for mask in (0, 1)])
-    own_b = jnp.concatenate([spread(half, mask) for mask in (2, 3)])
+    slabs = {mask: spread(half, mask) for mask in (0, 3, 1)}
+    slabs[2] = moved(slabs[0], ("yl",), lambda yl: {"yl": yl ^ 2})
+    own_a = jnp.concatenate([slabs[0], slabs[3]])
+    own_b = jnp.concatenate([slabs[2], slabs[1]])
     other_a, other_b = core_swap(own_a), core_swap(own_b)
     place = []
     for unit in range(8):
@@ -82,7 +84,7 @@
         place.append(jnp.where(u2 ^ (x & 1) == core, 1, 0))
         for rel in (0, 1):
             mask = yl ^ (2 * (yh ^ rel) + u4)
-            place += [jnp.where(mask < 2, 1, 0), (mask & 1) * 2 + u3]
+            place += [jnp.where(mask >> 1 == mask & 1, 1, 0), (mask & 1) * 2 + u3]
     place = jnp.stack(place).astype(jnp.int32)
     part = product(place, own_a, own_b, other_a, other_b, tiles)
     part = lax.all_to_all(part, "x", split_axis=0, concat_axis=0, tiled=True).sum(axis=0)

time: 98.5 us -> 96.2 us (0.977)
  blocking collectives: 20.5 us -> 18.3 us
    all_to_all x1, waiting for transfers between devices: 0.01 us -> 6.31 us  [per_device(): tiles = lax.all_to_all(copies, 'z', split_axis=0, concat_axis=0, tiled=True)]
    ppermute x7, waiting for transfers between devices: 24.5 us -> 18.4 us  [moved(): return lax.ppermute(value, axes, perm)]
    all_to_all x1, blocking collectives: 18.3 us -> 16.1 us  [per_device(): lax.all_to_all(part, 'x', split_axis=0, concat_axis=0, tiled=True)]
  transfers between devices with their start and end apart: 8 -> 8, of which waited for: 4 -> 5; matrix products, arithmetic and copies ran while one was open for 0% -> 0% of each run, Pallas kernels for 0% -> 0%
where the time goes in v10:
time: 96.2 us; the launch traced here: 95.7 us
  starting transfers between devices  46.6 us (48%)
  waiting for transfers between devices  24.7 us (26%)
  blocking collectives  18.3 us (19%)
  local copies, waits for them, and re-layouts  2.7 us (3%)
  Pallas kernels  2.46 us (3%)
    ppermute x7, starting transfers between devices, moved(): return lax.ppermute(value, axes, perm)  36.1 us
    ppermute x7, waiting for transfers between devices, moved(): return lax.ppermute(value, axes, perm)  18.4 us
    all_to_all x1, blocking collectives, per_device(): lax.all_to_all(part, 'x', split_axis=0, concat_axis=0, tiled=True)  16.1 us
    all_to_all x1, starting transfers between devices, per_device(): tiles = lax.all_to_all(copies, 'z', split_axis=0, concat_axis=0, tiled=True)  10.4 us
    all_to_all x1, waiting for transfers between devices, per_device(): tiles = lax.all_to_all(copies, 'z', split_axis=0, concat_axis=0, tiled=True)  6.31 us
    broadcast_in_dim x1, local copies, waits for them, and re-layouts, per_device(): copies = jnp.broadcast_to(amplitudes[None], (8,) + amplitudes.shape)  2.48 us
    pallas_call x1, Pallas kernels, product(): pl.pallas_call(product_kernel, out_shape=jax.ShapeDtypeStruct((4, 2, UNIT...  2.46 us
    all_gather x1, blocking collectives, per_device(): both = lax.all_gather(integrals, 'core', axis=0)  2.18 us
  transfers between devices with their start and end apart: 8, of which 5 were waited for; matrix products, arithmetic and copies ran while one was open for 0% of the time, Pallas kernels for 0%

profile of v10, /device:TPU:56, one launch (start us, length us, event | category | flops | bytes accessed | tf_op | source)
XLA Modules:
  0.0 95.7 jit_solution(1562127724829598311)
XLA Ops:
  0.0 2.5 %broadcast_in_dim.2 = bf16[8,256,512]{2,1,0:T(8,128)(2,1)} broadcast(bf16[256,512]{1,0:T(8,128)(2,1)} %param.3), dimensions={1,2} | broadcast | bytes 2359296 | tf_op jit(solution)/shard_map/broadcast_in_dim | solution.py:72
  2.5 0.0 copy-start
  2.5 10.4 %all-to-all-start = ((bf16[8,256,512]{2,1,0:T(8,128)(2,1)}), bf16[8,256,512]{2,1,0:T(8,128)(2,1)S(1)}, u32[]{:S(2)}, u32[]{:S(2)}) async-start(bf16[8,256,512]{2,1,0:T(8,128)(2,1)} %broadcast_in_dim.2), calls=%async_computation | async-start | bytes 4194304 | tf_op jit(solution)/shard_map/all_to_all | solution.py:73
  12.9 0.0 copy-done
  12.9 2.2 %all-gather = bf16[512,512]{1,0:T(8,128)(2,1)S(1)} all-gather(bf16[256,512]{1,0:T(8,128)(2,1)S(1)} %copy-done), channel_id=2, replica_groups=mesh['yh'=2,'z'=8,'yl'=4,'core'=2,'x'=4] {'core'}, dimensions={0}, use_global_device_ids=true | all-gather | bytes 786432 | tf_op jit(solution)/shard_map/all_gather | solution.py:74
  15.1 0.7 collective-permute-start
  15.8 6.4 %collective-permute-start.1 = (bf16[2,256,256]{2,1,0:T(8,128)(2,1)S(1)}, bf16[2,256,256]{2,1,0:T(8,128)(2,1)S(1)}, u32[]{:S(2)}, u32[]{:S(2)}) collective-permute-start(bf16[2,256,256]{2,1,0:T(8,128)(2,1)S(1)} %constant_dynamic-slice_fusion), channel_id=1, source_target_pairs={{0,24},{1,26},{2,25},{3,27},{4,29},{5,31},{6,28},{7,30},{8,16},{9,... | collective-permute-start | bytes 786440 | tf_op jit(solution)/shard_map/ppermute | solution.py:24
  22.2 0.0 collective-permute-done
  22.2 14.5 %collective-permute-start.2 = (bf16[2,256,256]{2,1,0:T(8,128)(2,1)S(1)}, bf16[2,256,256]{2,1,0:T(8,128)(2,1)S(1)}, u32[]{:S(2)}, u32[]{:S(2)}) collective-permute-start(bf16[2,256,256]{2,1,0:T(8,128)(2,1)S(1)} %collective-permute-done), channel_id=1, source_target_pairs={{0,16},{8,24},{16,0},{24,8},{1,17},{9,25},{17,1},{25,9},{2,18},{10... | collective-permute-start | bytes 786440 | tf_op jit(solution)/shard_map/ppermute | solution.py:24
  36.7 4.6 %collective-permute-start.3 = (bf16[2,256,256]{2,1,0:T(8,128)(2,1)S(1)}, bf16[2,256,256]{2,1,0:T(8,128)(2,1)S(1)}, u32[]{:S(2)}, u32[]{:S(2)}) collective-permute-start(bf16[2,256,256]{2,1,0:T(8,128)(2,1)S(1)} %constant_dynamic-slice_fusion), channel_id=1, source_target_pairs={{0,8},{1,10},{2,9},{3,11},{4,13},{5,15},{6,12},{7,14},{8,0},{9,2},... | collective-permute-start | bytes 786440 | tf_op jit(solution)/shard_map/ppermute | solution.py:24
  41.3 0.0 collective-permute-done.1
  41.4 2.4 %collective-permute-start.4 = (bf16[4,256,256]{2,1,0:T(8,128)(2,1)S(1)}, bf16[4,256,256]{2,1,0:T(8,128)(2,1)}, u32[]{:S(2)}, u32[]{:S(2)}) collective-permute-start(bf16[4,256,256]{2,1,0:T(8,128)(2,1)S(1)} %constant_dynamic-update-slice_fusion.own_a), channel_id=1, source_target_pairs={{0,4},{4,0},{1,5},{5,1},{2,6},{6,2},{3,7},{7,3},{8,12},{12,8},{9,1... | collective-permute-start | bytes 1572872 | tf_op jit(solution)/shard_map/ppermute | solution.py:24
  43.8 7.5 %collective-permute-done.2 = bf16[2,256,256]{2,1,0:T(8,128)(2,1)S(1)} collective-permute-done((bf16[2,256,256]{2,1,0:T(8,128)(2,1)S(1)}, bf16[2,256,256]{2,1,0:T(8,128)(2,1)S(1)}, u32[]{:S(2)}, u32[]{:S(2)}) %collective-permute-start.2) | collective-permute-done | bytes 262176 | tf_op jit(solution)/shard_map/ppermute | solution.py:24
  51.3 2.0 %collective-permute-done.3 = bf16[2,256,256]{2,1,0:T(8,128)(2,1)S(1)} collective-permute-done((bf16[2,256,256]{2,1,0:T(8,128)(2,1)S(1)}, bf16[2,256,256]{2,1,0:T(8,128)(2,1)S(1)}, u32[]{:S(2)}, u32[]{:S(2)}) %collective-permute-start.3) | collective-permute-done | bytes 262176 | tf_op jit(solution)/shard_map/ppermute | solution.py:24
  53.3 2.9 %collective-permute-start.5 = (bf16[4,256,256]{2,1,0:T(8,128)(2,1)S(1)}, bf16[4,256,256]{2,1,0:T(8,128)(2,1)}, u32[]{:S(2)}, u32[]{:S(2)}) collective-permute-start(bf16[4,256,256]{2,1,0:T(8,128)(2,1)S(1)} %constant_dynamic-update-slice_fusion.2.own_b), channel_id=1, source_target_pairs={{0,4},{4,0},{1,5},{5,1},{2,6},{6,2},{3,7},{7,3},{8,12},{12,8},{9,1... | collective-permute-start | bytes 1572872 | tf_op jit(solution)/shard_map/ppermute | solution.py:24
  56.2 0.1 stack.85.place
  56.3 0.0 collective-permute-done.4.other_a
  56.4 1.5 %collective-permute-done.5.other_b = bf16[4,256,256]{2,1,0:T(8,128)(2,1)} collective-permute-done((bf16[4,256,256]{2,1,0:T(8,128)(2,1)S(1)}, bf16[4,256,256]{2,1,0:T(8,128)(2,1)}, u32[]{:S(2)}, u32[]{:S(2)}) %collective-permute-start.5) | collective-permute-done | bytes 524320 | tf_op jit(solution)/shard_map/ppermute | solution.py:24
  57.8 6.3 %all-to-all-done.t_ref = bf16[8,256,512]{2,1,0:T(8,128)(2,1)S(1)} async-done(((bf16[8,256,512]{2,1,0:T(8,128)(2,1)}), bf16[8,256,512]{2,1,0:T(8,128)(2,1)S(1)}, u32[]{:S(2)}, u32[]{:S(2)}) %all-to-all-start) | async-done | bytes 2097184 | tf_op jit(solution)/shard_map/all_to_all | solution.py:73
  64.1 2.5 %shard_map.28 = f32[4,2,256,128]{3,2,1,0:T(8,128)S(1)} custom-call(s32[40]{0:T(128)S(1)} %stack.85.place, bf16[4,256,256]{2,1,0:T(8,128)(2,1)S(1)} %constant_dynamic-update-slice_fusion.own_a, bf16[4,256,256]{2,1,0:T(8,128)(2,1)S(1)} %constant_dynamic-update-slice_fusion.2.own_b, bf16[4,256,256]{2,1,0:T(8,128)(2,1)} %collective-permute-done.4.other_a, ...), custom_call_target="tpu_custom_call" | custom-call | tf_op jit(solution)/shard_map/pallas_call | solution.py:61
  66.6 16.1 %all_to_all.10 = f32[4,2,256,128]{3,2,1,0:T(8,128)S(1)} all-to-all(f32[4,2,256,128]{3,2,1,0:T(8,128)S(1)} %shard_map.28), channel_id=1, replica_groups=mesh['yh'=2,'z'=8,'yl'=4,'core'=2,'x'=4] {'x'}, dimensions={0} | all-to-all | bytes 2097152 | tf_op jit(solution)/shard_map/all_to_all | solution.py:90
  82.7 0.1 reduce_sum.9
  82.8 4.7 %collective-permute-start.6 = (f32[256,128]{1,0:T(8,128)S(1)}, f32[256,128]{1,0:T(8,128)S(1)}, u32[]{:S(2)}, u32[]{:S(2)}) collective-permute-start(f32[256,128]{1,0:T(8,128)S(1)} %slice_bitcast_fusion), channel_id=1, source_target_pairs={{0,256},{256,0},{1,257},{257,1},{2,258},{258,2},{3,259},{259,3},{4... | collective-permute-start | bytes 393224 | tf_op jit(solution)/shard_map/ppermute | solution.py:24
  87.5 7.5 %collective-permute-done.6 = f32[256,128]{1,0:T(8,128)S(1)} collective-permute-done((f32[256,128]{1,0:T(8,128)S(1)}, f32[256,128]{1,0:T(8,128)S(1)}, u32[]{:S(2)}, u32[]{:S(2)}) %collective-permute-start.6) | collective-permute-done | bytes 131104 | tf_op jit(solution)/shard_map/ppermute | solution.py:24
  95.0 0.7 fusion
  (6 shorter events, 0.1 us)
Async XLA Ops:
  2.5 10.5 %copy-start = (bf16[256,512]{1,0:T(8,128)(2,1)S(1)}, bf16[256,512]{1,0:T(8,128)(2,1)}, u32[]{:S(2)}) copy-start(bf16[256,512]{1,0:T(8,128)(2,1)} %param.2) | copy-start | bytes 786436
  2.5 61.6 %all-to-all-start = ((bf16[8,256,512]{2,1,0:T(8,128)(2,1)}), bf16[8,256,512]{2,1,0:T(8,128)(2,1)S(1)}, u32[]{:S(2)}, u32[]{:S(2)}) async-start(bf16[8,256,512]{2,1,0:T(8,128)(2,1)} %broadcast_in_dim.2), calls=%async_computation | async-start | bytes 4194304 | tf_op jit(solution)/shard_map/all_to_all | solution.py:73
  15.1 7.1 %collective-permute-start = (bf16[2,256,256]{2,1,0:T(8,128)(2,1)S(1)}, bf16[2,256,256]{2,1,0:T(8,128)(2,1)S(1)}, u32[]{:S(2)}, u32[]{:S(2)}) collective-permute-start(bf16[2,256,256]{2,1,0:T(8,128)(2,1)S(1)} %constant_dynamic-slice_fusion), channel_id=1, source_target_pairs={{0,0},{1,2},{2,1},{3,3},{4,5},{5,7},{6,4},{7,6},{8,8},{9,10},{10,9... | collective-permute-start | bytes 786440 | tf_op jit(solution)/shard_map/ppermute | solution.py:24
  15.8 25.5 %collective-permute-start.1 = (bf16[2,256,256]{2,1,0:T(8,128)(2,1)S(1)}, bf16[2,256,256]{2,1,0:T(8,128)(2,1)S(1)}, u32[]{:S(2)}, u32[]{:S(2)}) collective-permute-start(bf16[2,256,256]{2,1,0:T(8,128)(2,1)S(1)} %constant_dynamic-slice_fusion), channel_id=1, source_target_pairs={{0,24},{1,26},{2,25},{3,27},{4,29},{5,31},{6,28},{7,30},{8,16},{9,... | collective-permute-start | bytes 786440 | tf_op jit(solution)/shard_map/ppermute | solution.py:24
  22.2 29.1 %collective-permute-start.2 = (bf16[2,256,256]{2,1,0:T(8,128)(2,1)S(1)}, bf16[2,256,256]{2,1,0:T(8,128)(2,1)S(1)}, u32[]{:S(2)}, u32[]{:S(2)}) collective-permute-start(bf16[2,256,256]{2,1,0:T(8,128)(2,1)S(1)} %collective-permute-done), channel_id=1, source_target_pairs={{0,16},{8,24},{16,0},{24,8},{1,17},{9,25},{17,1},{25,9},{2,18},{10... | collective-permute-start | bytes 786440 | tf_op jit(solution)/shard_map/ppermute | solution.py:24
  36.7 16.6 %collective-permute-start.3 = (bf16[2,256,256]{2,1,0:T(8,128)(2,1)S(1)}, bf16[2,256,256]{2,1,0:T(8,128)(2,1)S(1)}, u32[]{:S(2)}, u32[]{:S(2)}) collective-permute-start(bf16[2,256,256]{2,1,0:T(8,128)(2,1)S(1)} %constant_dynamic-slice_fusion), channel_id=1, source_target_pairs={{0,8},{1,10},{2,9},{3,11},{4,13},{5,15},{6,12},{7,14},{8,0},{9,2},... | collective-permute-start | bytes 786440 | tf_op jit(solution)/shard_map/ppermute | solution.py:24
  41.4 15.0 %collective-permute-start.4 = (bf16[4,256,256]{2,1,0:T(8,128)(2,1)S(1)}, bf16[4,256,256]{2,1,0:T(8,128)(2,1)}, u32[]{:S(2)}, u32[]{:S(2)}) collective-permute-start(bf16[4,256,256]{2,1,0:T(8,128)(2,1)S(1)} %constant_dynamic-update-slice_fusion.own_a), channel_id=1, source_target_pairs={{0,4},{4,0},{1,5},{5,1},{2,6},{6,2},{3,7},{7,3},{8,12},{12,8},{9,1... | collective-permute-start | bytes 1572872 | tf_op jit(solution)/shard_map/ppermute | solution.py:24
  53.3 4.5 %collective-permute-start.5 = (bf16[4,256,256]{2,1,0:T(8,128)(2,1)S(1)}, bf16[4,256,256]{2,1,0:T(8,128)(2,1)}, u32[]{:S(2)}, u32[]{:S(2)}) collective-permute-start(bf16[4,256,256]{2,1,0:T(8,128)(2,1)S(1)} %constant_dynamic-update-slice_fusion.2.own_b), channel_id=1, source_target_pairs={{0,4},{4,0},{1,5},{5,1},{2,6},{6,2},{3,7},{7,3},{8,12},{12,8},{9,1... | collective-permute-start | bytes 1572872 | tf_op jit(solution)/shard_map/ppermute | solution.py:24
  82.8 12.2 %collective-permute-start.6 = (f32[256,128]{1,0:T(8,128)S(1)}, f32[256,128]{1,0:T(8,128)S(1)}, u32[]{:S(2)}, u32[]{:S(2)}) collective-permute-start(f32[256,128]{1,0:T(8,128)S(1)} %slice_bitcast_fusion), channel_id=1, source_target_pairs={{0,256},{256,0},{1,257},{257,1},{2,258},{258,2},{3,259},{259,3},{4... | collective-permute-start | bytes 393224 | tf_op jit(solution)/shard_map/ppermute | solution.py:24

commit v11 on v10

v11 whole, which is shorter than its diff:
```python
import functools

import jax
import jax.numpy as jnp
import numpy as np
from jax import lax
from jax.experimental import pallas as pl
from jax.experimental.pallas import tpu as pltpu
from jax.sharding import Mesh, PartitionSpec as P

AXES = ("yh", "zh", "zl", "yl", "core", "x")
SHAPE = (2, 4, 2, 4, 2, 4)
SIZES = dict(zip(AXES, SHAPE))
UNIT = 256


def moved(value, axes, where):
    shape = [SIZES[a] for a in axes]
    perm = []
    for i in range(int(np.prod(shape))):
        place = dict(zip(axes, (int(v) for v in np.unravel_index(i, shape))))
        there = where(**place)
        perm.append((i, int(np.ravel_multi_index([there[a] for a in axes], shape))))
    return lax.ppermute(value, axes, perm)


def along_z(value, by):
    def where(zh, zl):
        z = (2 * zh + zl + by) % 8
        return {"zh": z >> 1, "zl": z & 1}

    return moved(value, ("zh", "zl"), where)


def spread(value, mask):
    def where(yh, yl, core, x):
        half = (x >> 1) ^ core
        return {"yh": yl >> 1, "yl": (2 * yh + (yl & 1)) ^ mask, "core": core, "x": 2 * (x & 1) + half}

    return moved(value, ("yh", "yl", "core", "x"), where)


def core_swap(value):
    return moved(value, ("core",), lambda core: {"core": 1 - core})


VMEM = pl.BlockSpec(memory_space=pltpu.VMEM)
PARAMS = pltpu.CompilerParams(vmem_limit_bytes=24 * 1024 * 1024)


def split_kernel(tiles_ref, slab_ref, low_ref, high_ref, out_ref):
    low_ref[...] = tiles_ref[:2]
    high_ref[...] = tiles_ref[2:]
    out_ref[...] = slab_ref[...]


def split(tiles, slab):
    half = jax.ShapeDtypeStruct((2,) + tiles.shape[1:], tiles.dtype)
    return pl.pallas_call(
        split_kernel,
        out_shape=(half, half, jax.ShapeDtypeStruct(slab.shape, slab.dtype)),
        in_specs=[VMEM] * 2,
        out_specs=[VMEM] * 3,
        compiler_params=PARAMS,
    )(tiles, slab)


def product_kernel(place, own_a, own_b, other_a, other_b, low_ref, high_ref, up_ref, down_ref, out_ref):
    tiles = [ref.at[i] for ref in (low_ref, high_ref, up_ref, down_ref) for i in range(2)]
    for unit, t_ref in enumerate(tiles):
        t = t_ref[...]
        same = place[5 * unit] == 1
        for rel in range(2):
            first, slot = place[5 * unit + 1 + 2 * rel] == 1, place[5 * unit + 2 + 2 * rel]
            w = jnp.where(
                same,
                jnp.where(first, own_a[slot], own_b[slot]),
                jnp.where(first, other_a[slot], other_b[slot]),
            )
            part = jnp.dot(w, t, preferred_element_type=jnp.float32)
            for block in range(4):
                cols = part[:, block * 128 : (block + 1) * 128]
                if unit == 0:
                    out_ref[block, rel] = cols
                else:
                    out_ref[block, rel] += cols


def product(place, *operands):
    return pl.pallas_call(
        product_kernel,
        out_shape=jax.ShapeDtypeStruct((4, 2, UNIT, 128), jnp.float32),
        in_specs=[pl.BlockSpec(memory_space=pltpu.SMEM)] + [VMEM] * len(operands),
        out_specs=VMEM,
        compiler_params=PARAMS,
    )(place, *operands)


def per_device(integrals, amplitudes):
    yh, zh, zl, yl, core, x = (lax.axis_index(a) for a in AXES)
    both = lax.all_gather(integrals, "core", axis=0)
    half = lax.dynamic_slice_in_dim(both, ((x >> 1) ^ core) * UNIT, UNIT, 2)
    slabs = {mask: spread(half, mask) for mask in (0, 3, 1)}
    copies = jnp.broadcast_to(amplitudes[None], (4,) + amplitudes.shape)
    tiles = lax.all_to_all(copies, "zh", split_axis=0, concat_axis=0, tiled=True)
    low, high, slabs[0] = split(tiles, slabs[0])
    from_up = along_z(low, -1)
    from_down = along_z(high, 1)
    slabs[2] = moved(slabs[0], ("yl",), lambda yl: {"yl": yl ^ 2})
    own_a = jnp.concatenate([slabs[0], slabs[3]])
    own_b = jnp.concatenate([slabs[2], slabs[1]])
    other_a, other_b = core_swap(own_a), core_swap(own_b)
    place = []
    for u4, u3, u2 in [(i >> 1, i & 1, u2) for u2 in (zl, 1 - zl) for i in range(4)]:
        place.append(jnp.where(u2 ^ (x & 1) == core, 1, 0))
        for rel in (0, 1):
            mask = yl ^ (2 * (yh ^ rel) + u4)
            place += [jnp.where(mask >> 1 == mask & 1, 1, 0), (mask & 1) * 2 + u3]
    place = jnp.stack(place).astype(jnp.int32)
    part = product(place, own_a, own_b, other_a, other_b, low, high, from_up, from_down)
    part = lax.all_to_all(part, "x", split_axis=0, concat_axis=0, tiled=True).sum(axis=0)
    return part[0] + moved(part[1], ("yh",), lambda yh: {"yh": 1 - yh})


def solution(mesh):
    return jax.shard_map(
        per_device,
        mesh=Mesh(mesh.devices.reshape(SHAPE), AXES),
        in_specs=(P(("yh", "zh", "zl"), ("yl", "core", "x")), P(("yh", "zh", "zl", "x"), ("yl", "core"))),
        out_specs=P(("yh", "zh", "zl"), ("yl", "core", "x")),
        check_vma=False,
    )
```

time: 96.2 us -> 106 us (1.10); the launches traced: 95.7 us -> 104 us
  waiting for transfers between devices: 24.7 us -> 31.1 us
  blocking collectives: 18.3 us -> 20.9 us
    all_to_all x1, waiting for transfers between devices: 6.31 us -> 11 us  [per_device(): lax.all_to_all(copies, 'zh', split_axis=0, concat_axis=0, tiled=True)]
    all_to_all x1, blocking collectives: 16.1 us -> 18.7 us  [per_device(): lax.all_to_all(part, 'x', split_axis=0, concat_axis=0, tiled=True)]
    ppermute x7 -> x9, waiting for transfers between devices: 18.4 us -> 20.1 us  [moved(): return lax.ppermute(value, axes, perm)]
    ppermute x7 -> x9, starting transfers between devices: 36.1 us -> 36.1 us  [moved(): return lax.ppermute(value, axes, perm)]
  transfers between devices with their start and end apart: 8 -> 10, of which waited for: 5 -> 4; matrix products, arithmetic and copies ran while one was open for 0% -> 0% of each run, Pallas kernels for 0% -> 0%
where the time goes in v11:
time: 106 us; the launch traced here: 104 us
  starting transfers between devices  46.5 us (44%)
  waiting for transfers between devices  31.1 us (29%)
  blocking collectives  20.9 us (20%)
  Pallas kernels  2.54 us (2%)
  local copies, waits for them, and re-layouts  2.23 us (2%)
    ppermute x9, starting transfers between devices, moved(): return lax.ppermute(value, axes, perm)  36.1 us
    ppermute x9, waiting for transfers between devices, moved(): return lax.ppermute(value, axes, perm)  20.1 us
    all_to_all x1, blocking collectives, per_device(): lax.all_to_all(part, 'x', split_axis=0, concat_axis=0, tiled=True)  18.7 us
    all_to_all x1, waiting for transfers between devices, per_device(): lax.all_to_all(copies, 'zh', split_axis=0, concat_axis=0, tiled=True)  11 us
    all_to_all x1, starting transfers between devices, per_device(): lax.all_to_all(copies, 'zh', split_axis=0, concat_axis=0, tiled=True)  10.4 us
    pallas_call x1, Pallas kernels, product(): pl.pallas_call(product_kernel, out_shape=jax.ShapeDtypeStruct((4, 2, UNIT...  2.46 us
    all_gather x1, blocking collectives, per_device(): both = lax.all_gather(integrals, 'core', axis=0)  2.17 us
  transfers between devices with their start and end apart: 10, of which 4 were waited for; matrix products, arithmetic and copies ran while one was open for 0% of the time, Pallas kernels for 0%

profile of v11, /device:TPU:56, one launch (start us, length us, event | category | flops | bytes accessed | tf_op | source)
XLA Modules:
  0.0 104.2 jit_solution(10166861993815025697)
XLA Ops:
  0.0 2.0 %broadcast_in_dim.2 = bf16[4,256,512]{2,1,0:T(8,128)(2,1)} broadcast(bf16[256,512]{1,0:T(8,128)(2,1)} %param.3), dimensions={1,2} | broadcast | bytes 1310720 | tf_op jit(solution)/shard_map/broadcast_in_dim | solution.py:104
  2.0 0.0 copy-start
  2.0 10.4 %all-to-all-start = ((bf16[4,256,512]{2,1,0:T(8,128)(2,1)}), bf16[4,256,512]{2,1,0:T(8,128)(2,1)S(1)}, u32[]{:S(2)}, u32[]{:S(2)}) async-start(bf16[4,256,512]{2,1,0:T(8,128)(2,1)} %broadcast_in_dim.2), calls=%async_computation | async-start | bytes 2097152 | tf_op jit(solution)/shard_map/all_to_all | solution.py:105
  12.4 0.0 copy-done
  12.4 2.2 %all-gather = bf16[512,512]{1,0:T(8,128)(2,1)S(1)} all-gather(bf16[256,512]{1,0:T(8,128)(2,1)S(1)} %copy-done), channel_id=2, replica_groups=mesh['yh'=2,'zh'=4,'zl'=2,'yl'=4,'core'=2,'x'=4] {'core'}, dimensions={0}, use_global_device_ids=true | all-gather | bytes 786432 | tf_op jit(solution)/shard_map/all_gather | solution.py:101
  14.6 0.7 collective-permute-start
  15.3 6.4 %collective-permute-start.1 = (bf16[2,256,256]{2,1,0:T(8,128)(2,1)S(1)}, bf16[2,256,256]{2,1,0:T(8,128)(2,1)S(1)}, u32[]{:S(2)}, u32[]{:S(2)}) collective-permute-start(bf16[2,256,256]{2,1,0:T(8,128)(2,1)S(1)} %constant_dynamic-slice_fusion), channel_id=1, source_target_pairs={{0,24},{1,26},{2,25},{3,27},{4,29},{5,31},{6,28},{7,30},{8,16},{9,... | collective-permute-start | bytes 786440 | tf_op jit(solution)/shard_map/ppermute | solution.py:24
  21.7 0.0 collective-permute-done.slab_ref
  21.7 11.0 %all-to-all-done.tiles_ref = bf16[4,256,512]{2,1,0:T(8,128)(2,1)S(1)} async-done(((bf16[4,256,512]{2,1,0:T(8,128)(2,1)}), bf16[4,256,512]{2,1,0:T(8,128)(2,1)S(1)}, u32[]{:S(2)}, u32[]{:S(2)}) %all-to-all-start) | async-done | bytes 1048608 | tf_op jit(solution)/shard_map/all_to_all | solution.py:105
  32.7 0.1 shard_map.28
  32.8 4.0 %collective-permute-start.2 = (bf16[2,256,256]{2,1,0:T(8,128)(2,1)S(1)}, bf16[2,256,256]{2,1,0:T(8,128)(2,1)S(1)}, u32[]{:S(2)}, u32[]{:S(2)}) collective-permute-start(bf16[2,256,256]{2,1,0:T(8,128)(2,1)S(1)} %get-tuple-element.8), channel_id=1, source_target_pairs={{0,16},{8,24},{16,0},{24,8},{1,17},{9,25},{17,1},{25,9},{2,18},{10... | collective-permute-start | bytes 786440 | tf_op jit(solution)/shard_map/ppermute | solution.py:24
  36.8 4.0 %collective-permute-start.3 = (bf16[2,256,256]{2,1,0:T(8,128)(2,1)S(1)}, bf16[2,256,256]{2,1,0:T(8,128)(2,1)S(1)}, u32[]{:S(2)}, u32[]{:S(2)}) collective-permute-start(bf16[2,256,256]{2,1,0:T(8,128)(2,1)S(1)} %constant_dynamic-slice_fusion), channel_id=1, source_target_pairs={{0,8},{1,10},{2,9},{3,11},{4,13},{5,15},{6,12},{7,14},{8,0},{9,2},... | collective-permute-start | bytes 786440 | tf_op jit(solution)/shard_map/ppermute | solution.py:24
  40.9 0.0 collective-permute-done.1
  41.0 2.4 %collective-permute-start.4 = (bf16[4,256,256]{2,1,0:T(8,128)(2,1)S(1)}, bf16[4,256,256]{2,1,0:T(8,128)(2,1)S(1)}, u32[]{:S(2)}, u32[]{:S(2)}) collective-permute-start(bf16[4,256,256]{2,1,0:T(8,128)(2,1)S(1)} %constant_dynamic-update-slice_fusion.own_a), channel_id=1, source_target_pairs={{0,4},{4,0},{1,5},{5,1},{2,6},{6,2},{3,7},{7,3},{8,12},{12,8},{9,1... | collective-permute-start | bytes 1572872 | tf_op jit(solution)/shard_map/ppermute | solution.py:24
  43.4 9.7 %collective-permute-start.6 = (bf16[2,256,512]{2,1,0:T(8,128)(2,1)S(1)}, bf16[2,256,512]{2,1,0:T(8,128)(2,1)S(1)}, u32[]{:S(2)}, u32[]{:S(2)}) collective-permute-start(bf16[2,256,512]{2,1,0:T(8,128)(2,1)S(1)} %get-tuple-element.9.low_ref), channel_id=1, source_target_pairs={{0,224},{32,0},{64,32},{96,64},{128,96},{160,128},{192,160},{224,1... | collective-permute-start | bytes 1572872 | tf_op jit(solution)/shard_map/ppermute | solution.py:24
  53.0 1.9 %collective-permute-start.7 = (bf16[2,256,512]{2,1,0:T(8,128)(2,1)S(1)}, bf16[2,256,512]{2,1,0:T(8,128)(2,1)}, u32[]{:S(2)}, u32[]{:S(2)}) collective-permute-start(bf16[2,256,512]{2,1,0:T(8,128)(2,1)S(1)} %get-tuple-element.10.high_ref), channel_id=1, source_target_pairs={{0,32},{32,64},{64,96},{96,128},{128,160},{160,192},{192,224},{224... | collective-permute-start | bytes 1572872 | tf_op jit(solution)/shard_map/ppermute | solution.py:24
  55.0 0.0 collective-permute-done.2
  55.0 0.0 collective-permute-done.3
  55.1 2.1 %collective-permute-start.5 = (bf16[4,256,256]{2,1,0:T(8,128)(2,1)S(1)}, bf16[4,256,256]{2,1,0:T(8,128)(2,1)}, u32[]{:S(2)}, u32[]{:S(2)}) collective-permute-start(bf16[4,256,256]{2,1,0:T(8,128)(2,1)S(1)} %constant_dynamic-update-slice_fusion.2.own_b), channel_id=1, source_target_pairs={{0,4},{4,0},{1,5},{5,1},{2,6},{6,2},{3,7},{7,3},{8,12},{12,8},{9,1... | collective-permute-start | bytes 1572872 | tf_op jit(solution)/shard_map/ppermute | solution.py:24
  57.2 0.1 stack.85.place
  57.4 0.0 collective-permute-done.4.other_a
  57.4 8.2 %collective-permute-done.6.up_ref = bf16[2,256,512]{2,1,0:T(8,128)(2,1)S(1)} collective-permute-done((bf16[2,256,512]{2,1,0:T(8,128)(2,1)S(1)}, bf16[2,256,512]{2,1,0:T(8,128)(2,1)S(1)}, u32[]{:S(2)}, u32[]{:S(2)}) %collective-permute-start.6) | collective-permute-done | bytes 524320 | tf_op jit(solution)/shard_map/ppermute | solution.py:24
  65.6 4.7 %collective-permute-done.7.down_ref = bf16[2,256,512]{2,1,0:T(8,128)(2,1)} collective-permute-done((bf16[2,256,512]{2,1,0:T(8,128)(2,1)S(1)}, bf16[2,256,512]{2,1,0:T(8,128)(2,1)}, u32[]{:S(2)}, u32[]{:S(2)}) %collective-permute-start.7) | collective-permute-done | bytes 524320 | tf_op jit(solution)/shard_map/ppermute | solution.py:24
  70.3 0.0 collective-permute-done.5.other_b
  70.3 2.5 %shard_map.29 = f32[4,2,256,128]{3,2,1,0:T(8,128)S(1)} custom-call(s32[40]{0:T(128)S(1)} %stack.85.place, bf16[4,256,256]{2,1,0:T(8,128)(2,1)S(1)} %constant_dynamic-update-slice_fusion.own_a, bf16[4,256,256]{2,1,0:T(8,128)(2,1)S(1)} %constant_dynamic-update-slice_fusion.2.own_b, bf16[4,256,256]{2,1,0:T(8,128)(2,1)S(1)} %collective-permute-done.4.other_a, ...), custom_call_target="tpu_custom_call" | custom-call | tf_op jit(solution)/shard_map/pallas_call | solution.py:90
  72.8 18.7 %all_to_all.10 = f32[4,2,256,128]{3,2,1,0:T(8,128)S(1)} all-to-all(f32[4,2,256,128]{3,2,1,0:T(8,128)S(1)} %shard_map.29), channel_id=1, replica_groups=mesh['yh'=2,'zh'=4,'zl'=2,'yl'=4,'core'=2,'x'=4] {'x'}, dimensions={0} | all-to-all | bytes 2097152 | tf_op jit(solution)/shard_map/all_to_all | solution.py:121
  91.5 0.1 reduce_sum.9
  91.6 4.8 %collective-permute-start.8 = (f32[256,128]{1,0:T(8,128)S(1)}, f32[256,128]{1,0:T(8,128)S(1)}, u32[]{:S(2)}, u32[]{:S(2)}) collective-permute-start(f32[256,128]{1,0:T(8,128)S(1)} %slice_bitcast_fusion), channel_id=1, source_target_pairs={{0,256},{256,0},{1,257},{257,1},{2,258},{258,2},{3,259},{259,3},{4... | collective-permute-start | bytes 393224 | tf_op jit(solution)/shard_map/ppermute | solution.py:24
  96.4 7.1 %collective-permute-done.8 = f32[256,128]{1,0:T(8,128)S(1)} collective-permute-done((f32[256,128]{1,0:T(8,128)S(1)}, f32[256,128]{1,0:T(8,128)S(1)}, u32[]{:S(2)}, u32[]{:S(2)}) %collective-permute-start.8) | collective-permute-done | bytes 131104 | tf_op jit(solution)/shard_map/ppermute | solution.py:24
  103.5 0.7 fusion
  (6 shorter events, 0.1 us)
Async XLA Ops:
  2.0 10.4 %copy-start = (bf16[256,512]{1,0:T(8,128)(2,1)S(1)}, bf16[256,512]{1,0:T(8,128)(2,1)}, u32[]{:S(2)}) copy-start(bf16[256,512]{1,0:T(8,128)(2,1)} %param.2) | copy-start | bytes 786436
  2.0 30.7 %all-to-all-start = ((bf16[4,256,512]{2,1,0:T(8,128)(2,1)}), bf16[4,256,512]{2,1,0:T(8,128)(2,1)S(1)}, u32[]{:S(2)}, u32[]{:S(2)}) async-start(bf16[4,256,512]{2,1,0:T(8,128)(2,1)} %broadcast_in_dim.2), calls=%async_computation | async-start | bytes 2097152 | tf_op jit(solution)/shard_map/all_to_all | solution.py:105
  14.6 7.1 %collective-permute-start = (bf16[2,256,256]{2,1,0:T(8,128)(2,1)S(1)}, bf16[2,256,256]{2,1,0:T(8,128)(2,1)S(1)}, u32[]{:S(2)}, u32[]{:S(2)}) collective-permute-start(bf16[2,256,256]{2,1,0:T(8,128)(2,1)S(1)} %constant_dynamic-slice_fusion), channel_id=1, source_target_pairs={{0,0},{1,2},{2,1},{3,3},{4,5},{5,7},{6,4},{7,6},{8,8},{9,10},{10,9... | collective-permute-start | bytes 786440 | tf_op jit(solution)/shard_map/ppermute | solution.py:24
  15.3 25.6 %collective-permute-start.1 = (bf16[2,256,256]{2,1,0:T(8,128)(2,1)S(1)}, bf16[2,256,256]{2,1,0:T(8,128)(2,1)S(1)}, u32[]{:S(2)}, u32[]{:S(2)}) collective-permute-start(bf16[2,256,256]{2,1,0:T(8,128)(2,1)S(1)} %constant_dynamic-slice_fusion), channel_id=1, source_target_pairs={{0,24},{1,26},{2,25},{3,27},{4,29},{5,31},{6,28},{7,30},{8,16},{9,... | collective-permute-start | bytes 786440 | tf_op jit(solution)/shard_map/ppermute | solution.py:24
  32.8 22.2 %collective-permute-start.2 = (bf16[2,256,256]{2,1,0:T(8,128)(2,1)S(1)}, bf16[2,256,256]{2,1,0:T(8,128)(2,1)S(1)}, u32[]{:S(2)}, u32[]{:S(2)}) collective-permute-start(bf16[2,256,256]{2,1,0:T(8,128)(2,1)S(1)} %get-tuple-element.8), channel_id=1, source_target_pairs={{0,16},{8,24},{16,0},{24,8},{1,17},{9,25},{17,1},{25,9},{2,18},{10... | collective-permute-start | bytes 786440 | tf_op jit(solution)/shard_map/ppermute | solution.py:24
  36.8 18.2 %collective-permute-start.3 = (bf16[2,256,256]{2,1,0:T(8,128)(2,1)S(1)}, bf16[2,256,256]{2,1,0:T(8,128)(2,1)S(1)}, u32[]{:S(2)}, u32[]{:S(2)}) collective-permute-start(bf16[2,256,256]{2,1,0:T(8,128)(2,1)S(1)} %constant_dynamic-slice_fusion), channel_id=1, source_target_pairs={{0,8},{1,10},{2,9},{3,11},{4,13},{5,15},{6,12},{7,14},{8,0},{9,2},... | collective-permute-start | bytes 786440 | tf_op jit(solution)/shard_map/ppermute | solution.py:24
  41.0 16.4 %collective-permute-start.4 = (bf16[4,256,256]{2,1,0:T(8,128)(2,1)S(1)}, bf16[4,256,256]{2,1,0:T(8,128)(2,1)S(1)}, u32[]{:S(2)}, u32[]{:S(2)}) collective-permute-start(bf16[4,256,256]{2,1,0:T(8,128)(2,1)S(1)} %constant_dynamic-update-slice_fusion.own_a), channel_id=1, source_target_pairs={{0,4},{4,0},{1,5},{5,1},{2,6},{6,2},{3,7},{7,3},{8,12},{12,8},{9,1... | collective-permute-start | bytes 1572872 | tf_op jit(solution)/shard_map/ppermute | solution.py:24
  43.4 22.3 %collective-permute-start.6 = (bf16[2,256,512]{2,1,0:T(8,128)(2,1)S(1)}, bf16[2,256,512]{2,1,0:T(8,128)(2,1)S(1)}, u32[]{:S(2)}, u32[]{:S(2)}) collective-permute-start(bf16[2,256,512]{2,1,0:T(8,128)(2,1)S(1)} %get-tuple-element.9.low_ref), channel_id=1, source_target_pairs={{0,224},{32,0},{64,32},{96,64},{128,96},{160,128},{192,160},{224,1... | collective-permute-start | bytes 1572872 | tf_op jit(solution)/shard_map/ppermute | solution.py:24
  53.0 17.3 %collective-permute-start.7 = (bf16[2,256,512]{2,1,0:T(8,128)(2,1)S(1)}, bf16[2,256,512]{2,1,0:T(8,128)(2,1)}, u32[]{:S(2)}, u32[]{:S(2)}) collective-permute-start(bf16[2,256,512]{2,1,0:T(8,128)(2,1)S(1)} %get-tuple-element.10.high_ref), channel_id=1, source_target_pairs={{0,32},{32,64},{64,96},{96,128},{128,160},{160,192},{192,224},{224... | collective-permute-start | bytes 1572872 | tf_op jit(solution)/shard_map/ppermute | solution.py:24
  55.1 15.3 %collective-permute-start.5 = (bf16[4,256,256]{2,1,0:T(8,128)(2,1)S(1)}, bf16[4,256,256]{2,1,0:T(8,128)(2,1)}, u32[]{:S(2)}, u32[]{:S(2)}) collective-permute-start(bf16[4,256,256]{2,1,0:T(8,128)(2,1)S(1)} %constant_dynamic-update-slice_fusion.2.own_b), channel_id=1, source_target_pairs={{0,4},{4,0},{1,5},{5,1},{2,6},{6,2},{3,7},{7,3},{8,12},{12,8},{9,1... | collective-permute-start | bytes 1572872 | tf_op jit(solution)/shard_map/ppermute | solution.py:24
  91.6 11.9 %collective-permute-start.8 = (f32[256,128]{1,0:T(8,128)S(1)}, f32[256,128]{1,0:T(8,128)S(1)}, u32[]{:S(2)}, u32[]{:S(2)}) collective-permute-start(f32[256,128]{1,0:T(8,128)S(1)} %slice_bitcast_fusion), channel_id=1, source_target_pairs={{0,256},{256,0},{1,257},{257,1},{2,258},{258,2},{3,259},{259,3},{4... | collective-permute-start | bytes 393224 | tf_op jit(solution)/shard_map/ppermute | solution.py:24

commit v12 on v10

--- a/solution.py
+++ b/solution.py
@@ -36,7 +36,7 @@
     return moved(value, ("core",), lambda core: {"core": 1 - core})
 
 
-def product_kernel(place, own_a, own_b, other_a, other_b, t_ref, out_ref):
+def product_kernel(place, own_a, own_b, other_a, other_b, t_ref, mine_ref, theirs_ref):
     for unit in range(8):
         t = t_ref[unit]
         same = place[5 * unit] == 1
@@ -50,21 +50,44 @@
             part = jnp.dot(w, t, preferred_element_type=jnp.float32)
             for block in range(4):
                 cols = part[:, block * 128 : (block + 1) * 128]
+                out_ref = theirs_ref if rel else mine_ref
                 if unit == 0:
-                    out_ref[block, rel] = cols
+                    out_ref[block] = cols
                 else:
-                    out_ref[block, rel] += cols
+                    out_ref[block] += cols
+
+
+VMEM = pl.BlockSpec(memory_space=pltpu.VMEM)
+PARAMS = pltpu.CompilerParams(vmem_limit_bytes=40 * 1024 * 1024)
 
 
 def product(place, *operands):
-    vmem = pl.BlockSpec(memory_space=pltpu.VMEM)
+    out = jax.ShapeDtypeStruct((4, UNIT, 128), jnp.float32)
     return pl.pallas_call(
         product_kernel,
-        out_shape=jax.ShapeDtypeStruct((4, 2, UNIT, 128), jnp.float32),
-        in_specs=[pl.BlockSpec(memory_space=pltpu.SMEM)] + [vmem] * len(operands),
-        out_specs=vmem,
-        compiler_params=pltpu.CompilerParams(vmem_limit_bytes=40 * 1024 * 1024),
+        out_shape=(out, out),
+        in_specs=[pl.BlockSpec(memory_space=pltpu.SMEM)] + [VMEM] * len(operands),
+        out_specs=(VMEM, VMEM),
+        compiler_params=PARAMS,
     )(place, *operands)
+
+
+def after_kernel(value_ref, first_ref, out_ref):
+    out_ref[...] = value_ref[...]
+
+
+def after(value, first):
+    return pl.pallas_call(
+        after_kernel,
+        out_shape=jax.ShapeDtypeStruct(value.shape, value.dtype),
+        in_specs=[VMEM, VMEM],
+        out_specs=VMEM,
+        compiler_params=PARAMS,
+    )(value, first)
+
+
+def over_depth(part):
+    return lax.all_to_all(part, "x", split_axis=0, concat_axis=0, tiled=True).sum(axis=0)
 
 
 def per_device(integrals, amplitudes):
@@ -86,9 +109,10 @@
             mask = yl ^ (2 * (yh ^ rel) + u4)
             place += [jnp.where(mask >> 1 == mask & 1, 1, 0), (mask & 1) * 2 + u3]
     place = jnp.stack(place).astype(jnp.int32)
-    part = product(place, own_a, own_b, other_a, other_b, tiles)
-    part = lax.all_to_all(part, "x", split_axis=0, concat_axis=0, tiled=True).sum(axis=0)
-    return part[0] + moved(part[1], ("yh",), lambda yh: {"yh": 1 - yh})
+    mine, theirs = product(place, own_a, own_b, other_a, other_b, tiles)
+    theirs = over_depth(theirs)
+    arriving = moved(theirs, ("yh",), lambda yh: {"yh": 1 - yh})
+    return over_depth(after(mine, theirs)) + arriving
 
 
 def solution(mesh):

time: 96.2 us -> 98.8 us (1.027)
  blocking collectives: 18.3 us -> 14.3 us
  starting transfers between devices: 46.6 us -> 50 us
  local copies, waits for them, and re-layouts: 2.7 us -> 4.51 us
    all_to_all x1, blocking collectives: 16.1 us -> 12.2 us  [over_depth(): lax.all_to_all(part, 'x', split_axis=0, concat_axis=0, tiled=True)]
    all_to_all x0 -> x1, starting transfers between devices: none -> 3.47 us  [over_depth(): lax.all_to_all(part, 'x', split_axis=0, concat_axis=0, tiled=True)]
    ppermute x7, waiting for transfers between devices: 18.4 us -> 15 us  [moved(): return lax.ppermute(value, axes, perm)]
    all_to_all x0 -> x1, waiting for transfers between devices: none -> 3.32 us  [over_depth(): lax.all_to_all(part, 'x', split_axis=0, concat_axis=0, tiled=True)]
    unnamed x4 -> x8, local copies, waits for them, and re-layouts: 0.04 us -> 1.87 us
    pallas_call x1 -> x2, Pallas kernels: 2.46 us -> 3.29 us  [the longest x1 2.46 us: product(): pl.pallas_call(product_kernel, out_shape=(out, out), in_specs=[pl.BlockSp...]
  transfers between devices with their start and end apart: 8 -> 9, of which waited for: 5 -> 6; matrix products, arithmetic and copies ran while one was open for 0% -> 0% of each run, Pallas kernels for 0% -> 0%
where the time goes in v12:
time: 98.8 us; the launch traced here: 97.8 us
  starting transfers between devices  50 us (51%)
  waiting for transfers between devices  24.7 us (25%)
  blocking collectives  14.3 us (14%)
  local copies, waits for them, and re-layouts  4.51 us (5%)
  Pallas kernels  3.29 us (3%)
    ppermute x7, starting transfers between devices, moved(): return lax.ppermute(value, axes, perm)  36.1 us
    ppermute x7, waiting for transfers between devices, moved(): return lax.ppermute(value, axes, perm)  15 us
    all_to_all x1, blocking collectives, over_depth(): lax.all_to_all(part, 'x', split_axis=0, concat_axis=0, tiled=True)  12.2 us
    all_to_all x1, starting transfers between devices, per_device(): tiles = lax.all_to_all(copies, 'z', split_axis=0, concat_axis=0, tiled=True)  10.4 us
    all_to_all x1, waiting for transfers between devices, per_device(): tiles = lax.all_to_all(copies, 'z', split_axis=0, concat_axis=0, tiled=True)  6.31 us
    all_to_all x1, starting transfers between devices, over_depth(): lax.all_to_all(part, 'x', split_axis=0, concat_axis=0, tiled=True)  3.47 us
    all_to_all x1, waiting for transfers between devices, over_depth(): lax.all_to_all(part, 'x', split_axis=0, concat_axis=0, tiled=True)  3.32 us
    broadcast_in_dim x1, local copies, waits for them, and re-layouts, per_device(): copies = jnp.broadcast_to(amplitudes[None], (8,) + amplitudes.shape)  2.47 us
  transfers between devices with their start and end apart: 9, of which 6 were waited for; matrix products, arithmetic and copies ran while one was open for 0% of the time, Pallas kernels for 0%

profile of v12, /device:TPU:56, one launch (start us, length us, event | category | flops | bytes accessed | tf_op | source)
XLA Modules:
  0.0 97.8 jit_solution(9231736705559647699)
XLA Ops:
  0.0 2.5 %broadcast_in_dim.2 = bf16[8,256,512]{2,1,0:T(8,128)(2,1)} broadcast(bf16[256,512]{1,0:T(8,128)(2,1)} %param.3), dimensions={1,2} | broadcast | bytes 2359296 | tf_op jit(solution)/shard_map/broadcast_in_dim | solution.py:95
  2.5 0.0 copy-start.2
  2.5 10.4 %all-to-all-start = ((bf16[8,256,512]{2,1,0:T(8,128)(2,1)}), bf16[8,256,512]{2,1,0:T(8,128)(2,1)S(1)}, u32[]{:S(2)}, u32[]{:S(2)}) async-start(bf16[8,256,512]{2,1,0:T(8,128)(2,1)} %broadcast_in_dim.2), calls=%async_computation | async-start | bytes 4194304 | tf_op jit(solution)/shard_map/all_to_all | solution.py:96
  12.9 0.0 copy-done.2
  12.9 2.2 %all-gather = bf16[512,512]{1,0:T(8,128)(2,1)S(1)} all-gather(bf16[256,512]{1,0:T(8,128)(2,1)S(1)} %copy-done.2), channel_id=2, replica_groups=mesh['yh'=2,'z'=8,'yl'=4,'core'=2,'x'=4] {'core'}, dimensions={0}, use_global_device_ids=true | all-gather | bytes 786432 | tf_op jit(solution)/shard_map/all_gather | solution.py:97
  15.1 0.7 collective-permute-start
  15.8 6.4 %collective-permute-start.1 = (bf16[2,256,256]{2,1,0:T(8,128)(2,1)S(1)}, bf16[2,256,256]{2,1,0:T(8,128)(2,1)S(1)}, u32[]{:S(2)}, u32[]{:S(2)}) collective-permute-start(bf16[2,256,256]{2,1,0:T(8,128)(2,1)S(1)} %constant_dynamic-slice_fusion), channel_id=1, source_target_pairs={{0,24},{1,26},{2,25},{3,27},{4,29},{5,31},{6,28},{7,30},{8,16},{9,... | collective-permute-start | bytes 786440 | tf_op jit(solution)/shard_map/ppermute | solution.py:24
  22.2 0.0 collective-permute-done
  22.2 14.5 %collective-permute-start.2 = (bf16[2,256,256]{2,1,0:T(8,128)(2,1)S(1)}, bf16[2,256,256]{2,1,0:T(8,128)(2,1)S(1)}, u32[]{:S(2)}, u32[]{:S(2)}) collective-permute-start(bf16[2,256,256]{2,1,0:T(8,128)(2,1)S(1)} %collective-permute-done), channel_id=1, source_target_pairs={{0,16},{8,24},{16,0},{24,8},{1,17},{9,25},{17,1},{25,9},{2,18},{10... | collective-permute-start | bytes 786440 | tf_op jit(solution)/shard_map/ppermute | solution.py:24
  36.7 4.6 %collective-permute-start.3 = (bf16[2,256,256]{2,1,0:T(8,128)(2,1)S(1)}, bf16[2,256,256]{2,1,0:T(8,128)(2,1)S(1)}, u32[]{:S(2)}, u32[]{:S(2)}) collective-permute-start(bf16[2,256,256]{2,1,0:T(8,128)(2,1)S(1)} %constant_dynamic-slice_fusion), channel_id=1, source_target_pairs={{0,8},{1,10},{2,9},{3,11},{4,13},{5,15},{6,12},{7,14},{8,0},{9,2},... | collective-permute-start | bytes 786440 | tf_op jit(solution)/shard_map/ppermute | solution.py:24
  41.3 0.0 collective-permute-done.1
  41.3 2.4 %collective-permute-start.4 = (bf16[4,256,256]{2,1,0:T(8,128)(2,1)S(1)}, bf16[4,256,256]{2,1,0:T(8,128)(2,1)}, u32[]{:S(2)}, u32[]{:S(2)}) collective-permute-start(bf16[4,256,256]{2,1,0:T(8,128)(2,1)S(1)} %constant_dynamic-update-slice_fusion.own_a), channel_id=1, source_target_pairs={{0,4},{4,0},{1,5},{5,1},{2,6},{6,2},{3,7},{7,3},{8,12},{12,8},{9,1... | collective-permute-start | bytes 1572872 | tf_op jit(solution)/shard_map/ppermute | solution.py:24
  43.8 7.5 %collective-permute-done.2 = bf16[2,256,256]{2,1,0:T(8,128)(2,1)S(1)} collective-permute-done((bf16[2,256,256]{2,1,0:T(8,128)(2,1)S(1)}, bf16[2,256,256]{2,1,0:T(8,128)(2,1)S(1)}, u32[]{:S(2)}, u32[]{:S(2)}) %collective-permute-start.2) | collective-permute-done | bytes 262176 | tf_op jit(solution)/shard_map/ppermute | solution.py:24
  51.3 2.0 %collective-permute-done.3 = bf16[2,256,256]{2,1,0:T(8,128)(2,1)S(1)} collective-permute-done((bf16[2,256,256]{2,1,0:T(8,128)(2,1)S(1)}, bf16[2,256,256]{2,1,0:T(8,128)(2,1)S(1)}, u32[]{:S(2)}, u32[]{:S(2)}) %collective-permute-start.3) | collective-permute-done | bytes 262176 | tf_op jit(solution)/shard_map/ppermute | solution.py:24
  53.3 2.9 %collective-permute-start.5 = (bf16[4,256,256]{2,1,0:T(8,128)(2,1)S(1)}, bf16[4,256,256]{2,1,0:T(8,128)(2,1)}, u32[]{:S(2)}, u32[]{:S(2)}) collective-permute-start(bf16[4,256,256]{2,1,0:T(8,128)(2,1)S(1)} %constant_dynamic-update-slice_fusion.2.own_b), channel_id=1, source_target_pairs={{0,4},{4,0},{1,5},{5,1},{2,6},{6,2},{3,7},{7,3},{8,12},{12,8},{9,1... | collective-permute-start | bytes 1572872 | tf_op jit(solution)/shard_map/ppermute | solution.py:24
  56.2 0.1 stack.85.place
  56.3 0.0 collective-permute-done.4.other_a
  56.3 1.5 %collective-permute-done.5.other_b = bf16[4,256,256]{2,1,0:T(8,128)(2,1)} collective-permute-done((bf16[4,256,256]{2,1,0:T(8,128)(2,1)S(1)}, bf16[4,256,256]{2,1,0:T(8,128)(2,1)}, u32[]{:S(2)}, u32[]{:S(2)}) %collective-permute-start.5) | collective-permute-done | bytes 524320 | tf_op jit(solution)/shard_map/ppermute | solution.py:24
  57.8 6.3 %all-to-all-done.t_ref = bf16[8,256,512]{2,1,0:T(8,128)(2,1)S(1)} async-done(((bf16[8,256,512]{2,1,0:T(8,128)(2,1)}), bf16[8,256,512]{2,1,0:T(8,128)(2,1)S(1)}, u32[]{:S(2)}, u32[]{:S(2)}) %all-to-all-start) | async-done | bytes 2097184 | tf_op jit(solution)/shard_map/all_to_all | solution.py:96
  64.1 2.5 %shard_map.28 = (f32[4,256,128]{2,1,0:T(8,128)S(1)}, f32[4,256,128]{2,1,0:T(8,128)S(1)}) custom-call(s32[40]{0:T(128)S(1)} %stack.85.place, bf16[4,256,256]{2,1,0:T(8,128)(2,1)S(1)} %constant_dynamic-update-slice_fusion.own_a, bf16[4,256,256]{2,1,0:T(8,128)(2,1)S(1)} %constant_dynamic-update-slice_fusion.2.own_b, ...), custom_call_target="tpu_custom_call" | custom-call | tf_op jit(solution)/shard_map/pallas_call | solution.py:66
  66.6 0.0 copy-start
  66.6 0.8 copy-done
  67.4 12.2 %all_to_all.15 = f32[4,256,128]{2,1,0:T(8,128)S(1)} all-to-all(f32[4,256,128]{2,1,0:T(8,128)S(1)} %get-tuple-element.8), channel_id=1, replica_groups=mesh['yh'=2,'z'=8,'yl'=4,'core'=2,'x'=4] {'x'}, dimensions={0} | all-to-all | bytes 1048576 | tf_op jit(solution)/shard_map/all_to_all | solution.py:90
  79.6 0.0 copy-start.1
  79.6 1.0 %copy-done.1 = f32[4,256,128]{2,1,0:T(8,128)S(1)} copy-done((f32[4,256,128]{2,1,0:T(8,128)S(1)}, f32[4,256,128]{2,1,0:T(8,128)}, u32[]{:S(2)}) %copy-start.1) | copy-done | bytes 524312
  80.6 0.8 shard_map.29
  81.5 3.5 %all-to-all-start.2 = ((f32[4,256,128]{2,1,0:T(8,128)}), f32[4,256,128]{2,1,0:T(8,128)S(1)}, u32[]{:S(2)}, u32[]{:S(2)}) async-start(f32[4,256,128]{2,1,0:T(8,128)} %shard_map.29), calls=%async_computation.2 | async-start | bytes 1048576 | tf_op jit(solution)/shard_map/all_to_all | solution.py:90
  84.9 4.7 %collective-permute-start.6 = (f32[256,128]{1,0:T(8,128)S(1)}, f32[256,128]{1,0:T(8,128)S(1)}, u32[]{:S(2)}, u32[]{:S(2)}) collective-permute-start(f32[256,128]{1,0:T(8,128)S(1)} %reduce_sum.18.first_ref), channel_id=1, source_target_pairs={{0,256},{256,0},{1,257},{257,1},{2,258},{258,2},{3,259},{259,3},{4... | collective-permute-start | bytes 393224 | tf_op jit(solution)/shard_map/ppermute | solution.py:24
  89.7 3.3 %all-to-all-done.2 = f32[4,256,128]{2,1,0:T(8,128)S(1)} async-done(((f32[4,256,128]{2,1,0:T(8,128)}), f32[4,256,128]{2,1,0:T(8,128)S(1)}, u32[]{:S(2)}, u32[]{:S(2)}) %all-to-all-start.2) | async-done | bytes 524320 | tf_op jit(solution)/shard_map/all_to_all | solution.py:90
  93.0 4.1 %collective-permute-done.6 = f32[256,128]{1,0:T(8,128)S(1)} collective-permute-done((f32[256,128]{1,0:T(8,128)S(1)}, f32[256,128]{1,0:T(8,128)S(1)}, u32[]{:S(2)}, u32[]{:S(2)}) %collective-permute-start.6) | collective-permute-done | bytes 131104 | tf_op jit(solution)/shard_map/ppermute | solution.py:24
  97.1 0.7 add.41
  (7 shorter events, 0.1 us)
Async XLA Ops:
  2.5 10.5 %copy-start.2 = (bf16[256,512]{1,0:T(8,128)(2,1)S(1)}, bf16[256,512]{1,0:T(8,128)(2,1)}, u32[]{:S(2)}) copy-start(bf16[256,512]{1,0:T(8,128)(2,1)} %param.2) | copy-start | bytes 786436
  2.5 61.6 %all-to-all-start = ((bf16[8,256,512]{2,1,0:T(8,128)(2,1)}), bf16[8,256,512]{2,1,0:T(8,128)(2,1)S(1)}, u32[]{:S(2)}, u32[]{:S(2)}) async-start(bf16[8,256,512]{2,1,0:T(8,128)(2,1)} %broadcast_in_dim.2), calls=%async_computation | async-start | bytes 4194304 | tf_op jit(solution)/shard_map/all_to_all | solution.py:96
  15.1 7.1 %collective-permute-start = (bf16[2,256,256]{2,1,0:T(8,128)(2,1)S(1)}, bf16[2,256,256]{2,1,0:T(8,128)(2,1)S(1)}, u32[]{:S(2)}, u32[]{:S(2)}) collective-permute-start(bf16[2,256,256]{2,1,0:T(8,128)(2,1)S(1)} %constant_dynamic-slice_fusion), channel_id=1, source_target_pairs={{0,0},{1,2},{2,1},{3,3},{4,5},{5,7},{6,4},{7,6},{8,8},{9,10},{10,9... | collective-permute-start | bytes 786440 | tf_op jit(solution)/shard_map/ppermute | solution.py:24
  15.8 25.5 %collective-permute-start.1 = (bf16[2,256,256]{2,1,0:T(8,128)(2,1)S(1)}, bf16[2,256,256]{2,1,0:T(8,128)(2,1)S(1)}, u32[]{:S(2)}, u32[]{:S(2)}) collective-permute-start(bf16[2,256,256]{2,1,0:T(8,128)(2,1)S(1)} %constant_dynamic-slice_fusion), channel_id=1, source_target_pairs={{0,24},{1,26},{2,25},{3,27},{4,29},{5,31},{6,28},{7,30},{8,16},{9,... | collective-permute-start | bytes 786440 | tf_op jit(solution)/shard_map/ppermute | solution.py:24
  22.2 29.1 %collective-permute-start.2 = (bf16[2,256,256]{2,1,0:T(8,128)(2,1)S(1)}, bf16[2,256,256]{2,1,0:T(8,128)(2,1)S(1)}, u32[]{:S(2)}, u32[]{:S(2)}) collective-permute-start(bf16[2,256,256]{2,1,0:T(8,128)(2,1)S(1)} %collective-permute-done), channel_id=1, source_target_pairs={{0,16},{8,24},{16,0},{24,8},{1,17},{9,25},{17,1},{25,9},{2,18},{10... | collective-permute-start | bytes 786440 | tf_op jit(solution)/shard_map/ppermute | solution.py:24
  36.7 16.6 %collective-permute-start.3 = (bf16[2,256,256]{2,1,0:T(8,128)(2,1)S(1)}, bf16[2,256,256]{2,1,0:T(8,128)(2,1)S(1)}, u32[]{:S(2)}, u32[]{:S(2)}) collective-permute-start(bf16[2,256,256]{2,1,0:T(8,128)(2,1)S(1)} %constant_dynamic-slice_fusion), channel_id=1, source_target_pairs={{0,8},{1,10},{2,9},{3,11},{4,13},{5,15},{6,12},{7,14},{8,0},{9,2},... | collective-permute-start | bytes 786440 | tf_op jit(solution)/shard_map/ppermute | solution.py:24
  41.3 15.0 %collective-permute-start.4 = (bf16[4,256,256]{2,1,0:T(8,128)(2,1)S(1)}, bf16[4,256,256]{2,1,0:T(8,128)(2,1)}, u32[]{:S(2)}, u32[]{:S(2)}) collective-permute-start(bf16[4,256,256]{2,1,0:T(8,128)(2,1)S(1)} %constant_dynamic-update-slice_fusion.own_a), channel_id=1, source_target_pairs={{0,4},{4,0},{1,5},{5,1},{2,6},{6,2},{3,7},{7,3},{8,12},{12,8},{9,1... | collective-permute-start | bytes 1572872 | tf_op jit(solution)/shard_map/ppermute | solution.py:24
  53.3 4.5 %collective-permute-start.5 = (bf16[4,256,256]{2,1,0:T(8,128)(2,1)S(1)}, bf16[4,256,256]{2,1,0:T(8,128)(2,1)}, u32[]{:S(2)}, u32[]{:S(2)}) collective-permute-start(bf16[4,256,256]{2,1,0:T(8,128)(2,1)S(1)} %constant_dynamic-update-slice_fusion.2.own_b), channel_id=1, source_target_pairs={{0,4},{4,0},{1,5},{5,1},{2,6},{6,2},{3,7},{7,3},{8,12},{12,8},{9,1... | collective-permute-start | bytes 1572872 | tf_op jit(solution)/shard_map/ppermute | solution.py:24
  66.6 0.8 copy-start
  79.6 1.0 %copy-start.1 = (f32[4,256,128]{2,1,0:T(8,128)S(1)}, f32[4,256,128]{2,1,0:T(8,128)}, u32[]{:S(2)}) copy-start(f32[4,256,128]{2,1,0:T(8,128)} %copy-done) | copy-start | bytes 1572868
  81.5 11.5 %all-to-all-start.2 = ((f32[4,256,128]{2,1,0:T(8,128)}), f32[4,256,128]{2,1,0:T(8,128)S(1)}, u32[]{:S(2)}, u32[]{:S(2)}) async-start(f32[4,256,128]{2,1,0:T(8,128)} %shard_map.29), calls=%async_computation.2 | async-start | bytes 1048576 | tf_op jit(solution)/shard_map/all_to_all | solution.py:90
  84.9 12.2 %collective-permute-start.6 = (f32[256,128]{1,0:T(8,128)S(1)}, f32[256,128]{1,0:T(8,128)S(1)}, u32[]{:S(2)}, u32[]{:S(2)}) collective-permute-start(f32[256,128]{1,0:T(8,128)S(1)} %reduce_sum.18.first_ref), channel_id=1, source_target_pairs={{0,256},{256,0},{1,257},{257,1},{2,258},{258,2},{3,259},{259,3},{4... | collective-permute-start | bytes 393224 | tf_op jit(solution)/shard_map/ppermute | solution.py:24

commit v13 on v10

--- a/solution.py
+++ b/solution.py
@@ -36,24 +36,41 @@
     return moved(value, ("core",), lambda core: {"core": 1 - core})
 
 
+def copies_kernel(tile_ref, out_ref, sems):
+    copies = [pltpu.make_async_copy(tile_ref, out_ref.at[i], sems.at[i]) for i in range(8)]
+    for copy in copies:
+        copy.start()
+    for copy in copies:
+        copy.wait()
+
+
+def copies_of(tile):
+    return pl.pallas_call(
+        copies_kernel,
+        out_shape=jax.ShapeDtypeStruct((8,) + tile.shape, tile.dtype),
+        in_specs=[pl.BlockSpec(memory_space=pl.ANY)],
+        out_specs=pl.BlockSpec(memory_space=pl.ANY),
+        scratch_shapes=[pltpu.SemaphoreType.DMA((8,))],
+    )(tile)
+
+
 def product_kernel(place, own_a, own_b, other_a, other_b, t_ref, out_ref):
-    for unit in range(8):
-        t = t_ref[unit]
-        same = place[5 * unit] == 1
-        for rel in range(2):
+    t = t_ref[...].reshape(8 * UNIT, t_ref.shape[2])
+    for rel in range(2):
+        blocks = []
+        for unit in range(8):
+            same = place[5 * unit] == 1
             first, slot = place[5 * unit + 1 + 2 * rel] == 1, place[5 * unit + 2 + 2 * rel]
-            w = jnp.where(
-                same,
-                jnp.where(first, own_a[slot], own_b[slot]),
-                jnp.where(first, other_a[slot], other_b[slot]),
+            blocks.append(
+                jnp.where(
+                    same,
+                    jnp.where(first, own_a[slot], own_b[slot]),
+                    jnp.where(first, other_a[slot], other_b[slot]),
+                )
             )
-            part = jnp.dot(w, t, preferred_element_type=jnp.float32)
-            for block in range(4):
-                cols = part[:, block * 128 : (block + 1) * 128]
-                if unit == 0:
-                    out_ref[block, rel] = cols
-                else:
-                    out_ref[block, rel] += cols
+        part = jnp.dot(jnp.concatenate(blocks, axis=1), t, preferred_element_type=jnp.float32)
+        for block in range(4):
+            out_ref[block, rel] = part[:, block * 128 : (block + 1) * 128]
 
 
 def product(place, *operands):
@@ -69,8 +86,7 @@
 
 def per_device(integrals, amplitudes):
     yh, z, yl, core, x = (lax.axis_index(a) for a in AXES)
-    copies = jnp.broadcast_to(amplitudes[None], (8,) + amplitudes.shape)
-    tiles = lax.all_to_all(copies, "z", split_axis=0, concat_axis=0, tiled=True)
+    tiles = lax.all_to_all(copies_of(amplitudes), "z", split_axis=0, concat_axis=0, tiled=True)
     both = lax.all_gather(integrals, "core", axis=0)
     half = lax.dynamic_slice_in_dim(both, ((x >> 1) ^ core) * UNIT, UNIT, 2)
     slabs = {mask: spread(half, mask) for mask in (0, 3, 1)}

time: 96.2 us -> 158 us (1.64)
  Pallas kernels: 2.46 us -> 67.1 us
  local copies, waits for them, and re-layouts: 2.7 us -> 0.23 us
    pallas_call x0 -> x1, Pallas kernels: none -> 64.7 us  [copies_of(): pl.pallas_call(copies_kernel, out_shape=jax.ShapeDtypeStruct((8,) + tile....]
    broadcast_in_dim x1 -> x0, local copies, waits for them, and re-layouts: 2.48 us -> none  [per_device(): copies = jnp.broadcast_to(amplitudes[None], (8,) + amplitudes.shape)]
where the time goes in v13:
time: 158 us
  Pallas kernels  67.1 us (42%)
  starting transfers between devices  46.6 us (29%)
  waiting for transfers between devices  24.7 us (16%)
  blocking collectives  18.3 us (12%)
    pallas_call x1, Pallas kernels, copies_of(): pl.pallas_call(copies_kernel, out_shape=jax.ShapeDtypeStruct((8,) + tile....  64.7 us
    ppermute x7, starting transfers between devices, moved(): return lax.ppermute(value, axes, perm)  36.1 us
    ppermute x7, waiting for transfers between devices, moved(): return lax.ppermute(value, axes, perm)  18.4 us
    all_to_all x1, blocking collectives, per_device(): lax.all_to_all(part, 'x', split_axis=0, concat_axis=0, tiled=True)  16.1 us
    all_to_all x1, starting transfers between devices, per_device(): lax.all_to_all(copies_of(amplitudes), 'z', split_axis=0, concat_axis=0, t...  10.5 us
    all_to_all x1, waiting for transfers between devices, per_device(): lax.all_to_all(copies_of(amplitudes), 'z', split_axis=0, concat_axis=0, t...  6.31 us
  transfers between devices with their start and end apart: 8, of which 5 were waited for; matrix products, arithmetic and copies ran while one was open for 0% of the time, Pallas kernels for 0%

profile of v13, /device:TPU:56, one launch (start us, length us, event | category | flops | bytes accessed | tf_op | source)
XLA Modules:
  0.0 157.9 jit_solution(9158837705730109775)
XLA Ops:
  0.0 64.7 %shard_map.28 = bf16[8,256,512]{2,1,0:T(8,128)(2,1)} custom-call(bf16[256,512]{1,0:T(8,128)(2,1)} %tile_ref.1), custom_call_target="tpu_custom_call" | custom-call | tf_op jit(solution)/shard_map/pallas_call | solution.py:48
  64.7 0.0 copy-start
  64.7 10.5 %all-to-all-start = ((bf16[8,256,512]{2,1,0:T(8,128)(2,1)}), bf16[8,256,512]{2,1,0:T(8,128)(2,1)S(1)}, u32[]{:S(2)}, u32[]{:S(2)}) async-start(bf16[8,256,512]{2,1,0:T(8,128)(2,1)} %shard_map.28), calls=%async_computation | async-start | bytes 4194304 | tf_op jit(solution)/shard_map/all_to_all | solution.py:89
  75.2 0.0 copy-done
  75.2 2.2 %all-gather = bf16[512,512]{1,0:T(8,128)(2,1)S(1)} all-gather(bf16[256,512]{1,0:T(8,128)(2,1)S(1)} %copy-done), channel_id=2, replica_groups=mesh['yh'=2,'z'=8,'yl'=4,'core'=2,'x'=4] {'core'}, dimensions={0}, use_global_device_ids=true | all-gather | bytes 786432 | tf_op jit(solution)/shard_map/all_gather | solution.py:90
  77.4 0.7 collective-permute-start
  78.1 6.4 %collective-permute-start.1 = (bf16[2,256,256]{2,1,0:T(8,128)(2,1)S(1)}, bf16[2,256,256]{2,1,0:T(8,128)(2,1)S(1)}, u32[]{:S(2)}, u32[]{:S(2)}) collective-permute-start(bf16[2,256,256]{2,1,0:T(8,128)(2,1)S(1)} %constant_dynamic-slice_fusion), channel_id=1, source_target_pairs={{0,24},{1,26},{2,25},{3,27},{4,29},{5,31},{6,28},{7,30},{8,16},{9,... | collective-permute-start | bytes 786440 | tf_op jit(solution)/shard_map/ppermute | solution.py:24
  84.5 0.0 collective-permute-done
  84.5 14.5 %collective-permute-start.2 = (bf16[2,256,256]{2,1,0:T(8,128)(2,1)S(1)}, bf16[2,256,256]{2,1,0:T(8,128)(2,1)S(1)}, u32[]{:S(2)}, u32[]{:S(2)}) collective-permute-start(bf16[2,256,256]{2,1,0:T(8,128)(2,1)S(1)} %collective-permute-done), channel_id=1, source_target_pairs={{0,16},{8,24},{16,0},{24,8},{1,17},{9,25},{17,1},{25,9},{2,18},{10... | collective-permute-start | bytes 786440 | tf_op jit(solution)/shard_map/ppermute | solution.py:24
  99.0 4.6 %collective-permute-start.3 = (bf16[2,256,256]{2,1,0:T(8,128)(2,1)S(1)}, bf16[2,256,256]{2,1,0:T(8,128)(2,1)S(1)}, u32[]{:S(2)}, u32[]{:S(2)}) collective-permute-start(bf16[2,256,256]{2,1,0:T(8,128)(2,1)S(1)} %constant_dynamic-slice_fusion), channel_id=1, source_target_pairs={{0,8},{1,10},{2,9},{3,11},{4,13},{5,15},{6,12},{7,14},{8,0},{9,2},... | collective-permute-start | bytes 786440 | tf_op jit(solution)/shard_map/ppermute | solution.py:24
  103.6 0.0 collective-permute-done.1
  103.6 2.4 %collective-permute-start.4 = (bf16[4,256,256]{2,1,0:T(8,128)(2,1)S(1)}, bf16[4,256,256]{2,1,0:T(8,128)(2,1)}, u32[]{:S(2)}, u32[]{:S(2)}) collective-permute-start(bf16[4,256,256]{2,1,0:T(8,128)(2,1)S(1)} %constant_dynamic-update-slice_fusion.own_a), channel_id=1, source_target_pairs={{0,4},{4,0},{1,5},{5,1},{2,6},{6,2},{3,7},{7,3},{8,12},{12,8},{9,1... | collective-permute-start | bytes 1572872 | tf_op jit(solution)/shard_map/ppermute | solution.py:24
  106.0 7.5 %collective-permute-done.2 = bf16[2,256,256]{2,1,0:T(8,128)(2,1)S(1)} collective-permute-done((bf16[2,256,256]{2,1,0:T(8,128)(2,1)S(1)}, bf16[2,256,256]{2,1,0:T(8,128)(2,1)S(1)}, u32[]{:S(2)}, u32[]{:S(2)}) %collective-permute-start.2) | collective-permute-done | bytes 262176 | tf_op jit(solution)/shard_map/ppermute | solution.py:24
  113.6 2.0 %collective-permute-done.3 = bf16[2,256,256]{2,1,0:T(8,128)(2,1)S(1)} collective-permute-done((bf16[2,256,256]{2,1,0:T(8,128)(2,1)S(1)}, bf16[2,256,256]{2,1,0:T(8,128)(2,1)S(1)}, u32[]{:S(2)}, u32[]{:S(2)}) %collective-permute-start.3) | collective-permute-done | bytes 262176 | tf_op jit(solution)/shard_map/ppermute | solution.py:24
  115.5 2.9 %collective-permute-start.5 = (bf16[4,256,256]{2,1,0:T(8,128)(2,1)S(1)}, bf16[4,256,256]{2,1,0:T(8,128)(2,1)}, u32[]{:S(2)}, u32[]{:S(2)}) collective-permute-start(bf16[4,256,256]{2,1,0:T(8,128)(2,1)S(1)} %constant_dynamic-update-slice_fusion.2.own_b), channel_id=1, source_target_pairs={{0,4},{4,0},{1,5},{5,1},{2,6},{6,2},{3,7},{7,3},{8,12},{12,8},{9,1... | collective-permute-start | bytes 1572872 | tf_op jit(solution)/shard_map/ppermute | solution.py:24
  118.5 0.1 stack.85.place
  118.6 0.0 collective-permute-done.4.other_a
  118.6 1.5 collective-permute-done.5.other_b
  120.1 6.3 %all-to-all-done.t_ref = bf16[8,256,512]{2,1,0:T(8,128)(2,1)S(1)} async-done(((bf16[8,256,512]{2,1,0:T(8,128)(2,1)}), bf16[8,256,512]{2,1,0:T(8,128)(2,1)S(1)}, u32[]{:S(2)}, u32[]{:S(2)}) %all-to-all-start) | async-done | bytes 2097184 | tf_op jit(solution)/shard_map/all_to_all | solution.py:89
  126.4 2.4 %shard_map.29 = f32[4,2,256,128]{3,2,1,0:T(8,128)S(1)} custom-call(s32[40]{0:T(128)S(1)} %stack.85.place, bf16[4,256,256]{2,1,0:T(8,128)(2,1)S(1)} %constant_dynamic-update-slice_fusion.own_a, bf16[4,256,256]{2,1,0:T(8,128)(2,1)S(1)} %constant_dynamic-update-slice_fusion.2.own_b, bf16[4,256,256]{2,1,0:T(8,128)(2,1)} %collective-permute-done.4.other_a, ...), custom_call_target="tpu_custom_call" | custom-call | tf_op jit(solution)/shard_map/pallas_call | solution.py:78
  128.8 16.1 %all_to_all.10 = f32[4,2,256,128]{3,2,1,0:T(8,128)S(1)} all-to-all(f32[4,2,256,128]{3,2,1,0:T(8,128)S(1)} %shard_map.29), channel_id=1, replica_groups=mesh['yh'=2,'z'=8,'yl'=4,'core'=2,'x'=4] {'x'}, dimensions={0} | all-to-all | bytes 2097152 | tf_op jit(solution)/shard_map/all_to_all | solution.py:106
  145.0 0.1 reduce_sum.9
  145.1 4.7 %collective-permute-start.6 = (f32[256,128]{1,0:T(8,128)S(1)}, f32[256,128]{1,0:T(8,128)S(1)}, u32[]{:S(2)}, u32[]{:S(2)}) collective-permute-start(f32[256,128]{1,0:T(8,128)S(1)} %slice_bitcast_fusion), channel_id=1, source_target_pairs={{0,256},{256,0},{1,257},{257,1},{2,258},{258,2},{3,259},{259,3},{4... | collective-permute-start | bytes 393224 | tf_op jit(solution)/shard_map/ppermute | solution.py:24
  149.8 7.5 %collective-permute-done.6 = f32[256,128]{1,0:T(8,128)S(1)} collective-permute-done((f32[256,128]{1,0:T(8,128)S(1)}, f32[256,128]{1,0:T(8,128)S(1)}, u32[]{:S(2)}, u32[]{:S(2)}) %collective-permute-start.6) | collective-permute-done | bytes 131104 | tf_op jit(solution)/shard_map/ppermute | solution.py:24
  157.2 0.7 fusion
  (6 shorter events, 0.1 us)
Async XLA Ops:
  64.7 10.5 %copy-start = (bf16[256,512]{1,0:T(8,128)(2,1)S(1)}, bf16[256,512]{1,0:T(8,128)(2,1)}, u32[]{:S(2)}) copy-start(bf16[256,512]{1,0:T(8,128)(2,1)} %param.2) | copy-start | bytes 786436
  64.7 61.7 %all-to-all-start = ((bf16[8,256,512]{2,1,0:T(8,128)(2,1)}), bf16[8,256,512]{2,1,0:T(8,128)(2,1)S(1)}, u32[]{:S(2)}, u32[]{:S(2)}) async-start(bf16[8,256,512]{2,1,0:T(8,128)(2,1)} %shard_map.28), calls=%async_computation | async-start | bytes 4194304 | tf_op jit(solution)/shard_map/all_to_all | solution.py:89
  77.4 7.1 %collective-permute-start = (bf16[2,256,256]{2,1,0:T(8,128)(2,1)S(1)}, bf16[2,256,256]{2,1,0:T(8,128)(2,1)S(1)}, u32[]{:S(2)}, u32[]{:S(2)}) collective-permute-start(bf16[2,256,256]{2,1,0:T(8,128)(2,1)S(1)} %constant_dynamic-slice_fusion), channel_id=1, source_target_pairs={{0,0},{1,2},{2,1},{3,3},{4,5},{5,7},{6,4},{7,6},{8,8},{9,10},{10,9... | collective-permute-start | bytes 786440 | tf_op jit(solution)/shard_map/ppermute | solution.py:24
  78.1 25.5 %collective-permute-start.1 = (bf16[2,256,256]{2,1,0:T(8,128)(2,1)S(1)}, bf16[2,256,256]{2,1,0:T(8,128)(2,1)S(1)}, u32[]{:S(2)}, u32[]{:S(2)}) collective-permute-start(bf16[2,256,256]{2,1,0:T(8,128)(2,1)S(1)} %constant_dynamic-slice_fusion), channel_id=1, source_target_pairs={{0,24},{1,26},{2,25},{3,27},{4,29},{5,31},{6,28},{7,30},{8,16},{9,... | collective-permute-start | bytes 786440 | tf_op jit(solution)/shard_map/ppermute | solution.py:24
  84.5 29.1 %collective-permute-start.2 = (bf16[2,256,256]{2,1,0:T(8,128)(2,1)S(1)}, bf16[2,256,256]{2,1,0:T(8,128)(2,1)S(1)}, u32[]{:S(2)}, u32[]{:S(2)}) collective-permute-start(bf16[2,256,256]{2,1,0:T(8,128)(2,1)S(1)} %collective-permute-done), channel_id=1, source_target_pairs={{0,16},{8,24},{16,0},{24,8},{1,17},{9,25},{17,1},{25,9},{2,18},{10... | collective-permute-start | bytes 786440 | tf_op jit(solution)/shard_map/ppermute | solution.py:24
  99.0 16.6 %collective-permute-start.3 = (bf16[2,256,256]{2,1,0:T(8,128)(2,1)S(1)}, bf16[2,256,256]{2,1,0:T(8,128)(2,1)S(1)}, u32[]{:S(2)}, u32[]{:S(2)}) collective-permute-start(bf16[2,256,256]{2,1,0:T(8,128)(2,1)S(1)} %constant_dynamic-slice_fusion), channel_id=1, source_target_pairs={{0,8},{1,10},{2,9},{3,11},{4,13},{5,15},{6,12},{7,14},{8,0},{9,2},... | collective-permute-start | bytes 786440 | tf_op jit(solution)/shard_map/ppermute | solution.py:24
  103.6 15.0 %collective-permute-start.4 = (bf16[4,256,256]{2,1,0:T(8,128)(2,1)S(1)}, bf16[4,256,256]{2,1,0:T(8,128)(2,1)}, u32[]{:S(2)}, u32[]{:S(2)}) collective-permute-start(bf16[4,256,256]{2,1,0:T(8,128)(2,1)S(1)} %constant_dynamic-update-slice_fusion.own_a), channel_id=1, source_target_pairs={{0,4},{4,0},{1,5},{5,1},{2,6},{6,2},{3,7},{7,3},{8,12},{12,8},{9,1... | collective-permute-start | bytes 1572872 | tf_op jit(solution)/shard_map/ppermute | solution.py:24
  115.5 4.5 %collective-permute-start.5 = (bf16[4,256,256]{2,1,0:T(8,128)(2,1)S(1)}, bf16[4,256,256]{2,1,0:T(8,128)(2,1)}, u32[]{:S(2)}, u32[]{:S(2)}) collective-permute-start(bf16[4,256,256]{2,1,0:T(8,128)(2,1)S(1)} %constant_dynamic-update-slice_fusion.2.own_b), channel_id=1, source_target_pairs={{0,4},{4,0},{1,5},{5,1},{2,6},{6,2},{3,7},{7,3},{8,12},{12,8},{9,1... | collective-permute-start | bytes 1572872 | tf_op jit(solution)/shard_map/ppermute | solution.py:24
  145.1 12.2 %collective-permute-start.6 = (f32[256,128]{1,0:T(8,128)S(1)}, f32[256,128]{1,0:T(8,128)S(1)}, u32[]{:S(2)}, u32[]{:S(2)}) collective-permute-start(f32[256,128]{1,0:T(8,128)S(1)} %slice_bitcast_fusion), channel_id=1, source_target_pairs={{0,256},{256,0},{1,257},{257,1},{2,258},{258,2},{3,259},{259,3},{4... | collective-permute-start | bytes 393224 | tf_op jit(solution)/shard_map/ppermute | solution.py:24

commit v14 on v13

--- a/solution.py
+++ b/solution.py
@@ -48,9 +48,10 @@
     return pl.pallas_call(
         copies_kernel,
         out_shape=jax.ShapeDtypeStruct((8,) + tile.shape, tile.dtype),
-        in_specs=[pl.BlockSpec(memory_space=pl.ANY)],
+        in_specs=[pl.BlockSpec(memory_space=pltpu.VMEM)],
         out_specs=pl.BlockSpec(memory_space=pl.ANY),
         scratch_shapes=[pltpu.SemaphoreType.DMA((8,))],
+        compiler_params=pltpu.CompilerParams(vmem_limit_bytes=16 * 1024 * 1024),
     )(tile)
 
 
@@ -80,7 +81,7 @@
         out_shape=jax.ShapeDtypeStruct((4, 2, UNIT, 128), jnp.float32),
         in_specs=[pl.BlockSpec(memory_space=pltpu.SMEM)] + [vmem] * len(operands),
         out_specs=vmem,
-        compiler_params=pltpu.CompilerParams(vmem_limit_bytes=40 * 1024 * 1024),
+        compiler_params=pltpu.CompilerParams(vmem_limit_bytes=16 * 1024 * 1024),
     )(place, *operands)
 
 

time: 158 us -> 96.2 us (0.61)
  Pallas kernels: 67.1 us -> 2.67 us
  local copies, waits for them, and re-layouts: 0.23 us -> 2.51 us
    pallas_call x1, Pallas kernels: 64.7 us -> 0.23 us  [copies_of(): pl.pallas_call(copies_kernel, out_shape=jax.ShapeDtypeStruct((8,) + tile....]
    unnamed x4 -> x8, local copies, waits for them, and re-layouts: 0.04 us -> 2.32 us
where the time goes in v14:
time: 96.2 us; the launch traced here: 95.7 us
  starting transfers between devices  46.6 us (48%)
  waiting for transfers between devices  24.7 us (26%)
  blocking collectives  18.3 us (19%)
  Pallas kernels  2.67 us (3%)
  local copies, waits for them, and re-layouts  2.51 us (3%)
    ppermute x7, starting transfers between devices, moved(): return lax.ppermute(value, axes, perm)  36.1 us
    ppermute x7, waiting for transfers between devices, moved(): return lax.ppermute(value, axes, perm)  18.4 us
    all_to_all x1, blocking collectives, per_device(): lax.all_to_all(part, 'x', split_axis=0, concat_axis=0, tiled=True)  16.1 us
    all_to_all x1, starting transfers between devices, per_device(): lax.all_to_all(copies_of(amplitudes), 'z', split_axis=0, concat_axis=0, t...  10.4 us
    all_to_all x1, waiting for transfers between devices, per_device(): lax.all_to_all(copies_of(amplitudes), 'z', split_axis=0, concat_axis=0, t...  6.31 us
    pallas_call x1, Pallas kernels, product(): pl.pallas_call(product_kernel, out_shape=jax.ShapeDtypeStruct((4, 2, UNIT...  2.45 us
    unnamed x8, local copies, waits for them, and re-layouts  2.32 us
    all_gather x1, blocking collectives, per_device(): both = lax.all_gather(integrals, 'core', axis=0)  2.18 us
  transfers between devices with their start and end apart: 8, of which 5 were waited for; matrix products, arithmetic and copies ran while one was open for 0% of the time, Pallas kernels for 0%

profile of v14, /device:TPU:56, one launch (start us, length us, event | category | flops | bytes accessed | tf_op | source)
XLA Modules:
  0.0 95.7 jit_solution(12806949795484954392)
XLA Ops:
  0.0 0.0 copy-start.1
  0.0 0.9 copy-done.1
  1.0 0.2 shard_map.28
  1.2 0.0 copy-start
  1.2 1.3 %copy-done = bf16[8,256,512]{2,1,0:T(8,128)(2,1)} copy-done((bf16[8,256,512]{2,1,0:T(8,128)(2,1)}, bf16[8,256,512]{2,1,0:T(8,128)(2,1)S(1)}, u32[]{:S(2)}) %copy-start) | copy-done | bytes 2097176
  2.5 0.0 copy-start.2
  2.5 10.4 %all-to-all-start = ((bf16[8,256,512]{2,1,0:T(8,128)(2,1)}), bf16[8,256,512]{2,1,0:T(8,128)(2,1)S(1)}, u32[]{:S(2)}, u32[]{:S(2)}) async-start(bf16[8,256,512]{2,1,0:T(8,128)(2,1)} %copy-done), calls=%async_computation | async-start | bytes 4194304 | tf_op jit(solution)/shard_map/all_to_all | solution.py:90
  13.0 0.0 copy-done.2
  13.0 2.2 %all-gather = bf16[512,512]{1,0:T(8,128)(2,1)S(1)} all-gather(bf16[256,512]{1,0:T(8,128)(2,1)S(1)} %copy-done.2), channel_id=2, replica_groups=mesh['yh'=2,'z'=8,'yl'=4,'core'=2,'x'=4] {'core'}, dimensions={0}, use_global_device_ids=true | all-gather | bytes 786432 | tf_op jit(solution)/shard_map/all_gather | solution.py:91
  15.2 0.7 collective-permute-start
  15.9 6.4 %collective-permute-start.1 = (bf16[2,256,256]{2,1,0:T(8,128)(2,1)S(1)}, bf16[2,256,256]{2,1,0:T(8,128)(2,1)S(1)}, u32[]{:S(2)}, u32[]{:S(2)}) collective-permute-start(bf16[2,256,256]{2,1,0:T(8,128)(2,1)S(1)} %constant_dynamic-slice_fusion), channel_id=1, source_target_pairs={{0,24},{1,26},{2,25},{3,27},{4,29},{5,31},{6,28},{7,30},{8,16},{9,... | collective-permute-start | bytes 786440 | tf_op jit(solution)/shard_map/ppermute | solution.py:24
  22.3 0.0 collective-permute-done
  22.3 14.5 %collective-permute-start.2 = (bf16[2,256,256]{2,1,0:T(8,128)(2,1)S(1)}, bf16[2,256,256]{2,1,0:T(8,128)(2,1)S(1)}, u32[]{:S(2)}, u32[]{:S(2)}) collective-permute-start(bf16[2,256,256]{2,1,0:T(8,128)(2,1)S(1)} %collective-permute-done), channel_id=1, source_target_pairs={{0,16},{8,24},{16,0},{24,8},{1,17},{9,25},{17,1},{25,9},{2,18},{10... | collective-permute-start | bytes 786440 | tf_op jit(solution)/shard_map/ppermute | solution.py:24
  36.8 4.6 %collective-permute-start.3 = (bf16[2,256,256]{2,1,0:T(8,128)(2,1)S(1)}, bf16[2,256,256]{2,1,0:T(8,128)(2,1)S(1)}, u32[]{:S(2)}, u32[]{:S(2)}) collective-permute-start(bf16[2,256,256]{2,1,0:T(8,128)(2,1)S(1)} %constant_dynamic-slice_fusion), channel_id=1, source_target_pairs={{0,8},{1,10},{2,9},{3,11},{4,13},{5,15},{6,12},{7,14},{8,0},{9,2},... | collective-permute-start | bytes 786440 | tf_op jit(solution)/shard_map/ppermute | solution.py:24
  41.4 0.0 collective-permute-done.1
  41.4 2.4 %collective-permute-start.4 = (bf16[4,256,256]{2,1,0:T(8,128)(2,1)S(1)}, bf16[4,256,256]{2,1,0:T(8,128)(2,1)}, u32[]{:S(2)}, u32[]{:S(2)}) collective-permute-start(bf16[4,256,256]{2,1,0:T(8,128)(2,1)S(1)} %constant_dynamic-update-slice_fusion.own_a), channel_id=1, source_target_pairs={{0,4},{4,0},{1,5},{5,1},{2,6},{6,2},{3,7},{7,3},{8,12},{12,8},{9,1... | collective-permute-start | bytes 1572872 | tf_op jit(solution)/shard_map/ppermute | solution.py:24
  43.8 7.5 %collective-permute-done.2 = bf16[2,256,256]{2,1,0:T(8,128)(2,1)S(1)} collective-permute-done((bf16[2,256,256]{2,1,0:T(8,128)(2,1)S(1)}, bf16[2,256,256]{2,1,0:T(8,128)(2,1)S(1)}, u32[]{:S(2)}, u32[]{:S(2)}) %collective-permute-start.2) | collective-permute-done | bytes 262176 | tf_op jit(solution)/shard_map/ppermute | solution.py:24
  51.4 2.0 %collective-permute-done.3 = bf16[2,256,256]{2,1,0:T(8,128)(2,1)S(1)} collective-permute-done((bf16[2,256,256]{2,1,0:T(8,128)(2,1)S(1)}, bf16[2,256,256]{2,1,0:T(8,128)(2,1)S(1)}, u32[]{:S(2)}, u32[]{:S(2)}) %collective-permute-start.3) | collective-permute-done | bytes 262176 | tf_op jit(solution)/shard_map/ppermute | solution.py:24
  53.3 2.9 %collective-permute-start.5 = (bf16[4,256,256]{2,1,0:T(8,128)(2,1)S(1)}, bf16[4,256,256]{2,1,0:T(8,128)(2,1)}, u32[]{:S(2)}, u32[]{:S(2)}) collective-permute-start(bf16[4,256,256]{2,1,0:T(8,128)(2,1)S(1)} %constant_dynamic-update-slice_fusion.2.own_b), channel_id=1, source_target_pairs={{0,4},{4,0},{1,5},{5,1},{2,6},{6,2},{3,7},{7,3},{8,12},{12,8},{9,1... | collective-permute-start | bytes 1572872 | tf_op jit(solution)/shard_map/ppermute | solution.py:24
  56.3 0.1 stack.85.place
  56.4 0.0 collective-permute-done.4.other_a
  56.4 1.5 %collective-permute-done.5.other_b = bf16[4,256,256]{2,1,0:T(8,128)(2,1)} collective-permute-done((bf16[4,256,256]{2,1,0:T(8,128)(2,1)S(1)}, bf16[4,256,256]{2,1,0:T(8,128)(2,1)}, u32[]{:S(2)}, u32[]{:S(2)}) %collective-permute-start.5) | collective-permute-done | bytes 524320 | tf_op jit(solution)/shard_map/ppermute | solution.py:24
  57.9 6.3 %all-to-all-done.t_ref = bf16[8,256,512]{2,1,0:T(8,128)(2,1)S(1)} async-done(((bf16[8,256,512]{2,1,0:T(8,128)(2,1)}), bf16[8,256,512]{2,1,0:T(8,128)(2,1)S(1)}, u32[]{:S(2)}, u32[]{:S(2)}) %all-to-all-start) | async-done | bytes 2097184 | tf_op jit(solution)/shard_map/all_to_all | solution.py:90
  64.2 2.4 %shard_map.29 = f32[4,2,256,128]{3,2,1,0:T(8,128)S(1)} custom-call(s32[40]{0:T(128)S(1)} %stack.85.place, bf16[4,256,256]{2,1,0:T(8,128)(2,1)S(1)} %constant_dynamic-update-slice_fusion.own_a, bf16[4,256,256]{2,1,0:T(8,128)(2,1)S(1)} %constant_dynamic-update-slice_fusion.2.own_b, bf16[4,256,256]{2,1,0:T(8,128)(2,1)} %collective-permute-done.4.other_a, ...), custom_call_target="tpu_custom_call" | custom-call | tf_op jit(solution)/shard_map/pallas_call | solution.py:79
  66.6 16.1 %all_to_all.10 = f32[4,2,256,128]{3,2,1,0:T(8,128)S(1)} all-to-all(f32[4,2,256,128]{3,2,1,0:T(8,128)S(1)} %shard_map.29), channel_id=1, replica_groups=mesh['yh'=2,'z'=8,'yl'=4,'core'=2,'x'=4] {'x'}, dimensions={0} | all-to-all | bytes 2097152 | tf_op jit(solution)/shard_map/all_to_all | solution.py:107
  82.8 0.1 reduce_sum.9
  82.9 4.7 %collective-permute-start.6 = (f32[256,128]{1,0:T(8,128)S(1)}, f32[256,128]{1,0:T(8,128)S(1)}, u32[]{:S(2)}, u32[]{:S(2)}) collective-permute-start(f32[256,128]{1,0:T(8,128)S(1)} %slice_bitcast_fusion), channel_id=1, source_target_pairs={{0,256},{256,0},{1,257},{257,1},{2,258},{258,2},{3,259},{259,3},{4... | collective-permute-start | bytes 393224 | tf_op jit(solution)/shard_map/ppermute | solution.py:24
  87.6 7.5 %collective-permute-done.6 = f32[256,128]{1,0:T(8,128)S(1)} collective-permute-done((f32[256,128]{1,0:T(8,128)S(1)}, f32[256,128]{1,0:T(8,128)S(1)}, u32[]{:S(2)}, u32[]{:S(2)}) %collective-permute-start.6) | collective-permute-done | bytes 131104 | tf_op jit(solution)/shard_map/ppermute | solution.py:24
  95.0 0.7 fusion
  (6 shorter events, 0.1 us)
Async XLA Ops:
  0.0 0.9 copy-start.1
  1.2 1.3 %copy-start = (bf16[8,256,512]{2,1,0:T(8,128)(2,1)}, bf16[8,256,512]{2,1,0:T(8,128)(2,1)S(1)}, u32[]{:S(2)}) copy-start(bf16[8,256,512]{2,1,0:T(8,128)(2,1)S(1)} %shard_map.28) | copy-start | bytes 6291460
  2.5 10.5 %copy-start.2 = (bf16[256,512]{1,0:T(8,128)(2,1)S(1)}, bf16[256,512]{1,0:T(8,128)(2,1)}, u32[]{:S(2)}) copy-start(bf16[256,512]{1,0:T(8,128)(2,1)} %param.2) | copy-start | bytes 786436
  2.5 61.6 %all-to-all-start = ((bf16[8,256,512]{2,1,0:T(8,128)(2,1)}), bf16[8,256,512]{2,1,0:T(8,128)(2,1)S(1)}, u32[]{:S(2)}, u32[]{:S(2)}) async-start(bf16[8,256,512]{2,1,0:T(8,128)(2,1)} %copy-done), calls=%async_computation | async-start | bytes 4194304 | tf_op jit(solution)/shard_map/all_to_all | solution.py:90
  15.2 7.1 %collective-permute-start = (bf16[2,256,256]{2,1,0:T(8,128)(2,1)S(1)}, bf16[2,256,256]{2,1,0:T(8,128)(2,1)S(1)}, u32[]{:S(2)}, u32[]{:S(2)}) collective-permute-start(bf16[2,256,256]{2,1,0:T(8,128)(2,1)S(1)} %constant_dynamic-slice_fusion), channel_id=1, source_target_pairs={{0,0},{1,2},{2,1},{3,3},{4,5},{5,7},{6,4},{7,6},{8,8},{9,10},{10,9... | collective-permute-start | bytes 786440 | tf_op jit(solution)/shard_map/ppermute | solution.py:24
  15.9 25.5 %collective-permute-start.1 = (bf16[2,256,256]{2,1,0:T(8,128)(2,1)S(1)}, bf16[2,256,256]{2,1,0:T(8,128)(2,1)S(1)}, u32[]{:S(2)}, u32[]{:S(2)}) collective-permute-start(bf16[2,256,256]{2,1,0:T(8,128)(2,1)S(1)} %constant_dynamic-slice_fusion), channel_id=1, source_target_pairs={{0,24},{1,26},{2,25},{3,27},{4,29},{5,31},{6,28},{7,30},{8,16},{9,... | collective-permute-start | bytes 786440 | tf_op jit(solution)/shard_map/ppermute | solution.py:24
  22.3 29.1 %collective-permute-start.2 = (bf16[2,256,256]{2,1,0:T(8,128)(2,1)S(1)}, bf16[2,256,256]{2,1,0:T(8,128)(2,1)S(1)}, u32[]{:S(2)}, u32[]{:S(2)}) collective-permute-start(bf16[2,256,256]{2,1,0:T(8,128)(2,1)S(1)} %collective-permute-done), channel_id=1, source_target_pairs={{0,16},{8,24},{16,0},{24,8},{1,17},{9,25},{17,1},{25,9},{2,18},{10... | collective-permute-start | bytes 786440 | tf_op jit(solution)/shard_map/ppermute | solution.py:24
  36.8 16.6 %collective-permute-start.3 = (bf16[2,256,256]{2,1,0:T(8,128)(2,1)S(1)}, bf16[2,256,256]{2,1,0:T(8,128)(2,1)S(1)}, u32[]{:S(2)}, u32[]{:S(2)}) collective-permute-start(bf16[2,256,256]{2,1,0:T(8,128)(2,1)S(1)} %constant_dynamic-slice_fusion), channel_id=1, source_target_pairs={{0,8},{1,10},{2,9},{3,11},{4,13},{5,15},{6,12},{7,14},{8,0},{9,2},... | collective-permute-start | bytes 786440 | tf_op jit(solution)/shard_map/ppermute | solution.py:24
  41.4 15.0 %collective-permute-start.4 = (bf16[4,256,256]{2,1,0:T(8,128)(2,1)S(1)}, bf16[4,256,256]{2,1,0:T(8,128)(2,1)}, u32[]{:S(2)}, u32[]{:S(2)}) collective-permute-start(bf16[4,256,256]{2,1,0:T(8,128)(2,1)S(1)} %constant_dynamic-update-slice_fusion.own_a), channel_id=1, source_target_pairs={{0,4},{4,0},{1,5},{5,1},{2,6},{6,2},{3,7},{7,3},{8,12},{12,8},{9,1... | collective-permute-start | bytes 1572872 | tf_op jit(solution)/shard_map/ppermute | solution.py:24
  53.3 4.5 %collective-permute-start.5 = (bf16[4,256,256]{2,1,0:T(8,128)(2,1)S(1)}, bf16[4,256,256]{2,1,0:T(8,128)(2,1)}, u32[]{:S(2)}, u32[]{:S(2)}) collective-permute-start(bf16[4,256,256]{2,1,0:T(8,128)(2,1)S(1)} %constant_dynamic-update-slice_fusion.2.own_b), channel_id=1, source_target_pairs={{0,4},{4,0},{1,5},{5,1},{2,6},{6,2},{3,7},{7,3},{8,12},{12,8},{9,1... | collective-permute-start | bytes 1572872 | tf_op jit(solution)/shard_map/ppermute | solution.py:24
  82.9 12.2 %collective-permute-start.6 = (f32[256,128]{1,0:T(8,128)S(1)}, f32[256,128]{1,0:T(8,128)S(1)}, u32[]{:S(2)}, u32[]{:S(2)}) collective-permute-start(f32[256,128]{1,0:T(8,128)S(1)} %slice_bitcast_fusion), channel_id=1, source_target_pairs={{0,256},{256,0},{1,257},{257,1},{2,258},{258,2},{3,259},{259,3},{4... | collective-permute-start | bytes 393224 | tf_op jit(solution)/shard_map/ppermute | solution.py:24

commit v15 on v14

--- a/solution.py
+++ b/solution.py
@@ -36,22 +36,36 @@
     return moved(value, ("core",), lambda core: {"core": 1 - core})
 
 
-def copies_kernel(tile_ref, out_ref, sems):
-    copies = [pltpu.make_async_copy(tile_ref, out_ref.at[i], sems.at[i]) for i in range(8)]
-    for copy in copies:
-        copy.start()
-    for copy in copies:
-        copy.wait()
+def copies_kernel(tile_ref, out_ref, held, in_sems, out_sems):
+    rows = tile_ref.shape[0] // 4
+    reads = [
+        pltpu.make_async_copy(tile_ref.at[pl.ds(i * rows, rows)], held.at[pl.ds(i * rows, rows)], in_sems.at[i])
+        for i in range(4)
+    ]
+    for read in reads:
+        read.start()
+    writes = []
+    for i, read in enumerate(reads):
+        read.wait()
+        part = pl.ds(i * rows, rows)
+        for j in range(8):
+            writes.append(pltpu.make_async_copy(held.at[part], out_ref.at[j, part], out_sems.at[i, j]))
+            writes[-1].start()
+    for write in writes:
+        write.wait()
 
 
 def copies_of(tile):
     return pl.pallas_call(
         copies_kernel,
         out_shape=jax.ShapeDtypeStruct((8,) + tile.shape, tile.dtype),
-        in_specs=[pl.BlockSpec(memory_space=pltpu.VMEM)],
-        out_specs=pl.BlockSpec(memory_space=pl.ANY),
-        scratch_shapes=[pltpu.SemaphoreType.DMA((8,))],
-        compiler_params=pltpu.CompilerParams(vmem_limit_bytes=16 * 1024 * 1024),
+        in_specs=[pl.BlockSpec(memory_space=pltpu.HBM)],
+        out_specs=pl.BlockSpec(memory_space=pltpu.HBM),
+        scratch_shapes=[
+            pltpu.VMEM(tile.shape, tile.dtype),
+            pltpu.SemaphoreType.DMA((4,)),
+            pltpu.SemaphoreType.DMA((4, 8)),
+        ],
     )(tile)
 
 

time: 96.2 us -> 96.2 us (level)
  local copies, waits for them, and re-layouts: 2.51 us -> 0.23 us
  Pallas kernels: 2.67 us -> 4.92 us
    unnamed x8 -> x4, local copies, waits for them, and re-layouts: 2.32 us -> 0.04 us
    pallas_call x1, Pallas kernels: 0.23 us -> 2.47 us  [copies_of(): pl.pallas_call(copies_kernel, out_shape=jax.ShapeDtypeStruct((8,) + tile....]
where the time goes in v15:
time: 96.2 us; the launch traced here: 95.7 us
  starting transfers between devices  46.6 us (48%)
  waiting for transfers between devices  24.7 us (26%)
  blocking collectives  18.3 us (19%)
  Pallas kernels  4.92 us (5%)
    ppermute x7, starting transfers between devices, moved(): return lax.ppermute(value, axes, perm)  36.1 us
    ppermute x7, waiting for transfers between devices, moved(): return lax.ppermute(value, axes, perm)  18.4 us
    all_to_all x1, blocking collectives, per_device(): lax.all_to_all(part, 'x', split_axis=0, concat_axis=0, tiled=True)  16.1 us
    all_to_all x1, starting transfers between devices, per_device(): lax.all_to_all(copies_of(amplitudes), 'z', split_axis=0, concat_axis=0, t...  10.5 us
    all_to_all x1, waiting for transfers between devices, per_device(): lax.all_to_all(copies_of(amplitudes), 'z', split_axis=0, concat_axis=0, t...  6.31 us
    pallas_call x1, Pallas kernels, copies_of(): pl.pallas_call(copies_kernel, out_shape=jax.ShapeDtypeStruct((8,) + tile....  2.47 us
    pallas_call x1, Pallas kernels, product(): pl.pallas_call(product_kernel, out_shape=jax.ShapeDtypeStruct((4, 2, UNIT...  2.45 us
    all_gather x1, blocking collectives, per_device(): both = lax.all_gather(integrals, 'core', axis=0)  2.18 us
  transfers between devices with their start and end apart: 8, of which 5 were waited for; matrix products, arithmetic and copies ran while one was open for 0% of the time, Pallas kernels for 0%

profile of v15, /device:TPU:56, one launch (start us, length us, event | category | flops | bytes accessed | tf_op | source)
XLA Modules:
  0.0 95.7 jit_solution(9165791911048251459)
XLA Ops:
  0.0 2.5 %shard_map.28 = bf16[8,256,512]{2,1,0:T(8,128)(2,1)} custom-call(bf16[256,512]{1,0:T(8,128)(2,1)} %tile_ref.1), custom_call_target="tpu_custom_call" | custom-call | tf_op jit(solution)/shard_map/pallas_call | solution.py:59
  2.5 0.0 copy-start
  2.5 10.5 %all-to-all-start = ((bf16[8,256,512]{2,1,0:T(8,128)(2,1)}), bf16[8,256,512]{2,1,0:T(8,128)(2,1)S(1)}, u32[]{:S(2)}, u32[]{:S(2)}) async-start(bf16[8,256,512]{2,1,0:T(8,128)(2,1)} %shard_map.28), calls=%async_computation | async-start | bytes 4194304 | tf_op jit(solution)/shard_map/all_to_all | solution.py:104
  13.0 0.0 copy-done
  13.0 2.2 %all-gather = bf16[512,512]{1,0:T(8,128)(2,1)S(1)} all-gather(bf16[256,512]{1,0:T(8,128)(2,1)S(1)} %copy-done), channel_id=2, replica_groups=mesh['yh'=2,'z'=8,'yl'=4,'core'=2,'x'=4] {'core'}, dimensions={0}, use_global_device_ids=true | all-gather | bytes 786432 | tf_op jit(solution)/shard_map/all_gather | solution.py:105
  15.2 0.7 collective-permute-start
  15.8 6.4 %collective-permute-start.1 = (bf16[2,256,256]{2,1,0:T(8,128)(2,1)S(1)}, bf16[2,256,256]{2,1,0:T(8,128)(2,1)S(1)}, u32[]{:S(2)}, u32[]{:S(2)}) collective-permute-start(bf16[2,256,256]{2,1,0:T(8,128)(2,1)S(1)} %constant_dynamic-slice_fusion), channel_id=1, source_target_pairs={{0,24},{1,26},{2,25},{3,27},{4,29},{5,31},{6,28},{7,30},{8,16},{9,... | collective-permute-start | bytes 786440 | tf_op jit(solution)/shard_map/ppermute | solution.py:24
  22.2 0.0 collective-permute-done
  22.3 14.5 %collective-permute-start.2 = (bf16[2,256,256]{2,1,0:T(8,128)(2,1)S(1)}, bf16[2,256,256]{2,1,0:T(8,128)(2,1)S(1)}, u32[]{:S(2)}, u32[]{:S(2)}) collective-permute-start(bf16[2,256,256]{2,1,0:T(8,128)(2,1)S(1)} %collective-permute-done), channel_id=1, source_target_pairs={{0,16},{8,24},{16,0},{24,8},{1,17},{9,25},{17,1},{25,9},{2,18},{10... | collective-permute-start | bytes 786440 | tf_op jit(solution)/shard_map/ppermute | solution.py:24
  36.7 4.6 %collective-permute-start.3 = (bf16[2,256,256]{2,1,0:T(8,128)(2,1)S(1)}, bf16[2,256,256]{2,1,0:T(8,128)(2,1)S(1)}, u32[]{:S(2)}, u32[]{:S(2)}) collective-permute-start(bf16[2,256,256]{2,1,0:T(8,128)(2,1)S(1)} %constant_dynamic-slice_fusion), channel_id=1, source_target_pairs={{0,8},{1,10},{2,9},{3,11},{4,13},{5,15},{6,12},{7,14},{8,0},{9,2},... | collective-permute-start | bytes 786440 | tf_op jit(solution)/shard_map/ppermute | solution.py:24
  41.3 0.0 collective-permute-done.1
  41.4 2.4 %collective-permute-start.4 = (bf16[4,256,256]{2,1,0:T(8,128)(2,1)S(1)}, bf16[4,256,256]{2,1,0:T(8,128)(2,1)}, u32[]{:S(2)}, u32[]{:S(2)}) collective-permute-start(bf16[4,256,256]{2,1,0:T(8,128)(2,1)S(1)} %constant_dynamic-update-slice_fusion.own_a), channel_id=1, source_target_pairs={{0,4},{4,0},{1,5},{5,1},{2,6},{6,2},{3,7},{7,3},{8,12},{12,8},{9,1... | collective-permute-start | bytes 1572872 | tf_op jit(solution)/shard_map/ppermute | solution.py:24
  43.8 7.5 %collective-permute-done.2 = bf16[2,256,256]{2,1,0:T(8,128)(2,1)S(1)} collective-permute-done((bf16[2,256,256]{2,1,0:T(8,128)(2,1)S(1)}, bf16[2,256,256]{2,1,0:T(8,128)(2,1)S(1)}, u32[]{:S(2)}, u32[]{:S(2)}) %collective-permute-start.2) | collective-permute-done | bytes 262176 | tf_op jit(solution)/shard_map/ppermute | solution.py:24
  51.3 2.0 %collective-permute-done.3 = bf16[2,256,256]{2,1,0:T(8,128)(2,1)S(1)} collective-permute-done((bf16[2,256,256]{2,1,0:T(8,128)(2,1)S(1)}, bf16[2,256,256]{2,1,0:T(8,128)(2,1)S(1)}, u32[]{:S(2)}, u32[]{:S(2)}) %collective-permute-start.3) | collective-permute-done | bytes 262176 | tf_op jit(solution)/shard_map/ppermute | solution.py:24
  53.3 2.9 %collective-permute-start.5 = (bf16[4,256,256]{2,1,0:T(8,128)(2,1)S(1)}, bf16[4,256,256]{2,1,0:T(8,128)(2,1)}, u32[]{:S(2)}, u32[]{:S(2)}) collective-permute-start(bf16[4,256,256]{2,1,0:T(8,128)(2,1)S(1)} %constant_dynamic-update-slice_fusion.2.own_b), channel_id=1, source_target_pairs={{0,4},{4,0},{1,5},{5,1},{2,6},{6,2},{3,7},{7,3},{8,12},{12,8},{9,1... | collective-permute-start | bytes 1572872 | tf_op jit(solution)/shard_map/ppermute | solution.py:24
  56.2 0.1 stack.85.place
  56.4 0.0 collective-permute-done.4.other_a
  56.4 1.5 %collective-permute-done.5.other_b = bf16[4,256,256]{2,1,0:T(8,128)(2,1)} collective-permute-done((bf16[4,256,256]{2,1,0:T(8,128)(2,1)S(1)}, bf16[4,256,256]{2,1,0:T(8,128)(2,1)}, u32[]{:S(2)}, u32[]{:S(2)}) %collective-permute-start.5) | collective-permute-done | bytes 524320 | tf_op jit(solution)/shard_map/ppermute | solution.py:24
  57.8 6.3 %all-to-all-done.t_ref = bf16[8,256,512]{2,1,0:T(8,128)(2,1)S(1)} async-done(((bf16[8,256,512]{2,1,0:T(8,128)(2,1)}), bf16[8,256,512]{2,1,0:T(8,128)(2,1)S(1)}, u32[]{:S(2)}, u32[]{:S(2)}) %all-to-all-start) | async-done | bytes 2097184 | tf_op jit(solution)/shard_map/all_to_all | solution.py:104
  64.2 2.4 %shard_map.29 = f32[4,2,256,128]{3,2,1,0:T(8,128)S(1)} custom-call(s32[40]{0:T(128)S(1)} %stack.85.place, bf16[4,256,256]{2,1,0:T(8,128)(2,1)S(1)} %constant_dynamic-update-slice_fusion.own_a, bf16[4,256,256]{2,1,0:T(8,128)(2,1)S(1)} %constant_dynamic-update-slice_fusion.2.own_b, bf16[4,256,256]{2,1,0:T(8,128)(2,1)} %collective-permute-done.4.other_a, ...), custom_call_target="tpu_custom_call" | custom-call | tf_op jit(solution)/shard_map/pallas_call | solution.py:93
  66.6 16.1 %all_to_all.10 = f32[4,2,256,128]{3,2,1,0:T(8,128)S(1)} all-to-all(f32[4,2,256,128]{3,2,1,0:T(8,128)S(1)} %shard_map.29), channel_id=1, replica_groups=mesh['yh'=2,'z'=8,'yl'=4,'core'=2,'x'=4] {'x'}, dimensions={0} | all-to-all | bytes 2097152 | tf_op jit(solution)/shard_map/all_to_all | solution.py:121
  82.7 0.1 reduce_sum.9
  82.8 4.7 %collective-permute-start.6 = (f32[256,128]{1,0:T(8,128)S(1)}, f32[256,128]{1,0:T(8,128)S(1)}, u32[]{:S(2)}, u32[]{:S(2)}) collective-permute-start(f32[256,128]{1,0:T(8,128)S(1)} %slice_bitcast_fusion), channel_id=1, source_target_pairs={{0,256},{256,0},{1,257},{257,1},{2,258},{258,2},{3,259},{259,3},{4... | collective-permute-start | bytes 393224 | tf_op jit(solution)/shard_map/ppermute | solution.py:24
  87.6 7.5 %collective-permute-done.6 = f32[256,128]{1,0:T(8,128)S(1)} collective-permute-done((f32[256,128]{1,0:T(8,128)S(1)}, f32[256,128]{1,0:T(8,128)S(1)}, u32[]{:S(2)}, u32[]{:S(2)}) %collective-permute-start.6) | collective-permute-done | bytes 131104 | tf_op jit(solution)/shard_map/ppermute | solution.py:24
  95.0 0.7 fusion
  (6 shorter events, 0.1 us)
Async XLA Ops:
  2.5 10.5 %copy-start = (bf16[256,512]{1,0:T(8,128)(2,1)S(1)}, bf16[256,512]{1,0:T(8,128)(2,1)}, u32[]{:S(2)}) copy-start(bf16[256,512]{1,0:T(8,128)(2,1)} %param.2) | copy-start | bytes 786436
  2.5 61.7 %all-to-all-start = ((bf16[8,256,512]{2,1,0:T(8,128)(2,1)}), bf16[8,256,512]{2,1,0:T(8,128)(2,1)S(1)}, u32[]{:S(2)}, u32[]{:S(2)}) async-start(bf16[8,256,512]{2,1,0:T(8,128)(2,1)} %shard_map.28), calls=%async_computation | async-start | bytes 4194304 | tf_op jit(solution)/shard_map/all_to_all | solution.py:104
  15.2 7.1 %collective-permute-start = (bf16[2,256,256]{2,1,0:T(8,128)(2,1)S(1)}, bf16[2,256,256]{2,1,0:T(8,128)(2,1)S(1)}, u32[]{:S(2)}, u32[]{:S(2)}) collective-permute-start(bf16[2,256,256]{2,1,0:T(8,128)(2,1)S(1)} %constant_dynamic-slice_fusion), channel_id=1, source_target_pairs={{0,0},{1,2},{2,1},{3,3},{4,5},{5,7},{6,4},{7,6},{8,8},{9,10},{10,9... | collective-permute-start | bytes 786440 | tf_op jit(solution)/shard_map/ppermute | solution.py:24
  15.8 25.5 %collective-permute-start.1 = (bf16[2,256,256]{2,1,0:T(8,128)(2,1)S(1)}, bf16[2,256,256]{2,1,0:T(8,128)(2,1)S(1)}, u32[]{:S(2)}, u32[]{:S(2)}) collective-permute-start(bf16[2,256,256]{2,1,0:T(8,128)(2,1)S(1)} %constant_dynamic-slice_fusion), channel_id=1, source_target_pairs={{0,24},{1,26},{2,25},{3,27},{4,29},{5,31},{6,28},{7,30},{8,16},{9,... | collective-permute-start | bytes 786440 | tf_op jit(solution)/shard_map/ppermute | solution.py:24
  22.3 29.1 %collective-permute-start.2 = (bf16[2,256,256]{2,1,0:T(8,128)(2,1)S(1)}, bf16[2,256,256]{2,1,0:T(8,128)(2,1)S(1)}, u32[]{:S(2)}, u32[]{:S(2)}) collective-permute-start(bf16[2,256,256]{2,1,0:T(8,128)(2,1)S(1)} %collective-permute-done), channel_id=1, source_target_pairs={{0,16},{8,24},{16,0},{24,8},{1,17},{9,25},{17,1},{25,9},{2,18},{10... | collective-permute-start | bytes 786440 | tf_op jit(solution)/shard_map/ppermute | solution.py:24
  36.7 16.6 %collective-permute-start.3 = (bf16[2,256,256]{2,1,0:T(8,128)(2,1)S(1)}, bf16[2,256,256]{2,1,0:T(8,128)(2,1)S(1)}, u32[]{:S(2)}, u32[]{:S(2)}) collective-permute-start(bf16[2,256,256]{2,1,0:T(8,128)(2,1)S(1)} %constant_dynamic-slice_fusion), channel_id=1, source_target_pairs={{0,8},{1,10},{2,9},{3,11},{4,13},{5,15},{6,12},{7,14},{8,0},{9,2},... | collective-permute-start | bytes 786440 | tf_op jit(solution)/shard_map/ppermute | solution.py:24
  41.4 15.0 %collective-permute-start.4 = (bf16[4,256,256]{2,1,0:T(8,128)(2,1)S(1)}, bf16[4,256,256]{2,1,0:T(8,128)(2,1)}, u32[]{:S(2)}, u32[]{:S(2)}) collective-permute-start(bf16[4,256,256]{2,1,0:T(8,128)(2,1)S(1)} %constant_dynamic-update-slice_fusion.own_a), channel_id=1, source_target_pairs={{0,4},{4,0},{1,5},{5,1},{2,6},{6,2},{3,7},{7,3},{8,12},{12,8},{9,1... | collective-permute-start | bytes 1572872 | tf_op jit(solution)/shard_map/ppermute | solution.py:24
  53.3 4.5 %collective-permute-start.5 = (bf16[4,256,256]{2,1,0:T(8,128)(2,1)S(1)}, bf16[4,256,256]{2,1,0:T(8,128)(2,1)}, u32[]{:S(2)}, u32[]{:S(2)}) collective-permute-start(bf16[4,256,256]{2,1,0:T(8,128)(2,1)S(1)} %constant_dynamic-update-slice_fusion.2.own_b), channel_id=1, source_target_pairs={{0,4},{4,0},{1,5},{5,1},{2,6},{6,2},{3,7},{7,3},{8,12},{12,8},{9,1... | collective-permute-start | bytes 1572872 | tf_op jit(solution)/shard_map/ppermute | solution.py:24
  82.8 12.2 %collective-permute-start.6 = (f32[256,128]{1,0:T(8,128)S(1)}, f32[256,128]{1,0:T(8,128)S(1)}, u32[]{:S(2)}, u32[]{:S(2)}) collective-permute-start(f32[256,128]{1,0:T(8,128)S(1)} %slice_bitcast_fusion), channel_id=1, source_target_pairs={{0,256},{256,0},{1,257},{257,1},{2,258},{258,2},{3,259},{259,3},{4... | collective-permute-start | bytes 393224 | tf_op jit(solution)/shard_map/ppermute | solution.py:24

commit v16 on v15

--- a/solution.py
+++ b/solution.py
@@ -69,34 +69,48 @@
     )(tile)
 
 
-def product_kernel(place, own_a, own_b, other_a, other_b, t_ref, out_ref):
+VMEM = pl.BlockSpec(memory_space=pltpu.VMEM)
+PARAMS = pltpu.CompilerParams(vmem_limit_bytes=16 * 1024 * 1024)
+
+
+def order_kernel(place, own_a, own_b, other_a, other_b, out_ref):
+    for unit in range(8):
+        same = place[5 * unit] == 1
+        for rel in range(2):
+            first, slot = place[5 * unit + 1 + 2 * rel] == 1, place[5 * unit + 2 + 2 * rel]
+            out_ref[rel * UNIT : (rel + 1) * UNIT, unit * UNIT : (unit + 1) * UNIT] = jnp.where(
+                same,
+                jnp.where(first, own_a[slot], own_b[slot]),
+                jnp.where(first, other_a[slot], other_b[slot]),
+            )
+
+
+def ordered(place, *operands):
+    return pl.pallas_call(
+        order_kernel,
+        out_shape=jax.ShapeDtypeStruct((2 * UNIT, 8 * UNIT), jnp.bfloat16),
+        in_specs=[pl.BlockSpec(memory_space=pltpu.SMEM)] + [VMEM] * len(operands),
+        out_specs=VMEM,
+        compiler_params=PARAMS,
+    )(place, *operands)
+
+
+def product_kernel(w_ref, t_ref, out_ref):
     t = t_ref[...].reshape(8 * UNIT, t_ref.shape[2])
     for rel in range(2):
-        blocks = []
-        for unit in range(8):
-            same = place[5 * unit] == 1
-            first, slot = place[5 * unit + 1 + 2 * rel] == 1, place[5 * unit + 2 + 2 * rel]
-            blocks.append(
-                jnp.where(
-                    same,
-                    jnp.where(first, own_a[slot], own_b[slot]),
-                    jnp.where(first, other_a[slot], other_b[slot]),
-                )
-            )
-        part = jnp.dot(jnp.concatenate(blocks, axis=1), t, preferred_element_type=jnp.float32)
+        part = jnp.dot(w_ref[rel * UNIT : (rel + 1) * UNIT, :], t, preferred_element_type=jnp.float32)
         for block in range(4):
             out_ref[block, rel] = part[:, block * 128 : (block + 1) * 128]
 
 
-def product(place, *operands):
-    vmem = pl.BlockSpec(memory_space=pltpu.VMEM)
+def product(slab, tiles):
     return pl.pallas_call(
         product_kernel,
         out_shape=jax.ShapeDtypeStruct((4, 2, UNIT, 128), jnp.float32),
-        in_specs=[pl.BlockSpec(memory_space=pltpu.SMEM)] + [vmem] * len(operands),
-        out_specs=vmem,
-        compiler_params=pltpu.CompilerParams(vmem_limit_bytes=16 * 1024 * 1024),
-    )(place, *operands)
+        in_specs=[VMEM, VMEM],
+        out_specs=VMEM,
+        compiler_params=PARAMS,
+    )(slab, tiles)
 
 
 def per_device(integrals, amplitudes):
@@ -117,7 +131,7 @@
             mask = yl ^ (2 * (yh ^ rel) + u4)
             place += [jnp.where(mask >> 1 == mask & 1, 1, 0), (mask & 1) * 2 + u3]
     place = jnp.stack(place).astype(jnp.int32)
-    part = product(place, own_a, own_b, other_a, other_b, tiles)
+    part = product(ordered(place, own_a, own_b, other_a, other_b), tiles)
     part = lax.all_to_all(part, "x", split_axis=0, concat_axis=0, tiled=True).sum(axis=0)
     return part[0] + moved(part[1], ("yh",), lambda yh: {"yh": 1 - yh})
 

time: 96.2 us -> 98.6 us (1.025); the launches traced: 95.7 us -> 96.6 us
  local copies, waits for them, and re-layouts: 0.23 us -> 3.13 us
  waiting for transfers between devices: 24.7 us -> 22.4 us
  starting transfers between devices: 46.6 us -> 45.4 us
  blocking collectives: 18.3 us -> 19.5 us
    all_to_all x1, waiting for transfers between devices: 6.31 us -> 3.39 us  [per_device(): lax.all_to_all(copies_of(amplitudes), 'z', split_axis=0, concat_axis=0, t...]
    unnamed x4 -> x8, local copies, waits for them, and re-layouts: 0.04 us -> 2.94 us
    pallas_call x0 -> x1, Pallas kernels: none -> 1.6 us  [ordered(): pl.pallas_call(order_kernel, out_shape=jax.ShapeDtypeStruct((2 * UNIT, 8...]
    ppermute x7, starting transfers between devices: 36.1 us -> 34.9 us  [moved(): return lax.ppermute(value, axes, perm)]
    all_to_all x1, blocking collectives: 16.1 us -> 17.4 us  [per_device(): lax.all_to_all(part, 'x', split_axis=0, concat_axis=0, tiled=True)]
    pallas_call x1, Pallas kernels: 2.45 us -> 1.24 us  [product(): pl.pallas_call(product_kernel, out_shape=jax.ShapeDtypeStruct((4, 2, UNIT...]
  transfers between devices with their start and end apart: 8 -> 8, of which waited for: 5 -> 5; matrix products, arithmetic and copies ran while one was open for 0% -> 0% of each run, Pallas kernels for 0% -> 2%
where the time goes in v16:
time: 98.6 us; the launch traced here: 96.6 us
  starting transfers between devices  45.4 us (46%)
  waiting for transfers between devices  22.4 us (23%)
  blocking collectives  19.5 us (20%)
  Pallas kernels  5.32 us (5%)
  local copies, waits for them, and re-layouts  3.13 us (3%)
    ppermute x7, starting transfers between devices, moved(): return lax.ppermute(value, axes, perm)  34.9 us
    ppermute x7, waiting for transfers between devices, moved(): return lax.ppermute(value, axes, perm)  19 us
    all_to_all x1, blocking collectives, per_device(): lax.all_to_all(part, 'x', split_axis=0, concat_axis=0, tiled=True)  17.4 us
    all_to_all x1, starting transfers between devices, per_device(): lax.all_to_all(copies_of(amplitudes), 'z', split_axis=0, concat_axis=0, t...  10.5 us
    all_to_all x1, waiting for transfers between devices, per_device(): lax.all_to_all(copies_of(amplitudes), 'z', split_axis=0, concat_axis=0, t...  3.39 us
    unnamed x8, local copies, waits for them, and re-layouts  2.94 us
    pallas_call x1, Pallas kernels, copies_of(): pl.pallas_call(copies_kernel, out_shape=jax.ShapeDtypeStruct((8,) + tile....  2.49 us
    all_gather x1, blocking collectives, per_device(): both = lax.all_gather(integrals, 'core', axis=0)  2.18 us
  transfers between devices with their start and end apart: 8, of which 5 were waited for; matrix products, arithmetic and copies ran while one was open for 0% of the time, Pallas kernels for 2%

profile of v16, /device:TPU:56, one launch (start us, length us, event | category | flops | bytes accessed | tf_op | source)
XLA Modules:
  0.0 96.6 jit_solution(17327925588479050654)
XLA Ops:
  0.0 2.5 %shard_map.29 = bf16[8,256,512]{2,1,0:T(8,128)(2,1)} custom-call(bf16[256,512]{1,0:T(8,128)(2,1)} %tile_ref.1), custom_call_target="tpu_custom_call" | custom-call | tf_op jit(solution)/shard_map/pallas_call | solution.py:59
  2.5 0.0 copy-start.2
  2.5 10.5 %all-to-all-start = ((bf16[8,256,512]{2,1,0:T(8,128)(2,1)}), bf16[8,256,512]{2,1,0:T(8,128)(2,1)S(1)}, u32[]{:S(2)}, u32[]{:S(2)}) async-start(bf16[8,256,512]{2,1,0:T(8,128)(2,1)} %shard_map.29), calls=%async_computation | async-start | bytes 4194304 | tf_op jit(solution)/shard_map/all_to_all | solution.py:118
  13.0 0.0 copy-done.2
  13.0 2.2 %all-gather = bf16[512,512]{1,0:T(8,128)(2,1)S(1)} all-gather(bf16[256,512]{1,0:T(8,128)(2,1)S(1)} %copy-done.2), channel_id=2, replica_groups=mesh['yh'=2,'z'=8,'yl'=4,'core'=2,'x'=4] {'core'}, dimensions={0}, use_global_device_ids=true | all-gather | bytes 786432 | tf_op jit(solution)/shard_map/all_gather | solution.py:119
  15.2 0.7 collective-permute-start
  15.9 6.4 %collective-permute-start.1 = (bf16[2,256,256]{2,1,0:T(8,128)(2,1)S(1)}, bf16[2,256,256]{2,1,0:T(8,128)(2,1)S(1)}, u32[]{:S(2)}, u32[]{:S(2)}) collective-permute-start(bf16[2,256,256]{2,1,0:T(8,128)(2,1)S(1)} %constant_dynamic-slice_fusion), channel_id=1, source_target_pairs={{0,24},{1,26},{2,25},{3,27},{4,29},{5,31},{6,28},{7,30},{8,16},{9,... | collective-permute-start | bytes 786440 | tf_op jit(solution)/shard_map/ppermute | solution.py:24
  22.3 0.0 collective-permute-done
  22.3 14.5 %collective-permute-start.2 = (bf16[2,256,256]{2,1,0:T(8,128)(2,1)S(1)}, bf16[2,256,256]{2,1,0:T(8,128)(2,1)S(1)}, u32[]{:S(2)}, u32[]{:S(2)}) collective-permute-start(bf16[2,256,256]{2,1,0:T(8,128)(2,1)S(1)} %collective-permute-done), channel_id=1, source_target_pairs={{0,16},{8,24},{16,0},{24,8},{1,17},{9,25},{17,1},{25,9},{2,18},{10... | collective-permute-start | bytes 786440 | tf_op jit(solution)/shard_map/ppermute | solution.py:24
  36.8 4.6 %collective-permute-start.3 = (bf16[2,256,256]{2,1,0:T(8,128)(2,1)S(1)}, bf16[2,256,256]{2,1,0:T(8,128)(2,1)S(1)}, u32[]{:S(2)}, u32[]{:S(2)}) collective-permute-start(bf16[2,256,256]{2,1,0:T(8,128)(2,1)S(1)} %constant_dynamic-slice_fusion), channel_id=1, source_target_pairs={{0,8},{1,10},{2,9},{3,11},{4,13},{5,15},{6,12},{7,14},{8,0},{9,2},... | collective-permute-start | bytes 786440 | tf_op jit(solution)/shard_map/ppermute | solution.py:24
  41.4 0.0 collective-permute-done.1
  41.4 2.4 %collective-permute-start.4 = (bf16[4,256,256]{2,1,0:T(8,128)(2,1)S(1)}, bf16[4,256,256]{2,1,0:T(8,128)(2,1)}, u32[]{:S(2)}, u32[]{:S(2)}) collective-permute-start(bf16[4,256,256]{2,1,0:T(8,128)(2,1)S(1)} %constant_dynamic-update-slice_fusion.own_a), channel_id=1, source_target_pairs={{0,4},{4,0},{1,5},{5,1},{2,6},{6,2},{3,7},{7,3},{8,12},{12,8},{9,1... | collective-permute-start | bytes 1572872 | tf_op jit(solution)/shard_map/ppermute | solution.py:24
  43.8 7.5 %collective-permute-done.2 = bf16[2,256,256]{2,1,0:T(8,128)(2,1)S(1)} collective-permute-done((bf16[2,256,256]{2,1,0:T(8,128)(2,1)S(1)}, bf16[2,256,256]{2,1,0:T(8,128)(2,1)S(1)}, u32[]{:S(2)}, u32[]{:S(2)}) %collective-permute-start.2) | collective-permute-done | bytes 262176 | tf_op jit(solution)/shard_map/ppermute | solution.py:24
  51.4 2.0 %collective-permute-done.3 = bf16[2,256,256]{2,1,0:T(8,128)(2,1)S(1)} collective-permute-done((bf16[2,256,256]{2,1,0:T(8,128)(2,1)S(1)}, bf16[2,256,256]{2,1,0:T(8,128)(2,1)S(1)}, u32[]{:S(2)}, u32[]{:S(2)}) %collective-permute-start.3) | collective-permute-done | bytes 262176 | tf_op jit(solution)/shard_map/ppermute | solution.py:24
  53.3 2.9 %collective-permute-start.5 = (bf16[4,256,256]{2,1,0:T(8,128)(2,1)S(1)}, bf16[4,256,256]{2,1,0:T(8,128)(2,1)}, u32[]{:S(2)}, u32[]{:S(2)}) collective-permute-start(bf16[4,256,256]{2,1,0:T(8,128)(2,1)S(1)} %constant_dynamic-update-slice_fusion.2.own_b), channel_id=1, source_target_pairs={{0,4},{4,0},{1,5},{5,1},{2,6},{6,2},{3,7},{7,3},{8,12},{12,8},{9,1... | collective-permute-start | bytes 1572872 | tf_op jit(solution)/shard_map/ppermute | solution.py:24
  56.3 0.1 stack.85.place
  56.4 0.0 collective-permute-done.4.other_a
  56.4 1.5 %collective-permute-done.5.other_b = bf16[4,256,256]{2,1,0:T(8,128)(2,1)} collective-permute-done((bf16[4,256,256]{2,1,0:T(8,128)(2,1)S(1)}, bf16[4,256,256]{2,1,0:T(8,128)(2,1)}, u32[]{:S(2)}, u32[]{:S(2)}) %collective-permute-start.5) | collective-permute-done | bytes 524320 | tf_op jit(solution)/shard_map/ppermute | solution.py:24
  57.9 1.6 %shard_map.28.w_ref = bf16[512,2048]{1,0:T(8,128)(2,1)S(1)} custom-call(s32[40]{0:T(128)S(1)} %stack.85.place, bf16[4,256,256]{2,1,0:T(8,128)(2,1)S(1)} %constant_dynamic-update-slice_fusion.own_a, bf16[4,256,256]{2,1,0:T(8,128)(2,1)S(1)} %constant_dynamic-update-slice_fusion.2.own_b, bf16[4,256,256]{2,1,0:T(8,128)(2,1)} %collective-permute-done.4.other_a, ...), custom_call_target="tpu_custom_call" | custom-call | tf_op jit(solution)/shard_map/pallas_call | solution.py:89
  59.5 0.0 copy-start
  59.5 1.3 %copy-done = bf16[512,2048]{1,0:T(8,128)(2,1)} copy-done((bf16[512,2048]{1,0:T(8,128)(2,1)}, bf16[512,2048]{1,0:T(8,128)(2,1)S(1)}, u32[]{:S(2)}) %copy-start) | copy-done | bytes 2097176
  60.8 3.4 %all-to-all-done.t_ref = bf16[8,256,512]{2,1,0:T(8,128)(2,1)S(1)} async-done(((bf16[8,256,512]{2,1,0:T(8,128)(2,1)}), bf16[8,256,512]{2,1,0:T(8,128)(2,1)S(1)}, u32[]{:S(2)}, u32[]{:S(2)}) %all-to-all-start) | async-done | bytes 2097184 | tf_op jit(solution)/shard_map/all_to_all | solution.py:118
  64.2 0.0 copy-start.1
  64.2 1.6 %copy-done.1 = bf16[512,2048]{1,0:T(8,128)(2,1)S(1)} copy-done((bf16[512,2048]{1,0:T(8,128)(2,1)S(1)}, bf16[512,2048]{1,0:T(8,128)(2,1)}, u32[]{:S(2)}) %copy-start.1) | copy-done | bytes 2097176
  65.8 1.2 %shard_map.30 = f32[4,2,256,128]{3,2,1,0:T(8,128)S(1)} custom-call(bf16[512,2048]{1,0:T(8,128)(2,1)S(1)} %copy-done.1, bf16[8,256,512]{2,1,0:T(8,128)(2,1)S(1)} %all-to-all-done.t_ref), custom_call_target="tpu_custom_call" | custom-call | tf_op jit(solution)/shard_map/pallas_call | solution.py:107
  67.0 17.4 %all_to_all.10 = f32[4,2,256,128]{3,2,1,0:T(8,128)S(1)} all-to-all(f32[4,2,256,128]{3,2,1,0:T(8,128)S(1)} %shard_map.30), channel_id=1, replica_groups=mesh['yh'=2,'z'=8,'yl'=4,'core'=2,'x'=4] {'x'}, dimensions={0} | all-to-all | bytes 2097152 | tf_op jit(solution)/shard_map/all_to_all | solution.py:135
  84.4 0.1 reduce_sum.9
  84.5 3.5 %collective-permute-start.6 = (f32[256,128]{1,0:T(8,128)S(1)}, f32[256,128]{1,0:T(8,128)S(1)}, u32[]{:S(2)}, u32[]{:S(2)}) collective-permute-start(f32[256,128]{1,0:T(8,128)S(1)} %slice_bitcast_fusion), channel_id=1, source_target_pairs={{0,256},{256,0},{1,257},{257,1},{2,258},{258,2},{3,259},{259,3},{4... | collective-permute-start | bytes 393224 | tf_op jit(solution)/shard_map/ppermute | solution.py:24
  88.0 8.0 %collective-permute-done.6 = f32[256,128]{1,0:T(8,128)S(1)} collective-permute-done((f32[256,128]{1,0:T(8,128)S(1)}, f32[256,128]{1,0:T(8,128)S(1)}, u32[]{:S(2)}, u32[]{:S(2)}) %collective-permute-start.6) | collective-permute-done | bytes 131104 | tf_op jit(solution)/shard_map/ppermute | solution.py:24
  96.0 0.7 fusion
  (6 shorter events, 0.1 us)
Async XLA Ops:
  2.5 10.5 %copy-start.2 = (bf16[256,512]{1,0:T(8,128)(2,1)S(1)}, bf16[256,512]{1,0:T(8,128)(2,1)}, u32[]{:S(2)}) copy-start(bf16[256,512]{1,0:T(8,128)(2,1)} %param.2) | copy-start | bytes 786436
  2.5 61.7 %all-to-all-start = ((bf16[8,256,512]{2,1,0:T(8,128)(2,1)}), bf16[8,256,512]{2,1,0:T(8,128)(2,1)S(1)}, u32[]{:S(2)}, u32[]{:S(2)}) async-start(bf16[8,256,512]{2,1,0:T(8,128)(2,1)} %shard_map.29), calls=%async_computation | async-start | bytes 4194304 | tf_op jit(solution)/shard_map/all_to_all | solution.py:118
  15.2 7.1 %collective-permute-start = (bf16[2,256,256]{2,1,0:T(8,128)(2,1)S(1)}, bf16[2,256,256]{2,1,0:T(8,128)(2,1)S(1)}, u32[]{:S(2)}, u32[]{:S(2)}) collective-permute-start(bf16[2,256,256]{2,1,0:T(8,128)(2,1)S(1)} %constant_dynamic-slice_fusion), channel_id=1, source_target_pairs={{0,0},{1,2},{2,1},{3,3},{4,5},{5,7},{6,4},{7,6},{8,8},{9,10},{10,9... | collective-permute-start | bytes 786440 | tf_op jit(solution)/shard_map/ppermute | solution.py:24
  15.9 25.5 %collective-permute-start.1 = (bf16[2,256,256]{2,1,0:T(8,128)(2,1)S(1)}, bf16[2,256,256]{2,1,0:T(8,128)(2,1)S(1)}, u32[]{:S(2)}, u32[]{:S(2)}) collective-permute-start(bf16[2,256,256]{2,1,0:T(8,128)(2,1)S(1)} %constant_dynamic-slice_fusion), channel_id=1, source_target_pairs={{0,24},{1,26},{2,25},{3,27},{4,29},{5,31},{6,28},{7,30},{8,16},{9,... | collective-permute-start | bytes 786440 | tf_op jit(solution)/shard_map/ppermute | solution.py:24
  22.3 29.1 %collective-permute-start.2 = (bf16[2,256,256]{2,1,0:T(8,128)(2,1)S(1)}, bf16[2,256,256]{2,1,0:T(8,128)(2,1)S(1)}, u32[]{:S(2)}, u32[]{:S(2)}) collective-permute-start(bf16[2,256,256]{2,1,0:T(8,128)(2,1)S(1)} %collective-permute-done), channel_id=1, source_target_pairs={{0,16},{8,24},{16,0},{24,8},{1,17},{9,25},{17,1},{25,9},{2,18},{10... | collective-permute-start | bytes 786440 | tf_op jit(solution)/shard_map/ppermute | solution.py:24
  36.8 16.6 %collective-permute-start.3 = (bf16[2,256,256]{2,1,0:T(8,128)(2,1)S(1)}, bf16[2,256,256]{2,1,0:T(8,128)(2,1)S(1)}, u32[]{:S(2)}, u32[]{:S(2)}) collective-permute-start(bf16[2,256,256]{2,1,0:T(8,128)(2,1)S(1)} %constant_dynamic-slice_fusion), channel_id=1, source_target_pairs={{0,8},{1,10},{2,9},{3,11},{4,13},{5,15},{6,12},{7,14},{8,0},{9,2},... | collective-permute-start | bytes 786440 | tf_op jit(solution)/shard_map/ppermute | solution.py:24
  41.4 15.0 %collective-permute-start.4 = (bf16[4,256,256]{2,1,0:T(8,128)(2,1)S(1)}, bf16[4,256,256]{2,1,0:T(8,128)(2,1)}, u32[]{:S(2)}, u32[]{:S(2)}) collective-permute-start(bf16[4,256,256]{2,1,0:T(8,128)(2,1)S(1)} %constant_dynamic-update-slice_fusion.own_a), channel_id=1, source_target_pairs={{0,4},{4,0},{1,5},{5,1},{2,6},{6,2},{3,7},{7,3},{8,12},{12,8},{9,1... | collective-permute-start | bytes 1572872 | tf_op jit(solution)/shard_map/ppermute | solution.py:24
  53.3 4.5 %collective-permute-start.5 = (bf16[4,256,256]{2,1,0:T(8,128)(2,1)S(1)}, bf16[4,256,256]{2,1,0:T(8,128)(2,1)}, u32[]{:S(2)}, u32[]{:S(2)}) collective-permute-start(bf16[4,256,256]{2,1,0:T(8,128)(2,1)S(1)} %constant_dynamic-update-slice_fusion.2.own_b), channel_id=1, source_target_pairs={{0,4},{4,0},{1,5},{5,1},{2,6},{6,2},{3,7},{7,3},{8,12},{12,8},{9,1... | collective-permute-start | bytes 1572872 | tf_op jit(solution)/shard_map/ppermute | solution.py:24
  59.5 1.3 %copy-start = (bf16[512,2048]{1,0:T(8,128)(2,1)}, bf16[512,2048]{1,0:T(8,128)(2,1)S(1)}, u32[]{:S(2)}) copy-start(bf16[512,2048]{1,0:T(8,128)(2,1)S(1)} %shard_map.28.w_ref) | copy-start | bytes 6291460
  64.2 1.6 %copy-start.1 = (bf16[512,2048]{1,0:T(8,128)(2,1)S(1)}, bf16[512,2048]{1,0:T(8,128)(2,1)}, u32[]{:S(2)}) copy-start(bf16[512,2048]{1,0:T(8,128)(2,1)} %copy-done) | copy-start | bytes 6291460
  84.5 11.5 %collective-permute-start.6 = (f32[256,128]{1,0:T(8,128)S(1)}, f32[256,128]{1,0:T(8,128)S(1)}, u32[]{:S(2)}, u32[]{:S(2)}) collective-permute-start(f32[256,128]{1,0:T(8,128)S(1)} %slice_bitcast_fusion), channel_id=1, source_target_pairs={{0,256},{256,0},{1,257},{257,1},{2,258},{258,2},{3,259},{259,3},{4... | collective-permute-start | bytes 393224 | tf_op jit(solution)/shard_map/ppermute | solution.py:24

commit v17 on v15

--- a/solution.py
+++ b/solution.py
@@ -104,8 +104,9 @@
     tiles = lax.all_to_all(copies_of(amplitudes), "z", split_axis=0, concat_axis=0, tiled=True)
     both = lax.all_gather(integrals, "core", axis=0)
     half = lax.dynamic_slice_in_dim(both, ((x >> 1) ^ core) * UNIT, UNIT, 2)
-    slabs = {mask: spread(half, mask) for mask in (0, 3, 1)}
+    slabs = {mask: spread(half, mask) for mask in (0, 3)}
     slabs[2] = moved(slabs[0], ("yl",), lambda yl: {"yl": yl ^ 2})
+    slabs[1] = moved(slabs[0], ("yl",), lambda yl: {"yl": yl ^ 1})
     own_a = jnp.concatenate([slabs[0], slabs[3]])
     own_b = jnp.concatenate([slabs[2], slabs[1]])
     other_a, other_b = core_swap(own_a), core_swap(own_b)

time: 96.2 us -> 96.2 us (level)
  starting transfers between devices: 46.6 us -> 45.1 us
  waiting for transfers between devices: 24.7 us -> 26.2 us
    ppermute x7, starting transfers between devices: 36.1 us -> 34.7 us  [moved(): return lax.ppermute(value, axes, perm)]
where the time goes in v17:
time: 96.2 us; the launch traced here: 95.7 us
  starting transfers between devices  45.1 us (47%)
  waiting for transfers between devices  26.2 us (27%)
  blocking collectives  18.3 us (19%)
  Pallas kernels  4.92 us (5%)
    ppermute x7, starting transfers between devices, moved(): return lax.ppermute(value, axes, perm)  34.7 us
    ppermute x7, waiting for transfers between devices, moved(): return lax.ppermute(value, axes, perm)  19.3 us
    all_to_all x1, blocking collectives, per_device(): lax.all_to_all(part, 'x', split_axis=0, concat_axis=0, tiled=True)  16.1 us
    all_to_all x1, starting transfers between devices, per_device(): lax.all_to_all(copies_of(amplitudes), 'z', split_axis=0, concat_axis=0, t...  10.5 us
    all_to_all x1, waiting for transfers between devices, per_device(): lax.all_to_all(copies_of(amplitudes), 'z', split_axis=0, concat_axis=0, t...  6.8 us
    pallas_call x1, Pallas kernels, copies_of(): pl.pallas_call(copies_kernel, out_shape=jax.ShapeDtypeStruct((8,) + tile....  2.47 us
    pallas_call x1, Pallas kernels, product(): pl.pallas_call(product_kernel, out_shape=jax.ShapeDtypeStruct((4, 2, UNIT...  2.45 us
    all_gather x1, blocking collectives, per_device(): both = lax.all_gather(integrals, 'core', axis=0)  2.18 us
  transfers between devices with their start and end apart: 8, of which 5 were waited for; matrix products, arithmetic and copies ran while one was open for 0% of the time, Pallas kernels for 0%

profile of v17, /device:TPU:56, one launch (start us, length us, event | category | flops | bytes accessed | tf_op | source)
XLA Modules:
  0.0 95.7 jit_solution(5970685581958885182)
XLA Ops:
  0.0 2.5 %shard_map.28 = bf16[8,256,512]{2,1,0:T(8,128)(2,1)} custom-call(bf16[256,512]{1,0:T(8,128)(2,1)} %tile_ref.1), custom_call_target="tpu_custom_call" | custom-call | tf_op jit(solution)/shard_map/pallas_call | solution.py:59
  2.5 0.0 copy-start
  2.5 10.5 %all-to-all-start = ((bf16[8,256,512]{2,1,0:T(8,128)(2,1)}), bf16[8,256,512]{2,1,0:T(8,128)(2,1)S(1)}, u32[]{:S(2)}, u32[]{:S(2)}) async-start(bf16[8,256,512]{2,1,0:T(8,128)(2,1)} %shard_map.28), calls=%async_computation | async-start | bytes 4194304 | tf_op jit(solution)/shard_map/all_to_all | solution.py:104
  13.0 0.0 copy-done
  13.0 2.2 %all-gather = bf16[512,512]{1,0:T(8,128)(2,1)S(1)} all-gather(bf16[256,512]{1,0:T(8,128)(2,1)S(1)} %copy-done), channel_id=2, replica_groups=mesh['yh'=2,'z'=8,'yl'=4,'core'=2,'x'=4] {'core'}, dimensions={0}, use_global_device_ids=true | all-gather | bytes 786432 | tf_op jit(solution)/shard_map/all_gather | solution.py:105
  15.2 0.7 collective-permute-start
  15.8 6.4 %collective-permute-start.1 = (bf16[2,256,256]{2,1,0:T(8,128)(2,1)S(1)}, bf16[2,256,256]{2,1,0:T(8,128)(2,1)S(1)}, u32[]{:S(2)}, u32[]{:S(2)}) collective-permute-start(bf16[2,256,256]{2,1,0:T(8,128)(2,1)S(1)} %constant_dynamic-slice_fusion), channel_id=1, source_target_pairs={{0,24},{1,26},{2,25},{3,27},{4,29},{5,31},{6,28},{7,30},{8,16},{9,... | collective-permute-start | bytes 786440 | tf_op jit(solution)/shard_map/ppermute | solution.py:24
  22.2 0.0 collective-permute-done
  22.3 14.5 %collective-permute-start.2 = (bf16[2,256,256]{2,1,0:T(8,128)(2,1)S(1)}, bf16[2,256,256]{2,1,0:T(8,128)(2,1)S(1)}, u32[]{:S(2)}, u32[]{:S(2)}) collective-permute-start(bf16[2,256,256]{2,1,0:T(8,128)(2,1)S(1)} %collective-permute-done), channel_id=1, source_target_pairs={{0,16},{8,24},{16,0},{24,8},{1,17},{9,25},{17,1},{25,9},{2,18},{10... | collective-permute-start | bytes 786440 | tf_op jit(solution)/shard_map/ppermute | solution.py:24
  36.7 4.6 %collective-permute-start.3 = (bf16[2,256,256]{2,1,0:T(8,128)(2,1)S(1)}, bf16[2,256,256]{2,1,0:T(8,128)(2,1)S(1)}, u32[]{:S(2)}, u32[]{:S(2)}) collective-permute-start(bf16[2,256,256]{2,1,0:T(8,128)(2,1)S(1)} %collective-permute-done), channel_id=1, source_target_pairs={{0,8},{8,0},{16,24},{24,16},{1,9},{9,1},{17,25},{25,17},{2,10},{10... | collective-permute-start | bytes 786440 | tf_op jit(solution)/shard_map/ppermute | solution.py:24
  41.3 0.0 collective-permute-done.1
  41.4 1.9 %collective-permute-start.4 = (bf16[4,256,256]{2,1,0:T(8,128)(2,1)S(1)}, bf16[4,256,256]{2,1,0:T(8,128)(2,1)}, u32[]{:S(2)}, u32[]{:S(2)}) collective-permute-start(bf16[4,256,256]{2,1,0:T(8,128)(2,1)S(1)} %constant_dynamic-update-slice_fusion.own_a), channel_id=1, source_target_pairs={{0,4},{4,0},{1,5},{5,1},{2,6},{6,2},{3,7},{7,3},{8,12},{12,8},{9,1... | collective-permute-start | bytes 1572872 | tf_op jit(solution)/shard_map/ppermute | solution.py:24
  43.3 8.0 %collective-permute-done.2 = bf16[2,256,256]{2,1,0:T(8,128)(2,1)S(1)} collective-permute-done((bf16[2,256,256]{2,1,0:T(8,128)(2,1)S(1)}, bf16[2,256,256]{2,1,0:T(8,128)(2,1)S(1)}, u32[]{:S(2)}, u32[]{:S(2)}) %collective-permute-start.2) | collective-permute-done | bytes 262176 | tf_op jit(solution)/shard_map/ppermute | solution.py:24
  51.3 2.1 %collective-permute-done.3 = bf16[2,256,256]{2,1,0:T(8,128)(2,1)S(1)} collective-permute-done((bf16[2,256,256]{2,1,0:T(8,128)(2,1)S(1)}, bf16[2,256,256]{2,1,0:T(8,128)(2,1)S(1)}, u32[]{:S(2)}, u32[]{:S(2)}) %collective-permute-start.3) | collective-permute-done | bytes 262176 | tf_op jit(solution)/shard_map/ppermute | solution.py:24
  53.4 1.9 %collective-permute-start.5 = (bf16[4,256,256]{2,1,0:T(8,128)(2,1)S(1)}, bf16[4,256,256]{2,1,0:T(8,128)(2,1)}, u32[]{:S(2)}, u32[]{:S(2)}) collective-permute-start(bf16[4,256,256]{2,1,0:T(8,128)(2,1)S(1)} %constant_dynamic-update-slice_fusion.2.own_b), channel_id=1, source_target_pairs={{0,4},{4,0},{1,5},{5,1},{2,6},{6,2},{3,7},{7,3},{8,12},{12,8},{9,1... | collective-permute-start | bytes 1572872 | tf_op jit(solution)/shard_map/ppermute | solution.py:24
  55.4 0.1 stack.85.place
  55.5 0.0 collective-permute-done.4.other_a
  55.5 1.8 %collective-permute-done.5.other_b = bf16[4,256,256]{2,1,0:T(8,128)(2,1)} collective-permute-done((bf16[4,256,256]{2,1,0:T(8,128)(2,1)S(1)}, bf16[4,256,256]{2,1,0:T(8,128)(2,1)}, u32[]{:S(2)}, u32[]{:S(2)}) %collective-permute-start.5) | collective-permute-done | bytes 524320 | tf_op jit(solution)/shard_map/ppermute | solution.py:24
  57.4 6.8 %all-to-all-done.t_ref = bf16[8,256,512]{2,1,0:T(8,128)(2,1)S(1)} async-done(((bf16[8,256,512]{2,1,0:T(8,128)(2,1)}), bf16[8,256,512]{2,1,0:T(8,128)(2,1)S(1)}, u32[]{:S(2)}, u32[]{:S(2)}) %all-to-all-start) | async-done | bytes 2097184 | tf_op jit(solution)/shard_map/all_to_all | solution.py:104
  64.2 2.4 %shard_map.29 = f32[4,2,256,128]{3,2,1,0:T(8,128)S(1)} custom-call(s32[40]{0:T(128)S(1)} %stack.85.place, bf16[4,256,256]{2,1,0:T(8,128)(2,1)S(1)} %constant_dynamic-update-slice_fusion.own_a, bf16[4,256,256]{2,1,0:T(8,128)(2,1)S(1)} %constant_dynamic-update-slice_fusion.2.own_b, bf16[4,256,256]{2,1,0:T(8,128)(2,1)} %collective-permute-done.4.other_a, ...), custom_call_target="tpu_custom_call" | custom-call | tf_op jit(solution)/shard_map/pallas_call | solution.py:93
  66.6 16.1 %all_to_all.10 = f32[4,2,256,128]{3,2,1,0:T(8,128)S(1)} all-to-all(f32[4,2,256,128]{3,2,1,0:T(8,128)S(1)} %shard_map.29), channel_id=1, replica_groups=mesh['yh'=2,'z'=8,'yl'=4,'core'=2,'x'=4] {'x'}, dimensions={0} | all-to-all | bytes 2097152 | tf_op jit(solution)/shard_map/all_to_all | solution.py:122
  82.7 0.1 reduce_sum.9
  82.8 4.7 %collective-permute-start.6 = (f32[256,128]{1,0:T(8,128)S(1)}, f32[256,128]{1,0:T(8,128)S(1)}, u32[]{:S(2)}, u32[]{:S(2)}) collective-permute-start(f32[256,128]{1,0:T(8,128)S(1)} %slice_bitcast_fusion), channel_id=1, source_target_pairs={{0,256},{256,0},{1,257},{257,1},{2,258},{258,2},{3,259},{259,3},{4... | collective-permute-start | bytes 393224 | tf_op jit(solution)/shard_map/ppermute | solution.py:24
  87.6 7.5 %collective-permute-done.6 = f32[256,128]{1,0:T(8,128)S(1)} collective-permute-done((f32[256,128]{1,0:T(8,128)S(1)}, f32[256,128]{1,0:T(8,128)S(1)}, u32[]{:S(2)}, u32[]{:S(2)}) %collective-permute-start.6) | collective-permute-done | bytes 131104 | tf_op jit(solution)/shard_map/ppermute | solution.py:24
  95.0 0.7 fusion
  (6 shorter events, 0.1 us)
Async XLA Ops:
  2.5 10.5 %copy-start = (bf16[256,512]{1,0:T(8,128)(2,1)S(1)}, bf16[256,512]{1,0:T(8,128)(2,1)}, u32[]{:S(2)}) copy-start(bf16[256,512]{1,0:T(8,128)(2,1)} %param.2) | copy-start | bytes 786436
  2.5 61.7 %all-to-all-start = ((bf16[8,256,512]{2,1,0:T(8,128)(2,1)}), bf16[8,256,512]{2,1,0:T(8,128)(2,1)S(1)}, u32[]{:S(2)}, u32[]{:S(2)}) async-start(bf16[8,256,512]{2,1,0:T(8,128)(2,1)} %shard_map.28), calls=%async_computation | async-start | bytes 4194304 | tf_op jit(solution)/shard_map/all_to_all | solution.py:104
  15.2 7.1 %collective-permute-start = (bf16[2,256,256]{2,1,0:T(8,128)(2,1)S(1)}, bf16[2,256,256]{2,1,0:T(8,128)(2,1)S(1)}, u32[]{:S(2)}, u32[]{:S(2)}) collective-permute-start(bf16[2,256,256]{2,1,0:T(8,128)(2,1)S(1)} %constant_dynamic-slice_fusion), channel_id=1, source_target_pairs={{0,0},{1,2},{2,1},{3,3},{4,5},{5,7},{6,4},{7,6},{8,8},{9,10},{10,9... | collective-permute-start | bytes 786440 | tf_op jit(solution)/shard_map/ppermute | solution.py:24
  15.8 25.5 %collective-permute-start.1 = (bf16[2,256,256]{2,1,0:T(8,128)(2,1)S(1)}, bf16[2,256,256]{2,1,0:T(8,128)(2,1)S(1)}, u32[]{:S(2)}, u32[]{:S(2)}) collective-permute-start(bf16[2,256,256]{2,1,0:T(8,128)(2,1)S(1)} %constant_dynamic-slice_fusion), channel_id=1, source_target_pairs={{0,24},{1,26},{2,25},{3,27},{4,29},{5,31},{6,28},{7,30},{8,16},{9,... | collective-permute-start | bytes 786440 | tf_op jit(solution)/shard_map/ppermute | solution.py:24
  22.3 29.0 %collective-permute-start.2 = (bf16[2,256,256]{2,1,0:T(8,128)(2,1)S(1)}, bf16[2,256,256]{2,1,0:T(8,128)(2,1)S(1)}, u32[]{:S(2)}, u32[]{:S(2)}) collective-permute-start(bf16[2,256,256]{2,1,0:T(8,128)(2,1)S(1)} %collective-permute-done), channel_id=1, source_target_pairs={{0,16},{8,24},{16,0},{24,8},{1,17},{9,25},{17,1},{25,9},{2,18},{10... | collective-permute-start | bytes 786440 | tf_op jit(solution)/shard_map/ppermute | solution.py:24
  36.7 16.7 %collective-permute-start.3 = (bf16[2,256,256]{2,1,0:T(8,128)(2,1)S(1)}, bf16[2,256,256]{2,1,0:T(8,128)(2,1)S(1)}, u32[]{:S(2)}, u32[]{:S(2)}) collective-permute-start(bf16[2,256,256]{2,1,0:T(8,128)(2,1)S(1)} %collective-permute-done), channel_id=1, source_target_pairs={{0,8},{8,0},{16,24},{24,16},{1,9},{9,1},{17,25},{25,17},{2,10},{10... | collective-permute-start | bytes 786440 | tf_op jit(solution)/shard_map/ppermute | solution.py:24
  41.4 14.1 %collective-permute-start.4 = (bf16[4,256,256]{2,1,0:T(8,128)(2,1)S(1)}, bf16[4,256,256]{2,1,0:T(8,128)(2,1)}, u32[]{:S(2)}, u32[]{:S(2)}) collective-permute-start(bf16[4,256,256]{2,1,0:T(8,128)(2,1)S(1)} %constant_dynamic-update-slice_fusion.own_a), channel_id=1, source_target_pairs={{0,4},{4,0},{1,5},{5,1},{2,6},{6,2},{3,7},{7,3},{8,12},{12,8},{9,1... | collective-permute-start | bytes 1572872 | tf_op jit(solution)/shard_map/ppermute | solution.py:24
  53.4 3.9 %collective-permute-start.5 = (bf16[4,256,256]{2,1,0:T(8,128)(2,1)S(1)}, bf16[4,256,256]{2,1,0:T(8,128)(2,1)}, u32[]{:S(2)}, u32[]{:S(2)}) collective-permute-start(bf16[4,256,256]{2,1,0:T(8,128)(2,1)S(1)} %constant_dynamic-update-slice_fusion.2.own_b), channel_id=1, source_target_pairs={{0,4},{4,0},{1,5},{5,1},{2,6},{6,2},{3,7},{7,3},{8,12},{12,8},{9,1... | collective-permute-start | bytes 1572872 | tf_op jit(solution)/shard_map/ppermute | solution.py:24
  82.8 12.2 %collective-permute-start.6 = (f32[256,128]{1,0:T(8,128)S(1)}, f32[256,128]{1,0:T(8,128)S(1)}, u32[]{:S(2)}, u32[]{:S(2)}) collective-permute-start(f32[256,128]{1,0:T(8,128)S(1)} %slice_bitcast_fusion), channel_id=1, source_target_pairs={{0,256},{256,0},{1,257},{257,1},{2,258},{258,2},{3,259},{259,3},{4... | collective-permute-start | bytes 393224 | tf_op jit(solution)/shard_map/ppermute | solution.py:24

commit v18 on v15

--- a/solution.py
+++ b/solution.py
@@ -104,8 +104,9 @@
     tiles = lax.all_to_all(copies_of(amplitudes), "z", split_axis=0, concat_axis=0, tiled=True)
     both = lax.all_gather(integrals, "core", axis=0)
     half = lax.dynamic_slice_in_dim(both, ((x >> 1) ^ core) * UNIT, UNIT, 2)
-    slabs = {mask: spread(half, mask) for mask in (0, 3, 1)}
-    slabs[2] = moved(slabs[0], ("yl",), lambda yl: {"yl": yl ^ 2})
+    slabs = {0: spread(half, 0)}
+    for mask in (3, 2, 1):
+        slabs[mask] = moved(slabs[0], ("yl",), lambda yl: {"yl": yl ^ mask})
     own_a = jnp.concatenate([slabs[0], slabs[3]])
     own_b = jnp.concatenate([slabs[2], slabs[1]])
     other_a, other_b = core_swap(own_a), core_swap(own_b)

time: 96.2 us -> 98.6 us (1.025)
  the two profiles are of different devices: /device:TPU:56 before, /device:TPU:2 now
where the time goes in v18:
time: 98.6 us; the launch traced here: 98.2 us
  starting transfers between devices  42.8 us (43%)
  waiting for transfers between devices  30 us (30%)
  blocking collectives  19.2 us (19%)
  Pallas kernels  4.92 us (5%)
    ppermute x7, starting transfers between devices, moved(): return lax.ppermute(value, axes, perm)  32.4 us
    ppermute x7, waiting for transfers between devices, moved(): return lax.ppermute(value, axes, perm)  30 us
    all_to_all x1, blocking collectives, per_device(): lax.all_to_all(part, 'x', split_axis=0, concat_axis=0, tiled=True)  17 us
    all_to_all x1, starting transfers between devices, per_device(): lax.all_to_all(copies_of(amplitudes), 'z', split_axis=0, concat_axis=0, t...  10.5 us
    pallas_call x1, Pallas kernels, copies_of(): pl.pallas_call(copies_kernel, out_shape=jax.ShapeDtypeStruct((8,) + tile....  2.47 us
    pallas_call x1, Pallas kernels, product(): pl.pallas_call(product_kernel, out_shape=jax.ShapeDtypeStruct((4, 2, UNIT...  2.45 us
    all_gather x1, blocking collectives, per_device(): both = lax.all_gather(integrals, 'core', axis=0)  2.18 us
  transfers between devices with their start and end apart: 8, of which 5 were waited for; matrix products, arithmetic and copies ran while one was open for 0% of the time, Pallas kernels for 0%

profile of v18, /device:TPU:2, one launch (start us, length us, event | category | flops | bytes accessed | tf_op | source)
XLA Modules:
  0.0 98.2 jit_solution(12934586639446713687)
XLA Ops:
  0.0 2.5 %shard_map.28 = bf16[8,256,512]{2,1,0:T(8,128)(2,1)} custom-call(bf16[256,512]{1,0:T(8,128)(2,1)} %tile_ref.1), custom_call_target="tpu_custom_call" | custom-call | tf_op jit(solution)/shard_map/pallas_call | solution.py:59
  2.5 0.0 copy-start
  2.5 10.5 %all-to-all-start = ((bf16[8,256,512]{2,1,0:T(8,128)(2,1)}), bf16[8,256,512]{2,1,0:T(8,128)(2,1)S(1)}, u32[]{:S(2)}, u32[]{:S(2)}) async-start(bf16[8,256,512]{2,1,0:T(8,128)(2,1)} %shard_map.28), calls=%async_computation | async-start | bytes 4194304 | tf_op jit(solution)/shard_map/all_to_all | solution.py:104
  13.0 0.0 copy-done
  13.0 2.2 %all-gather = bf16[512,512]{1,0:T(8,128)(2,1)S(1)} all-gather(bf16[256,512]{1,0:T(8,128)(2,1)S(1)} %copy-done), channel_id=2, replica_groups=mesh['yh'=2,'z'=8,'yl'=4,'core'=2,'x'=4] {'core'}, dimensions={0}, use_global_device_ids=true | all-gather | bytes 786432 | tf_op jit(solution)/shard_map/all_gather | solution.py:105
  15.2 3.4 %collective-permute-start = (bf16[2,256,256]{2,1,0:T(8,128)(2,1)S(1)}, bf16[2,256,256]{2,1,0:T(8,128)(2,1)S(1)}, u32[]{:S(2)}, u32[]{:S(2)}) collective-permute-start(bf16[2,256,256]{2,1,0:T(8,128)(2,1)S(1)} %constant_dynamic-slice_fusion), channel_id=1, source_target_pairs={{0,0},{1,2},{2,1},{3,3},{4,5},{5,7},{6,4},{7,6},{8,8},{9,10},{10,9... | collective-permute-start | bytes 786440 | tf_op jit(solution)/shard_map/ppermute | solution.py:24
  18.6 4.9 %collective-permute-done = bf16[2,256,256]{2,1,0:T(8,128)(2,1)S(1)} collective-permute-done((bf16[2,256,256]{2,1,0:T(8,128)(2,1)S(1)}, bf16[2,256,256]{2,1,0:T(8,128)(2,1)S(1)}, u32[]{:S(2)}, u32[]{:S(2)}) %collective-permute-start) | collective-permute-done | bytes 262176 | tf_op jit(solution)/shard_map/ppermute | solution.py:24
  23.4 15.1 %collective-permute-start.1 = (bf16[2,256,256]{2,1,0:T(8,128)(2,1)S(1)}, bf16[2,256,256]{2,1,0:T(8,128)(2,1)S(1)}, u32[]{:S(2)}, u32[]{:S(2)}) collective-permute-start(bf16[2,256,256]{2,1,0:T(8,128)(2,1)S(1)} %collective-permute-done), channel_id=1, source_target_pairs={{0,24},{8,16},{16,8},{24,0},{1,25},{9,17},{17,9},{25,1},{2,26},{10... | collective-permute-start | bytes 786440 | tf_op jit(solution)/shard_map/ppermute | solution.py:24
  38.5 1.9 %collective-permute-start.2 = (bf16[2,256,256]{2,1,0:T(8,128)(2,1)S(1)}, bf16[2,256,256]{2,1,0:T(8,128)(2,1)S(1)}, u32[]{:S(2)}, u32[]{:S(2)}) collective-permute-start(bf16[2,256,256]{2,1,0:T(8,128)(2,1)S(1)} %collective-permute-done), channel_id=1, source_target_pairs={{0,16},{8,24},{16,0},{24,8},{1,17},{9,25},{17,1},{25,9},{2,18},{10... | collective-permute-start | bytes 786440 | tf_op jit(solution)/shard_map/ppermute | solution.py:24
  40.4 2.5 %collective-permute-start.3 = (bf16[2,256,256]{2,1,0:T(8,128)(2,1)S(1)}, bf16[2,256,256]{2,1,0:T(8,128)(2,1)S(1)}, u32[]{:S(2)}, u32[]{:S(2)}) collective-permute-start(bf16[2,256,256]{2,1,0:T(8,128)(2,1)S(1)} %collective-permute-done), channel_id=1, source_target_pairs={{0,8},{8,0},{16,24},{24,16},{1,9},{9,1},{17,25},{25,17},{2,10},{10... | collective-permute-start | bytes 786440 | tf_op jit(solution)/shard_map/ppermute | solution.py:24
  42.9 2.8 %collective-permute-done.1 = bf16[2,256,256]{2,1,0:T(8,128)(2,1)S(1)} collective-permute-done((bf16[2,256,256]{2,1,0:T(8,128)(2,1)S(1)}, bf16[2,256,256]{2,1,0:T(8,128)(2,1)S(1)}, u32[]{:S(2)}, u32[]{:S(2)}) %collective-permute-start.1) | collective-permute-done | bytes 262176 | tf_op jit(solution)/shard_map/ppermute | solution.py:24
  45.7 1.9 %collective-permute-start.4 = (bf16[4,256,256]{2,1,0:T(8,128)(2,1)S(1)}, bf16[4,256,256]{2,1,0:T(8,128)(2,1)}, u32[]{:S(2)}, u32[]{:S(2)}) collective-permute-start(bf16[4,256,256]{2,1,0:T(8,128)(2,1)S(1)} %constant_dynamic-update-slice_fusion.own_a), channel_id=1, source_target_pairs={{0,4},{4,0},{1,5},{5,1},{2,6},{6,2},{3,7},{7,3},{8,12},{12,8},{9,1... | collective-permute-start | bytes 1572872 | tf_op jit(solution)/shard_map/ppermute | solution.py:24
  47.7 14.1 %collective-permute-done.2 = bf16[2,256,256]{2,1,0:T(8,128)(2,1)S(1)} collective-permute-done((bf16[2,256,256]{2,1,0:T(8,128)(2,1)S(1)}, bf16[2,256,256]{2,1,0:T(8,128)(2,1)S(1)}, u32[]{:S(2)}, u32[]{:S(2)}) %collective-permute-start.2) | collective-permute-done | bytes 262176 | tf_op jit(solution)/shard_map/ppermute | solution.py:24
  61.8 0.0 collective-permute-done.3
  61.8 2.0 %collective-permute-start.5 = (bf16[4,256,256]{2,1,0:T(8,128)(2,1)S(1)}, bf16[4,256,256]{2,1,0:T(8,128)(2,1)}, u32[]{:S(2)}, u32[]{:S(2)}) collective-permute-start(bf16[4,256,256]{2,1,0:T(8,128)(2,1)S(1)} %constant_dynamic-update-slice_fusion.2.own_b), channel_id=1, source_target_pairs={{0,4},{4,0},{1,5},{5,1},{2,6},{6,2},{3,7},{7,3},{8,12},{12,8},{9,1... | collective-permute-start | bytes 1572872 | tf_op jit(solution)/shard_map/ppermute | solution.py:24
  63.8 0.1 stack.85.place
  63.9 0.0 collective-permute-done.4.other_a
  63.9 1.8 %collective-permute-done.5.other_b = bf16[4,256,256]{2,1,0:T(8,128)(2,1)} collective-permute-done((bf16[4,256,256]{2,1,0:T(8,128)(2,1)S(1)}, bf16[4,256,256]{2,1,0:T(8,128)(2,1)}, u32[]{:S(2)}, u32[]{:S(2)}) %collective-permute-start.5) | collective-permute-done | bytes 524320 | tf_op jit(solution)/shard_map/ppermute | solution.py:24
  65.7 0.0 all-to-all-done.t_ref
  65.7 2.4 %shard_map.29 = f32[4,2,256,128]{3,2,1,0:T(8,128)S(1)} custom-call(s32[40]{0:T(128)S(1)} %stack.85.place, bf16[4,256,256]{2,1,0:T(8,128)(2,1)S(1)} %constant_dynamic-update-slice_fusion.own_a, bf16[4,256,256]{2,1,0:T(8,128)(2,1)S(1)} %constant_dynamic-update-slice_fusion.2.own_b, bf16[4,256,256]{2,1,0:T(8,128)(2,1)} %collective-permute-done.4.other_a, ...), custom_call_target="tpu_custom_call" | custom-call | tf_op jit(solution)/shard_map/pallas_call | solution.py:93
  68.2 17.0 %all_to_all.10 = f32[4,2,256,128]{3,2,1,0:T(8,128)S(1)} all-to-all(f32[4,2,256,128]{3,2,1,0:T(8,128)S(1)} %shard_map.29), channel_id=1, replica_groups=mesh['yh'=2,'z'=8,'yl'=4,'core'=2,'x'=4] {'x'}, dimensions={0} | all-to-all | bytes 2097152 | tf_op jit(solution)/shard_map/all_to_all | solution.py:122
  85.2 0.1 reduce_sum.9
  85.3 5.6 %collective-permute-start.6 = (f32[256,128]{1,0:T(8,128)S(1)}, f32[256,128]{1,0:T(8,128)S(1)}, u32[]{:S(2)}, u32[]{:S(2)}) collective-permute-start(f32[256,128]{1,0:T(8,128)S(1)} %slice_bitcast_fusion), channel_id=1, source_target_pairs={{0,256},{256,0},{1,257},{257,1},{2,258},{258,2},{3,259},{259,3},{4... | collective-permute-start | bytes 393224 | tf_op jit(solution)/shard_map/ppermute | solution.py:24
  90.9 6.5 %collective-permute-done.6 = f32[256,128]{1,0:T(8,128)S(1)} collective-permute-done((f32[256,128]{1,0:T(8,128)S(1)}, f32[256,128]{1,0:T(8,128)S(1)}, u32[]{:S(2)}, u32[]{:S(2)}) %collective-permute-start.6) | collective-permute-done | bytes 131104 | tf_op jit(solution)/shard_map/ppermute | solution.py:24
  97.5 0.7 fusion
  (6 shorter events, 0.1 us)
Async XLA Ops:
  2.5 10.5 %copy-start = (bf16[256,512]{1,0:T(8,128)(2,1)S(1)}, bf16[256,512]{1,0:T(8,128)(2,1)}, u32[]{:S(2)}) copy-start(bf16[256,512]{1,0:T(8,128)(2,1)} %param.2) | copy-start | bytes 786436
  2.5 63.2 %all-to-all-start = ((bf16[8,256,512]{2,1,0:T(8,128)(2,1)}), bf16[8,256,512]{2,1,0:T(8,128)(2,1)S(1)}, u32[]{:S(2)}, u32[]{:S(2)}) async-start(bf16[8,256,512]{2,1,0:T(8,128)(2,1)} %shard_map.28), calls=%async_computation | async-start | bytes 4194304 | tf_op jit(solution)/shard_map/all_to_all | solution.py:104
  15.2 8.3 %collective-permute-start = (bf16[2,256,256]{2,1,0:T(8,128)(2,1)S(1)}, bf16[2,256,256]{2,1,0:T(8,128)(2,1)S(1)}, u32[]{:S(2)}, u32[]{:S(2)}) collective-permute-start(bf16[2,256,256]{2,1,0:T(8,128)(2,1)S(1)} %constant_dynamic-slice_fusion), channel_id=1, source_target_pairs={{0,0},{1,2},{2,1},{3,3},{4,5},{5,7},{6,4},{7,6},{8,8},{9,10},{10,9... | collective-permute-start | bytes 786440 | tf_op jit(solution)/shard_map/ppermute | solution.py:24
  23.4 22.3 %collective-permute-start.1 = (bf16[2,256,256]{2,1,0:T(8,128)(2,1)S(1)}, bf16[2,256,256]{2,1,0:T(8,128)(2,1)S(1)}, u32[]{:S(2)}, u32[]{:S(2)}) collective-permute-start(bf16[2,256,256]{2,1,0:T(8,128)(2,1)S(1)} %collective-permute-done), channel_id=1, source_target_pairs={{0,24},{8,16},{16,8},{24,0},{1,25},{9,17},{17,9},{25,1},{2,26},{10... | collective-permute-start | bytes 786440 | tf_op jit(solution)/shard_map/ppermute | solution.py:24
  38.5 23.2 %collective-permute-start.2 = (bf16[2,256,256]{2,1,0:T(8,128)(2,1)S(1)}, bf16[2,256,256]{2,1,0:T(8,128)(2,1)S(1)}, u32[]{:S(2)}, u32[]{:S(2)}) collective-permute-start(bf16[2,256,256]{2,1,0:T(8,128)(2,1)S(1)} %collective-permute-done), channel_id=1, source_target_pairs={{0,16},{8,24},{16,0},{24,8},{1,17},{9,25},{17,1},{25,9},{2,18},{10... | collective-permute-start | bytes 786440 | tf_op jit(solution)/shard_map/ppermute | solution.py:24
  40.4 21.3 %collective-permute-start.3 = (bf16[2,256,256]{2,1,0:T(8,128)(2,1)S(1)}, bf16[2,256,256]{2,1,0:T(8,128)(2,1)S(1)}, u32[]{:S(2)}, u32[]{:S(2)}) collective-permute-start(bf16[2,256,256]{2,1,0:T(8,128)(2,1)S(1)} %collective-permute-done), channel_id=1, source_target_pairs={{0,8},{8,0},{16,24},{24,16},{1,9},{9,1},{17,25},{25,17},{2,10},{10... | collective-permute-start | bytes 786440 | tf_op jit(solution)/shard_map/ppermute | solution.py:24
  45.7 18.2 %collective-permute-start.4 = (bf16[4,256,256]{2,1,0:T(8,128)(2,1)S(1)}, bf16[4,256,256]{2,1,0:T(8,128)(2,1)}, u32[]{:S(2)}, u32[]{:S(2)}) collective-permute-start(bf16[4,256,256]{2,1,0:T(8,128)(2,1)S(1)} %constant_dynamic-update-slice_fusion.own_a), channel_id=1, source_target_pairs={{0,4},{4,0},{1,5},{5,1},{2,6},{6,2},{3,7},{7,3},{8,12},{12,8},{9,1... | collective-permute-start | bytes 1572872 | tf_op jit(solution)/shard_map/ppermute | solution.py:24
  61.8 3.9 %collective-permute-start.5 = (bf16[4,256,256]{2,1,0:T(8,128)(2,1)S(1)}, bf16[4,256,256]{2,1,0:T(8,128)(2,1)}, u32[]{:S(2)}, u32[]{:S(2)}) collective-permute-start(bf16[4,256,256]{2,1,0:T(8,128)(2,1)S(1)} %constant_dynamic-update-slice_fusion.2.own_b), channel_id=1, source_target_pairs={{0,4},{4,0},{1,5},{5,1},{2,6},{6,2},{3,7},{7,3},{8,12},{12,8},{9,1... | collective-permute-start | bytes 1572872 | tf_op jit(solution)/shard_map/ppermute | solution.py:24
  85.3 12.2 %collective-permute-start.6 = (f32[256,128]{1,0:T(8,128)S(1)}, f32[256,128]{1,0:T(8,128)S(1)}, u32[]{:S(2)}, u32[]{:S(2)}) collective-permute-start(f32[256,128]{1,0:T(8,128)S(1)} %slice_bitcast_fusion), channel_id=1, source_target_pairs={{0,256},{256,0},{1,257},{257,1},{2,258},{258,2},{3,259},{259,3},{4... | collective-permute-start | bytes 393224 | tf_op jit(solution)/shard_map/ppermute | solution.py:24
